TPU v7x, 32 devices: a whole 2x2x4 slice. The times are simulated.
32 devices in a mesh: copy: 2 (over y), dp: 4 (over x, core), fsdp: 4 (over z).
Axes of the slice: x: 2, y: 2, z: 4, core: 2. Of those that a mesh axis runs over, the one named last changes fastest.
Arguments:
- queries: bfloat16 [2, 16, 256, 2560], P('copy', ('dp', 'fsdp')), may hold values from -25 to 25
- keys: bfloat16 [2, 16, 256, 2560], P('copy', ('dp', 'fsdp')), may hold values from -25 to 25
- values: bfloat16 [2, 16, 256, 2560], P('copy', ('dp', 'fsdp')), may hold values from -6 to 6
- residual: bfloat16 [2, 16, 256, 2560], P('copy', ('dp', 'fsdp')), may hold values from -6 to 6
- event_ids: int32 [16, 256], P(('dp', 'fsdp')), may hold values from 0 to 1023
- lengths: int32 [16], replicated, may hold values from 8 to 256, as said below
- type_weight: float32 [1024], replicated, may hold values from 0.25 to 4
- w_out: bfloat16 [2, 2560, 2560], P('copy', 'fsdp'), may hold values from -0.125 to 0.125
- gain: float32 [2, 2560], P('copy'), may hold values from 0.5 to 1.5
Outputs:
- loss: float32 [2, 16], P('copy', ('dp', 'fsdp'))
- d_queries: bfloat16 [2, 16, 256, 2560], P('copy', ('dp', 'fsdp'))
- d_keys: bfloat16 [2, 16, 256, 2560], P('copy', ('dp', 'fsdp'))
- d_values: bfloat16 [2, 16, 256, 2560], P('copy', ('dp', 'fsdp'))
- d_wo: float32 [2, 2560, 2560], P('copy', 'fsdp')
Inputs may be any that keep to these rules, and one draw needn't show every extreme that they name: `lengths`: every history has at least 8 valid events and some history has all 256.
All inputs are finite; a program needn't handle non-finite values.
Results may differ from a plain program's by a relative error of at most 0.02.
Values may be sent and summed in bfloat16 or wider, within the bound.
No kernel may reach another device: no remote copies, remote signals or barrier semaphores. Data moves between devices by JAX's collectives and lax.ppermute only.
A program may use at most 128 MiB of HBM per device.

v0:
```python
import jax
import jax.numpy as jnp
from jax import lax
from jax.sharding import PartitionSpec as P

DH = 128


def partner_2(value, axis, bit):
    return lax.ppermute(value, axis, [(i, i ^ 1 << bit) for i in range(lax.axis_size(axis))])


def to_gathered(matrix, groups, replicas):
    rows = matrix.shape[0]
    width = matrix.shape[1] // (groups * replicas)
    return matrix.reshape(rows, groups, replicas, width).transpose(0, 2, 1, 3).reshape(rows, -1)


def from_gathered(matrix, groups, replicas):
    rows = matrix.shape[0]
    width = matrix.shape[1] // (groups * replicas)
    return matrix.reshape(rows, replicas, groups, width).transpose(0, 2, 1, 3).reshape(rows, -1)


def body(queries, keys, values, residual, event_ids, lengths, type_weight, w_out, gain):
    seq = queries.shape[2]
    heads_width = queries.shape[3]
    width = residual.shape[3]
    head_size = DH
    heads = heads_width // head_size
    groups = lax.axis_size("fsdp")
    replicas = lax.axis_size("dp")
    shard_rows = w_out.shape[1]
    own = lax.axis_index(("dp", "fsdp"))
    length = lengths[own]
    count = jnp.sum(lengths).astype(jnp.float32)
    my_gain = gain[0]
    block = shard_rows // replicas
    piece = lax.dynamic_slice_in_dim(w_out[0], lax.axis_index("dp") * block, block, 0)
    full_weight = lax.all_gather(piece, ("dp", "fsdp"), axis=0, tiled=True)
    arrange = lambda matrix: to_gathered(matrix, groups, replicas)
    restore = lambda matrix: from_gathered(matrix, groups, replicas)
    query_heads = queries[0, 0].reshape(seq, heads, head_size)
    key_heads = keys[0, 0].reshape(seq, heads, head_size)
    value_heads = values[0, 0].reshape(seq, heads, head_size)
    scale = jnp.sqrt(jnp.float32(head_size))
    scores = (
        jnp.einsum("qhd,khd->hqk", query_heads, key_heads, preferred_element_type=jnp.float32)
        / scale
    )
    rows = jnp.arange(seq, dtype=jnp.int32)[:, None]
    cols = jnp.arange(seq, dtype=jnp.int32)[None, :]
    valid = (cols <= rows) & (cols < length)
    scores = jnp.where(valid[None], scores, jnp.float32(-1e30))
    probs = jax.nn.softmax(scores, axis=-1)
    probs_b = probs.astype(jnp.bfloat16)
    attn = (
        jnp.einsum("hqk,khd->qhd", probs_b, value_heads, preferred_element_type=jnp.float32)
        .reshape(seq, heads_width)
        .astype(jnp.bfloat16)
    )
    hidden = residual[0, 0].astype(jnp.float32) + jnp.dot(
        arrange(attn), full_weight, preferred_element_type=jnp.float32
    )
    inv = lax.rsqrt(jnp.mean(hidden * hidden, axis=-1, keepdims=True) + 1e-06)
    normed = hidden * inv
    feat = normed * my_gain[None, :]
    partner = partner_2(feat.astype(jnp.bfloat16), "copy", 0)
    type_count = type_weight.shape[0]
    matches = event_ids[0][:, None] == jnp.arange(type_count, dtype=jnp.int32)[None, :]
    looked_up = jnp.sum(jnp.where(matches, type_weight[None, :], jnp.float32(0.0)), axis=-1)
    live = jnp.arange(seq, dtype=jnp.int32) < length
    tok_w = jnp.where(live, looked_up, jnp.float32(0.0))
    diff = feat - partner.astype(jnp.float32)
    loss = jnp.sum(tok_w * jnp.sum(diff * diff, axis=-1)) / (width * count)
    dfeat = 2.0 * tok_w[:, None] * diff / (width * count)
    scaled = dfeat * my_gain[None, :]
    d_hidden = (inv * (scaled - normed * jnp.mean(normed * scaled, axis=-1, keepdims=True))).astype(
        jnp.bfloat16
    )
    partial_term = jnp.dot(attn.T, d_hidden, preferred_element_type=jnp.float32).astype(
        jnp.bfloat16
    )
    row_sum = lax.psum_scatter(partial_term, "fsdp", scatter_dimension=0, tiled=True).astype(
        jnp.float32
    )
    d_wo = lax.psum(row_sum.astype(jnp.bfloat16), "dp").astype(jnp.float32)
    d_attn_arranged = lax.dot_general(
        d_hidden, full_weight, (((1,), (1,)), ((), ())), preferred_element_type=jnp.float32
    )
    d_attn = restore(d_attn_arranged).astype(jnp.bfloat16)
    d_heads = d_attn.reshape(seq, heads, head_size)
    d_values = (
        jnp.einsum("hqk,qhd->khd", probs_b, d_heads, preferred_element_type=jnp.float32)
        .reshape(seq, heads_width)
        .astype(jnp.bfloat16)
    )
    dprob = jnp.einsum("qhd,khd->hqk", d_heads, value_heads, preferred_element_type=jnp.float32)
    delta = jnp.sum(dprob * probs, axis=-1, keepdims=True)
    ds = (probs * (dprob - delta) / scale).astype(jnp.bfloat16)
    d_queries = (
        jnp.einsum("hqk,khd->qhd", ds, key_heads, preferred_element_type=jnp.float32)
        .reshape(seq, heads_width)
        .astype(jnp.bfloat16)
    )
    d_keys = (
        jnp.einsum("hqk,qhd->khd", ds, query_heads, preferred_element_type=jnp.float32)
        .reshape(seq, heads_width)
        .astype(jnp.bfloat16)
    )
    return (
        loss.reshape(1, 1),
        d_queries[None, None],
        d_keys[None, None],
        d_values[None, None],
        d_wo[None],
    )


def solution(mesh):
    in_specs = (
        P("copy", ("dp", "fsdp"), None, None),
        P("copy", ("dp", "fsdp"), None, None),
        P("copy", ("dp", "fsdp"), None, None),
        P("copy", ("dp", "fsdp"), None, None),
        P(("dp", "fsdp"), None),
        P(),
        P(),
        P("copy", "fsdp", None),
        P("copy", None),
    )
    out_specs = (
        P("copy", ("dp", "fsdp")),
        P("copy", ("dp", "fsdp"), None, None),
        P("copy", ("dp", "fsdp"), None, None),
        P("copy", ("dp", "fsdp"), None, None),
        P("copy", "fsdp", None),
    )
    return jax.shard_map(body, mesh=mesh, in_specs=in_specs, out_specs=out_specs, check_vma=False)
```

profile of v0, /device:TPU:1, one launch (start us, length us, event | category | flops | bytes accessed | tf_op | source)
XLA Modules:
  0.0 475.2 jit_solution(5678256151510799368)
XLA Ops:
  7.2 0.0 copy-start
  7.2 0.0 all-gather.3.cloned.1.call-start
  7.2 1.9 copy-done
  9.1 1.0 constant_dynamic-slice_fusion
  10.1 0.0 all-gather.3.cloned.1.call-update
  10.1 0.0 reduce-scatter.2.cloned.1.call-start
  10.1 1.7 copy.66
  11.9 0.0 copy-start.13
  11.9 1.4 copy.62
  13.3 2.5 copy.63
  15.8 0.6 dynamic_slice.8
  16.4 0.6 iota_compare_fusion.2
  17.1 0.1 fusion.35
  17.2 0.0 copy-done.6
  17.2 5.5 %fusion.44 = (f32[20,256]{1,0:T(8,128)S(1)}, f32[20,256,256]{1,2,0:T(8,128)}) fusion(pred[256,256]{0,1:T(8,128)(4,1)S(1)} %fusion.35, bf16[256,20,128]{0,2,1:T(8,128)(2,1)S(1)} %bitcast.61, bf16[256,20,128]{0,2,1:T(8,128)(2,1)} %bitcast.63), kind=kOutput, calls=%fused_computation.53 | convolution fusion | flops 340787456 | bytes 7950336 | tf_op jit(solution)/shard_map/sub | solution.py:55
  22.8 3.1 convolution_convert_fusion.1
  25.8 0.0 copy-start.10
  25.8 1.2 copy.68
  27.1 89.8 %all-gather.3.cloned.1.call-done = bf16[1,2560,2560]{2,1,0:T(8,128)(2,1)} async-done(((bf16[1,160,2560]{2,1,0:T(8,128)(2,1)}), bf16[1,2560,2560]{2,1,0:T(8,128)(2,1)}) %all-gather.3.cloned.1.call-update) | async-done | bytes 13107216 | tf_op jit(solution)/shard_map/all_gather | solution.py:40
  116.9 0.0 copy-done.8
  116.9 9.2 %multiply_reduce_fusion.3 = (f32[256]{0:T(256)S(1)}, f32[256,2560]{1,0:T(8,128)S(1)}) fusion(bf16[256,2560]{0,1:T(8,128)(2,1)} %bitcast.54, bf16[1,2560,2560]{2,1,0:T(8,128)(2,1)} %all-gather.3.cloned.1.call-done, bf16[1,1,256,2560]{3,2,1,0:T(8,128)(2,1)} %param.12), kind=kOutput, calls=%fused_computation.22 | convolution fusion | flops 3358064384 | bytes 18351104 | tf_op jit(solution)/shard_map/dot_general | solution.py:62
  126.0 0.0 copy-start.11
  126.1 0.0 copy-start.12
  126.1 1.3 multiply_convert_fusion.2
  127.4 1.2 collective-permute-start
  128.6 0.7 reduce_sum.77
  130.0 0.2 select_reduce_fusion
  130.3 0.8 select_multiply_fusion
  131.0 26.8 %collective-permute-done = bf16[256,2560]{1,0:T(8,128)(2,1)} collective-permute-done((bf16[256,2560]{1,0:T(8,128)(2,1)}, bf16[256,2560]{1,0:T(8,128)(2,1)}, u32[]{:S(2)}, u32[]{:S(2)}) %collective-permute-start) | collective-permute-done | bytes 1310752 | tf_op jit(solution)/shard_map/ppermute | solution.py:10
  157.9 2.4 multiply_reduce_fusion.1
  160.3 8.6 %convolution_convert_fusion = bf16[2560,2560]{1,0:T(8,128)(2,1)} fusion(bf16[256,2560]{0,1:T(8,128)(2,1)S(1)} %bitcast.66, f32[256,2560]{1,0:T(8,128)S(1)} %get-tuple-element.30, bf16[256,2560]{1,0:T(8,128)(2,1)} %collective-permute-done, f32[256]{0:T(256)S(1)} %broadcast_multiply_fusion, f32[]{:T(128)S(6)} %mul.95, f32[256]{0:T(256)S(1)} %select_multiply_fusion, ...), kind=kOutput, calls=%fused_computation.2 | convolution fusion | flops 3369205760 | bytes 18363396 | tf_op jit(solution)/shard_map/dot_general | solution.py:81
  168.9 0.0 reduce-scatter.2.cloned.1.call-update
  169.0 0.2 all-reduce.2.cloned.1.call-start
  169.2 1.2 multiply_reduce_fusion.4
  171.1 11.3 %fusion.11 = bf16[256,2560]{1,0:T(8,128)(2,1)} fusion(bf16[1,2560,2560]{2,1,0:T(8,128)(2,1)} %all-gather.3.cloned.1.call-done, f32[256,2560]{1,0:T(8,128)S(1)} %get-tuple-element.30, bf16[256,2560]{1,0:T(8,128)(2,1)} %collective-permute-done, f32[256]{0:T(256)S(1)} %broadcast_multiply_fusion, f32[]{:T(128)S(6)} %mul.95, f32[256]{0:T(256)S(1)} %select_multiply_fusion, ...), kind=kOutput, calls=%fused_computation.14 | convolution fusion | flops 3363307520 | bytes 18363396 | tf_op jit(solution)/shard_map/dot_general | solution.py:88
  182.4 1.6 copy.69
  184.0 1.1 copy.70
  185.1 202.9 %reduce-scatter.2.cloned.1.call-done = bf16[640,2560]{1,0:T(8,128)(2,1)} async-done(((bf16[2560,2560]{1,0:T(8,128)(2,1)}), bf16[640,2560]{1,0:T(8,128)(2,1)}) %reduce-scatter.2.cloned.1.call-update) | async-done | bytes 3276816 | tf_op jit(solution)/shard_map/reduce_scatter | solution.py:84
  388.1 0.0 all-reduce.2.cloned.1.call-update
  388.1 3.2 fusion.45
  391.3 10.9 %fusion.27 = bf16[20,256,128]{1,2,0:T(8,128)(2,1)} fusion(bf16[256,20,128]{0,2,1:T(8,128)(2,1)} %bitcast.64, f32[20,256,256]{1,2,0:T(8,128)} %fusion.45, f32[20,256,256]{1,2,0:T(8,128)} %get-tuple-element.28, f32[20,256]{1,0:T(8,128)S(1)} %get-tuple-element.27), kind=kOutput, calls=%fused_computation.30 | convolution fusion | flops 345380096 | bytes 13127680 | tf_op jit(solution)/shard_map/hqk,khd->qhd/dot_general | solution.py:102
  402.2 2.5 copy.76
  404.7 10.1 %fusion.30 = bf16[20,256,128]{1,2,0:T(8,128)(2,1)} fusion(bf16[256,20,128]{0,2,1:T(8,128)(2,1)S(1)} %bitcast.62, f32[20,256,256]{1,2,0:T(8,128)} %fusion.45, f32[20,256,256]{1,2,0:T(8,128)} %get-tuple-element.28, f32[20,256]{1,0:T(8,128)S(1)} %get-tuple-element.27), kind=kOutput, calls=%fused_computation.31 | convolution fusion | flops 345380096 | bytes 13127680 | tf_op jit(solution)/shard_map/hqk,qhd->khd/dot_general | solution.py:107
  414.8 2.4 copy.77
  417.2 4.6 convolution_convert_fusion.2
  421.8 2.6 copy.78
  424.4 37.6 %all-reduce.2.cloned.1.call-done = bf16[1,640,2560]{2,1,0:T(8,128)(2,1)} async-done(((bf16[1,640,2560]{2,1,0:T(8,128)(2,1)}), bf16[1,640,2560]{2,1,0:T(8,128)(2,1)}) %all-reduce.2.cloned.1.call-update) | async-done | bytes 3276816 | tf_op jit(solution)/shard_map/psum | solution.py:87
  461.9 5.6 %broadcast_in_dim.54 = f32[1,640,2560]{2,1,0:T(8,128)} convert(bf16[1,640,2560]{2,1,0:T(8,128)(2,1)} %all-reduce.2.cloned.1.call-done) | non-fusion elementwise | flops 1638400 | bytes 9830400 | tf_op jit(solution)/shard_map/broadcast_in_dim | solution.py:116
  (23 shorter events, 0.1 us)
Async XLA Ops:
  7.2 1.9 copy-start
  7.2 109.7 %all-gather.3.cloned.1.call-start = ((), (), s32[]{:S(2)}) async-start(), calls=%async_computation.3 | async-start | bytes 13926400 | tf_op jit(solution)/shard_map/all_gather | solution.py:40
  10.1 1.8 copy-start.5
  10.1 378.0 %reduce-scatter.2.cloned.1.call-start = ((), (), s32[]{:S(2)}) async-start(), calls=%async_computation.1 | async-start | bytes 16384000 | tf_op jit(solution)/shard_map/reduce_scatter | solution.py:84
  11.8 10.9 %copy-start.2 = (bf16[1,1,256,2560]{2,3,1,0:T(8,128)(2,1)}, bf16[1,1,256,2560]{2,3,1,0:T(8,128)(2,1)S(1)}, u32[]{:S(2)}) copy-start(bf16[1,1,256,2560]{2,3,1,0:T(8,128)(2,1)S(1)} %copy.66) | copy-start | bytes 3932164
  11.9 4.0 copy-start.13
  13.3 3.9 copy-start.6
  25.8 91.1 %copy-start.8 = (bf16[20,256,128]{1,2,0:T(8,128)(2,1)}, bf16[20,256,128]{1,2,0:T(8,128)(2,1)S(1)}, u32[]{:S(2)}) copy-start(bf16[20,256,128]{1,2,0:T(8,128)(2,1)S(1)} %convolution_convert_fusion.1) | copy-start | bytes 3932164
  25.8 1.2 copy-start.10
  126.0 4.0 copy-start.11
  126.1 4.0 copy-start.12
  127.4 30.4 %collective-permute-start = (bf16[256,2560]{1,0:T(8,128)(2,1)}, bf16[256,2560]{1,0:T(8,128)(2,1)}, u32[]{:S(2)}, u32[]{:S(2)}) collective-permute-start(bf16[256,2560]{1,0:T(8,128)(2,1)} %multiply_convert_fusion.2), channel_id=1, source_target_pairs={{0,16},{16,0},{1,17},{17,1},{2,18},{18,2},{3,19},{19,3},{4,20},{20... | collective-permute-start | bytes 3932168 | tf_op jit(solution)/shard_map/ppermute | solution.py:10
  130.0 30.3 %copy-start.9 = (bf16[20,256,128]{1,2,0:T(8,128)(2,1)S(1)}, bf16[20,256,128]{1,2,0:T(8,128)(2,1)}, u32[]{:S(2)}) copy-start(bf16[20,256,128]{1,2,0:T(8,128)(2,1)} %copy-done.8) | copy-start | bytes 3932164
  169.0 293.0 %all-reduce.2.cloned.1.call-start = ((), (), s32[]{:S(2)}) async-start(), calls=%async_computation.2 | async-start | bytes 6553600 | tf_op jit(solution)/shard_map/psum | solution.py:87
  184.0 204.1 %copy-start.3 = (bf16[1,1,256,2560]{2,3,1,0:T(8,128)(2,1)S(1)}, bf16[1,1,256,2560]{2,3,1,0:T(8,128)(2,1)}, u32[]{:S(2)}) copy-start(bf16[1,1,256,2560]{2,3,1,0:T(8,128)(2,1)} %copy-done.2) | copy-start | bytes 3932164
  185.1 203.0 %copy-start.4 = (bf16[256,4,4,160]{0,3,2,1:T(8,128)(2,1)S(1)}, bf16[256,4,4,160]{0,3,2,1:T(8,128)(2,1)}, u32[]{:S(2)}) copy-start(bf16[256,4,4,160]{0,3,2,1:T(8,128)(2,1)} %copy.70) | copy-start | bytes 3932164
  402.2 2.5 copy-start.7
  421.8 45.8 %copy-start.1 = (bf16[1,640,2560]{2,1,0:T(8,128)(2,1)S(1)}, bf16[1,640,2560]{2,1,0:T(8,128)(2,1)}, u32[]{:S(2)}) copy-start(bf16[1,640,2560]{2,1,0:T(8,128)(2,1)} %param.16) | copy-start | bytes 9830404
Sparse Core Ops, SparseCore 0:
  10.3 106.5 all-gather.2
  169.1 218.9 reduce-scatter.1
  390.4 71.4 all-reduce.1
where the time goes:
time: 476 us; the launch traced here: 475 us
  waiting for transfers between devices  357 us (75%)
  matrix products  66.3 us (14%)
  local copies, waits for them, and re-layouts  20.6 us (4%)
  between operations  16.4 us (3%)
  other arithmetic  13.1 us (3%)
    reduce_scatter x1, waiting for transfers between devices, body(): lax.psum_scatter(partial_term, 'fsdp', scatter_dimension=0, tiled=True)  203 us
    all_gather x1, waiting for transfers between devices, body(): full_weight = lax.all_gather(piece, ('dp', 'fsdp'), axis=0, tiled=True)  89.8 us
    psum x1, waiting for transfers between devices, body(): d_wo = lax.psum(row_sum.astype(jnp.bfloat16), 'dp').astype(jnp.float32)  37.6 us
    ppermute x1, waiting for transfers between devices, partner_2(): lax.ppermute(value, axis, [(i, i ^ 1 << bit) for i in range(lax.axis_size...  26.8 us
    unnamed x34, local copies, waits for them, and re-layouts  15.1 us
    dot_general x1, matrix products, body(): lax.dot_general(d_hidden, full_weight, (((1,), (1,)), ((), ())), preferre...  11.3 us
    dot_general x1, matrix products, body(): jnp.einsum('hqk,khd->qhd', ds, key_heads, preferred_element_type=jnp.floa...  10.9 us
    dot_general x1, matrix products, body(): jnp.einsum('hqk,qhd->khd', ds, query_heads, preferred_element_type=jnp.fl...  10.1 us
  transfers between devices with their start and end apart: 4, of which 4 were waited for; matrix products, arithmetic and copies ran while one was open for 15% of the time, Pallas kernels for 0%

commit v1 on v0

v1 whole, which is shorter than its diff:
```python
import jax
import jax.numpy as jnp
from jax import lax
from jax.experimental import pallas as pl
from jax.experimental.pallas import tpu as pltpu
from jax.sharding import PartitionSpec as P

DH = 128
LANES = 128
NEG = -1e30


def swap(value, axis, bit):
    return lax.ppermute(value, axis, [(i, i ^ bit) for i in range(lax.axis_size(axis))])


def bits_of(size):
    return [1 << j for j in range(size.bit_length() - 1)]


def ring_shift(value, axis):
    size = lax.axis_size(axis)
    return lax.ppermute(value, axis, [(i, (i + 1) % size) for i in range(size)])


def head_probs(query, key, valid):
    scores = lax.dot_general(query, key, (((1,), (1,)), ((), ())), preferred_element_type=jnp.float32)
    scores = jnp.where(valid, scores * (DH**-0.5), NEG)
    top = jnp.max(scores, axis=-1, keepdims=True)
    exps = jnp.exp(scores - top)
    return exps * (1.0 / jnp.sum(exps, axis=-1, keepdims=True))


def valid_mask(seq, length):
    rows = lax.broadcasted_iota(jnp.int32, (seq, seq), 0)
    cols = lax.broadcasted_iota(jnp.int32, (seq, seq), 1)
    return (cols <= rows) & (cols < length)


def forward_kernel(length_ref, q_ref, k_ref, v_ref, out_ref):
    seq, wide = q_ref.shape
    valid = valid_mask(seq, length_ref[0])
    for head in range(wide // DH):
        at = slice(head * DH, (head + 1) * DH)
        probs = head_probs(q_ref[:, at], k_ref[:, at], valid).astype(jnp.bfloat16)
        out_ref[:, at] = jnp.dot(probs, v_ref[:, at], preferred_element_type=jnp.float32).astype(out_ref.dtype)


def backward_kernel(length_ref, q_ref, k_ref, v_ref, one_ref, two_ref, dq_ref, dk_ref, dv_ref):
    seq, wide = q_ref.shape
    valid = valid_mask(seq, length_ref[0])
    for head in range(wide // DH):
        at = slice(head * DH, (head + 1) * DH)
        query, key, value = q_ref[:, at], k_ref[:, at], v_ref[:, at]
        probs = head_probs(query, key, valid)
        d_attn = (one_ref[:, at].astype(jnp.float32) + two_ref[:, at].astype(jnp.float32)).astype(jnp.bfloat16)
        dv_ref[:, at] = lax.dot_general(
            probs.astype(jnp.bfloat16), d_attn, (((0,), (0,)), ((), ())), preferred_element_type=jnp.float32
        ).astype(dv_ref.dtype)
        dprob = lax.dot_general(d_attn, value, (((1,), (1,)), ((), ())), preferred_element_type=jnp.float32)
        delta = jnp.sum(dprob * probs, axis=-1, keepdims=True)
        ds = (probs * (dprob - delta) * (DH**-0.5)).astype(jnp.bfloat16)
        dq_ref[:, at] = jnp.dot(ds, key, preferred_element_type=jnp.float32).astype(dq_ref.dtype)
        dk_ref[:, at] = lax.dot_general(
            ds, query, (((0,), (0,)), ((), ())), preferred_element_type=jnp.float32
        ).astype(dk_ref.dtype)


def group_width(heads_width):
    heads = heads_width // DH
    return DH * max(g for g in (4, 2, 1) if heads % g == 0)


def attention_call(kernel, length, arrays, outs, products):
    seq, wide = arrays[0].shape
    group = group_width(wide)
    block = pl.BlockSpec((seq, group), lambda i, *_: (0, i))
    shape = jax.ShapeDtypeStruct((seq, wide), jnp.bfloat16)
    return pl.pallas_call(
        kernel,
        grid_spec=pltpu.PrefetchScalarGridSpec(
            num_scalar_prefetch=1,
            grid=(wide // group,),
            in_specs=[block] * len(arrays),
            out_specs=[block] * outs,
        ),
        out_shape=[shape] * outs,
        cost_estimate=pl.CostEstimate(
            flops=products * 2 * seq * seq * wide,
            bytes_accessed=2 * seq * wide * (len(arrays) + outs),
            transcendentals=seq * seq * wide // DH,
        ),
        compiler_params=pltpu.CompilerParams(vmem_limit_bytes=32 << 20),
    )(length.reshape(1), *arrays)


def chunks_of(wide):
    lanes = -(-wide // LANES)
    first = min(wide, -(-lanes * 3 // 5) * LANES)
    return [(0, first), (first, wide)] if first < wide else [(0, wide)]


def body(queries, keys, values, residual, event_ids, lengths, type_weight, w_out, gain):
    seq, heads_width = queries.shape[2:]
    width = residual.shape[3]
    parts = lax.axis_size("fsdp")
    team = lax.axis_size("dp")
    bits = bits_of(team)
    shard_rows = w_out.shape[1]
    part = lax.axis_index("fsdp")
    member = lax.axis_index("dp")
    own = lax.axis_index(("dp", "fsdp"))
    length = lengths[own]
    count = jnp.sum(lengths).astype(jnp.float32)
    wide = width // team
    chunks = chunks_of(wide)

    weights = []
    for low, high in chunks:
        block = lax.dynamic_slice(w_out[0], (0, member * wide + low), (shard_rows, high - low))
        whole = jnp.zeros((heads_width, high - low), block.dtype)
        whole = lax.dynamic_update_slice(whole, block, (part * shard_rows, 0))
        for step in range(1, parts):
            block = ring_shift(block, "fsdp")
            at = lax.rem(part + parts - step, parts) * shard_rows
            whole = lax.dynamic_update_slice(whole, block, (at, 0))
        weights.append(whole)

    order = [0]
    for bit in reversed(bits):
        order = order + [s ^ bit for s in order]

    home = residual[0, 0]
    rest = {}
    for s in order:
        block = lax.dynamic_slice(home, (0, (member ^ s) * wide), (seq, wide))
        rest[s] = swap(block, "dp", s) if s else block
    rest = jnp.concatenate([rest[s] for s in order], axis=0)

    types = jnp.arange(type_weight.shape[0], dtype=jnp.int32)
    matches = event_ids[0][:, None] == types[None, :]
    looked_up = jnp.sum(jnp.where(matches, type_weight[None, :], jnp.float32(0.0)), axis=-1)
    tok_w = jnp.where(jnp.arange(seq, dtype=jnp.int32) < length, looked_up, jnp.float32(0.0))
    tok_w = tok_w.reshape(1, seq)
    for bit in reversed(bits):
        tok_w = jnp.concatenate([tok_w, swap(tok_w, "dp", bit)], axis=0)
    tok_w = tok_w.reshape(-1, 1)

    q, k, v = queries[0, 0], keys[0, 0], values[0, 0]
    (attn_own,) = attention_call(forward_kernel, length, (q, k, v), 1, 2)
    attn = [attn_own]
    for bit in reversed(bits):
        attn = attn + [swap(a, "dp", bit) for a in attn]
    attn = jnp.concatenate(attn, axis=0)

    def team_sum(value):
        value = value.reshape((2,) * len(bits) + (-1,))
        for axis, bit in enumerate(bits):
            value = value + jnp.flip(swap(value, "dp", bit), axis)
        return value.reshape(team * seq, -1)

    my_gain = lax.dynamic_slice(gain[0], (member * wide,), (wide,))
    hidden, sent, gains = [], [], []
    for (low, high), weight in zip(chunks, weights):
        h = rest[:, low:high].astype(jnp.float32) + jnp.dot(attn, weight, preferred_element_type=jnp.float32)
        g = my_gain[None, low:high]
        hidden.append(h)
        gains.append(g)
        sent.append(swap((h * g).astype(jnp.bfloat16), "copy", 1))
    square = sum(jnp.sum(h * h, axis=-1, keepdims=True) for h in hidden)
    inv = lax.rsqrt(team_sum(square) / width + 1e-06)
    inv_other = swap(inv, "copy", 1)

    normed = [h * inv for h in hidden]
    diff = [n * g - p.astype(jnp.float32) * inv_other for n, g, p in zip(normed, gains, sent)]
    scaled = [2.0 * tok_w * d / (width * count) * g for d, g in zip(diff, gains)]
    square = sum(jnp.sum(d * d, axis=-1, keepdims=True) for d in diff)
    cross = sum(jnp.sum(n * s, axis=-1, keepdims=True) for n, s in zip(normed, scaled))
    both = team_sum(jnp.concatenate([square, cross], axis=1))
    loss = jnp.sum(tok_w[:seq] * both[:seq, :1]) / (width * count)
    mean = both[:, 1:] / width
    d_hidden = [(inv * (s - n * mean)).astype(jnp.bfloat16) for s, n in zip(scaled, normed)]

    d_attn = sum(
        lax.dot_general(d, w, (((1,), (1,)), ((), ())), preferred_element_type=jnp.float32)
        for d, w in zip(d_hidden, weights)
    ).astype(jnp.bfloat16)
    for bit in bits[:-1]:
        half = d_attn.shape[0] // 2
        d_attn = (d_attn[:half].astype(jnp.float32) + swap(d_attn[half:], "dp", bit).astype(jnp.float32)).astype(jnp.bfloat16)
    kept, got = d_attn[:seq], swap(d_attn[seq:], "dp", bits[-1])
    d_queries, d_keys, d_values = attention_call(backward_kernel, length, (q, k, v, kept, got), 3, 5)

    out = jnp.zeros((shard_rows, width), jnp.float32)
    for (low, high), d in zip(chunks, d_hidden):
        terms = lax.dot_general(attn, d, (((0,), (0,)), ((), ())), preferred_element_type=jnp.float32).astype(jnp.bfloat16)

        def term(step):
            at = lax.rem(part + parts - step, parts) * shard_rows
            return lax.dynamic_slice(terms, (at, 0), (shard_rows, high - low))

        total = term(1 % parts)
        for step in range(1, parts):
            got = ring_shift(total, "fsdp")
            total = (got.astype(jnp.float32) + term((step + 1) % parts).astype(jnp.float32)).astype(jnp.bfloat16)
        pieces = {0: total}
        for bit in reversed(bits):
            pieces.update({s ^ bit: swap(p, "dp", bit) for s, p in pieces.items()})
        for s, piece in pieces.items():
            out = lax.dynamic_update_slice(out, piece.astype(jnp.float32), (0, (member ^ s) * wide + low))
    return (
        loss.reshape(1, 1),
        d_queries[None, None],
        d_keys[None, None],
        d_values[None, None],
        out[None],
    )


def solution(mesh):
    whole = P("copy", ("dp", "fsdp"), None, None)
    in_specs = (
        whole,
        whole,
        whole,
        whole,
        P(("dp", "fsdp"), None),
        P(),
        P(),
        P("copy", "fsdp", None),
        P("copy", None),
    )
    out_specs = (P("copy", ("dp", "fsdp")), whole, whole, whole, P("copy", "fsdp", None))
    return jax.shard_map(body, mesh=mesh, in_specs=in_specs, out_specs=out_specs, check_vma=False)
```

time: 476 us -> 293 us (0.62)
  waiting for transfers between devices: 357 us -> 124 us
  starting transfers between devices: 1.5 us -> 38.7 us
  matrix products: 66.3 us -> 33.4 us
  local copies, waits for them, and re-layouts: 20.6 us -> 44.7 us
  Pallas kernels: 0 us -> 22.6 us
  between operations: 16.4 us -> 3.52 us
  other arithmetic: 13.1 us -> 25 us
    reduce_scatter x1 -> x0, waiting for transfers between devices: 203 us -> none  [body(): lax.psum_scatter(partial_term, 'fsdp', scatter_dimension=0, tiled=True)]
    ppermute x1 -> x35, waiting for transfers between devices: 26.8 us -> 124 us  [the longest x23 70.9 us: swap(): lax.ppermute(value, axis, [(i, i ^ bit) for i in range(lax.axis_size(axis...]
    all_gather x1 -> x0, waiting for transfers between devices: 89.8 us -> none  [body(): full_weight = lax.all_gather(piece, ('dp', 'fsdp'), axis=0, tiled=True)]
    psum x1 -> x0, waiting for transfers between devices: 37.6 us -> none  [body(): d_wo = lax.psum(row_sum.astype(jnp.bfloat16), 'dp').astype(jnp.float32)]
    ppermute x1 -> x35, starting transfers between devices: 1.2 us -> 38.7 us  [the longest x23 32 us: swap(): lax.ppermute(value, axis, [(i, i ^ bit) for i in range(lax.axis_size(axis...]
    dot_general x8 -> x6, matrix products: 60.8 us -> 33.4 us  [the longest x2 14.9 us: body(): jnp.dot(attn, weight, preferred_element_type=jnp.float32)]
    pallas_call x0 -> x2, Pallas kernels: none -> 22.6 us  [attention_call(): pl.pallas_call(kernel, grid_spec=pltpu.PrefetchScalarGridSpec(num_scalar_...]
    dynamic_slice x1 -> x7, local copies, waits for them, and re-layouts: 0.97 us -> 11.6 us  [the longest x5 9.89 us: body(): block = lax.dynamic_slice(home, (0, (member ^ s) * wide), (seq, wide))]
  transfers between devices with their start and end apart: 4 -> 35, of which waited for: 4 -> 16; matrix products, arithmetic and copies ran while one was open for 15% -> 22% of each run, Pallas kernels for 0% -> 0%
where the time goes in v1:
time: 293 us; the launch traced here: 292 us
  waiting for transfers between devices  124 us (42%)
  local copies, waits for them, and re-layouts  44.7 us (15%)
  starting transfers between devices  38.7 us (13%)
  matrix products  33.4 us (11%)
  other arithmetic  25 us (9%)
  Pallas kernels  22.6 us (8%)
  between operations  3.52 us (1%)
    ppermute x23, waiting for transfers between devices, swap(): lax.ppermute(value, axis, [(i, i ^ bit) for i in range(lax.axis_size(axis...  70.9 us
    ppermute x12, waiting for transfers between devices, ring_shift(): return lax.ppermute(value, axis, [(i, (i + 1) % size) for i in range(size)])  53 us
    ppermute x23, starting transfers between devices, swap(): lax.ppermute(value, axis, [(i, i ^ bit) for i in range(lax.axis_size(axis...  32 us
    pallas_call x2, Pallas kernels, attention_call(): pl.pallas_call(kernel, grid_spec=pltpu.PrefetchScalarGridSpec(num_scalar_...  22.6 us
    dot_general x2, matrix products, body(): jnp.dot(attn, weight, preferred_element_type=jnp.float32)  14.9 us
    dynamic_slice x5, local copies, waits for them, and re-layouts, body(): block = lax.dynamic_slice(home, (0, (member ^ s) * wide), (seq, wide))  9.89 us
    dynamic_update_slice x8, other arithmetic, body(): lax.dynamic_update_slice(out, piece.astype(jnp.float32), (0, (member ^ s)...  9.88 us
    dot_general x2, matrix products, body(): lax.dot_general(attn, d, (((0,), (0,)), ((), ())), preferred_element_type...  9.86 us
  transfers between devices with their start and end apart: 35, of which 16 were waited for; matrix products, arithmetic and copies ran while one was open for 22% of the time, Pallas kernels for 0%

profile of v1, /device:TPU:1, one launch (start us, length us, event | category | flops | bytes accessed | tf_op | source)
XLA Modules:
  0.0 291.6 jit_solution(11290462330716896859)
XLA Ops:
  5.9 6.7 %shard_map.128 = bf16[256,2560]{1,0:T(8,128)(2,1)S(1)} custom-call(s32[1]{0:T(128)} %dynamic_slice.60.length_ref, bf16[256,2560]{1,0:T(8,128)(2,1)S(1)} %bitcast.58, bf16[256,2560]{1,0:T(8,128)(2,1)S(1)} %bitcast.60, bf16[256,2560]{1,0:T(8,128)(2,1)S(1)} %bitcast.62), custom_call_target="tpu_custom_call" | custom-call | flops 671088640 | bytes 5242880 | tf_op jit(solution)/shard_map/pallas_call | solution.py:79
  12.6 2.1 collective-permute-start.3
  14.9 1.9 constant_dynamic-update-slice_fusion.7
  19.2 1.8 constant_dynamic-update-slice_fusion.3
  22.4 2.4 constant_dynamic-slice_fusion.7
  24.7 1.9 copy.26
  26.6 1.5 collective-permute-start.1
  28.2 1.9 copy.27
  30.2 7.6 %collective-permute-done.9 = bf16[640,256]{1,0:T(8,128)(2,1)} collective-permute-done((bf16[640,256]{1,0:T(8,128)(2,1)}, bf16[640,256]{1,0:T(8,128)(2,1)}, u32[]{:S(2)}, u32[]{:S(2)}) %collective-permute-start.9) | collective-permute-done | bytes 327712 | tf_op jit(solution)/shard_map/ppermute | solution.py:23
  37.8 1.8 collective-permute-start.4
  39.6 3.7 %collective-permute-done.3 = bf16[256,2560]{1,0:T(8,128)(2,1)} collective-permute-done((bf16[256,2560]{1,0:T(8,128)(2,1)S(1)}, bf16[256,2560]{1,0:T(8,128)(2,1)}, u32[]{:S(2)}, u32[]{:S(2)}) %collective-permute-start.3) | collective-permute-done | bytes 1310752 | tf_op jit(solution)/shard_map/ppermute | solution.py:14
  43.3 2.1 collective-permute-start.5
  45.4 1.9 collective-permute-start.7
  47.2 1.9 copy.25
  51.2 1.5 collective-permute-start.10
  52.7 1.9 copy.24
  54.9 3.6 %collective-permute-done = bf16[256,640]{0,1:T(8,128)(2,1)} collective-permute-done((bf16[256,640]{0,1:T(8,128)(2,1)}, bf16[256,640]{0,1:T(8,128)(2,1)}, u32[]{:S(2)}, u32[]{:S(2)}) %collective-permute-start) | collective-permute-done | bytes 327712 | tf_op jit(solution)/shard_map/ppermute | solution.py:14
  59.9 8.3 %collective-permute-done.10 = bf16[640,256]{1,0:T(8,128)(2,1)} collective-permute-done((bf16[640,256]{1,0:T(8,128)(2,1)}, bf16[640,256]{1,0:T(8,128)(2,1)}, u32[]{:S(2)}, u32[]{:S(2)}) %collective-permute-start.10) | collective-permute-done | bytes 327712 | tf_op jit(solution)/shard_map/ppermute | solution.py:23
  68.7 1.7 constant_dynamic-update-slice_fusion.2
  71.6 1.8 constant_dynamic-update-slice_fusion.1
  73.3 5.5 %collective-permute-done.11 = bf16[640,256]{1,0:T(8,128)(2,1)S(1)} collective-permute-done((bf16[640,256]{1,0:T(8,128)(2,1)}, bf16[640,256]{1,0:T(8,128)(2,1)S(1)}, u32[]{:S(2)}, u32[]{:S(2)}) %collective-permute-start.11) | collective-permute-done | bytes 327712 | tf_op jit(solution)/shard_map/ppermute | solution.py:23
  80.8 8.7 %collective-permute-done.8 = bf16[640,384]{1,0:T(8,128)(2,1)S(1)} collective-permute-done((bf16[640,384]{1,0:T(8,128)(2,1)}, bf16[640,384]{1,0:T(8,128)(2,1)S(1)}, u32[]{:S(2)}, u32[]{:S(2)}) %collective-permute-start.8) | collective-permute-done | bytes 491552 | tf_op jit(solution)/shard_map/ppermute | solution.py:23
  89.5 7.4 %multiply_convert_fusion.3 = (bf16[1024,256]{0,1:T(8,128)(2,1)}, f32[1024]{0:T(1024)S(1)}, f32[1024,256]{0,1:T(8,128)}) fusion(f32[256]{0:T(256)S(1)} %bitcast.90, bf16[2560,256]{1,0:T(8,128)(2,1)} %constant_dynamic-update-slice_fusion, bf16[256,2560]{1,0:T(8,128)(2,1)} %collective-permute-done.5, bf16[256,2560]{1,0:T(8,128)(2,1)} %collective-permute-done.4, ...), kind=kOutput, calls=%fused_computation.20 | convolution fusion | flops 1366555648 | bytes 9442304 | tf_op jit(solution)/shard_map/dot_general | solution.py:165
  97.0 7.4 %multiply_reduce_fusion.2 = (f32[1024]{0:T(1024)S(1)}, bf16[1024,384]{0,1:T(8,128)(2,1)}, f32[1024,384]{0,1:T(8,128)}) fusion(f32[384]{0:T(512)S(1)} %fusion.2, bf16[2560,384]{1,0:T(8,128)(2,1)S(1)} %constant_dynamic-update-slice_fusion.4, bf16[256,2560]{1,0:T(8,128)(2,1)} %collective-permute-done.5, bf16[256,2560]{1,0:T(8,128)(2,1)} %collective-permute-done.4, ...), kind=kOutput, calls=%fused_computation.11 | convolution fusion | flops 2036595712 | bytes 10360320 | tf_op jit(solution)/shard_map/dot_general | solution.py:165
  104.4 1.5 collective-permute-start.12
  114.9 24.7 %collective-permute-done.15 = f32[1024,1]{0,1:T(1,128)S(1)} collective-permute-done((f32[1024,1]{0,1:T(1,128)S(1)}, f32[1024,1]{0,1:T(1,128)S(1)}, u32[]{:S(2)}, u32[]{:S(2)}) %collective-permute-start.15) | collective-permute-done | bytes 4128 | tf_op jit(solution)/shard_map/ppermute | solution.py:14
  139.6 1.9 multiply_reduce_fusion.4
  141.5 1.9 multiply_reduce_fusion.1
  148.2 2.1 collective-permute-done.20
  153.1 5.8 %convolution_convert_fusion = bf16[2560,384]{1,0:T(8,128)(2,1)S(1)} fusion(f32[1024,384]{0,1:T(8,128)} %get-tuple-element.33, bf16[1024,384]{0,1:T(8,128)(2,1)} %collective-permute-done.14, f32[1024]{0:T(1024)S(1)} %fusion, f32[]{:T(128)S(6)} %mul.248, f32[1024]{0:T(1024)S(1)} %bitcast.73, f32[1024]{0:T(1024)S(1)} %bitcast.85, f32[384]{0:T(512)S(1)} %fusion.2, ...), kind=kOutput, calls=%fused_computation.3 | convolution fusion | flops 2039939072 | bytes 9586180 | tf_op jit(solution)/shard_map/dot_general | solution.py:196
  160.4 3.4 %fusion.5 = f32[1024,2560]{1,0:T(8,128)S(1)} fusion(bf16[2560,256]{1,0:T(8,128)(2,1)} %constant_dynamic-update-slice_fusion, f32[1024,256]{0,1:T(8,128)S(1)} %copy-done.11, bf16[1024,256]{0,1:T(8,128)(2,1)} %collective-permute-done.16, f32[1024]{0:T(1024)S(1)} %fusion, f32[]{:T(128)S(6)} %mul.248, f32[1024]{0:T(1024)S(1)} %bitcast.74, ...), kind=kOutput, calls=%fused_computation.70 | convolution fusion | flops 1345323008 | bytes 13386756 | tf_op jit(solution)/shard_map/dot_general | solution.py:185
  163.7 5.3 %add_convert_fusion = bf16[1024,2560]{1,0:T(8,128)(2,1)S(1)} fusion(f32[1024,2560]{1,0:T(8,128)S(1)} %fusion.5, bf16[2560,384]{1,0:T(8,128)(2,1)S(1)} %constant_dynamic-update-slice_fusion.4, f32[1024,384]{0,1:T(8,128)S(1)} %copy-done.10, bf16[1024,384]{0,1:T(8,128)(2,1)} %collective-permute-done.14, f32[1024]{0:T(1024)S(1)} %fusion, f32[]{:T(128)S(6)} %mul.248, ...), kind=kOutput, calls=%fused_computation | convolution fusion | flops 2023227392 | bytes 20071940 | tf_op jit(solution)/shard_map/dot_general | solution.py:185
  169.1 1.7 slice.48
  170.8 1.9 copy-done.8
  172.7 1.5 collective-permute-start.21
  175.4 4.0 %convolution_convert_fusion.1 = bf16[2560,256]{1,0:T(8,128)(2,1)S(1)} fusion(f32[1024,256]{0,1:T(8,128)S(1)} %copy-done.12, bf16[1024,256]{0,1:T(8,128)(2,1)} %collective-permute-done.16, f32[1024]{0:T(1024)S(1)} %fusion, f32[]{:T(128)S(6)} %mul.248, f32[1024]{0:T(1024)S(1)} %bitcast.76, f32[1024]{0:T(1024)S(1)} %bitcast.88, f32[256]{0:T(256)S(1)} %bitcast.93, ...), kind=kOutput, calls=%fused_computation.4 | convolution fusion | flops 1366949888 | bytes 8143876 | tf_op jit(solution)/shard_map/dot_general | solution.py:196
  181.3 7.2 %collective-permute-done.24 = bf16[640,384]{1,0:T(8,128)(2,1)S(1)} collective-permute-done((bf16[640,384]{1,0:T(8,128)(2,1)S(1)}, bf16[640,384]{1,0:T(8,128)(2,1)S(1)}, u32[]{:S(2)}, u32[]{:S(2)}) %collective-permute-start.24) | collective-permute-done | bytes 491552 | tf_op jit(solution)/shard_map/ppermute | solution.py:23
  189.4 6.2 %collective-permute-done.29 = bf16[640,256]{1,0:T(8,128)(2,1)} collective-permute-done((bf16[640,256]{1,0:T(8,128)(2,1)}, bf16[640,256]{1,0:T(8,128)(2,1)}, u32[]{:S(2)}, u32[]{:S(2)}) %collective-permute-start.29) | collective-permute-done | bytes 327712 | tf_op jit(solution)/shard_map/ppermute | solution.py:23
  196.7 9.4 %collective-permute-done.25 = bf16[640,384]{1,0:T(8,128)(2,1)} collective-permute-done((bf16[640,384]{1,0:T(8,128)(2,1)}, bf16[640,384]{1,0:T(8,128)(2,1)}, u32[]{:S(2)}, u32[]{:S(2)}) %collective-permute-start.25) | collective-permute-done | bytes 491552 | tf_op jit(solution)/shard_map/ppermute | solution.py:23
  206.1 3.6 %broadcast_in_dim.88 = f32[1,640,2560]{2,1,0:T(8,128)} broadcast(f32[]{:T(128)} %constant.62.clone.1), dimensions={} | broadcast | bytes 6553604 | tf_op jit(solution)/shard_map/broadcast_in_dim | solution.py:216
  209.7 2.2 convert_dynamic-update-slice_fusion.3
  212.3 4.6 %collective-permute-start.27 = (bf16[640,384]{1,0:T(8,128)(2,1)S(1)}, bf16[640,384]{1,0:T(8,128)(2,1)S(1)}, u32[]{:S(2)}, u32[]{:S(2)}) collective-permute-start(bf16[640,384]{1,0:T(8,128)(2,1)S(1)} %get-tuple-element.18), channel_id=1, source_target_pairs={{0,4},{4,0},{8,12},{12,8},{1,5},{5,1},{9,13},{13,9},{2,6},{6,2},{1... | collective-permute-start | bytes 1474568 | tf_op jit(solution)/shard_map/ppermute | solution.py:14
  217.1 3.2 %collective-permute-done.26 = bf16[640,384]{1,0:T(8,128)(2,1)S(1)} collective-permute-done((bf16[640,384]{1,0:T(8,128)(2,1)S(1)}, bf16[640,384]{1,0:T(8,128)(2,1)S(1)}, u32[]{:S(2)}, u32[]{:S(2)}) %collective-permute-start.26) | collective-permute-done | bytes 491552 | tf_op jit(solution)/shard_map/ppermute | solution.py:14
  220.3 5.3 %collective-permute-start.28 = (bf16[640,384]{1,0:T(8,128)(2,1)S(1)}, bf16[640,384]{1,0:T(8,128)(2,1)S(1)}, u32[]{:S(2)}, u32[]{:S(2)}) collective-permute-start(bf16[640,384]{1,0:T(8,128)(2,1)S(1)} %collective-permute-done.26), channel_id=1, source_target_pairs={{0,4},{4,0},{8,12},{12,8},{1,5},{5,1},{9,13},{13,9},{2,6},{6,2},{1... | collective-permute-start | bytes 1474568 | tf_op jit(solution)/shard_map/ppermute | solution.py:14
  228.6 2.3 add_convert_fusion.1
  232.6 2.0 convert_dynamic-update-slice_fusion.7
  239.2 30.6 %collective-permute-done.32 = bf16[640,256]{1,0:T(8,128)(2,1)S(1)} collective-permute-done((bf16[640,256]{1,0:T(8,128)(2,1)}, bf16[640,256]{1,0:T(8,128)(2,1)S(1)}, u32[]{:S(2)}, u32[]{:S(2)}) %collective-permute-start.32) | collective-permute-done | bytes 327712 | tf_op jit(solution)/shard_map/ppermute | solution.py:14
  274.6 15.9 %shard_map.129 = (bf16[256,2560]{1,0:T(8,128)(2,1)}, bf16[256,2560]{1,0:T(8,128)(2,1)}, bf16[256,2560]{1,0:T(8,128)(2,1)}) custom-call(s32[1]{0:T(128)} %dynamic_slice.60.length_ref, bf16[256,2560]{1,0:T(8,128)(2,1)S(1)} %bitcast.59, bf16[256,2560]{1,0:T(8,128)(2,1)S(1)} %bitcast.61, bf16[256,2560]{1,0:T(8,128)(2,1)S(1)} %bitcast.63, ...), custom_call_target="tpu_custom_call" | custom-call | flops 1677721600 | bytes 10485760 | tf_op jit(solution)/shard_map/pallas_call | solution.py:79
  (142 shorter events, 53.0 us)
Async XLA Ops:
  0.6 52.1 %copy-start = (f32[1,2560]{1,0:T(1,128)S(1)}, f32[1,2560]{1,0:T(1,128)}, u32[]{:S(2)}) copy-start(f32[1,2560]{1,0:T(1,128)} %param.17) | copy-start | bytes 30724
  12.6 30.7 %collective-permute-start.3 = (bf16[256,2560]{1,0:T(8,128)(2,1)S(1)}, bf16[256,2560]{1,0:T(8,128)(2,1)}, u32[]{:S(2)}, u32[]{:S(2)}) collective-permute-start(bf16[256,2560]{1,0:T(8,128)(2,1)S(1)} %shard_map.128), channel_id=1, source_target_pairs={{0,8},{4,12},{8,0},{12,4},{1,9},{5,13},{9,1},{13,5},{2,10},{6,14},... | collective-permute-start | bytes 3932168 | tf_op jit(solution)/shard_map/ppermute | solution.py:14
  16.8 28.6 %collective-permute-start.6 = (bf16[640,384]{1,0:T(8,128)(2,1)}, bf16[640,384]{1,0:T(8,128)(2,1)}, u32[]{:S(2)}, u32[]{:S(2)}) collective-permute-start(bf16[640,384]{1,0:T(8,128)(2,1)} %get-tuple-element.22), channel_id=1, source_target_pairs={{0,1},{1,2},{2,3},{3,0},{4,5},{5,6},{6,7},{7,4},{8,9},{9,10},{10,1... | collective-permute-start | bytes 1474568 | tf_op jit(solution)/shard_map/ppermute | solution.py:23
  21.1 16.7 %collective-permute-start.9 = (bf16[640,256]{1,0:T(8,128)(2,1)}, bf16[640,256]{1,0:T(8,128)(2,1)}, u32[]{:S(2)}, u32[]{:S(2)}) collective-permute-start(bf16[640,256]{1,0:T(8,128)(2,1)} %get-tuple-element.20), channel_id=1, source_target_pairs={{0,1},{1,2},{2,3},{3,0},{4,5},{5,6},{6,7},{7,4},{8,9},{9,10},{10,1... | collective-permute-start | bytes 983048 | tf_op jit(solution)/shard_map/ppermute | solution.py:23
  24.7 29.9 %copy-start.18 = (f32[1024]{0:T(1024)S(1)}, f32[1024]{0:T(1024)}, u32[]{:S(2)}) copy-start(f32[1024]{0:T(1024)} %param.15) | copy-start | bytes 12292
  24.7 29.9 %copy-start.19 = (s32[1,256]{1,0:T(1,128)S(1)}, s32[1,256]{1,0:T(1,128)}, u32[]{:S(2)}) copy-start(s32[1,256]{1,0:T(1,128)} %param.13) | copy-start | bytes 3076
  26.6 22.5 %collective-permute-start.1 = (bf16[256,640]{0,1:T(8,128)(2,1)}, bf16[256,640]{0,1:T(8,128)(2,1)}, u32[]{:S(2)}, u32[]{:S(2)}) collective-permute-start(bf16[256,640]{0,1:T(8,128)(2,1)} %bitcast.70), channel_id=1, source_target_pairs={{0,4},{4,0},{8,12},{12,8},{1,5},{5,1},{9,13},{13,9},{2,6},{6,2},{1... | collective-permute-start | bytes 983048 | tf_op jit(solution)/shard_map/ppermute | solution.py:14
  30.0 21.1 %collective-permute-start.2 = (bf16[256,640]{0,1:T(8,128)(2,1)}, bf16[256,640]{0,1:T(8,128)(2,1)}, u32[]{:S(2)}, u32[]{:S(2)}) collective-permute-start(bf16[256,640]{0,1:T(8,128)(2,1)} %bitcast.69), channel_id=1, source_target_pairs={{0,12},{4,8},{8,4},{12,0},{1,13},{5,9},{9,5},{13,1},{2,14},{6,10},... | collective-permute-start | bytes 983048 | tf_op jit(solution)/shard_map/ppermute | solution.py:14
  37.8 51.7 %collective-permute-start.4 = (bf16[256,2560]{1,0:T(8,128)(2,1)S(1)}, bf16[256,2560]{1,0:T(8,128)(2,1)}, u32[]{:S(2)}, u32[]{:S(2)}) collective-permute-start(bf16[256,2560]{1,0:T(8,128)(2,1)S(1)} %shard_map.128), channel_id=1, source_target_pairs={{0,4},{4,0},{8,12},{12,8},{1,5},{5,1},{9,13},{13,9},{2,6},{6,2},{1... | collective-permute-start | bytes 3932168 | tf_op jit(solution)/shard_map/ppermute | solution.py:14
  43.3 46.2 %collective-permute-start.5 = (bf16[256,2560]{1,0:T(8,128)(2,1)}, bf16[256,2560]{1,0:T(8,128)(2,1)}, u32[]{:S(2)}, u32[]{:S(2)}) collective-permute-start(bf16[256,2560]{1,0:T(8,128)(2,1)} %collective-permute-done.3), channel_id=1, source_target_pairs={{0,4},{4,0},{8,12},{12,8},{1,5},{5,1},{9,13},{13,9},{2,6},{6,2},{1... | collective-permute-start | bytes 3932168 | tf_op jit(solution)/shard_map/ppermute | solution.py:14
  45.4 22.8 %collective-permute-start.7 = (bf16[640,384]{1,0:T(8,128)(2,1)}, bf16[640,384]{1,0:T(8,128)(2,1)}, u32[]{:S(2)}, u32[]{:S(2)}) collective-permute-start(bf16[640,384]{1,0:T(8,128)(2,1)} %collective-permute-done.6), channel_id=1, source_target_pairs={{0,1},{1,2},{2,3},{3,0},{4,5},{5,6},{6,7},{7,4},{8,9},{9,10},{10,1... | collective-permute-start | bytes 1474568 | tf_op jit(solution)/shard_map/ppermute | solution.py:23
  49.1 9.3 %collective-permute-start = (bf16[256,640]{0,1:T(8,128)(2,1)}, bf16[256,640]{0,1:T(8,128)(2,1)}, u32[]{:S(2)}, u32[]{:S(2)}) collective-permute-start(bf16[256,640]{0,1:T(8,128)(2,1)} %bitcast.68), channel_id=1, source_target_pairs={{0,8},{4,12},{8,0},{12,4},{1,9},{5,13},{9,1},{13,5},{2,10},{6,14},... | collective-permute-start | bytes 983048 | tf_op jit(solution)/shard_map/ppermute | solution.py:14
  51.2 17.0 %collective-permute-start.10 = (bf16[640,256]{1,0:T(8,128)(2,1)}, bf16[640,256]{1,0:T(8,128)(2,1)}, u32[]{:S(2)}, u32[]{:S(2)}) collective-permute-start(bf16[640,256]{1,0:T(8,128)(2,1)} %collective-permute-done.9), channel_id=1, source_target_pairs={{0,1},{1,2},{2,3},{3,0},{4,5},{5,6},{6,7},{7,4},{8,9},{9,10},{10,1... | collective-permute-start | bytes 983048 | tf_op jit(solution)/shard_map/ppermute | solution.py:23
  68.2 10.7 %collective-permute-start.11 = (bf16[640,256]{1,0:T(8,128)(2,1)}, bf16[640,256]{1,0:T(8,128)(2,1)S(1)}, u32[]{:S(2)}, u32[]{:S(2)}) collective-permute-start(bf16[640,256]{1,0:T(8,128)(2,1)} %collective-permute-done.10), channel_id=1, source_target_pairs={{0,1},{1,2},{2,3},{3,0},{4,5},{5,6},{6,7},{7,4},{8,9},{9,10},{10,1... | collective-permute-start | bytes 983048 | tf_op jit(solution)/shard_map/ppermute | solution.py:23
  68.2 21.2 %collective-permute-start.8 = (bf16[640,384]{1,0:T(8,128)(2,1)}, bf16[640,384]{1,0:T(8,128)(2,1)S(1)}, u32[]{:S(2)}, u32[]{:S(2)}) collective-permute-start(bf16[640,384]{1,0:T(8,128)(2,1)} %collective-permute-done.7), channel_id=1, source_target_pairs={{0,1},{1,2},{2,3},{3,0},{4,5},{5,6},{6,7},{7,4},{8,9},{9,10},{10,1... | collective-permute-start | bytes 1474568 | tf_op jit(solution)/shard_map/ppermute | solution.py:23
  71.6 18.0 %copy-start.15 = (bf16[1,1,256,640]{2,3,1,0:T(8,128)(2,1)S(1)}, bf16[1,1,256,640]{2,3,1,0:T(8,128)(2,1)}, u32[]{:S(2)}) copy-start(bf16[1,1,256,640]{2,3,1,0:T(8,128)(2,1)} %copy.24) | copy-start | bytes 983044
  97.0 10.8 %copy-start.20 = (s32[16]{0:T(128)S(1)}, s32[16]{0:T(128)}, u32[]{:S(2)}) copy-start(s32[16]{0:T(128)} %param.14) | copy-start | bytes 196
  104.4 6.2 %collective-permute-start.12 = (f32[2,2,256]{2,1,0:T(2,128)S(1)}, f32[2,2,256]{2,1,0:T(2,128)S(1)}, u32[]{:S(2)}, u32[]{:S(2)}) collective-permute-start(f32[2,2,256]{2,1,0:T(2,128)S(1)} %add.220), channel_id=1, source_target_pairs={{0,4},{4,0},{8,12},{12,8},{1,5},{5,1},{9,13},{13,9},{2,6},{6,2},{1... | collective-permute-start | bytes 12296 | tf_op jit(solution)/shard_map/ppermute | solution.py:14
  106.6 4.4 %collective-permute-start.17 = (f32[1,256]{1,0:T(1,128)S(1)}, f32[1,256]{1,0:T(1,128)S(1)}, u32[]{:S(2)}, u32[]{:S(2)}) collective-permute-start(f32[1,256]{1,0:T(1,128)S(1)} %compare_select_fusion), channel_id=1, source_target_pairs={{0,8},{4,12},{8,0},{12,4},{1,9},{5,13},{9,1},{13,5},{2,10},{6,14},... | collective-permute-start | bytes 3080 | tf_op jit(solution)/shard_map/ppermute | solution.py:14
  109.1 30.6 %collective-permute-start.16 = (bf16[1024,256]{0,1:T(8,128)(2,1)}, bf16[1024,256]{0,1:T(8,128)(2,1)}, u32[]{:S(2)}, u32[]{:S(2)}) collective-permute-start(bf16[1024,256]{0,1:T(8,128)(2,1)} %get-tuple-element.31), channel_id=1, source_target_pairs={{0,16},{16,0},{1,17},{17,1},{2,18},{18,2},{3,19},{19,3},{4,20},{20... | collective-permute-start | bytes 1572872 | tf_op jit(solution)/shard_map/ppermute | solution.py:14
  110.4 31.1 %collective-permute-start.14 = (bf16[1024,384]{0,1:T(8,128)(2,1)}, bf16[1024,384]{0,1:T(8,128)(2,1)}, u32[]{:S(2)}, u32[]{:S(2)}) collective-permute-start(bf16[1024,384]{0,1:T(8,128)(2,1)} %get-tuple-element.26), channel_id=1, source_target_pairs={{0,16},{16,0},{1,17},{17,1},{2,18},{18,2},{3,19},{19,3},{4,20},{20... | collective-permute-start | bytes 2359304 | tf_op jit(solution)/shard_map/ppermute | solution.py:14
  110.6 2.9 collective-permute-start.13
  111.0 3.9 %collective-permute-start.18 = (f32[2,256]{1,0:T(2,128)S(1)}, f32[2,256]{1,0:T(2,128)S(1)}, u32[]{:S(2)}, u32[]{:S(2)}) collective-permute-start(f32[2,256]{1,0:T(2,128)S(1)} %pad_maximum_fusion.3), channel_id=1, source_target_pairs={{0,4},{4,0},{8,12},{12,8},{1,5},{5,1},{9,13},{13,9},{2,6},{6,2},{1... | collective-permute-start | bytes 6152 | tf_op jit(solution)/shard_map/ppermute | solution.py:14
  113.6 27.9 %copy-start.9 = (f32[1024,384]{0,1:T(8,128)S(1)}, f32[1024,384]{0,1:T(8,128)}, u32[]{:S(2)}) copy-start(f32[1024,384]{0,1:T(8,128)} %get-tuple-element.33) | copy-start | bytes 4718596
  113.6 26.0 %collective-permute-start.15 = (f32[1024,1]{0,1:T(1,128)S(1)}, f32[1024,1]{0,1:T(1,128)S(1)}, u32[]{:S(2)}, u32[]{:S(2)}) collective-permute-start(f32[1024,1]{0,1:T(1,128)S(1)} %rsqrt.20), channel_id=1, source_target_pairs={{0,16},{16,0},{1,17},{17,1},{2,18},{18,2},{3,19},{19,3},{4,20},{20... | collective-permute-start | bytes 12296 | tf_op jit(solution)/shard_map/ppermute | solution.py:14
  145.8 2.0 collective-permute-start.19
  147.8 2.5 collective-permute-start.20
  153.1 7.3 %copy-start.11 = (f32[1024,256]{0,1:T(8,128)S(1)}, f32[1024,256]{0,1:T(8,128)}, u32[]{:S(2)}) copy-start(f32[1024,256]{0,1:T(8,128)} %get-tuple-element.34) | copy-start | bytes 3145732
  159.9 14.3 %collective-permute-start.23 = (bf16[640,384]{1,0:T(8,128)(2,1)}, bf16[640,384]{1,0:T(8,128)(2,1)}, u32[]{:S(2)}, u32[]{:S(2)}) collective-permute-start(bf16[640,384]{1,0:T(8,128)(2,1)} %constant_dynamic-slice_fusion.2), channel_id=1, source_target_pairs={{0,1},{1,2},{2,3},{3,0},{4,5},{5,6},{6,7},{7,4},{8,9},{9,10},{10,1... | collective-permute-start | bytes 1474568 | tf_op jit(solution)/shard_map/ppermute | solution.py:23
  172.7 55.9 %collective-permute-start.21 = (bf16[512,2560]{1,0:T(8,128)(2,1)}, bf16[512,2560]{1,0:T(8,128)(2,1)}, u32[]{:S(2)}, u32[]{:S(2)}) collective-permute-start(bf16[512,2560]{1,0:T(8,128)(2,1)} %slice.48), channel_id=1, source_target_pairs={{0,4},{4,0},{8,12},{12,8},{1,5},{5,1},{9,13},{13,9},{2,6},{6,2},{1... | collective-permute-start | bytes 7864328 | tf_op jit(solution)/shard_map/ppermute | solution.py:14
  175.3 13.1 %collective-permute-start.24 = (bf16[640,384]{1,0:T(8,128)(2,1)S(1)}, bf16[640,384]{1,0:T(8,128)(2,1)S(1)}, u32[]{:S(2)}, u32[]{:S(2)}) collective-permute-start(bf16[640,384]{1,0:T(8,128)(2,1)S(1)} %add_convert_fusion.4), channel_id=1, source_target_pairs={{0,1},{1,2},{2,3},{3,0},{4,5},{5,6},{6,7},{7,4},{8,9},{9,10},{10,1... | collective-permute-start | bytes 1474568 | tf_op jit(solution)/shard_map/ppermute | solution.py:23
  181.3 14.3 %copy-start.17 = (bf16[2560,256]{1,0:T(8,128)(2,1)S(1)}, bf16[2560,256]{1,0:T(8,128)(2,1)}, u32[]{:S(2)}) copy-start(bf16[2560,256]{1,0:T(8,128)(2,1)} %copy-done.16) | copy-start | bytes 3932164
  181.3 14.3 %collective-permute-start.29 = (bf16[640,256]{1,0:T(8,128)(2,1)}, bf16[640,256]{1,0:T(8,128)(2,1)}, u32[]{:S(2)}, u32[]{:S(2)}) collective-permute-start(bf16[640,256]{1,0:T(8,128)(2,1)} %constant_dynamic-slice_fusion.1), channel_id=1, source_target_pairs={{0,1},{1,2},{2,3},{3,0},{4,5},{5,6},{6,7},{7,4},{8,9},{9,10},{10,1... | collective-permute-start | bytes 983048 | tf_op jit(solution)/shard_map/ppermute | solution.py:23
  189.4 16.8 %collective-permute-start.25 = (bf16[640,384]{1,0:T(8,128)(2,1)}, bf16[640,384]{1,0:T(8,128)(2,1)}, u32[]{:S(2)}, u32[]{:S(2)}) collective-permute-start(bf16[640,384]{1,0:T(8,128)(2,1)} %add_convert_fusion.3), channel_id=1, source_target_pairs={{0,1},{1,2},{2,3},{3,0},{4,5},{5,6},{6,7},{7,4},{8,9},{9,10},{10,1... | collective-permute-start | bytes 1474568 | tf_op jit(solution)/shard_map/ppermute | solution.py:23
  196.7 20.3 %collective-permute-start.30 = (bf16[640,256]{1,0:T(8,128)(2,1)S(1)}, bf16[640,256]{1,0:T(8,128)(2,1)S(1)}, u32[]{:S(2)}, u32[]{:S(2)}) collective-permute-start(bf16[640,256]{1,0:T(8,128)(2,1)S(1)} %add_convert_fusion.7), channel_id=1, source_target_pairs={{0,1},{1,2},{2,3},{3,0},{4,5},{5,6},{6,7},{7,4},{8,9},{9,10},{10,1... | collective-permute-start | bytes 983048 | tf_op jit(solution)/shard_map/ppermute | solution.py:23
  206.1 22.5 %slice-start = ((s8[5242880]{0:T(1024)(128)(4,1)}), s8[4194304]{0:T(1024)(128)(4,1)S(1)}, s32[]{:S(2)}) async-start(s8[5242880]{0:T(1024)(128)(4,1)} %bitcast.64), calls=%async_computation | async-start | bytes 8388608
  209.7 18.9 %slice-start.1 = ((s8[5242880]{0:T(1024)(128)(4,1)}), s8[1048576]{0:T(1024)(128)(4,1)S(1)}, s32[]{:S(2)}) async-start(s8[5242880]{0:T(1024)(128)(4,1)} %bitcast.64), calls=%async_computation.1 | async-start | bytes 2097152
  211.9 8.4 %collective-permute-start.26 = (bf16[640,384]{1,0:T(8,128)(2,1)S(1)}, bf16[640,384]{1,0:T(8,128)(2,1)S(1)}, u32[]{:S(2)}, u32[]{:S(2)}) collective-permute-start(bf16[640,384]{1,0:T(8,128)(2,1)S(1)} %get-tuple-element.18), channel_id=1, source_target_pairs={{0,8},{4,12},{8,0},{12,4},{1,9},{5,13},{9,1},{13,5},{2,10},{6,14},... | collective-permute-start | bytes 1474568 | tf_op jit(solution)/shard_map/ppermute | solution.py:14
  212.3 14.3 %collective-permute-start.27 = (bf16[640,384]{1,0:T(8,128)(2,1)S(1)}, bf16[640,384]{1,0:T(8,128)(2,1)S(1)}, u32[]{:S(2)}, u32[]{:S(2)}) collective-permute-start(bf16[640,384]{1,0:T(8,128)(2,1)S(1)} %get-tuple-element.18), channel_id=1, source_target_pairs={{0,4},{4,0},{8,12},{12,8},{1,5},{5,1},{9,13},{13,9},{2,6},{6,2},{1... | collective-permute-start | bytes 1474568 | tf_op jit(solution)/shard_map/ppermute | solution.py:14
  217.0 15.5 %collective-permute-start.31 = (bf16[640,256]{1,0:T(8,128)(2,1)S(1)}, bf16[640,256]{1,0:T(8,128)(2,1)S(1)}, u32[]{:S(2)}, u32[]{:S(2)}) collective-permute-start(bf16[640,256]{1,0:T(8,128)(2,1)S(1)} %add_convert_fusion.6), channel_id=1, source_target_pairs={{0,1},{1,2},{2,3},{3,0},{4,5},{5,6},{6,7},{7,4},{8,9},{9,10},{10,1... | collective-permute-start | bytes 983048 | tf_op jit(solution)/shard_map/ppermute | solution.py:23
  220.3 7.3 %collective-permute-start.28 = (bf16[640,384]{1,0:T(8,128)(2,1)S(1)}, bf16[640,384]{1,0:T(8,128)(2,1)S(1)}, u32[]{:S(2)}, u32[]{:S(2)}) collective-permute-start(bf16[640,384]{1,0:T(8,128)(2,1)S(1)} %collective-permute-done.26), channel_id=1, source_target_pairs={{0,4},{4,0},{8,12},{12,8},{1,5},{5,1},{9,13},{13,9},{2,6},{6,2},{1... | collective-permute-start | bytes 1474568 | tf_op jit(solution)/shard_map/ppermute | solution.py:14
  232.2 41.1 %collective-permute-start.22 = (bf16[256,2560]{1,0:T(8,128)(2,1)}, bf16[256,2560]{1,0:T(8,128)(2,1)}, u32[]{:S(2)}, u32[]{:S(2)}) collective-permute-start(bf16[256,2560]{1,0:T(8,128)(2,1)} %get-tuple-element.23), channel_id=1, source_target_pairs={{0,8},{4,12},{8,0},{12,4},{1,9},{5,13},{9,1},{13,5},{2,10},{6,14},... | collective-permute-start | bytes 3932168 | tf_op jit(solution)/shard_map/ppermute | solution.py:14
  234.6 35.2 %collective-permute-start.32 = (bf16[640,256]{1,0:T(8,128)(2,1)}, bf16[640,256]{1,0:T(8,128)(2,1)S(1)}, u32[]{:S(2)}, u32[]{:S(2)}) collective-permute-start(bf16[640,256]{1,0:T(8,128)(2,1)} %get-tuple-element.16), channel_id=1, source_target_pairs={{0,8},{4,12},{8,0},{12,4},{1,9},{5,13},{9,1},{13,5},{2,10},{6,14},... | collective-permute-start | bytes 983048 | tf_op jit(solution)/shard_map/ppermute | solution.py:14
  236.6 36.7 %copy-start.3 = (bf16[1,1,256,2560]{3,2,1,0:T(8,128)(2,1)S(1)}, bf16[1,1,256,2560]{3,2,1,0:T(8,128)(2,1)}, u32[]{:S(2)}) copy-start(bf16[1,1,256,2560]{3,2,1,0:T(8,128)(2,1)} %param.9) | copy-start | bytes 3932164
  236.7 34.8 %collective-permute-start.33 = (bf16[640,256]{1,0:T(8,128)(2,1)}, bf16[640,256]{1,0:T(8,128)(2,1)S(1)}, u32[]{:S(2)}, u32[]{:S(2)}) collective-permute-start(bf16[640,256]{1,0:T(8,128)(2,1)} %get-tuple-element.16), channel_id=1, source_target_pairs={{0,4},{4,0},{8,12},{12,8},{1,5},{5,1},{9,13},{13,9},{2,6},{6,2},{1... | collective-permute-start | bytes 983048 | tf_op jit(solution)/shard_map/ppermute | solution.py:14
  239.2 34.1 %copy-start.5 = (bf16[1,1,256,2560]{3,2,1,0:T(8,128)(2,1)S(1)}, bf16[1,1,256,2560]{3,2,1,0:T(8,128)(2,1)}, u32[]{:S(2)}) copy-start(bf16[1,1,256,2560]{3,2,1,0:T(8,128)(2,1)} %param.10) | copy-start | bytes 3932164
  269.8 2.6 collective-permute-start.34
  274.6 15.9 %copy-start.1 = (f32[1,2560]{1,0:T(1,128)S(1)}, f32[1,2560]{1,0:T(1,128)}, u32[]{:S(2)}) copy-start(f32[1,2560]{1,0:T(1,128)} %param.17) | copy-start | bytes 30724
  (10 other events, 26.8 us)

commit v2 on v1

v2 whole, which is shorter than its diff:
```python
import functools
import math

import jax
import jax.numpy as jnp
from jax import lax
from jax.experimental import pallas as pl
from jax.experimental.pallas import tpu as pltpu
from jax.sharding import PartitionSpec as P

DH = 128
LANES = 128
NEG = -1e30
MIB = 1 << 20
SCALE = MIB


def cost(micros):
    return pl.CostEstimate(flops=0, bytes_accessed=int(micros * SCALE), transcendentals=0)


def vmem(blocks):
    size = sum(math.prod(shape) * jnp.dtype(kind).itemsize for shape, kind in blocks)
    return pltpu.CompilerParams(vmem_limit_bytes=min(2 * size + 6 * MIB, 60 * MIB))


def swap(value, axis, bit):
    return lax.ppermute(value, axis, [(i, i ^ bit) for i in range(lax.axis_size(axis))])


def bits_of(size):
    return [1 << j for j in range(size.bit_length() - 1)]


def head_probs(query, key, valid):
    scores = lax.dot_general(query, key, (((1,), (1,)), ((), ())), preferred_element_type=jnp.float32)
    scores = jnp.where(valid, scores * (DH**-0.5), NEG)
    top = jnp.max(scores, axis=-1, keepdims=True)
    exps = jnp.exp(scores - top)
    return exps * (1.0 / jnp.sum(exps, axis=-1, keepdims=True))


def valid_mask(seq, length):
    rows = lax.broadcasted_iota(jnp.int32, (seq, seq), 0)
    cols = lax.broadcasted_iota(jnp.int32, (seq, seq), 1)
    return (cols <= rows) & (cols < length)


def forward_kernel(length_ref, q_ref, k_ref, v_ref, out_ref):
    seq, wide = q_ref.shape
    valid = valid_mask(seq, length_ref[0])
    for head in range(wide // DH):
        at = slice(head * DH, (head + 1) * DH)
        probs = head_probs(q_ref[:, at], k_ref[:, at], valid).astype(jnp.bfloat16)
        out_ref[:, at] = jnp.dot(probs, v_ref[:, at], preferred_element_type=jnp.float32).astype(out_ref.dtype)


def backward_kernel(length_ref, q_ref, k_ref, v_ref, one_ref, two_ref, *refs):
    dq_ref, dk_ref, dv_ref = refs[-3:]
    seq, wide = q_ref.shape
    valid = valid_mask(seq, length_ref[0])
    for head in range(wide // DH):
        at = slice(head * DH, (head + 1) * DH)
        query, key, value = q_ref[:, at], k_ref[:, at], v_ref[:, at]
        probs = head_probs(query, key, valid)
        d_attn = (one_ref[:, at].astype(jnp.float32) + two_ref[:, at].astype(jnp.float32)).astype(jnp.bfloat16)
        dv_ref[:, at] = lax.dot_general(
            probs.astype(jnp.bfloat16), d_attn, (((0,), (0,)), ((), ())), preferred_element_type=jnp.float32
        ).astype(dv_ref.dtype)
        dprob = lax.dot_general(d_attn, value, (((1,), (1,)), ((), ())), preferred_element_type=jnp.float32)
        delta = jnp.sum(dprob * probs, axis=-1, keepdims=True)
        ds = (probs * (dprob - delta) * (DH**-0.5)).astype(jnp.bfloat16)
        dq_ref[:, at] = jnp.dot(ds, key, preferred_element_type=jnp.float32).astype(dq_ref.dtype)
        dk_ref[:, at] = lax.dot_general(
            ds, query, (((0,), (0,)), ((), ())), preferred_element_type=jnp.float32
        ).astype(dk_ref.dtype)


def partial_kernel(at_ref, *refs):
    count = (len(refs) - 1) // 2
    total = 0.0
    for attn_ref, weight_ref in zip(refs[:count], refs[count:-1]):
        total = total + jnp.dot(attn_ref[...], weight_ref[...], preferred_element_type=jnp.float32)
    refs[-1][...] = total


def hidden_kernel(pieces, before, at_ref, attn_ref, gain_ref, *refs):
    rest = refs[:pieces]
    weights = refs[pieces + before : -3]
    hidden_ref, sent_ref, square_ref = refs[-3:]
    weight = weights[0][...]
    for other in weights[1:]:
        weight = weight + other[...]
    n = rest[0].shape[0]
    for i in range(pieces):
        at = slice(i * n, (i + 1) * n)
        hidden = rest[i][...].astype(jnp.float32) + jnp.dot(attn_ref[at], weight, preferred_element_type=jnp.float32)
        if before:
            hidden = hidden + refs[pieces][at]
        hidden_ref[at] = hidden
        sent_ref[at] = (hidden * gain_ref[...]).astype(sent_ref.dtype)
        square_ref[i] = to_lanes(jnp.sum(hidden * hidden, axis=-1, keepdims=True))


def to_lanes(column):
    return jnp.transpose(jnp.broadcast_to(column, (column.shape[0], LANES)))[:1]


def to_column(row):
    return jnp.transpose(jnp.broadcast_to(row, (LANES, row.shape[1])))[:, :1]


def matched(hidden, sent, gain, inv, inv_other, weight):
    normed = hidden * inv
    diff = normed * gain - sent.astype(jnp.float32) * inv_other
    return normed, diff, weight * diff * gain


def match_kernel(hidden_ref, sent_ref, gain_ref, inv_ref, other_ref, weight_ref, out_ref):
    n = inv_ref.shape[-1]
    for i in range(inv_ref.shape[0]):
        at = slice(i * n, (i + 1) * n)
        inv, other, weight = to_column(inv_ref[i]), to_column(other_ref[i]), to_column(weight_ref[i])
        normed, diff, scaled = matched(hidden_ref[at], sent_ref[at], gain_ref[...], inv, other, weight)
        out_ref[i, :1] = to_lanes(jnp.sum(diff * diff, axis=-1, keepdims=True))
        out_ref[i, 1:] = to_lanes(jnp.sum(normed * scaled, axis=-1, keepdims=True))


def d_hidden_kernel(halves, at_ref, attn_ref, gain_ref, inv_ref, other_ref, weight_ref, mean_ref, *refs):
    n = inv_ref.shape[-1]
    deep = inv_ref.shape[0] // halves
    total = 0.0
    for i in range(inv_ref.shape[0]):
        half, at = i // deep, slice(i % deep * n, (i % deep + 1) * n)
        inv, other, weight = to_column(inv_ref[i]), to_column(other_ref[i]), to_column(weight_ref[i])
        hidden, sent = refs[half][at], refs[halves + half][at]
        normed, _, scaled = matched(hidden, sent, gain_ref[...], inv, other, weight)
        d_hidden = (inv * (scaled - normed * to_column(mean_ref[i]))).astype(jnp.bfloat16)
        refs[2 * halves + half][at] = d_hidden
        total = total + lax.dot_general(
            attn_ref[i * n : (i + 1) * n], d_hidden, (((0,), (0,)), ((), ())), preferred_element_type=jnp.float32
        )
    refs[-1][...] = total.astype(refs[-1].dtype)


def terms_kernel(at_ref, attn_ref, *refs):
    total, at = 0.0, 0
    for d_ref in refs[:-1]:
        n = d_ref.shape[0]
        total = total + lax.dot_general(
            attn_ref[at : at + n], d_ref[...], (((0,), (0,)), ((), ())), preferred_element_type=jnp.float32
        )
        at += n
    refs[-1][...] = total.astype(refs[-1].dtype)


def d_attn_kernel(d_ref, weight_ref, out_ref):
    out_ref[...] = lax.dot_general(
        d_ref[...], weight_ref[...], (((1,), (1,)), ((), ())), preferred_element_type=jnp.float32
    ).astype(out_ref.dtype)


def assemble_kernel(wide, places, member_ref, *refs):
    for ref, other in zip(refs[:-1], places):
        at = pl.multiple_of((member_ref[0] ^ other) * wide, LANES)
        refs[-1][:, pl.ds(at, wide)] = ref[...].astype(refs[-1].dtype)


ANY = pl.BlockSpec(memory_space=pl.ANY)


def small_call(kernel, indices, ins, outs, into=None, micros=1.0, grid=1):
    out = pl.pallas_call(
        kernel,
        grid_spec=pltpu.PrefetchScalarGridSpec(
            num_scalar_prefetch=1,
            grid=(grid,),
            in_specs=[pl.BlockSpec(b, m) for _, b, m in ins] + [ANY] * (into is not None),
            out_specs=[pl.BlockSpec(b, m) for _, _, b, m in outs],
        ),
        out_shape=[jax.ShapeDtypeStruct(shape, d) for shape, d, _, _ in outs],
        input_output_aliases={} if into is None else {1 + len(ins): 0},
        cost_estimate=cost(micros),
        compiler_params=vmem([(b, a.dtype) for a, b, _ in ins] + [(b, d) for _, d, b, _ in outs]),
    )(jnp.stack([jnp.int32(i) for i in indices]), *[a for a, _, _ in ins], *(() if into is None else (into,)))
    return out


ORIGIN = lambda i, at: (0, 0)
DOWN = lambda i, at: (at[0], 0)


def split_kernel(at_ref, in_ref, *outs):
    for i, out in enumerate(outs):
        out[...] = in_ref[:, pl.ds(pl.multiple_of(at_ref[i], LANES), out.shape[1])]


def cut_columns(array, places, widths):
    if any(w % LANES for w in widths):
        return [lax.dynamic_slice(array, (0, p), (array.shape[0], w)) for p, w in zip(places, widths)]
    n = array.shape[0]
    outs = [((n, w), array.dtype, (n, w), ORIGIN) for w in widths]
    return small_call(split_kernel, places, [(array, array.shape, ORIGIN)], outs)


def copy_kernel(at_ref, in_ref, *refs):
    refs[-1][...] = in_ref[...]


def place_rows(whole, piece, index):
    new = isinstance(whole, tuple)
    shape = whole if new else whole.shape
    outs = [(shape, piece.dtype, piece.shape, DOWN)]
    return small_call(copy_kernel, [index], [(piece, piece.shape, ORIGIN)], outs, None if new else whole)[0]


def take_rows(array, index, rows):
    block = (rows, array.shape[1])
    return small_call(copy_kernel, [index], [(array, block, DOWN)], [(block, array.dtype, block, ORIGIN)])[0]


def stack_kernel(across, at_ref, *refs):
    n = refs[0].shape[0]
    column = 0
    for i, ref in enumerate(refs[:-1]):
        row, wide = i // across * n, ref.shape[1]
        refs[-1][row : row + n, column : column + wide] = ref[...]
        column = (column + wide) % refs[-1].shape[1]


def stack_blocks(columns):
    n = columns[0][0].shape[0]
    shape = (n * len(columns[0]), sum(c[0].shape[1] for c in columns))
    pieces = [p for row in zip(*columns) for p in row]
    ins = [(p, p.shape, ORIGIN) for p in pieces]
    kernel = functools.partial(stack_kernel, len(columns))
    return small_call(kernel, [0], ins, [(shape, pieces[0].dtype, shape, ORIGIN)])[0]


def whole_kernel(at_ref, *refs):
    n = refs[0].shape[0]
    count = at_ref.shape[0]
    for i in range(count):
        block = refs[i][...]
        if i == count - 1 and len(refs) - 1 > count:
            block = block + refs[count][...]
        refs[-1][pl.ds(pl.multiple_of(at_ref[i] * n, 16), n)] = block


def stack_rows(pieces):
    return stack_blocks([pieces])


def add_kernel(at_ref, *refs):
    total = sum(ref[...].astype(jnp.float32) for ref in refs[:-1])
    refs[-1][...] = total.astype(refs[-1].dtype)


def sum_terms(got, terms, index):
    block = got[0].shape
    ins = [(g, block, ORIGIN) for g in got] + [(terms, block, DOWN)]
    return small_call(add_kernel, [index], ins, [(block, terms.dtype, block, ORIGIN)])[0]


def add_term(got, terms, index):
    return sum_terms([got], terms, index)


def fold_kernel(near_ref, far_ref, kept_ref, sent_ref):
    half = kept_ref.shape[0]
    total = near_ref[...].astype(jnp.float32) + far_ref[...].astype(jnp.float32)
    total = total.astype(kept_ref.dtype)
    kept_ref[...] = total[:half]
    sent_ref[...] = total[half:]


def fold(near, far, first, last, group):
    rows = near.shape[0]
    n = (last - first) * group
    there = pl.BlockSpec((rows, group), lambda i: (0, i + first))
    here = pl.BlockSpec((rows // 2, group), lambda i: (0, i))
    return pl.pallas_call(
        fold_kernel,
        grid=(last - first,),
        in_specs=[there] * 2,
        out_specs=[here] * 2,
        out_shape=[jax.ShapeDtypeStruct((rows // 2, n), near.dtype)] * 2,
        cost_estimate=cost(1.0),
        compiler_params=vmem([((rows, group), near.dtype)] * 3),
    )(near, far)


def call(micros, kernel, grid, ins, outs):
    return pl.pallas_call(
        kernel,
        grid=grid,
        in_specs=[pl.BlockSpec(b, m) for _, b, m in ins],
        out_specs=[pl.BlockSpec(b, m) for _, _, b, m in outs],
        out_shape=[jax.ShapeDtypeStruct(s, d) for s, d, _, _ in outs],
        cost_estimate=cost(micros),
        compiler_params=vmem([(b, a.dtype) for a, b, _ in ins] + [(b, d) for _, d, b, _ in outs]),
    )(*[a for a, _, _ in ins])


def attention_call(micros, kernel, length, arrays, moved, outs, first, number, group, into=None):
    seq = arrays[0].shape[0]
    there = pl.BlockSpec((seq, group), lambda i, *_: (0, i + first))
    here = pl.BlockSpec((seq, group), lambda i, *_: (0, i))
    alone = into is None
    into = into or ()
    shape = jax.ShapeDtypeStruct((seq, group * number) if alone else arrays[0].shape, jnp.bfloat16)
    given = 1 + len(arrays) + len(moved)
    return pl.pallas_call(
        kernel,
        grid_spec=pltpu.PrefetchScalarGridSpec(
            num_scalar_prefetch=1,
            grid=(number,),
            in_specs=[there] * len(arrays) + [here] * len(moved) + [pl.BlockSpec(memory_space=pl.ANY)] * len(into),
            out_specs=[here if alone else there] * outs,
        ),
        out_shape=[shape] * outs,
        input_output_aliases={given + i: i for i in range(len(into))},
        cost_estimate=cost(micros),
        compiler_params=vmem([((seq, group), jnp.bfloat16)] * (given - 1 + outs)),
    )(length.reshape(1), *arrays, *moved, *into)


def group_width(heads_width):
    heads = heads_width // DH
    return DH * max(g for g in (4, 2, 1) if heads % g == 0)


def tie(*values):
    return lax.optimization_barrier(values)


def split(values, *counts):
    lists, at = [], 0
    for count in counts:
        lists.append(list(values[at : at + count]))
        at += count
    return *lists, list(values[at:])


def send(value, axis, pairs):
    return lax.ppermute(value, axis, pairs)


LINE = 4
ENDS_OUT = [(2, 3), (1, 0)]
ENDS_IN = [(0, 1), (3, 2)]
MIDDLE = [(1, 2), (2, 1)]


def body(queries, keys, values, residual, event_ids, lengths, type_weight, w_out, gain):
    seq, heads_width = queries.shape[2:]
    width = residual.shape[3]
    parts = lax.axis_size("fsdp")
    team = lax.axis_size("dp")
    bits = bits_of(team)
    rows = team * seq
    shard_rows = w_out.shape[1]
    part = lax.axis_index("fsdp")
    member = lax.axis_index("dp")
    own = lax.axis_index(("dp", "fsdp"))
    length = lengths[own]
    count = jnp.sum(lengths).astype(jnp.float32)
    wide = width // team
    line = parts == LINE
    f32, bf16 = jnp.float32, jnp.bfloat16
    group = group_width(heads_width)
    steps = heads_width // group
    middle = -(-steps // 2)
    cuts = [(0, middle), (middle, steps)] if steps > 1 else [(0, steps)]
    q, k, v = queries[0, 0], keys[0, 0], values[0, 0]

    order = [0]
    for bit in reversed(bits):
        order = order + [s ^ bit for s in order]

    (block,) = cut_columns(w_out[0], [member * wide], [wide])
    mine = cut_columns(residual[0, 0], [(member ^ s) * wide for s in order], [wide] * team)
    block, *mine = tie(block, *mine)
    others = [1, 2] if line else list(range(1, parts))
    came = [swap(block, "fsdp", s) for s in others]

    types = jnp.arange(type_weight.shape[0], dtype=jnp.int32)
    matches = event_ids[0][:, None] == types[None, :]
    looked_up = jnp.sum(jnp.where(matches, type_weight[None, :], f32(0.0)), axis=-1)
    tok_w = jnp.where(jnp.arange(seq, dtype=jnp.int32) < length, looked_up, f32(0.0))
    tok_w = tok_w.reshape(1, 1, seq)
    for bit in reversed(bits):
        tok_w = jnp.concatenate([tok_w, swap(tok_w, "dp", bit)], axis=0)

    attn = []
    for first, last in cuts:
        attn += attention_call(1.5 * (last - first), forward_kernel, length, (q, k, v), (), 1, first, last - first, group)
    far = [swap(a, "dp", bits[-1]) for a in attn]
    tok_w, block, *rest = tie(tok_w, block, *came, *mine, *attn, *far)
    came, mine, attn, far = split(rest, len(others), team, len(cuts))

    last = [send(block, "fsdp", MIDDLE), send(came[1], "fsdp", ENDS_OUT)] if line else []
    rest = [swap(piece, "dp", s) if s else piece for s, piece in zip(order, mine)]
    found = [[a, b] for a, b in zip(attn, far)]
    for bit in reversed(bits[:-1]):
        found = [f + [swap(x, "dp", bit) for x in f] for f in found]
    attn = stack_blocks(found)

    row_at = lambda i: (i, 0)
    fixed = lambda i, *_: (0, 0)
    halves = 2
    tall = rows // halves
    deep = team // halves
    blocks, spots = [block, *came], [part, *[part ^ s for s in others]]
    before = []
    if line:
        picks = [(attn, (tall, shard_rows), lambda i, at, k=k: (i, at[k])) for k in range(len(blocks))]
        before = small_call(
            partial_kernel,
            spots,
            picks + [(b, b.shape, fixed) for b in blocks],
            [((rows, wide), f32, (tall, wide), lambda i, at: (i, 0))],
            micros=4.0,
            grid=halves,
        )
    attn, *tied = tie(attn, *before, *rest, *last)
    before, rest, last = split(tied, len(before), team)

    def whole_weight(blocks, last):
        ins = [(b, b.shape, fixed) for b in blocks + last]
        outs = [((heads_width, wide), bf16, (heads_width, wide), fixed)]
        return small_call(whole_kernel, spots + ([part ^ 3] if last else []), ins, outs, micros=2.0)[0]

    if not line:
        weight = whole_weight(blocks, last)

    def team_sum(value):
        shape = value.shape
        value = value.reshape((2,) * len(bits) + shape[1:])
        for axis, bit in enumerate(bits):
            value = value + jnp.flip(swap(value, "dp", bit), axis)
        return value.reshape(shape)

    my_gain = lax.dynamic_slice(gain[0], (member * wide,), (wide,))[None]
    gain_in = (my_gain, (1, wide), fixed)
    final = last if line else [weight]
    columns = shard_rows if line else heads_width

    def half_hidden(half):
        at = lambda i, at: (half, 0)
        return small_call(
            functools.partial(hidden_kernel, deep, len(before)),
            [part ^ 3 if line else 0],
            [(attn, (tall, columns), lambda i, at: (half, at[0])), gain_in]
            + [(r, (seq, wide), fixed) for r in rest[half * deep : (half + 1) * deep]]
            + [(b, (tall, wide), at) for b in before]
            + [(w, w.shape, fixed) for w in final],
            [
                ((tall, wide), f32, (tall, wide), fixed),
                ((tall, wide), bf16, (tall, wide), fixed),
                ((deep, 1, seq), f32, (deep, 1, seq), lambda i, at: (0, 0, 0)),
            ],
            micros=2.0,
        )

    hidden, sent, square = [list(x) for x in zip(*[half_hidden(half) for half in range(halves)])]
    first_sent = swap(sent[0], "copy", 1)
    inv = lax.rsqrt(team_sum(jnp.concatenate(square, axis=0)) / width + 1e-06)
    inv_other = swap(inv, "copy", 1)
    inv_late, sent_late = tie(inv, sent[1])
    second_sent = swap(sent_late, "copy", 1)
    row_scale = 2.0 * tok_w / (width * count)
    if line:
        *tied, _ = tie(*blocks, *last, sent_late)
        blocks, last = split(tied, len(blocks))
        weight = whole_weight(blocks, last)

    def match(half, sent):
        stat = (deep, 1, seq)
        stats = [(x, stat, lambda i: (half, 0, 0)) for x in (inv, inv_other, row_scale)]
        return call(
            2.0,
            match_kernel,
            (1,),
            [(hidden[half], (tall, wide), fixed), (sent, (tall, wide), fixed), gain_in] + stats,
            [((deep, 2, seq), f32, (deep, 2, seq), lambda i: (0, 0, 0))],
        )[0]

    both = [match(0, first_sent)]
    both[0], second_sent, weight = tie(both[0], second_sent, weight)
    both.append(match(1, second_sent))
    both = team_sum(jnp.concatenate(both, axis=0))
    loss = jnp.sum(tok_w[0] * both[0, :1]) / (width * count)
    mean = both[:, 1:] / width

    stats = [(x, (team, 1, seq), lambda i, at: (0, 0, 0)) for x in (inv, inv_other, row_scale, mean)]
    *d_hidden, terms = small_call(
        functools.partial(d_hidden_kernel, halves),
        [part ^ 3 if line else 0],
        [(attn, (rows, columns), lambda i, at: (0, at[0])), gain_in]
        + stats
        + [(x, (tall, wide), fixed) for x in (*hidden, first_sent, second_sent)],
        [((tall, wide), bf16, (tall, wide), fixed)] * halves + [((columns, wide), bf16, (columns, wide), fixed)],
        micros=4.0,
    )
    across = next(w for w in (512, 256, 128, heads_width) if heads_width % w == 0)
    terms, *d_hidden = tie(terms, *d_hidden)
    if line:
        got = [send(terms, "fsdp", MIDDLE), send(terms, "fsdp", ENDS_IN)]
    else:
        got = [swap(take_rows(terms, part ^ s, shard_rows), "fsdp", s) for s in range(1, parts)]

    def d_attn_rows(half):
        return call(
            3.0,
            d_attn_kernel,
            (heads_width // across,),
            [(d_hidden[half], (tall, wide), fixed), (weight, (across, wide), row_at)],
            [((tall, heads_width), bf16, (tall, across), lambda i: (0, i))],
        )[0]

    far = d_attn_rows(1)
    far, *d_hidden = tie(far, *d_hidden)
    far = swap(far, "dp", bits[0])
    if line:
        (terms,) = small_call(
            terms_kernel,
            [part ^ 1, part ^ 2, part],
            [(attn, (rows, shard_rows), lambda i, at: (0, at[i]))] + [(d, (tall, wide), fixed) for d in d_hidden],
            [((3 * shard_rows, wide), bf16, (shard_rows, wide), lambda i, at: (i, 0))],
            micros=4.0,
            grid=3,
        )
    near = d_attn_rows(0)
    for bit in bits[1:-1]:
        near, far = fold(near, far, 0, steps, group)
        far = swap(far, "dp", bit)
    kept, far = zip(*[fold(near, far, first, last, group) for first, last in cuts])
    kept, far = list(kept), list(far)
    tied = tie(terms, *got, *kept, *far)
    terms, got = tied[0], list(tied[1 : 1 + len(got)])
    kept, far = tied[1 + len(got) : 1 + len(got) + len(cuts)], tied[1 + len(got) + len(cuts) :]

    if line:
        near_by = swap(take_rows(terms, 0, shard_rows), "fsdp", 1)
        beyond = swap(add_term(got[1], terms, 1), "fsdp", 2)
        got = [got[0], near_by, beyond]
    far = [swap(f, "dp", bits[-1]) for f in far]
    grads = ()
    for (first, last), *back in zip(cuts, kept, far):
        grads = attention_call(
            1.5 * (last - first) + 1.0, backward_kernel, length, (q, k, v), back, 3, first, last - first, group, grads
        )
    *got, d_queries, d_keys, d_values = tie(*got, *grads)

    total = sum_terms(got, terms, 2 if line else part)
    pieces = {0: total}
    for bit in reversed(bits):
        pieces.update({s ^ bit: swap(p, "dp", bit) for s, p in pieces.items()})
    placed = [pieces[s] for s in order]
    if wide % LANES == 0:
        tall = next(t for t in (128, 64, 32, 16, shard_rows) if shard_rows % t == 0)
        out = pl.pallas_call(
            functools.partial(assemble_kernel, wide, order),
            grid_spec=pltpu.PrefetchScalarGridSpec(
                num_scalar_prefetch=1,
                grid=(shard_rows // tall,),
                in_specs=[pl.BlockSpec((tall, wide), lambda i, *_: (i, 0))] * team,
                out_specs=pl.BlockSpec((tall, width), lambda i, *_: (i, 0)),
            ),
            out_shape=jax.ShapeDtypeStruct((shard_rows, width), f32),
            cost_estimate=cost(1.0),
            compiler_params=vmem([((tall, wide), bf16)] * team + [((tall, width), f32)]),
        )(member.reshape(1), *placed)
    else:
        out = jnp.zeros((shard_rows, width), f32)
        for piece, s in zip(placed, order):
            out = lax.dynamic_update_slice(out, piece.astype(f32), (0, (member ^ s) * wide))
    return (
        loss.reshape(1, 1),
        d_queries[None, None],
        d_keys[None, None],
        d_values[None, None],
        out[None],
    )


def solution(mesh):
    whole = P("copy", ("dp", "fsdp"), None, None)
    in_specs = (
        whole,
        whole,
        whole,
        whole,
        P(("dp", "fsdp"), None),
        P(),
        P(),
        P("copy", "fsdp", None),
        P("copy", None),
    )
    out_specs = (P("copy", ("dp", "fsdp")), whole, whole, whole, P("copy", "fsdp", None))
    return jax.shard_map(body, mesh=mesh, in_specs=in_specs, out_specs=out_specs, check_vma=False)
```

time: 293 us -> 229 us (0.78)
  Pallas kernels: 22.6 us -> 66.3 us
  waiting for transfers between devices: 124 us -> 89.3 us
  matrix products: 33.4 us -> 0 us
  other arithmetic: 25 us -> 2.58 us
  local copies, waits for them, and re-layouts: 44.7 us -> 24.9 us
    ppermute x12 -> x4, waiting for transfers between devices: 53 us -> 7.86 us  [send(): return lax.ppermute(value, axis, pairs)]
    pallas_call x0 -> x19, Pallas kernels: none -> 42.5 us  [the longest x12 27.1 us: small_call(): pl.pallas_call(kernel, grid_spec=pltpu.PrefetchScalarGridSpec(num_scalar_...]
    dot_general x6 -> x0, matrix products: 33.4 us -> none  [the longest x2 14.9 us: body(): jnp.dot(attn, weight, preferred_element_type=jnp.float32)]
    unnamed x49 -> x78, local copies, waits for them, and re-layouts: 8.83 us -> 24.3 us
    dynamic_slice x7 -> x1, local copies, waits for them, and re-layouts: 11.6 us -> 0.01 us  [body(): my_gain = lax.dynamic_slice(gain[0], (member * wide,), (wide,))[None]]
    ppermute x23 -> x28, waiting for transfers between devices: 70.9 us -> 81.4 us  [swap(): lax.ppermute(value, axis, [(i, i ^ bit) for i in range(lax.axis_size(axis...]
    dynamic_update_slice x8 -> x0, local copies, waits for them, and re-layouts: 10.3 us -> none  [the longest x6 6.52 us: body(): whole = lax.dynamic_update_slice(whole, block, (at, 0))]
    dynamic_update_slice x8 -> x0, other arithmetic: 9.88 us -> none  [body(): lax.dynamic_update_slice(out, piece.astype(jnp.float32), (0, (member ^ s)...]
  transfers between devices with their start and end apart: 35 -> 32, of which waited for: 16 -> 11; matrix products, arithmetic and copies ran while one was open for 22% -> 1% of each run, Pallas kernels for 0% -> 20%
where the time goes in v2:
time: 229 us; the launch traced here: 228 us
  waiting for transfers between devices  89.3 us (39%)
  Pallas kernels  66.3 us (29%)
  starting transfers between devices  41.3 us (18%)
  local copies, waits for them, and re-layouts  24.9 us (11%)
  between operations  3.55 us (2%)
  other arithmetic  2.58 us (1%)
    ppermute x28, waiting for transfers between devices, swap(): lax.ppermute(value, axis, [(i, i ^ bit) for i in range(lax.axis_size(axis...  81.4 us
    ppermute x28, starting transfers between devices, swap(): lax.ppermute(value, axis, [(i, i ^ bit) for i in range(lax.axis_size(axis...  31.3 us
    pallas_call x12, Pallas kernels, small_call(): pl.pallas_call(kernel, grid_spec=pltpu.PrefetchScalarGridSpec(num_scalar_...  27.1 us
    unnamed x78, local copies, waits for them, and re-layouts  24.3 us
    pallas_call x4, Pallas kernels, attention_call(): pl.pallas_call(kernel, grid_spec=pltpu.PrefetchScalarGridSpec(num_scalar_...  23.8 us
    pallas_call x4, Pallas kernels, call(): pl.pallas_call(kernel, grid=grid, in_specs=[pl.BlockSpec(b, m) for _, b,...  10.7 us
    ppermute x4, starting transfers between devices, send(): return lax.ppermute(value, axis, pairs)  10.1 us
    ppermute x4, waiting for transfers between devices, send(): return lax.ppermute(value, axis, pairs)  7.86 us
  transfers between devices with their start and end apart: 32, of which 11 were waited for; matrix products, arithmetic and copies ran while one was open for 1% of the time, Pallas kernels for 20%

profile of v2, /device:TPU:1, one launch (start us, length us, event | category | flops | bytes accessed | tf_op | source)
XLA Modules:
  0.0 228.0 jit_solution(3237238436017784969)
XLA Ops:
  0.7 1.9 copy-done.14
  2.8 1.4 copy-done.19
  4.2 1.6 shard_map.129
  6.5 2.1 collective-permute-start.2
  8.7 2.3 %collective-permute-start.3 = (bf16[640,640]{1,0:T(8,128)(2,1)S(1)}, bf16[640,640]{1,0:T(8,128)(2,1)}, u32[]{:S(2)}, u32[]{:S(2)}) collective-permute-start(bf16[640,640]{1,0:T(8,128)(2,1)S(1)} %shard_map.128.refs_3_.refs_0_), channel_id=1, source_target_pairs={{0,2},{1,3},{2,0},{3,1},{4,6},{5,7},{6,4},{7,5},{8,10},{9,11},{10,... | collective-permute-start | bytes 2457608 | tf_op jit(solution)/shard_map/ppermute | solution.py:28
  11.6 1.3 copy-done.5
  13.0 4.2 %shard_map.130.refs_0_ = bf16[256,1536]{1,0:T(8,128)(2,1)S(1)} custom-call(s32[1]{0:T(128)} %dynamic_slice.6.length_ref, bf16[256,2560]{1,0:T(8,128)(2,1)S(1)} %bitcast.28, bf16[256,2560]{1,0:T(8,128)(2,1)S(1)} %bitcast.32, bf16[256,2560]{1,0:T(8,128)(2,1)S(1)} %bitcast.36), custom_call_target="tpu_custom_call" | custom-call | bytes 4718592 | tf_op jit(solution)/shard_map/pallas_call | solution.py:313
  17.2 1.3 collective-permute-start.4
  18.5 3.1 %shard_map.131.refs_1_ = bf16[256,1024]{1,0:T(8,128)(2,1)S(1)} custom-call(s32[1]{0:T(128)} %dynamic_slice.6.length_ref, bf16[256,2560]{1,0:T(8,128)(2,1)S(1)} %bitcast.29, bf16[256,2560]{1,0:T(8,128)(2,1)S(1)} %bitcast.33, bf16[256,2560]{1,0:T(8,128)(2,1)S(1)} %bitcast.37), custom_call_target="tpu_custom_call" | custom-call | bytes 3145728 | tf_op jit(solution)/shard_map/pallas_call | solution.py:313
  22.8 1.3 collective-permute-start
  24.1 22.4 %collective-permute-done = f32[1,1,256]{2,1,0:T(1,128)S(1)} collective-permute-done((f32[1,1,256]{2,1,0:T(1,128)S(1)}, f32[1,1,256]{2,1,0:T(1,128)S(1)}, u32[]{:S(2)}, u32[]{:S(2)}) %collective-permute-start) | collective-permute-done | bytes 1056 | tf_op jit(solution)/shard_map/ppermute | solution.py:28
  46.5 2.1 collective-permute-start.1
  54.5 1.5 collective-permute-start.14
  56.8 1.2 collective-permute-start.10
  60.7 1.1 copy-done.16
  62.8 1.1 copy-done.21
  64.0 1.1 copy-done.23
  65.1 1.1 copy-done.25
  70.5 7.2 %shard_map.133.refs_2_ = f32[1024,640]{1,0:T(8,128)S(1)} custom-call(s32[3]{0:T(128)S(1)} %pad_add_fusion.1.at_ref, bf16[1024,2560]{1,0:T(8,128)(2,1)S(1)} %shard_map.132.refs_0_.refs_1_.refs_2_.attn_ref, bf16[1024,2560]{1,0:T(8,128)(2,1)S(1)} %shard_map.132.refs_0_.refs_1_.refs_2_.attn_ref, ...), custom_call_target="tpu_custom_call" | custom-call | bytes 4194304 | tf_op jit(solution)/shard_map/pallas_call | solution.py:173
  77.8 3.0 %shard_map.134 = (f32[512,640]{1,0:T(8,128)S(1)}, bf16[512,640]{1,0:T(8,128)(2,1)}, f32[2,1,256]{2,1,0:T(1,128)S(1)}) custom-call(s32[1]{0:T(128)} %bitcast.12.at_ref, bf16[1024,2560]{1,0:T(8,128)(2,1)S(1)} %shard_map.132.refs_0_.refs_1_.refs_2_.attn_ref, f32[1,640]{1,0:T(1,128)S(1)} %constant_dynamic-slice_fusion.gain_ref, bf16[256,640]{1,0:T(8,128)(2,1)S(1)} %copy-done.33, ...), custom_call_target="tpu_custom_call" | custom-call | bytes 2097152 | tf_op jit(solution)/shard_map/pallas_call | solution.py:173
  81.9 3.1 %shard_map.135 = (f32[512,640]{1,0:T(8,128)S(1)}, bf16[512,640]{1,0:T(8,128)(2,1)}, f32[2,1,256]{2,1,0:T(1,128)S(1)}) custom-call(s32[1]{0:T(128)} %bitcast.12.at_ref, bf16[1024,2560]{1,0:T(8,128)(2,1)S(1)} %shard_map.132.refs_0_.refs_1_.refs_2_.attn_ref, f32[1,640]{1,0:T(1,128)S(1)} %constant_dynamic-slice_fusion.gain_ref, ...), custom_call_target="tpu_custom_call" | custom-call | bytes 2097152 | tf_op jit(solution)/shard_map/pallas_call | solution.py:173
  87.3 1.2 collective-permute-start.17
  88.5 1.2 collective-permute-start.15
  89.8 1.3 collective-permute-start.19
  92.8 1.3 copy-done.9
  94.1 2.6 %shard_map.137.weight_ref = bf16[2560,640]{1,0:T(8,128)(2,1)S(1)} custom-call(s32[4]{0:T(128)S(1)} %pad_add_fusion.2.at_ref, bf16[640,640]{1,0:T(8,128)(2,1)S(1)} %copy-done.9, bf16[640,640]{1,0:T(8,128)(2,1)} %collective-permute-done.2.refs_4_.refs_1_, bf16[640,640]{1,0:T(8,128)(2,1)} %collective-permute-done.3.refs_5_.refs_2_, ...), custom_call_target="tpu_custom_call" | custom-call | bytes 2097152 | tf_op jit(solution)/shard_map/pallas_call | solution.py:173
  96.7 21.9 %collective-permute-done.18.other_ref = f32[4,1,256]{2,1,0:T(1,128)S(1)} collective-permute-done((f32[4,1,256]{2,1,0:T(1,128)S(1)}, f32[4,1,256]{2,1,0:T(1,128)S(1)}, u32[]{:S(2)}, u32[]{:S(2)}) %collective-permute-start.18) | collective-permute-done | bytes 4128 | tf_op jit(solution)/shard_map/ppermute | solution.py:28
  118.6 2.2 shard_map.136
  120.9 2.2 shard_map.138
  123.1 1.5 collective-permute-start.20
  125.7 2.2 collective-permute-done.21
  128.0 3.9 %shard_map.139 = (bf16[512,640]{1,0:T(8,128)(2,1)S(1)}, bf16[512,640]{1,0:T(8,128)(2,1)S(1)}, bf16[640,640]{1,0:T(8,128)(2,1)S(1)}) custom-call(s32[1]{0:T(128)} %bitcast.12.at_ref, bf16[1024,2560]{1,0:T(8,128)(2,1)S(1)} %bitcast.27, f32[1,640]{1,0:T(1,128)S(1)} %constant_dynamic-slice_fusion.gain_ref, f32[4,1,256]{2,1,0:T(1,128)S(1)} %bitcast.45, ...), custom_call_target="tpu_custom_call" | custom-call | bytes 4194304 | tf_op jit(solution)/shard_map/pallas_call | solution.py:173
  131.8 3.2 %shard_map.140 = bf16[512,2560]{1,0:T(8,128)(2,1)S(1)} custom-call(bf16[512,640]{1,0:T(8,128)(2,1)S(1)} %get-tuple-element.131.d_ref.refs_1_, bf16[2560,640]{1,0:T(8,128)(2,1)S(1)} %shard_map.137.weight_ref), custom_call_target="tpu_custom_call" | custom-call | bytes 3145728 | tf_op jit(solution)/shard_map/pallas_call | solution.py:294
  135.0 1.6 collective-permute-start.24
  137.3 7.2 %collective-permute-start.23 = (bf16[640,640]{1,0:T(8,128)(2,1)S(1)}, bf16[640,640]{1,0:T(8,128)(2,1)S(1)}, u32[]{:S(2)}, u32[]{:S(2)}) collective-permute-start(bf16[640,640]{1,0:T(8,128)(2,1)S(1)} %get-tuple-element.132), channel_id=1, source_target_pairs={{0,1},{3,2},{4,5},{7,6},{8,9},{11,10},{12,13},{15,14},{16,17},{19,... | collective-permute-start | bytes 2457608 | tf_op jit(solution)/shard_map/ppermute | solution.py:346
  144.6 3.2 %shard_map.142.near_ref = bf16[512,2560]{1,0:T(8,128)(2,1)S(1)} custom-call(bf16[512,640]{1,0:T(8,128)(2,1)S(1)} %get-tuple-element.130.refs_0_.d_ref, bf16[2560,640]{1,0:T(8,128)(2,1)S(1)} %shard_map.137.weight_ref), custom_call_target="tpu_custom_call" | custom-call | bytes 3145728 | tf_op jit(solution)/shard_map/pallas_call | solution.py:294
  147.8 4.6 %shard_map.141.in_ref.refs_1_.refs_3_ = bf16[1920,640]{1,0:T(8,128)(2,1)S(1)} custom-call(s32[3]{0:T(128)S(1)} %pad_add_fusion.3.at_ref, bf16[1024,2560]{1,0:T(8,128)(2,1)S(1)} %bitcast.27, bf16[512,640]{1,0:T(8,128)(2,1)S(1)} %get-tuple-element.130.refs_0_.d_ref, bf16[512,640]{1,0:T(8,128)(2,1)S(1)} %get-tuple-element.131.d_ref.refs_1_), custom_call_target="tpu_custom_call" | custom-call | bytes 4194304 | tf_op jit(solution)/shard_map/pallas_call | solution.py:173
  153.7 7.9 %collective-permute-done.23.refs_0_ = bf16[640,640]{1,0:T(8,128)(2,1)S(1)} collective-permute-done((bf16[640,640]{1,0:T(8,128)(2,1)S(1)}, bf16[640,640]{1,0:T(8,128)(2,1)S(1)}, u32[]{:S(2)}, u32[]{:S(2)}) %collective-permute-start.23) | collective-permute-done | bytes 819232 | tf_op jit(solution)/shard_map/ppermute | solution.py:346
  161.8 2.7 %collective-permute-start.26 = (bf16[640,640]{1,0:T(8,128)(2,1)S(1)}, bf16[640,640]{1,0:T(8,128)(2,1)S(1)}, u32[]{:S(2)}, u32[]{:S(2)}) collective-permute-start(bf16[640,640]{1,0:T(8,128)(2,1)S(1)} %shard_map.146), channel_id=1, source_target_pairs={{0,2},{1,3},{2,0},{3,1},{4,6},{5,7},{6,4},{7,5},{8,10},{9,11},{10,... | collective-permute-start | bytes 2457608 | tf_op jit(solution)/shard_map/ppermute | solution.py:28
  164.8 1.2 collective-permute-start.27
  166.0 16.2 %collective-permute-done.28.two_ref = bf16[256,1536]{1,0:T(8,128)(2,1)S(1)} collective-permute-done((bf16[256,1536]{1,0:T(8,128)(2,1)S(1)}, bf16[256,1536]{1,0:T(8,128)(2,1)S(1)}, u32[]{:S(2)}, u32[]{:S(2)}) %collective-permute-start.28) | collective-permute-done | bytes 786464 | tf_op jit(solution)/shard_map/ppermute | solution.py:28
  182.2 9.6 %shard_map.147 = (bf16[256,2560]{1,0:T(8,128)(2,1)}, bf16[256,2560]{1,0:T(8,128)(2,1)}, bf16[256,2560]{1,0:T(8,128)(2,1)}) custom-call(s32[1]{0:T(128)} %dynamic_slice.6.length_ref, bf16[256,2560]{1,0:T(8,128)(2,1)S(1)} %bitcast.30, bf16[256,2560]{1,0:T(8,128)(2,1)S(1)} %bitcast.34, bf16[256,2560]{1,0:T(8,128)(2,1)S(1)} %bitcast.38, ...), custom_call_target="tpu_custom_call" | custom-call | bytes 5767168 | tf_op jit(solution)/shard_map/pallas_call | solution.py:313
  191.8 1.6 collective-permute-done.27.two_ref
  193.4 6.9 %shard_map.148 = (bf16[256,2560]{1,0:T(8,128)(2,1)}, bf16[256,2560]{1,0:T(8,128)(2,1)}, bf16[256,2560]{1,0:T(8,128)(2,1)}) custom-call(s32[1]{0:T(128)} %dynamic_slice.6.length_ref, bf16[256,2560]{1,0:T(8,128)(2,1)S(1)} %bitcast.31, bf16[256,2560]{1,0:T(8,128)(2,1)S(1)} %bitcast.35, ...), custom_call_target="tpu_custom_call", output_to_operand_aliasing={{0}: (6, {}), {1}: (7, {}), {2}: (8, {})} | custom-call | bytes 4194304 | tf_op jit(solution)/shard_map/pallas_call | solution.py:313
  201.1 2.9 %collective-permute-start.30 = (bf16[640,640]{1,0:T(8,128)(2,1)S(1)}, bf16[640,640]{1,0:T(8,128)(2,1)S(1)}, u32[]{:S(2)}, u32[]{:S(2)}) collective-permute-start(bf16[640,640]{1,0:T(8,128)(2,1)S(1)} %shard_map.149.refs_0_), channel_id=1, source_target_pairs={{0,4},{4,0},{8,12},{12,8},{1,5},{5,1},{9,13},{13,9},{2,6},{6,2},{1... | collective-permute-start | bytes 2457608 | tf_op jit(solution)/shard_map/ppermute | solution.py:28
  204.0 13.9 %collective-permute-done.29.refs_1_ = bf16[640,640]{1,0:T(8,128)(2,1)S(1)} collective-permute-done((bf16[640,640]{1,0:T(8,128)(2,1)S(1)}, bf16[640,640]{1,0:T(8,128)(2,1)S(1)}, u32[]{:S(2)}, u32[]{:S(2)}) %collective-permute-start.29) | collective-permute-done | bytes 819232 | tf_op jit(solution)/shard_map/ppermute | solution.py:28
  217.9 3.6 %collective-permute-start.31 = (bf16[640,640]{1,0:T(8,128)(2,1)S(1)}, bf16[640,640]{1,0:T(8,128)(2,1)S(1)}, u32[]{:S(2)}, u32[]{:S(2)}) collective-permute-start(bf16[640,640]{1,0:T(8,128)(2,1)S(1)} %collective-permute-done.29.refs_1_), channel_id=1, source_target_pairs={{0,4},{4,0},{8,12},{12,8},{1,5},{5,1},{9,13},{13,9},{2,6},{6,2},{1... | collective-permute-start | bytes 2457608 | tf_op jit(solution)/shard_map/ppermute | solution.py:28
  223.4 3.4 %shard_map.150 = f32[640,2560]{1,0:T(8,128)} custom-call(s32[1]{0:T(128)} %bitcast.24.member_ref, bf16[640,640]{1,0:T(8,128)(2,1)S(1)} %shard_map.149.refs_0_, bf16[640,640]{1,0:T(8,128)(2,1)S(1)} %collective-permute-done.29.refs_1_, bf16[640,640]{1,0:T(8,128)(2,1)S(1)} %collective-permute-done.30.refs_2_, bf16[640,640]{1,0:T(8,128)(2,1)S(1)} %collective-permute-done.31.refs_3_), custom_call_target="tpu_custom_call" | custom-call | bytes 1048576 | tf_op jit(solution)/shard_map/pallas_call | solution.py:563
  (138 shorter events, 27.7 us)
Async XLA Ops:
  0.6 60.0 %copy-start = (f32[1,2560]{1,0:T(1,128)S(1)}, f32[1,2560]{1,0:T(1,128)}, u32[]{:S(2)}) copy-start(f32[1,2560]{1,0:T(1,128)} %param.17) | copy-start | bytes 30724
  2.6 9.0 %copy-start.4 = (bf16[1,1,256,2560]{3,2,1,0:T(8,128)(2,1)S(1)}, bf16[1,1,256,2560]{3,2,1,0:T(8,128)(2,1)}, u32[]{:S(2)}) copy-start(bf16[1,1,256,2560]{3,2,1,0:T(8,128)(2,1)} %param.10) | copy-start | bytes 3932164
  2.7 18.9 %copy-start.7 = (bf16[640,640]{1,0:T(8,128)(2,1)}, bf16[640,640]{1,0:T(8,128)(2,1)S(1)}, u32[]{:S(2)}) copy-start(bf16[640,640]{1,0:T(8,128)(2,1)S(1)} %shard_map.128.refs_3_.refs_0_) | copy-start | bytes 2457604
  2.7 8.3 %copy-start.36 = (s32[16]{0:T(128)S(1)}, s32[16]{0:T(128)}, u32[]{:S(2)}) copy-start(s32[16]{0:T(128)} %param.14) | copy-start | bytes 196
  2.7 8.9 %copy-start.3 = (bf16[1,1,256,2560]{3,2,1,0:T(8,128)(2,1)S(1)}, bf16[1,1,256,2560]{3,2,1,0:T(8,128)(2,1)}, u32[]{:S(2)}) copy-start(bf16[1,1,256,2560]{3,2,1,0:T(8,128)(2,1)} %param.9) | copy-start | bytes 3932164
  6.5 42.9 %collective-permute-start.2 = (bf16[640,640]{1,0:T(8,128)(2,1)S(1)}, bf16[640,640]{1,0:T(8,128)(2,1)}, u32[]{:S(2)}, u32[]{:S(2)}) collective-permute-start(bf16[640,640]{1,0:T(8,128)(2,1)S(1)} %shard_map.128.refs_3_.refs_0_), channel_id=1, source_target_pairs={{0,1},{1,0},{2,3},{3,2},{4,5},{5,4},{6,7},{7,6},{8,9},{9,8},{10,11... | collective-permute-start | bytes 2457608 | tf_op jit(solution)/shard_map/ppermute | solution.py:28
  8.7 40.7 %collective-permute-start.3 = (bf16[640,640]{1,0:T(8,128)(2,1)S(1)}, bf16[640,640]{1,0:T(8,128)(2,1)}, u32[]{:S(2)}, u32[]{:S(2)}) collective-permute-start(bf16[640,640]{1,0:T(8,128)(2,1)S(1)} %shard_map.128.refs_3_.refs_0_), channel_id=1, source_target_pairs={{0,2},{1,3},{2,0},{3,1},{4,6},{5,7},{6,4},{7,5},{8,10},{9,11},{10,... | collective-permute-start | bytes 2457608 | tf_op jit(solution)/shard_map/ppermute | solution.py:28
  17.2 32.6 %copy-start.15 = (bf16[256,1536]{1,0:T(8,128)(2,1)}, bf16[256,1536]{1,0:T(8,128)(2,1)S(1)}, u32[]{:S(2)}) copy-start(bf16[256,1536]{1,0:T(8,128)(2,1)S(1)} %shard_map.130.refs_0_) | copy-start | bytes 2359300
  17.2 4.7 %copy-start.34 = (f32[1024]{0:T(1024)S(1)}, f32[1024]{0:T(1024)}, u32[]{:S(2)}) copy-start(f32[1024]{0:T(1024)} %param.15) | copy-start | bytes 12292
  17.2 4.7 %copy-start.35 = (s32[1,256]{1,0:T(1,128)S(1)}, s32[1,256]{1,0:T(1,128)}, u32[]{:S(2)}) copy-start(s32[1,256]{1,0:T(1,128)} %param.13) | copy-start | bytes 3076
  17.2 32.2 %collective-permute-start.4 = (bf16[256,1536]{1,0:T(8,128)(2,1)S(1)}, bf16[256,1536]{1,0:T(8,128)(2,1)S(1)}, u32[]{:S(2)}, u32[]{:S(2)}) collective-permute-start(bf16[256,1536]{1,0:T(8,128)(2,1)S(1)} %shard_map.130.refs_0_), channel_id=1, source_target_pairs={{0,8},{4,12},{8,0},{12,4},{1,9},{5,13},{9,1},{13,5},{2,10},{6,14},... | collective-permute-start | bytes 2359304 | tf_op jit(solution)/shard_map/ppermute | solution.py:28
  21.6 27.8 %collective-permute-start.5 = (bf16[256,1024]{1,0:T(8,128)(2,1)S(1)}, bf16[256,1024]{1,0:T(8,128)(2,1)S(1)}, u32[]{:S(2)}, u32[]{:S(2)}) collective-permute-start(bf16[256,1024]{1,0:T(8,128)(2,1)S(1)} %shard_map.131.refs_1_), channel_id=1, source_target_pairs={{0,8},{4,12},{8,0},{12,4},{1,9},{5,13},{9,1},{13,5},{2,10},{6,14},... | collective-permute-start | bytes 1572872 | tf_op jit(solution)/shard_map/ppermute | solution.py:28
  22.8 23.6 %collective-permute-start = (f32[1,1,256]{2,1,0:T(1,128)S(1)}, f32[1,1,256]{2,1,0:T(1,128)S(1)}, u32[]{:S(2)}, u32[]{:S(2)}) collective-permute-start(f32[1,1,256]{2,1,0:T(1,128)S(1)} %compare_select_fusion), channel_id=1, source_target_pairs={{0,8},{4,12},{8,0},{12,4},{1,9},{5,13},{9,1},{13,5},{2,10},{6,14},... | collective-permute-start | bytes 3080 | tf_op jit(solution)/shard_map/ppermute | solution.py:28
  46.5 2.9 %collective-permute-start.1 = (f32[2,1,256]{2,1,0:T(1,128)S(1)}, f32[2,1,256]{2,1,0:T(1,128)S(1)}, u32[]{:S(2)}, u32[]{:S(2)}) collective-permute-start(f32[2,1,256]{2,1,0:T(1,128)S(1)} %pad_maximum_fusion.3), channel_id=1, source_target_pairs={{0,4},{4,0},{8,12},{12,8},{1,5},{5,1},{9,13},{13,9},{2,6},{6,2},{1... | collective-permute-start | bytes 6152 | tf_op jit(solution)/shard_map/ppermute | solution.py:28
  49.4 4.3 %collective-permute-start.7 = (bf16[256,1024]{1,0:T(8,128)(2,1)S(1)}, bf16[256,1024]{1,0:T(8,128)(2,1)S(1)}, u32[]{:S(2)}, u32[]{:S(2)}) collective-permute-start(bf16[256,1024]{1,0:T(8,128)(2,1)S(1)} %shard_map.131.refs_1_), channel_id=1, source_target_pairs={{0,4},{4,0},{8,12},{12,8},{1,5},{5,1},{9,13},{13,9},{2,6},{6,2},{1... | collective-permute-start | bytes 1572872 | tf_op jit(solution)/shard_map/ppermute | solution.py:28
  50.7 7.4 %collective-permute-start.6 = (bf16[256,1536]{1,0:T(8,128)(2,1)S(1)}, bf16[256,1536]{1,0:T(8,128)(2,1)S(1)}, u32[]{:S(2)}, u32[]{:S(2)}) collective-permute-start(bf16[256,1536]{1,0:T(8,128)(2,1)S(1)} %shard_map.130.refs_0_), channel_id=1, source_target_pairs={{0,4},{4,0},{8,12},{12,8},{1,5},{5,1},{9,13},{13,9},{2,6},{6,2},{1... | collective-permute-start | bytes 2359304 | tf_op jit(solution)/shard_map/ppermute | solution.py:28
  50.8 8.7 %collective-permute-start.8 = (bf16[256,1536]{1,0:T(8,128)(2,1)S(1)}, bf16[256,1536]{1,0:T(8,128)(2,1)S(1)}, u32[]{:S(2)}, u32[]{:S(2)}) collective-permute-start(bf16[256,1536]{1,0:T(8,128)(2,1)S(1)} %collective-permute-done.4.refs_2_), channel_id=1, source_target_pairs={{0,4},{4,0},{8,12},{12,8},{1,5},{5,1},{9,13},{13,9},{2,6},{6,2},{1... | collective-permute-start | bytes 2359304 | tf_op jit(solution)/shard_map/ppermute | solution.py:28
  52.1 4.0 %collective-permute-start.9 = (bf16[256,1024]{1,0:T(8,128)(2,1)S(1)}, bf16[256,1024]{1,0:T(8,128)(2,1)S(1)}, u32[]{:S(2)}, u32[]{:S(2)}) collective-permute-start(bf16[256,1024]{1,0:T(8,128)(2,1)S(1)} %collective-permute-done.5.refs_3_), channel_id=1, source_target_pairs={{0,4},{4,0},{8,12},{12,8},{1,5},{5,1},{9,13},{13,9},{2,6},{6,2},{1... | collective-permute-start | bytes 1572872 | tf_op jit(solution)/shard_map/ppermute | solution.py:28
  53.0 24.7 %collective-permute-start.13 = (bf16[640,640]{1,0:T(8,128)(2,1)}, bf16[640,640]{1,0:T(8,128)(2,1)S(1)}, u32[]{:S(2)}, u32[]{:S(2)}) collective-permute-start(bf16[640,640]{1,0:T(8,128)(2,1)} %copy-done.7), channel_id=1, source_target_pairs={{1,2},{2,1},{5,6},{6,5},{9,10},{10,9},{13,14},{14,13},{17,18},{18,... | collective-permute-start | bytes 2457608 | tf_op jit(solution)/shard_map/ppermute | solution.py:346
  54.5 23.2 %collective-permute-start.14 = (bf16[640,640]{1,0:T(8,128)(2,1)}, bf16[640,640]{1,0:T(8,128)(2,1)}, u32[]{:S(2)}, u32[]{:S(2)}) collective-permute-start(bf16[640,640]{1,0:T(8,128)(2,1)} %collective-permute-done.3.refs_5_.refs_2_), channel_id=1, source_target_pairs={{2,3},{1,0},{6,7},{5,4},{10,11},{9,8},{14,15},{13,12},{18,19},{17,... | collective-permute-start | bytes 2457608 | tf_op jit(solution)/shard_map/ppermute | solution.py:346
  56.8 20.9 %collective-permute-start.10 = (bf16[256,640]{1,0:T(8,128)(2,1)}, bf16[256,640]{1,0:T(8,128)(2,1)}, u32[]{:S(2)}, u32[]{:S(2)}) collective-permute-start(bf16[256,640]{1,0:T(8,128)(2,1)} %get-tuple-element.99), channel_id=1, source_target_pairs={{0,8},{4,12},{8,0},{12,4},{1,9},{5,13},{9,1},{13,5},{2,10},{6,14},... | collective-permute-start | bytes 983048 | tf_op jit(solution)/shard_map/ppermute | solution.py:28
  58.9 18.8 %collective-permute-start.11 = (bf16[256,640]{1,0:T(8,128)(2,1)}, bf16[256,640]{1,0:T(8,128)(2,1)}, u32[]{:S(2)}, u32[]{:S(2)}) collective-permute-start(bf16[256,640]{1,0:T(8,128)(2,1)} %get-tuple-element.100), channel_id=1, source_target_pairs={{0,4},{4,0},{8,12},{12,8},{1,5},{5,1},{9,13},{13,9},{2,6},{6,2},{1... | collective-permute-start | bytes 983048 | tf_op jit(solution)/shard_map/ppermute | solution.py:28
  60.4 17.3 %collective-permute-start.12 = (bf16[256,640]{1,0:T(8,128)(2,1)}, bf16[256,640]{1,0:T(8,128)(2,1)}, u32[]{:S(2)}, u32[]{:S(2)}) collective-permute-start(bf16[256,640]{1,0:T(8,128)(2,1)} %get-tuple-element.101), channel_id=1, source_target_pairs={{0,12},{4,8},{8,4},{12,0},{1,13},{5,9},{9,5},{13,1},{2,14},{6,10},... | collective-permute-start | bytes 983048 | tf_op jit(solution)/shard_map/ppermute | solution.py:28
  70.5 10.3 %copy-start.2 = (bf16[1024,2560]{1,0:T(8,128)(2,1)}, bf16[1024,2560]{1,0:T(8,128)(2,1)S(1)}, u32[]{:S(2)}) copy-start(bf16[1024,2560]{1,0:T(8,128)(2,1)S(1)} %shard_map.132.refs_0_.refs_1_.refs_2_.attn_ref) | copy-start | bytes 15728644
  70.5 7.3 %copy-start.33 = (bf16[256,640]{1,0:T(8,128)(2,1)S(1)}, bf16[256,640]{1,0:T(8,128)(2,1)}, u32[]{:S(2)}) copy-start(bf16[256,640]{1,0:T(8,128)(2,1)} %copy-done.32) | copy-start | bytes 983044
  86.0 1.3 collective-permute-start.16
  87.3 2.5 %collective-permute-start.17 = (f32[2,2,1,256]{3,2,1,0:T(1,128)S(1)}, f32[2,2,1,256]{3,2,1,0:T(1,128)S(1)}, u32[]{:S(2)}, u32[]{:S(2)}) collective-permute-start(f32[2,2,1,256]{3,2,1,0:T(1,128)S(1)} %reverse_add_fusion.2), channel_id=1, source_target_pairs={{0,8},{4,12},{8,0},{12,4},{1,9},{5,13},{9,1},{13,5},{2,10},{6,14},... | collective-permute-start | bytes 12296 | tf_op jit(solution)/shard_map/ppermute | solution.py:28
  88.5 30.1 %collective-permute-start.15 = (bf16[512,640]{1,0:T(8,128)(2,1)}, bf16[512,640]{1,0:T(8,128)(2,1)}, u32[]{:S(2)}, u32[]{:S(2)}) collective-permute-start(bf16[512,640]{1,0:T(8,128)(2,1)} %get-tuple-element.109), channel_id=1, source_target_pairs={{0,16},{16,0},{1,17},{17,1},{2,18},{18,2},{3,19},{19,3},{4,20},{20... | collective-permute-start | bytes 1966088 | tf_op jit(solution)/shard_map/ppermute | solution.py:28
  89.8 31.0 %collective-permute-start.19 = (bf16[512,640]{1,0:T(8,128)(2,1)}, bf16[512,640]{1,0:T(8,128)(2,1)}, u32[]{:S(2)}, u32[]{:S(2)}) collective-permute-start(bf16[512,640]{1,0:T(8,128)(2,1)} %get-tuple-element.115), channel_id=1, source_target_pairs={{0,16},{16,0},{1,17},{17,1},{2,18},{18,2},{3,19},{19,3},{4,20},{20... | collective-permute-start | bytes 1966088 | tf_op jit(solution)/shard_map/ppermute | solution.py:28
  92.5 26.1 %collective-permute-start.18 = (f32[4,1,256]{2,1,0:T(1,128)S(1)}, f32[4,1,256]{2,1,0:T(1,128)S(1)}, u32[]{:S(2)}, u32[]{:S(2)}) collective-permute-start(f32[4,1,256]{2,1,0:T(1,128)S(1)} %bitcast.42), channel_id=1, source_target_pairs={{0,16},{16,0},{1,17},{17,1},{2,18},{18,2},{3,19},{19,3},{4,20},{20... | collective-permute-start | bytes 12296 | tf_op jit(solution)/shard_map/ppermute | solution.py:28
  92.7 35.2 %slice-start = ((s8[5242880]{0:T(1024)(128)(4,1)}), s8[4194304]{0:T(1024)(128)(4,1)S(1)}, s32[]{:S(2)}) async-start(s8[5242880]{0:T(1024)(128)(4,1)} %bitcast.26), calls=%async_computation | async-start | bytes 8388608
  94.1 24.6 %copy-start.11 = (f32[512,640]{1,0:T(8,128)S(1)}, f32[512,640]{1,0:T(8,128)}, u32[]{:S(2)}) copy-start(f32[512,640]{1,0:T(8,128)} %copy-done.10) | copy-start | bytes 3932164
  94.1 33.9 %slice-start.1 = ((s8[5242880]{0:T(1024)(128)(4,1)}), s8[1048576]{0:T(1024)(128)(4,1)S(1)}, s32[]{:S(2)}) async-start(s8[5242880]{0:T(1024)(128)(4,1)} %bitcast.26), calls=%async_computation.1 | async-start | bytes 2097152
  96.7 24.1 %copy-start.13 = (f32[512,640]{1,0:T(8,128)S(1)}, f32[512,640]{1,0:T(8,128)}, u32[]{:S(2)}) copy-start(f32[512,640]{1,0:T(8,128)} %copy-done.12) | copy-start | bytes 3932164
  123.1 2.3 %collective-permute-start.20 = (f32[2,2,2,256]{3,2,1,0:T(2,128)S(1)}, f32[2,2,2,256]{3,2,1,0:T(2,128)S(1)}, u32[]{:S(2)}, u32[]{:S(2)}) collective-permute-start(f32[2,2,2,256]{3,2,1,0:T(2,128)S(1)} %bitcast.50), channel_id=1, source_target_pairs={{0,4},{4,0},{8,12},{12,8},{1,5},{5,1},{9,13},{13,9},{2,6},{6,2},{1... | collective-permute-start | bytes 24584 | tf_op jit(solution)/shard_map/ppermute | solution.py:28
  125.4 2.5 %collective-permute-start.21 = (f32[2,2,2,256]{3,2,1,0:T(2,128)S(1)}, f32[2,2,2,256]{3,2,1,0:T(2,128)S(1)}, u32[]{:S(2)}, u32[]{:S(2)}) collective-permute-start(f32[2,2,2,256]{3,2,1,0:T(2,128)S(1)} %reverse_add_fusion.1), channel_id=1, source_target_pairs={{0,8},{4,12},{8,0},{12,4},{1,9},{5,13},{9,1},{13,5},{2,10},{6,14},... | collective-permute-start | bytes 24584 | tf_op jit(solution)/shard_map/ppermute | solution.py:28
  135.0 17.3 %collective-permute-start.24 = (bf16[512,2560]{1,0:T(8,128)(2,1)S(1)}, bf16[512,2560]{1,0:T(8,128)(2,1)S(1)}, u32[]{:S(2)}, u32[]{:S(2)}) collective-permute-start(bf16[512,2560]{1,0:T(8,128)(2,1)S(1)} %shard_map.140), channel_id=1, source_target_pairs={{0,4},{4,0},{8,12},{12,8},{1,5},{5,1},{9,13},{13,9},{2,6},{6,2},{1... | collective-permute-start | bytes 7864328 | tf_op jit(solution)/shard_map/ppermute | solution.py:28
  136.6 17.1 %collective-permute-start.22 = (bf16[640,640]{1,0:T(8,128)(2,1)S(1)}, bf16[640,640]{1,0:T(8,128)(2,1)S(1)}, u32[]{:S(2)}, u32[]{:S(2)}) collective-permute-start(bf16[640,640]{1,0:T(8,128)(2,1)S(1)} %get-tuple-element.132), channel_id=1, source_target_pairs={{1,2},{2,1},{5,6},{6,5},{9,10},{10,9},{13,14},{14,13},{17,18},{18,... | collective-permute-start | bytes 2457608 | tf_op jit(solution)/shard_map/ppermute | solution.py:346
  137.3 24.2 %collective-permute-start.23 = (bf16[640,640]{1,0:T(8,128)(2,1)S(1)}, bf16[640,640]{1,0:T(8,128)(2,1)S(1)}, u32[]{:S(2)}, u32[]{:S(2)}) collective-permute-start(bf16[640,640]{1,0:T(8,128)(2,1)S(1)} %get-tuple-element.132), channel_id=1, source_target_pairs={{0,1},{3,2},{4,5},{7,6},{8,9},{11,10},{12,13},{15,14},{16,17},{19,... | collective-permute-start | bytes 2457608 | tf_op jit(solution)/shard_map/ppermute | solution.py:346
  161.6 20.5 %copy-start.6 = (bf16[1,1,256,2560]{3,2,1,0:T(8,128)(2,1)S(1)}, bf16[1,1,256,2560]{3,2,1,0:T(8,128)(2,1)}, u32[]{:S(2)}) copy-start(bf16[1,1,256,2560]{3,2,1,0:T(8,128)(2,1)} %param.11) | copy-start | bytes 3932164
  161.8 38.5 %collective-permute-start.26 = (bf16[640,640]{1,0:T(8,128)(2,1)S(1)}, bf16[640,640]{1,0:T(8,128)(2,1)S(1)}, u32[]{:S(2)}, u32[]{:S(2)}) collective-permute-start(bf16[640,640]{1,0:T(8,128)(2,1)S(1)} %shard_map.146), channel_id=1, source_target_pairs={{0,2},{1,3},{2,0},{3,1},{4,6},{5,7},{6,4},{7,5},{8,10},{9,11},{10,... | collective-permute-start | bytes 2457608 | tf_op jit(solution)/shard_map/ppermute | solution.py:28
  164.5 35.8 %collective-permute-start.25 = (bf16[640,640]{1,0:T(8,128)(2,1)S(1)}, bf16[640,640]{1,0:T(8,128)(2,1)S(1)}, u32[]{:S(2)}, u32[]{:S(2)}) collective-permute-start(bf16[640,640]{1,0:T(8,128)(2,1)S(1)} %shard_map.145), channel_id=1, source_target_pairs={{0,1},{1,0},{2,3},{3,2},{4,5},{5,4},{6,7},{7,6},{8,9},{9,8},{10,11... | collective-permute-start | bytes 2457608 | tf_op jit(solution)/shard_map/ppermute | solution.py:28
  164.5 17.6 %collective-permute-start.28 = (bf16[256,1536]{1,0:T(8,128)(2,1)S(1)}, bf16[256,1536]{1,0:T(8,128)(2,1)S(1)}, u32[]{:S(2)}, u32[]{:S(2)}) collective-permute-start(bf16[256,1536]{1,0:T(8,128)(2,1)S(1)} %get-tuple-element.144), channel_id=1, source_target_pairs={{0,8},{4,12},{8,0},{12,4},{1,9},{5,13},{9,1},{13,5},{2,10},{6,14},... | collective-permute-start | bytes 2359304 | tf_op jit(solution)/shard_map/ppermute | solution.py:28
  164.8 28.6 %collective-permute-start.27 = (bf16[256,1024]{1,0:T(8,128)(2,1)S(1)}, bf16[256,1024]{1,0:T(8,128)(2,1)S(1)}, u32[]{:S(2)}, u32[]{:S(2)}) collective-permute-start(bf16[256,1024]{1,0:T(8,128)(2,1)S(1)} %get-tuple-element.142), channel_id=1, source_target_pairs={{0,8},{4,12},{8,0},{12,4},{1,9},{5,13},{9,1},{13,5},{2,10},{6,14},... | collective-permute-start | bytes 1572872 | tf_op jit(solution)/shard_map/ppermute | solution.py:28
  200.7 17.2 %collective-permute-start.29 = (bf16[640,640]{1,0:T(8,128)(2,1)S(1)}, bf16[640,640]{1,0:T(8,128)(2,1)S(1)}, u32[]{:S(2)}, u32[]{:S(2)}) collective-permute-start(bf16[640,640]{1,0:T(8,128)(2,1)S(1)} %shard_map.149.refs_0_), channel_id=1, source_target_pairs={{0,8},{4,12},{8,0},{12,4},{1,9},{5,13},{9,1},{13,5},{2,10},{6,14},... | collective-permute-start | bytes 2457608 | tf_op jit(solution)/shard_map/ppermute | solution.py:28
  201.1 21.7 %collective-permute-start.30 = (bf16[640,640]{1,0:T(8,128)(2,1)S(1)}, bf16[640,640]{1,0:T(8,128)(2,1)S(1)}, u32[]{:S(2)}, u32[]{:S(2)}) collective-permute-start(bf16[640,640]{1,0:T(8,128)(2,1)S(1)} %shard_map.149.refs_0_), channel_id=1, source_target_pairs={{0,4},{4,0},{8,12},{12,8},{1,5},{5,1},{9,13},{13,9},{2,6},{6,2},{1... | collective-permute-start | bytes 2457608 | tf_op jit(solution)/shard_map/ppermute | solution.py:28
  217.9 5.5 %collective-permute-start.31 = (bf16[640,640]{1,0:T(8,128)(2,1)S(1)}, bf16[640,640]{1,0:T(8,128)(2,1)S(1)}, u32[]{:S(2)}, u32[]{:S(2)}) collective-permute-start(bf16[640,640]{1,0:T(8,128)(2,1)S(1)} %collective-permute-done.29.refs_1_), channel_id=1, source_target_pairs={{0,4},{4,0},{8,12},{12,8},{1,5},{5,1},{9,13},{13,9},{2,6},{6,2},{1... | collective-permute-start | bytes 2457608 | tf_op jit(solution)/shard_map/ppermute | solution.py:28
  223.4 3.4 %copy-start.1 = (f32[1,2560]{1,0:T(1,128)S(1)}, f32[1,2560]{1,0:T(1,128)}, u32[]{:S(2)}) copy-start(f32[1,2560]{1,0:T(1,128)} %param.17) | copy-start | bytes 30724
  (23 other events, 24.7 us)

commit v3 on v1

v3 whole, which is shorter than its diff:
```python
import functools
import math

import jax
import jax.numpy as jnp
from jax import lax
from jax.experimental import pallas as pl
from jax.experimental.pallas import tpu as pltpu
from jax.sharding import PartitionSpec as P

DH = 128
LANES = 128
NEG = -1e30
MIB = 1 << 20
VALUES = 6
SCALE = MIB


def cost(micros):
    return pl.CostEstimate(flops=0, bytes_accessed=int(micros * SCALE), transcendentals=0)


def vmem(blocks, times=2):
    size = sum(math.prod(shape) * jnp.dtype(kind).itemsize for shape, kind in blocks)
    return pltpu.CompilerParams(vmem_limit_bytes=min(times * size + VALUES * MIB, 60 * MIB))


def spec(block, index, shape):
    if block == shape:
        return pl.BlockSpec(block, index, pipeline_mode=pl.Buffered(1))
    return pl.BlockSpec(block, index)


def room(ins, outs):
    once = [(b, a.dtype) for a, b, _ in ins if b == a.shape]
    twice = [(b, a.dtype) for a, b, _ in ins if b != a.shape] + [(b, d) for _, d, b, _ in outs]
    size = sum(math.prod(shape) * jnp.dtype(kind).itemsize for shape, kind in once + twice + twice)
    return pltpu.CompilerParams(vmem_limit_bytes=min(size + VALUES * MIB, 60 * MIB))


def swap(value, axis, bit):
    return lax.ppermute(value, axis, [(i, i ^ bit) for i in range(lax.axis_size(axis))])


def bits_of(size):
    return [1 << j for j in range(size.bit_length() - 1)]


def head_probs(query, key, valid):
    scores = lax.dot_general(query, key, (((1,), (1,)), ((), ())), preferred_element_type=jnp.float32)
    scores = jnp.where(valid, scores * (DH**-0.5), NEG)
    top = jnp.max(scores, axis=-1, keepdims=True)
    exps = jnp.exp(scores - top)
    return exps * (1.0 / jnp.sum(exps, axis=-1, keepdims=True))


def valid_mask(seq, length):
    rows = lax.broadcasted_iota(jnp.int32, (seq, seq), 0)
    cols = lax.broadcasted_iota(jnp.int32, (seq, seq), 1)
    return (cols <= rows) & (cols < length)


def forward_kernel(length_ref, q_ref, k_ref, v_ref, out_ref):
    seq, wide = q_ref.shape
    valid = valid_mask(seq, length_ref[0])
    for head in range(wide // DH):
        at = slice(head * DH, (head + 1) * DH)
        probs = head_probs(q_ref[:, at], k_ref[:, at], valid).astype(jnp.bfloat16)
        out_ref[:, at] = jnp.dot(probs, v_ref[:, at], preferred_element_type=jnp.float32).astype(out_ref.dtype)


def backward_kernel(length_ref, q_ref, k_ref, v_ref, one_ref, two_ref, *refs):
    dq_ref, dk_ref, dv_ref = refs[-3:]
    seq, wide = q_ref.shape
    valid = valid_mask(seq, length_ref[0])
    for head in range(wide // DH):
        at = slice(head * DH, (head + 1) * DH)
        query, key, value = q_ref[:, at], k_ref[:, at], v_ref[:, at]
        probs = head_probs(query, key, valid)
        d_attn = (one_ref[:, at].astype(jnp.float32) + two_ref[:, at].astype(jnp.float32)).astype(jnp.bfloat16)
        dv_ref[:, at] = lax.dot_general(
            probs.astype(jnp.bfloat16), d_attn, (((0,), (0,)), ((), ())), preferred_element_type=jnp.float32
        ).astype(dv_ref.dtype)
        dprob = lax.dot_general(d_attn, value, (((1,), (1,)), ((), ())), preferred_element_type=jnp.float32)
        delta = jnp.sum(dprob * probs, axis=-1, keepdims=True)
        ds = (probs * (dprob - delta) * (DH**-0.5)).astype(jnp.bfloat16)
        dq_ref[:, at] = jnp.dot(ds, key, preferred_element_type=jnp.float32).astype(dq_ref.dtype)
        dk_ref[:, at] = lax.dot_general(
            ds, query, (((0,), (0,)), ((), ())), preferred_element_type=jnp.float32
        ).astype(dk_ref.dtype)


def hidden_kernel(team, low, gathered, *refs):
    if gathered:
        pairs, refs, attn_ref = refs[: team // 2], refs[team // 2 : -1], refs[-1]
    else:
        attn_ref, refs = refs[0], refs[1:]
    weight_ref, gain_ref, *rest = refs[: 2 + team]
    hidden_ref, sent_ref, square_ref = refs[2 + team :]
    n = rest[0].shape[0]

    def gather(i):
        attn_ref[...] = pairs[i][...]

    def finish(i):
        for j in range(2):
            at = slice(j * n, (j + 1) * n)
            hidden = rest[2 * i + j][:, low : low + pair.shape[1]].astype(jnp.float32) + pair[at]
            hidden_ref[at] = hidden
            sent_ref[at] = (hidden * gain_ref[...]).astype(sent_ref.dtype)
            square_ref[j] = to_lanes(jnp.sum(hidden * hidden, axis=-1, keepdims=True))

    for i in range(team // 2 if gathered else 0):
        pl.when(pl.program_id(0) == i)(functools.partial(gather, i))
    pair = jnp.dot(attn_ref[...], weight_ref[...], preferred_element_type=jnp.float32)
    for i in range(team // 2):
        pl.when(pl.program_id(0) == i)(functools.partial(finish, i))


def to_lanes(column):
    return jnp.transpose(jnp.broadcast_to(column, (column.shape[0], LANES)))[:1]


def to_column(row):
    return jnp.transpose(jnp.broadcast_to(row, (LANES, row.shape[1])))[:, :1]


def matched(hidden, sent, gain, inv, inv_other, weight):
    normed = hidden * inv
    diff = normed * gain - sent.astype(jnp.float32) * inv_other
    return normed, diff, weight * diff * gain


def match_kernel(hidden_ref, sent_ref, gain_ref, inv_ref, other_ref, weight_ref, *refs):
    n = inv_ref.shape[-1]
    for i in range(inv_ref.shape[0]):
        at = slice(i * n, (i + 1) * n)
        inv, other, weight = to_column(inv_ref[i]), to_column(other_ref[i]), to_column(weight_ref[i])
        normed, diff, scaled = matched(hidden_ref[at], sent_ref[at], gain_ref[...], inv, other, weight)
        square = to_lanes(jnp.sum(diff * diff, axis=-1, keepdims=True))
        cross = to_lanes(jnp.sum(normed * scaled, axis=-1, keepdims=True))
        if len(refs) > 1:
            square, cross = square + refs[0][i, :1], cross + refs[0][i, 1:]
        refs[-1][i, :1] = square
        refs[-1][i, 1:] = cross


def d_hidden_kernel(lows, at_ref, attn_ref, inv_ref, other_ref, weight_ref, mean_ref, *refs):
    d_ref, terms_ref, total_ref = refs[-3:]
    n, count = inv_ref.shape[-1], len(lows)
    for i in range(inv_ref.shape[0]):
        at = slice(i * n, (i + 1) * n)
        inv, other, weight = to_column(inv_ref[i]), to_column(other_ref[i]), to_column(weight_ref[i])
        mean = to_column(mean_ref[i])
        for low, hidden_ref, sent_ref, gain_ref in zip(lows, refs, refs[count:], refs[2 * count :]):
            normed, _, scaled = matched(hidden_ref[at], sent_ref[at], gain_ref[...], inv, other, weight)
            d_hidden = (inv * (scaled - normed * mean)).astype(d_ref.dtype)
            d_ref[at, low : low + d_hidden.shape[1]] = d_hidden
    terms = lax.dot_general(attn_ref[...], d_ref[...], (((0,), (0,)), ((), ())), preferred_element_type=jnp.float32)
    step, last = pl.program_id(0), pl.num_programs(0) - 1

    @pl.when(step == 0)
    def _():
        total_ref[...] = terms

    @pl.when((step > 0) & (step < last))
    def _():
        total_ref[...] += terms

    @pl.when(step == last)
    def _():
        terms_ref[...] = (total_ref[...] + terms).astype(terms_ref.dtype)


def terms_kernel(lows, at_ref, attn_ref, d_ref, *outs):
    terms = lax.dot_general(
        attn_ref[...], d_ref[...], (((0,), (0,)), ((), ())), preferred_element_type=jnp.float32
    ).astype(jnp.bfloat16)
    for low, out in zip(lows, outs):
        out[...] = terms[:, low : low + out.shape[1]]


def d_attn_kernel(lows, d_ref, *refs):
    outs = refs[len(lows) :]
    total = 0.0
    for low, weight_ref in zip(lows, refs):
        total = total + lax.dot_general(
            d_ref[:, low : low + weight_ref.shape[1]],
            weight_ref[...],
            (((1,), (1,)), ((), ())),
            preferred_element_type=jnp.float32,
        )
    total = total.astype(outs[0].dtype)
    n = outs[0].shape[1]
    for i, out in enumerate(outs):
        out[...] = total[:, i * n : (i + 1) * n]


def assemble_kernel(wide, places, member_ref, *refs):
    for ref, (other, low) in zip(refs[:-1], places):
        at = pl.multiple_of((member_ref[0] ^ other) * wide + low, LANES)
        refs[-1][:, pl.ds(at, ref.shape[1])] = ref[...].astype(refs[-1].dtype)


ANY = pl.BlockSpec(memory_space=pl.ANY)


def small_call(kernel, indices, ins, outs, into=None, micros=1.0, grid=1, scratch=()):
    out = pl.pallas_call(
        kernel,
        grid_spec=pltpu.PrefetchScalarGridSpec(
            num_scalar_prefetch=1,
            grid=(grid,),
            in_specs=[spec(b, m, a.shape) for a, b, m in ins] + [ANY] * (into is not None),
            out_specs=[pl.BlockSpec(b, m) for _, _, b, m in outs],
            scratch_shapes=list(scratch),
        ),
        out_shape=[jax.ShapeDtypeStruct(shape, d) for shape, d, _, _ in outs],
        input_output_aliases={} if into is None else {1 + len(ins): 0},
        cost_estimate=cost(micros),
        compiler_params=room(ins, outs),
    )(jnp.stack([jnp.int32(i) for i in indices]), *[a for a, _, _ in ins], *(() if into is None else (into,)))
    return out


ORIGIN = lambda i, at: (0, 0)
DOWN = lambda i, at: (at[0], 0)


def split_kernel(count, at_ref, in_ref, *outs):
    for i in range(0, len(outs), count):
        at = at_ref[i // count]
        for out in outs[i : i + count]:
            n = out.shape[1]
            out[...] = in_ref[:, pl.ds(at if isinstance(at, int) else pl.multiple_of(at, LANES), n)]
            at = at + n


def cut_columns(array, places, widths):
    n = array.shape[0]
    if any(w % LANES for w in widths):
        return [lax.dynamic_slice(array, (0, p), (n, w)) for p in places for w in widths]
    outs = [((n, w), array.dtype, (n, w), ORIGIN) for _ in places for w in widths]
    return small_call(
        functools.partial(split_kernel, len(widths)), places, [(array, array.shape, ORIGIN)], outs
    )


def copy_kernel(at_ref, in_ref, *refs):
    refs[-1][...] = in_ref[...]


def place_rows(whole, piece, index):
    new = isinstance(whole, tuple)
    shape = whole if new else whole.shape
    outs = [(shape, piece.dtype, piece.shape, DOWN)]
    return small_call(copy_kernel, [index], [(piece, piece.shape, ORIGIN)], outs, None if new else whole)[0]


def take_rows(array, index, rows):
    block = (rows, array.shape[1])
    return small_call(copy_kernel, [index], [(array, block, DOWN)], [(block, array.dtype, block, ORIGIN)])[0]


def stack_kernel(across, at_ref, *refs):
    n, column = refs[0].shape[0], 0
    for i, ref in enumerate(refs[:-1]):
        row = i // across * n
        refs[-1][row : row + n, column : column + ref.shape[1]] = ref[...]
        column = (column + ref.shape[1]) % refs[-1].shape[1]


def stack_blocks(rows):
    n = rows[0][0].shape[0]
    shape = (n * len(rows), sum(x.shape[1] for x in rows[0]))
    pieces = [x for row in rows for x in row]
    ins = [(x, x.shape, ORIGIN) for x in pieces]
    kernel = functools.partial(stack_kernel, len(rows[0]))
    return small_call(kernel, [0], ins, [(shape, pieces[0].dtype, shape, ORIGIN)])[0]


def whole_kernel(low, count, at_ref, *refs):
    out = refs[-1]
    n, wide = refs[0].shape[0], out.shape[1]
    for i in range(count):
        block = refs[i][:, low : low + wide]
        if i == count - 1 and len(refs) - 1 > count:
            block = block + refs[count][:, low : low + wide]
        out[pl.ds(pl.multiple_of(at_ref[i] * n, 16), n)] = block


def add_kernel(low, at_ref, *refs):
    out_ref = refs[-1]
    total = 0.0
    for ref in refs[:-1]:
        n = out_ref.shape[1]
        part = ref[...] if ref.shape[1] == n else ref[:, low : low + n]
        total = total + part.astype(jnp.float32)
    out_ref[...] = total.astype(out_ref.dtype)


def sum_terms(got, low, terms, index):
    block = (got[0].shape[0], terms.shape[1])
    ins = [(g, g.shape, ORIGIN) for g in got] + [(terms, block, DOWN)]
    kernel = functools.partial(add_kernel, low)
    return small_call(kernel, [index], ins, [(block, terms.dtype, block, ORIGIN)])[0]


def fold_kernel(pieces, *refs):
    kept_ref, sent_ref = refs[2 * pieces :]
    half = kept_ref.shape[0]
    at = 0
    for near_ref, far_ref in zip(refs[:pieces], refs[pieces : 2 * pieces]):
        n = far_ref.shape[1]
        total = near_ref[...].astype(jnp.float32) + far_ref[...].astype(jnp.float32)
        total = total.astype(kept_ref.dtype)
        kept_ref[:, at : at + n] = total[:half]
        sent_ref[:, at : at + n] = total[half:]
        at += n


def fold(near, far):
    n, wide = near[0].shape[0], sum(x.shape[1] for x in near)
    ins = [(x, x.shape, lambda i: (0, 0)) for x in (*near, *far)]
    outs = [((n // 2, wide), near[0].dtype, (n // 2, wide), lambda i: (0, 0))] * 2
    return call(1.0, functools.partial(fold_kernel, len(near)), (1,), ins, outs)


def call(micros, kernel, grid, ins, outs):
    return pl.pallas_call(
        kernel,
        grid=grid,
        in_specs=[spec(b, m, a.shape) for a, b, m in ins],
        out_specs=[pl.BlockSpec(b, m) for _, _, b, m in outs],
        out_shape=[jax.ShapeDtypeStruct(s, d) for s, d, _, _ in outs],
        cost_estimate=cost(micros),
        compiler_params=room(ins, outs),
    )(*[a for a, _, _ in ins])


def attention_call(micros, kernel, length, arrays, moved, outs, first, number, group, into=None):
    seq = arrays[0].shape[0]
    there = pl.BlockSpec((seq, group), lambda i, *_: (0, i + first))
    here = pl.BlockSpec((seq, group), lambda i, *_: (0, i))
    alone = into is None
    into = into or ()
    shape = jax.ShapeDtypeStruct((seq, group * number) if alone else arrays[0].shape, jnp.bfloat16)
    given = 1 + len(arrays) + len(moved)
    return pl.pallas_call(
        kernel,
        grid_spec=pltpu.PrefetchScalarGridSpec(
            num_scalar_prefetch=1,
            grid=(number,),
            in_specs=[there] * len(arrays) + [here] * len(moved) + [pl.BlockSpec(memory_space=pl.ANY)] * len(into),
            out_specs=[here if alone else there] * outs,
        ),
        out_shape=[shape] * outs,
        input_output_aliases={given + i: i for i in range(len(into))},
        cost_estimate=cost(micros),
        compiler_params=vmem([((seq, group), jnp.bfloat16)] * (given - 1 + outs)),
    )(length.reshape(1), *arrays, *moved, *into)


def group_width(heads_width):
    heads = heads_width // DH
    return DH * max(g for g in (4, 2, 1) if heads % g == 0)


def tie(*values):
    return lax.optimization_barrier(values)


def split(values, *counts):
    lists, at = [], 0
    for count in counts:
        lists.append(list(values[at : at + count]))
        at += count
    return *lists, list(values[at:])


def send(value, axis, pairs):
    return lax.ppermute(value, axis, pairs)


LINE = 4
ENDS_OUT = [(2, 3), (1, 0)]
ENDS_IN = [(0, 1), (3, 2)]
MIDDLE = [(1, 2), (2, 1)]


def body(queries, keys, values, residual, event_ids, lengths, type_weight, w_out, gain):
    seq, heads_width = queries.shape[2:]
    width = residual.shape[3]
    parts = lax.axis_size("fsdp")
    team = lax.axis_size("dp")
    bits = bits_of(team)
    rows = team * seq
    shard_rows = w_out.shape[1]
    part = lax.axis_index("fsdp")
    member = lax.axis_index("dp")
    own = lax.axis_index(("dp", "fsdp"))
    length = lengths[own]
    count = jnp.sum(lengths).astype(jnp.float32)
    wide = width // team
    line = parts == LINE and shard_rows % LANES == 0
    two = line and wide % LANES == 0 and wide > LANES
    cut = -(-wide * 3 // (5 * LANES)) * LANES
    chunks = [(0, cut), (cut, wide)] if two else [(0, wide)]
    f32, bf16 = jnp.float32, jnp.bfloat16
    group = group_width(heads_width)
    steps = heads_width // group
    ends = sorted({0, 2 * steps // 5, 4 * steps // 5, steps})
    cuts = list(zip(ends[:-1], ends[1:]))
    q, k, v = queries[0, 0], keys[0, 0], values[0, 0]

    row_at = lambda i: (i, 0)
    fixed = lambda i, *_: (0, 0)
    fixed3 = lambda i, *_: (0, 0, 0)
    stat_at = lambda i, *_: (i, 0, 0)
    lows = [low for low, _ in chunks]
    sizes = [high - low for low, high in chunks]

    order = [0]
    for bit in reversed(bits):
        order = order + [s ^ bit for s in order]

    column = (w_out[0], (shard_rows, wide), lambda i, at: (0, at[0]))
    if wide % LANES == 0:
        (block,) = small_call(copy_kernel, [member], [column], [((shard_rows, wide), bf16, (shard_rows, wide), ORIGIN)])
    else:
        (block,) = cut_columns(w_out[0], [member * wide], [wide])
    others = [1, 2] if line else list(range(1, parts))
    came = [swap(block, "fsdp", s) for s in others]

    attn = []
    middle = max(1, 2 * steps // 5)
    for first, final in [(0, middle), (middle, steps)] if steps > 1 else [(0, steps)]:
        attn += attention_call(
            1.5 * (final - first), forward_kernel, length, (q, k, v), (), 1, first, final - first, group
        )
    far = [swap(a, "dp", bits[-1]) for a in attn]
    home, _ = tie(residual[0, 0], attn[-1])
    mine = cut_columns(home, [(member ^ s) * wide for s in order], [wide])
    if team == 4:
        mine = [mine[0], mine[2], stack_blocks([[mine[1]], [mine[3]]])]
    tied = tie(*came, block, count, *attn, *far, *mine)
    came, (block, count), attn, far, mine = split(tied, len(others), 2, len(attn), len(attn))

    last = [send(block, "fsdp", MIDDLE), send(came[1], "fsdp", ENDS_OUT)] if line else []
    pairs = [stack_blocks([attn, far])]
    for bit in reversed(bits[:-1]):
        pairs = pairs + [swap(x, "dp", bit) for x in pairs]
    if team == 4:
        here, beside, across = mine
        across = swap(across, "dp", 2)
        rest = [across, swap(beside, "dp", 1), swap(take_rows(across, 1, seq), "dp", 1)]
        rest = [here, *rest]
    else:
        rest = [swap(piece, "dp", s) if s else piece for s, piece in zip(order, mine)]
    tied = tie(*last, *pairs, *rest)
    last, pairs, rest = split(tied, len(last), len(pairs))
    spots = [part, *[part ^ s for s in others], *([part ^ 3] if line else [])]
    shapes = [(heads_width, n) for n in sizes]

    def whole_weight(i):
        ins = [(b, b.shape, fixed) for b in [block, *came, *last]]
        kernel = functools.partial(whole_kernel, lows[i], len(spots))
        return small_call(kernel, spots, ins, [(shapes[i], bf16, shapes[i], fixed)], micros=2.0)[0]

    def team_sum(value):
        shape = value.shape
        value = value.reshape((2,) * len(bits) + shape[1:])
        for axis, bit in enumerate(bits):
            value = value + jnp.flip(swap(value, "dp", bit), axis)
        return value.reshape(shape)

    my_gain = lax.dynamic_slice(gain[0], (member * wide,), (wide,))[None]
    gains = [my_gain[:, low:high] for low, high in chunks]
    tall = rows // 2

    hidden, sent, square, partner, weights = [], [], [], [], []
    for i, n in enumerate(sizes):
        weights.append(whole_weight(i))
        ins = [(a, a.shape, fixed) for a in (weights[i], gains[i])] + [(a, (seq, wide), fixed) for a in rest]
        outs = [
            ((rows, n), f32, (2 * seq, n), row_at),
            ((rows, n), bf16, (2 * seq, n), row_at),
            ((team, 1, seq), f32, (2, 1, seq), stat_at),
        ]
        whole = ((rows, heads_width), bf16, (2 * seq, heads_width), row_at)
        if i:
            ins = [(attn, whole[2], row_at), *ins]
        else:
            ins = [(a, a.shape, fixed) for a in pairs] + ins
            outs.append(whole)
        kernel = functools.partial(hidden_kernel, team, lows[i], i == 0)
        h, x, sq, *new = call(2.0, kernel, (team // 2,), ins, outs)
        attn = new[0] if new else attn
        if i + 1 < len(chunks):
            partner.append(swap(x, "copy", 1))
        hidden.append(h)
        sent.append(x)
        square.append(sq)
    inv = lax.rsqrt(team_sum(sum(square)) / width + 1e-06)
    inv_other = swap(inv, "copy", 1)
    partner.append(swap(sent[-1], "copy", 1))

    types = jnp.arange(type_weight.shape[0], dtype=jnp.int32)
    ids, _ = tie(event_ids, x)
    matches = ids[0][:, None] == types[None, :]
    looked_up = jnp.sum(jnp.where(matches, type_weight[None, :], f32(0.0)), axis=-1)
    tok_w = jnp.where(jnp.arange(seq, dtype=jnp.int32) < length, looked_up, f32(0.0))
    tok_w = tok_w.reshape(1, 1, seq)
    for bit in reversed(bits):
        tok_w = jnp.concatenate([tok_w, swap(tok_w, "dp", bit)], axis=0)
    row_scale = 2.0 * tok_w / (width * count)
    stats = [inv, inv_other, row_scale]

    both = []
    for i in range(len(chunks)):
        n = sizes[i]
        (found,) = call(
            3.0,
            match_kernel,
            (team // 2,),
            [(hidden[i], (2 * seq, n), row_at), (partner[i], (2 * seq, n), row_at), (gains[i], (1, n), fixed)]
            + [(a, (2, *a.shape[1:]), stat_at) for a in (*stats, *both[-1:])],
            [((team, 2, seq), f32, (2, 2, seq), stat_at)],
        )
        if i + 1 < len(chunks):
            found, partner[i + 1] = tie(found, partner[i + 1])
        both.append(found)
    both = team_sum(both[-1])
    loss = jnp.sum(tok_w[0] * both[0, :1]) / (width * count)
    mean = both[:, 1:] / width

    columns = shard_rows if line else heads_width
    d_hidden, terms = small_call(
        functools.partial(d_hidden_kernel, lows),
        [part ^ 3 if line else 0],
        [(attn, (2 * seq, columns), lambda i, at: (i, at[0]))]
        + [(x, (2, 1, seq), stat_at) for x in (*stats, mean)]
        + [(x, (2 * seq, x.shape[1]), lambda i, at: (i, 0)) for x in (*hidden, *partner)]
        + [(x, x.shape, fixed) for x in gains],
        [((rows, wide), bf16, (2 * seq, wide), lambda i, at: (i, 0)), ((columns, wide), bf16, (columns, wide), fixed)],
        grid=team // 2,
        scratch=[pltpu.VMEM((columns, wide), f32)],
        micros=4.0,
    )
    if line:
        early = [send(terms, "fsdp", MIDDLE), send(terms, "fsdp", ENDS_IN)]
        terms = small_call(
            functools.partial(terms_kernel, lows),
            [part ^ 1, part ^ 2, part],
            [(attn, (rows, shard_rows), lambda i, at: (0, at[i])), (d_hidden, (rows, wide), fixed)],
            [((3 * shard_rows, n), bf16, (shard_rows, n), lambda i, at: (i, 0)) for n in sizes],
            micros=4.0,
            grid=3,
        )
    else:
        early = [swap(take_rows(terms, part ^ s, shard_rows), "fsdp", s) for s in range(1, parts)]
        terms = [terms]

    across, each = group, 1

    def d_attn_rows(half, d_hidden):
        return call(
            3.0,
            functools.partial(d_attn_kernel, lows),
            (1,),
            [(d_hidden, (tall, wide), lambda i: (half, 0))] + [(w, w.shape, fixed) for w in weights],
            [((tall, across), bf16, (tall, across), fixed)] * (heads_width // across),
        )

    far = [swap(x, "dp", bits[0]) for x in d_attn_rows(1, d_hidden)]
    near = d_attn_rows(0, d_hidden)
    for bit in bits[1:-1]:
        near, far = zip(*[fold([x], [y]) for x, y in zip(near, far)])
        far = [swap(x, "dp", bit) for x in far]
    folded = [fold(near[each * first : each * final], far[each * first : each * final]) for first, final in cuts]
    kept, passed = zip(*folded)
    tied = tie(*early, *terms, *kept, *passed)
    early, terms, kept, passed, _ = split(tied, len(early), len(chunks), len(cuts), len(cuts))

    def late_sends(i):
        if not line:
            return []
        beyond = sum_terms([early[1]], lows[i], terms[i], 1)
        return [swap(beyond, "fsdp", 2), swap(take_rows(terms[i], 0, shard_rows), "fsdp", 1)]

    def team_pieces(i, got):
        got = early[:1] + got if line else early
        total = sum_terms(got, lows[i], terms[i], 2 if line else part)
        pieces = {0: total}
        for bit in reversed(bits):
            pieces.update({s ^ bit: swap(p, "dp", bit) for s, p in pieces.items()})
        return [pieces[s] for s in order]

    def back(j, grads):
        first, last = cuts[j]
        arrays = (q, k, v), (kept[j], passed[j])
        micros = 1.5 * (last - first) + 1.0
        return attention_call(micros, backward_kernel, length, *arrays, 3, first, last - first, group, grads)

    got = late_sends(0)
    passed = [swap(x, "dp", bits[-1]) for x in passed]
    grads = back(0, ())
    early_parts = passed
    tied = tie(*got, *grads, *terms, *early, loss, *early_parts)
    got, grads, terms, early, (loss,), early_parts = split(tied, len(got), 3, len(chunks), len(early), 1)
    passed = [*early_parts, *passed[len(early_parts) :]]

    placed = []
    for i in range(1, len(chunks)):
        late = late_sends(i)
        placed += team_pieces(i - 1, got)
        if i == 1:
            for j in range(1, len(cuts)):
                grads = back(j, grads)
        tied = tie(*late, *grads)
        got, grads, _ = split(tied, len(late), 3)
    placed += team_pieces(len(chunks) - 1, got)
    if len(chunks) == 1:
        for j in range(1, len(cuts)):
            grads = back(j, grads)
    d_queries, d_keys, d_values = grads
    places = [(s, low) for low in lows for s in order]

    if wide % LANES == 0:
        tall = next(t for t in (128, 64, 32, 16, shard_rows) if shard_rows % t == 0)
        out = pl.pallas_call(
            functools.partial(assemble_kernel, wide, places),
            grid_spec=pltpu.PrefetchScalarGridSpec(
                num_scalar_prefetch=1,
                grid=(shard_rows // tall,),
                in_specs=[pl.BlockSpec((tall, p.shape[1]), lambda i, *_: (i, 0)) for p in placed],
                out_specs=pl.BlockSpec((tall, width), lambda i, *_: (i, 0)),
            ),
            out_shape=jax.ShapeDtypeStruct((shard_rows, width), f32),
            cost_estimate=cost(1.0),
            compiler_params=vmem([((tall, width), bf16), ((tall, width), f32)]),
        )(member.reshape(1), *placed)
    else:
        out = jnp.zeros((shard_rows, width), f32)
        for piece, (s, low) in zip(placed, places):
            out = lax.dynamic_update_slice(out, piece.astype(f32), (0, (member ^ s) * wide + low))
    return (
        loss.reshape(1, 1),
        d_queries[None, None],
        d_keys[None, None],
        d_values[None, None],
        out[None],
    )


def solution(mesh):
    whole = P("copy", ("dp", "fsdp"), None, None)
    in_specs = (
        whole,
        whole,
        whole,
        whole,
        P(("dp", "fsdp"), None),
        P(),
        P(),
        P("copy", "fsdp", None),
        P("copy", None),
    )
    out_specs = (P("copy", ("dp", "fsdp")), whole, whole, whole, P("copy", "fsdp", None))
    return jax.shard_map(body, mesh=mesh, in_specs=in_specs, out_specs=out_specs, check_vma=False)
```

time: 293 us -> 218 us (0.74)
  Pallas kernels: 22.6 us -> 77.7 us
  waiting for transfers between devices: 124 us -> 78.5 us
  local copies, waits for them, and re-layouts: 44.7 us -> 8.47 us
  matrix products: 33.4 us -> 0 us
  other arithmetic: 25 us -> 3.81 us
  starting transfers between devices: 38.7 us -> 45.4 us
    pallas_call x0 -> x25, Pallas kernels: none -> 48.1 us  [the longest x15 23.9 us: small_call(): pl.pallas_call(kernel, grid_spec=pltpu.PrefetchScalarGridSpec(num_scalar_...]
    ppermute x12 -> x4, waiting for transfers between devices: 53 us -> 9.77 us  [send(): return lax.ppermute(value, axis, pairs)]
    dot_general x6 -> x0, matrix products: 33.4 us -> none  [the longest x2 14.9 us: body(): jnp.dot(attn, weight, preferred_element_type=jnp.float32)]
    dynamic_slice x7 -> x0, local copies, waits for them, and re-layouts: 11.6 us -> none  [the longest x5 9.89 us: body(): block = lax.dynamic_slice(home, (0, (member ^ s) * wide), (seq, wide))]
    dynamic_update_slice x8 -> x0, local copies, waits for them, and re-layouts: 10.3 us -> none  [the longest x6 6.52 us: body(): whole = lax.dynamic_update_slice(whole, block, (at, 0))]
    dynamic_update_slice x8 -> x0, other arithmetic: 9.88 us -> none  [body(): lax.dynamic_update_slice(out, piece.astype(jnp.float32), (0, (member ^ s)...]
    ppermute x23 -> x35, starting transfers between devices: 32 us -> 40.3 us  [swap(): lax.ppermute(value, axis, [(i, i ^ bit) for i in range(lax.axis_size(axis...]
    pallas_call x2 -> x5, Pallas kernels: 22.6 us -> 29.5 us  [attention_call(): pl.pallas_call(kernel, grid_spec=pltpu.PrefetchScalarGridSpec(num_scalar_...]
  transfers between devices with their start and end apart: 35 -> 39, of which waited for: 16 -> 12; matrix products, arithmetic and copies ran while one was open for 22% -> 2% of each run, Pallas kernels for 0% -> 22%
where the time goes in v3:
time: 218 us; the launch traced here: 217 us
  waiting for transfers between devices  78.5 us (36%)
  Pallas kernels  77.7 us (36%)
  starting transfers between devices  45.4 us (21%)
  local copies, waits for them, and re-layouts  8.47 us (4%)
  other arithmetic  3.81 us (2%)
  between operations  3.4 us (2%)
    ppermute x35, waiting for transfers between devices, swap(): lax.ppermute(value, axis, [(i, i ^ bit) for i in range(lax.axis_size(axis...  68.8 us
    ppermute x35, starting transfers between devices, swap(): lax.ppermute(value, axis, [(i, i ^ bit) for i in range(lax.axis_size(axis...  40.3 us
    pallas_call x5, Pallas kernels, attention_call(): pl.pallas_call(kernel, grid_spec=pltpu.PrefetchScalarGridSpec(num_scalar_...  29.5 us
    pallas_call x15, Pallas kernels, small_call(): pl.pallas_call(kernel, grid_spec=pltpu.PrefetchScalarGridSpec(num_scalar_...  23.9 us
    pallas_call x9, Pallas kernels, call(): pl.pallas_call(kernel, grid=grid, in_specs=[spec(b, m, a.shape) for a, b,...  20.8 us
    ppermute x4, waiting for transfers between devices, send(): return lax.ppermute(value, axis, pairs)  9.77 us
    unnamed x54, local copies, waits for them, and re-layouts  7.81 us
    ppermute x4, starting transfers between devices, send(): return lax.ppermute(value, axis, pairs)  5.11 us
  transfers between devices with their start and end apart: 39, of which 12 were waited for; matrix products, arithmetic and copies ran while one was open for 2% of the time, Pallas kernels for 22%

profile of v3, /device:TPU:1, one launch (start us, length us, event | category | flops | bytes accessed | tf_op | source)
XLA Modules:
  0.0 217.3 jit_solution(13057094592507677366)
XLA Ops:
  0.7 1.9 copy-done.11
  2.7 3.2 %collective-permute-start.1 = (bf16[640,640]{1,0:T(8,128)(2,1)S(1)}, bf16[640,640]{1,0:T(8,128)(2,1)}, u32[]{:S(2)}, u32[]{:S(2)}) collective-permute-start(bf16[640,640]{1,0:T(8,128)(2,1)S(1)} %shard_map.128.refs_0_), channel_id=1, source_target_pairs={{0,2},{1,3},{2,0},{3,1},{4,6},{5,7},{6,4},{7,5},{8,10},{9,11},{10,... | collective-permute-start | bytes 2457608 | tf_op jit(solution)/shard_map/ppermute | solution.py:42
  5.9 1.3 collective-permute-start
  7.9 1.3 copy-done.4
  9.2 5.0 %shard_map.130.refs_1_ = bf16[256,1536]{1,0:T(8,128)(2,1)} custom-call(s32[1]{0:T(128)} %dynamic_slice.6.length_ref, bf16[256,2560]{1,0:T(8,128)(2,1)S(1)} %bitcast.35, bf16[256,2560]{1,0:T(8,128)(2,1)S(1)} %bitcast.40, bf16[256,2560]{1,0:T(8,128)(2,1)S(1)} %bitcast.45), custom_call_target="tpu_custom_call" | custom-call | bytes 4718592 | tf_op jit(solution)/shard_map/pallas_call | solution.py:349
  15.4 3.8 %shard_map.129.refs_0_ = bf16[256,1024]{1,0:T(8,128)(2,1)} custom-call(s32[1]{0:T(128)} %dynamic_slice.6.length_ref, bf16[256,2560]{1,0:T(8,128)(2,1)S(1)} %bitcast.36, bf16[256,2560]{1,0:T(8,128)(2,1)S(1)} %bitcast.41, bf16[256,2560]{1,0:T(8,128)(2,1)S(1)} %bitcast.46), custom_call_target="tpu_custom_call" | custom-call | bytes 3145728 | tf_op jit(solution)/shard_map/pallas_call | solution.py:349
  20.7 1.3 copy-done.16
  23.6 19.9 %collective-permute-done.2.refs_2_ = bf16[256,1024]{1,0:T(8,128)(2,1)} collective-permute-done((bf16[256,1024]{1,0:T(8,128)(2,1)}, bf16[256,1024]{1,0:T(8,128)(2,1)}, u32[]{:S(2)}, u32[]{:S(2)}) %collective-permute-start.2) | collective-permute-done | bytes 524320 | tf_op jit(solution)/shard_map/ppermute | solution.py:42
  43.5 3.3 %shard_map.133.refs_0_ = bf16[512,2560]{1,0:T(8,128)(2,1)} custom-call(s32[1]{0:T(128)} %constant.16.clone.1.at_ref, bf16[256,1024]{1,0:T(8,128)(2,1)} %shard_map.129.refs_0_, bf16[256,1536]{1,0:T(8,128)(2,1)} %shard_map.130.refs_1_, bf16[256,1024]{1,0:T(8,128)(2,1)} %collective-permute-done.2.refs_2_, bf16[256,1536]{1,0:T(8,128)(2,1)} %collective-permute-done.3.refs_3_), custom_call_target="tpu_custom_call" | custom-call | bytes 1048576 | tf_op jit(solution)/shard_map/pallas_call | solution.py:209
  46.9 2.2 collective-permute-start.6
  50.3 1.6 collective-permute-start.4
  51.9 1.5 collective-permute-start.5
  53.7 12.0 %collective-permute-done.7.in_ref.refs_5_.refs_4_ = bf16[512,640]{1,0:T(8,128)(2,1)} collective-permute-done((bf16[512,640]{1,0:T(8,128)(2,1)}, bf16[512,640]{1,0:T(8,128)(2,1)}, u32[]{:S(2)}, u32[]{:S(2)}) %collective-permute-start.7) | collective-permute-done | bytes 655392 | tf_op jit(solution)/shard_map/ppermute | solution.py:42
  65.7 1.7 shard_map.134
  68.4 5.3 %collective-permute-done.5.refs_4_ = bf16[640,640]{1,0:T(8,128)(2,1)} collective-permute-done((bf16[640,640]{1,0:T(8,128)(2,1)}, bf16[640,640]{1,0:T(8,128)(2,1)}, u32[]{:S(2)}, u32[]{:S(2)}) %collective-permute-start.5) | collective-permute-done | bytes 819232 | tf_op jit(solution)/shard_map/ppermute | solution.py:382
  73.6 2.5 %shard_map.137.refs_1_ = bf16[2560,256]{1,0:T(8,128)(2,1)S(1)} custom-call(s32[4]{0:T(128)S(1)} %pad_add_fusion.1.at_ref, bf16[640,640]{1,0:T(8,128)(2,1)S(1)} %shard_map.128.refs_0_, bf16[640,640]{1,0:T(8,128)(2,1)} %collective-permute-done.refs_1_, bf16[640,640]{1,0:T(8,128)(2,1)} %collective-permute-done.1.refs_2_, ...), custom_call_target="tpu_custom_call" | custom-call | bytes 2097152 | tf_op jit(solution)/shard_map/pallas_call | solution.py:209
  76.2 2.6 %shard_map.135.refs_2_.refs_0_ = bf16[2560,384]{1,0:T(8,128)(2,1)S(1)} custom-call(s32[4]{0:T(128)S(1)} %pad_add_fusion.1.at_ref, bf16[640,640]{1,0:T(8,128)(2,1)S(1)} %shard_map.128.refs_0_, bf16[640,640]{1,0:T(8,128)(2,1)} %collective-permute-done.refs_1_, bf16[640,640]{1,0:T(8,128)(2,1)} %collective-permute-done.1.refs_2_, ...), custom_call_target="tpu_custom_call" | custom-call | bytes 2097152 | tf_op jit(solution)/shard_map/pallas_call | solution.py:209
  78.8 6.6 %shard_map.136 = (f32[1024,384]{1,0:T(8,128)S(1)}, bf16[1024,384]{1,0:T(8,128)(2,1)S(1)}, f32[4,1,256]{2,1,0:T(1,128)S(1)}, bf16[1024,2560]{1,0:T(8,128)(2,1)S(1)}) custom-call(bf16[512,2560]{1,0:T(8,128)(2,1)} %shard_map.133.refs_0_, bf16[512,2560]{1,0:T(8,128)(2,1)} %collective-permute-done.6.refs_1_, bf16[2560,384]{1,0:T(8,128)(2,1)S(1)} %shard_map.135.refs_2_.refs_0_, ...), custom_call_target="tpu_custom_call" | custom-call | bytes 2097152 | tf_op jit(solution)/shard_map/pallas_call | solution.py:330
  85.5 3.3 %shard_map.138 = (f32[1024,256]{1,0:T(8,128)S(1)}, bf16[1024,256]{1,0:T(8,128)(2,1)S(1)}, f32[4,1,256]{2,1,0:T(1,128)S(1)}) custom-call(bf16[1024,2560]{1,0:T(8,128)(2,1)S(1)} %get-tuple-element.118.refs_0_.attn_ref, bf16[2560,256]{1,0:T(8,128)(2,1)S(1)} %shard_map.137.refs_1_, f32[1,256]{1,0:T(1,128)S(1)} %constant_dynamic-slice_fusion.1.refs_2_.gain_ref.refs_5_, ...), custom_call_target="tpu_custom_call" | custom-call | bytes 2097152 | tf_op jit(solution)/shard_map/pallas_call | solution.py:330
  88.8 1.3 collective-permute-start.16
  90.1 1.4 collective-permute-start.10
  97.4 1.3 collective-permute-start.12
  98.7 19.4 %collective-permute-done.12.other_ref = f32[4,1,256]{2,1,0:T(1,128)S(1)} collective-permute-done((f32[4,1,256]{2,1,0:T(1,128)S(1)}, f32[4,1,256]{2,1,0:T(1,128)S(1)}, u32[]{:S(2)}, u32[]{:S(2)}) %collective-permute-start.12) | collective-permute-done | bytes 4128 | tf_op jit(solution)/shard_map/ppermute | solution.py:42
  118.1 1.8 shard_map.139.refs_0_
  120.0 1.7 shard_map.140
  121.7 2.1 collective-permute-start.17
  124.9 2.2 %collective-permute-done.18 = f32[2,2,2,256]{3,2,1,0:T(2,128)S(1)} collective-permute-done((f32[2,2,2,256]{3,2,1,0:T(2,128)S(1)}, f32[2,2,2,256]{3,2,1,0:T(2,128)S(1)}, u32[]{:S(2)}, u32[]{:S(2)}) %collective-permute-start.18) | collective-permute-done | bytes 8224 | tf_op jit(solution)/shard_map/ppermute | solution.py:42
  127.1 3.6 %shard_map.141 = (bf16[1024,640]{1,0:T(8,128)(2,1)S(1)}, bf16[640,640]{1,0:T(8,128)(2,1)S(1)}) custom-call(s32[1]{0:T(128)} %bitcast.at_ref, bf16[1024,2560]{1,0:T(8,128)(2,1)S(1)} %get-tuple-element.118.refs_0_.attn_ref, f32[4,1,256]{2,1,0:T(1,128)S(1)} %bitcast.55, f32[4,1,256]{2,1,0:T(1,128)S(1)} %collective-permute-done.12.other_ref, ...), custom_call_target="tpu_custom_call" | custom-call | bytes 4194304 | tf_op jit(solution)/shard_map/pallas_call | solution.py:209
  130.7 2.3 %shard_map.144 = (bf16[512,512]{1,0:T(8,128)(2,1)S(1)}, bf16[512,512]{1,0:T(8,128)(2,1)S(1)}, bf16[512,512]{1,0:T(8,128)(2,1)S(1)}, bf16[512,512]{1,0:T(8,128)(2,1)S(1)}, bf16[512,512]{1,0:T(8,128)(2,1)S(1)}) custom-call(bf16[1024,640]{1,0:T(8,128)(2,1)S(1)} %get-tuple-element.130.d_ref, bf16[2560,384]{1,0:T(8,128)(2,1)S(1)} %shard_map.135.refs_2_.refs_0_, ...), custom_call_target="tpu_custom_call" | custom-call | bytes 3145728 | tf_op jit(solution)/shard_map/pallas_call | solution.py:330
  133.0 1.6 collective-permute-start.21
  134.6 1.3 collective-permute-start.20
  137.9 2.3 %shard_map.143 = (bf16[512,512]{1,0:T(8,128)(2,1)S(1)}, bf16[512,512]{1,0:T(8,128)(2,1)S(1)}, bf16[512,512]{1,0:T(8,128)(2,1)S(1)}, bf16[512,512]{1,0:T(8,128)(2,1)S(1)}, bf16[512,512]{1,0:T(8,128)(2,1)S(1)}) custom-call(bf16[1024,640]{1,0:T(8,128)(2,1)S(1)} %get-tuple-element.130.d_ref, bf16[2560,384]{1,0:T(8,128)(2,1)S(1)} %shard_map.135.refs_2_.refs_0_, ...), custom_call_target="tpu_custom_call" | custom-call | bytes 3145728 | tf_op jit(solution)/shard_map/pallas_call | solution.py:330
  140.2 4.9 %shard_map.142 = (bf16[1920,384]{1,0:T(8,128)(2,1)S(1)}, bf16[1920,256]{1,0:T(8,128)(2,1)S(1)}) custom-call(s32[3]{0:T(128)S(1)} %pad_add_fusion.2.at_ref, bf16[1024,2560]{1,0:T(8,128)(2,1)S(1)} %get-tuple-element.118.refs_0_.attn_ref, bf16[1024,640]{1,0:T(8,128)(2,1)S(1)} %get-tuple-element.130.d_ref), custom_call_target="tpu_custom_call" | custom-call | bytes 4194304 | tf_op jit(solution)/shard_map/pallas_call | solution.py:209
  148.7 4.5 %collective-permute-done.20.refs_0_ = bf16[640,640]{1,0:T(8,128)(2,1)S(1)} collective-permute-done((bf16[640,640]{1,0:T(8,128)(2,1)S(1)}, bf16[640,640]{1,0:T(8,128)(2,1)S(1)}, u32[]{:S(2)}, u32[]{:S(2)}) %collective-permute-start.20) | collective-permute-done | bytes 819232 | tf_op jit(solution)/shard_map/ppermute | solution.py:382
  156.4 3.2 %collective-permute-start.27 = (bf16[640,384]{1,0:T(8,128)(2,1)}, bf16[640,384]{1,0:T(8,128)(2,1)}, u32[]{:S(2)}, u32[]{:S(2)}) collective-permute-start(bf16[640,384]{1,0:T(8,128)(2,1)} %shard_map.149), channel_id=1, source_target_pairs={{0,1},{1,0},{2,3},{3,2},{4,5},{5,4},{6,7},{7,6},{8,9},{9,8},{10,11... | collective-permute-start | bytes 1474568 | tf_op jit(solution)/shard_map/ppermute | solution.py:42
  159.9 1.3 fusion.2
  161.9 3.9 %collective-permute-done.28.two_ref = bf16[256,1024]{1,0:T(8,128)(2,1)} collective-permute-done((bf16[256,1024]{1,0:T(8,128)(2,1)}, bf16[256,1024]{1,0:T(8,128)(2,1)}, u32[]{:S(2)}, u32[]{:S(2)}) %collective-permute-start.28) | collective-permute-done | bytes 524320 | tf_op jit(solution)/shard_map/ppermute | solution.py:42
  165.8 1.3 copy-done.5
  168.2 7.9 %shard_map.150 = (bf16[256,2560]{1,0:T(8,128)(2,1)}, bf16[256,2560]{1,0:T(8,128)(2,1)}, bf16[256,2560]{1,0:T(8,128)(2,1)}) custom-call(s32[1]{0:T(128)} %dynamic_slice.6.length_ref, bf16[256,2560]{1,0:T(8,128)(2,1)S(1)} %bitcast.37, bf16[256,2560]{1,0:T(8,128)(2,1)S(1)} %bitcast.42, bf16[256,2560]{1,0:T(8,128)(2,1)S(1)} %bitcast.47, ...), custom_call_target="tpu_custom_call" | custom-call | bytes 4194304 | tf_op jit(solution)/shard_map/pallas_call | solution.py:349
  176.0 6.6 %collective-permute-done.30.two_ref = bf16[256,512]{1,0:T(8,128)(2,1)} collective-permute-done((bf16[256,512]{1,0:T(8,128)(2,1)}, bf16[256,512]{1,0:T(8,128)(2,1)}, u32[]{:S(2)}, u32[]{:S(2)}) %collective-permute-start.30) | collective-permute-done | bytes 262176 | tf_op jit(solution)/shard_map/ppermute | solution.py:42
  182.8 3.2 %collective-permute-start.32 = (bf16[640,256]{1,0:T(8,128)(2,1)S(1)}, bf16[640,256]{1,0:T(8,128)(2,1)S(1)}, u32[]{:S(2)}, u32[]{:S(2)}) collective-permute-start(bf16[640,256]{1,0:T(8,128)(2,1)S(1)} %shard_map.152), channel_id=1, source_target_pairs={{0,1},{1,0},{2,3},{3,2},{4,5},{5,4},{6,7},{7,6},{8,9},{9,8},{10,11... | collective-permute-start | bytes 983048 | tf_op jit(solution)/shard_map/ppermute | solution.py:42
  186.2 1.5 shard_map.155.refs_0_
  188.0 7.8 %shard_map.153 = (bf16[256,2560]{1,0:T(8,128)(2,1)}, bf16[256,2560]{1,0:T(8,128)(2,1)}, bf16[256,2560]{1,0:T(8,128)(2,1)}) custom-call(s32[1]{0:T(128)} %dynamic_slice.6.length_ref, bf16[256,2560]{1,0:T(8,128)(2,1)S(1)} %bitcast.38, bf16[256,2560]{1,0:T(8,128)(2,1)S(1)} %bitcast.43, ...), custom_call_target="tpu_custom_call", output_to_operand_aliasing={{0}: (6, {}), {1}: (7, {}), {2}: (8, {})} | custom-call | bytes 4194304 | tf_op jit(solution)/shard_map/pallas_call | solution.py:349
  195.8 5.1 %shard_map.154 = (bf16[256,2560]{1,0:T(8,128)(2,1)}, bf16[256,2560]{1,0:T(8,128)(2,1)}, bf16[256,2560]{1,0:T(8,128)(2,1)}) custom-call(s32[1]{0:T(128)} %dynamic_slice.6.length_ref, bf16[256,2560]{1,0:T(8,128)(2,1)S(1)} %bitcast.39, bf16[256,2560]{1,0:T(8,128)(2,1)S(1)} %bitcast.44, ...), custom_call_target="tpu_custom_call", output_to_operand_aliasing={{0}: (6, {}), {1}: (7, {}), {2}: (8, {})} | custom-call | bytes 2621440 | tf_op jit(solution)/shard_map/pallas_call | solution.py:349
  202.4 2.9 %collective-permute-start.34 = (bf16[640,384]{1,0:T(8,128)(2,1)S(1)}, bf16[640,384]{1,0:T(8,128)(2,1)S(1)}, u32[]{:S(2)}, u32[]{:S(2)}) collective-permute-start(bf16[640,384]{1,0:T(8,128)(2,1)S(1)} %shard_map.155.refs_0_), channel_id=1, source_target_pairs={{0,4},{4,0},{8,12},{12,8},{1,5},{5,1},{9,13},{13,9},{2,6},{6,2},{1... | collective-permute-start | bytes 1474568 | tf_op jit(solution)/shard_map/ppermute | solution.py:42
  205.8 1.3 collective-permute-done.36.refs_5_
  207.1 4.4 %collective-permute-start.38 = (bf16[640,256]{1,0:T(8,128)(2,1)S(1)}, bf16[640,256]{1,0:T(8,128)(2,1)S(1)}, u32[]{:S(2)}, u32[]{:S(2)}) collective-permute-start(bf16[640,256]{1,0:T(8,128)(2,1)S(1)} %collective-permute-done.36.refs_5_), channel_id=1, source_target_pairs={{0,4},{4,0},{8,12},{12,8},{1,5},{5,1},{9,13},{13,9},{2,6},{6,2},{1... | collective-permute-start | bytes 983048 | tf_op jit(solution)/shard_map/ppermute | solution.py:42
  212.7 3.5 %shard_map.157 = f32[640,2560]{1,0:T(8,128)} custom-call(s32[1]{0:T(128)} %bitcast.1.at_ref.member_ref, bf16[640,384]{1,0:T(8,128)(2,1)S(1)} %shard_map.155.refs_0_, bf16[640,384]{1,0:T(8,128)(2,1)S(1)} %collective-permute-done.33.refs_1_, bf16[640,384]{1,0:T(8,128)(2,1)S(1)} %collective-permute-done.34.refs_2_, ...), custom_call_target="tpu_custom_call" | custom-call | bytes 1048576 | tf_op jit(solution)/shard_map/pallas_call | solution.py:631
  (133 shorter events, 28.0 us)
Async XLA Ops:
  0.6 67.7 %copy-start = (f32[1,2560]{1,0:T(1,128)S(1)}, f32[1,2560]{1,0:T(1,128)}, u32[]{:S(2)}) copy-start(f32[1,2560]{1,0:T(1,128)} %param.17) | copy-start | bytes 30724
  2.7 40.8 %collective-permute-start.1 = (bf16[640,640]{1,0:T(8,128)(2,1)S(1)}, bf16[640,640]{1,0:T(8,128)(2,1)}, u32[]{:S(2)}, u32[]{:S(2)}) collective-permute-start(bf16[640,640]{1,0:T(8,128)(2,1)S(1)} %shard_map.128.refs_0_), channel_id=1, source_target_pairs={{0,2},{1,3},{2,0},{3,1},{4,6},{5,7},{6,4},{7,5},{8,10},{9,11},{10,... | collective-permute-start | bytes 2457608 | tf_op jit(solution)/shard_map/ppermute | solution.py:42
  5.9 37.6 %collective-permute-start = (bf16[640,640]{1,0:T(8,128)(2,1)S(1)}, bf16[640,640]{1,0:T(8,128)(2,1)}, u32[]{:S(2)}, u32[]{:S(2)}) collective-permute-start(bf16[640,640]{1,0:T(8,128)(2,1)S(1)} %shard_map.128.refs_0_), channel_id=1, source_target_pairs={{0,1},{1,0},{2,3},{3,2},{4,5},{5,4},{6,7},{7,6},{8,9},{9,8},{10,11... | collective-permute-start | bytes 2457608 | tf_op jit(solution)/shard_map/ppermute | solution.py:42
  14.2 29.3 %collective-permute-start.3 = (bf16[256,1536]{1,0:T(8,128)(2,1)}, bf16[256,1536]{1,0:T(8,128)(2,1)}, u32[]{:S(2)}, u32[]{:S(2)}) collective-permute-start(bf16[256,1536]{1,0:T(8,128)(2,1)} %shard_map.130.refs_1_), channel_id=1, source_target_pairs={{0,8},{4,12},{8,0},{12,4},{1,9},{5,13},{9,1},{13,5},{2,10},{6,14},... | collective-permute-start | bytes 2359304 | tf_op jit(solution)/shard_map/ppermute | solution.py:42
  19.2 24.3 %collective-permute-start.2 = (bf16[256,1024]{1,0:T(8,128)(2,1)}, bf16[256,1024]{1,0:T(8,128)(2,1)}, u32[]{:S(2)}, u32[]{:S(2)}) collective-permute-start(bf16[256,1024]{1,0:T(8,128)(2,1)} %shard_map.129.refs_0_), channel_id=1, source_target_pairs={{0,8},{4,12},{8,0},{12,4},{1,9},{5,13},{9,1},{13,5},{2,10},{6,14},... | collective-permute-start | bytes 1572872 | tf_op jit(solution)/shard_map/ppermute | solution.py:42
  22.6 20.9 %copy-start.14 = (bf16[256,640]{1,0:T(8,128)(2,1)}, bf16[256,640]{1,0:T(8,128)(2,1)S(1)}, u32[]{:S(2)}) copy-start(bf16[256,640]{1,0:T(8,128)(2,1)S(1)} %get-tuple-element.114.refs_4_.refs_3_) | copy-start | bytes 983044
  22.7 20.9 %copy-start.23 = (bf16[256,640]{1,0:T(8,128)(2,1)}, bf16[256,640]{1,0:T(8,128)(2,1)S(1)}, u32[]{:S(2)}) copy-start(bf16[256,640]{1,0:T(8,128)(2,1)S(1)} %get-tuple-element.108) | copy-start | bytes 983044
  46.9 26.7 %collective-permute-start.6 = (bf16[512,2560]{1,0:T(8,128)(2,1)}, bf16[512,2560]{1,0:T(8,128)(2,1)}, u32[]{:S(2)}, u32[]{:S(2)}) collective-permute-start(bf16[512,2560]{1,0:T(8,128)(2,1)} %shard_map.133.refs_0_), channel_id=1, source_target_pairs={{0,4},{4,0},{8,12},{12,8},{1,5},{5,1},{9,13},{13,9},{2,6},{6,2},{1... | collective-permute-start | bytes 7864328 | tf_op jit(solution)/shard_map/ppermute | solution.py:42
  49.1 16.7 %collective-permute-start.7 = (bf16[512,640]{1,0:T(8,128)(2,1)}, bf16[512,640]{1,0:T(8,128)(2,1)}, u32[]{:S(2)}, u32[]{:S(2)}) collective-permute-start(bf16[512,640]{1,0:T(8,128)(2,1)} %shard_map.132), channel_id=1, source_target_pairs={{0,8},{4,12},{8,0},{12,4},{1,9},{5,13},{9,1},{13,5},{2,10},{6,14},... | collective-permute-start | bytes 1966088 | tf_op jit(solution)/shard_map/ppermute | solution.py:42
  50.3 18.1 %collective-permute-start.4 = (bf16[640,640]{1,0:T(8,128)(2,1)S(1)}, bf16[640,640]{1,0:T(8,128)(2,1)}, u32[]{:S(2)}, u32[]{:S(2)}) collective-permute-start(bf16[640,640]{1,0:T(8,128)(2,1)S(1)} %shard_map.128.refs_0_), channel_id=1, source_target_pairs={{1,2},{2,1},{5,6},{6,5},{9,10},{10,9},{13,14},{14,13},{17,18},{18,... | collective-permute-start | bytes 2457608 | tf_op jit(solution)/shard_map/ppermute | solution.py:382
  51.9 21.8 %collective-permute-start.5 = (bf16[640,640]{1,0:T(8,128)(2,1)}, bf16[640,640]{1,0:T(8,128)(2,1)}, u32[]{:S(2)}, u32[]{:S(2)}) collective-permute-start(bf16[640,640]{1,0:T(8,128)(2,1)} %collective-permute-done.1.refs_2_), channel_id=1, source_target_pairs={{2,3},{1,0},{6,7},{5,4},{10,11},{9,8},{14,15},{13,12},{18,19},{17,... | collective-permute-start | bytes 2457608 | tf_op jit(solution)/shard_map/ppermute | solution.py:382
  53.3 15.0 %collective-permute-start.8 = (bf16[256,640]{1,0:T(8,128)(2,1)}, bf16[256,640]{1,0:T(8,128)(2,1)}, u32[]{:S(2)}, u32[]{:S(2)}) collective-permute-start(bf16[256,640]{1,0:T(8,128)(2,1)} %copy-done.23), channel_id=1, source_target_pairs={{0,4},{4,0},{8,12},{12,8},{1,5},{5,1},{9,13},{13,9},{2,6},{6,2},{1... | collective-permute-start | bytes 983048 | tf_op jit(solution)/shard_map/ppermute | solution.py:42
  67.5 6.2 %collective-permute-start.9 = (bf16[256,640]{1,0:T(8,128)(2,1)}, bf16[256,640]{1,0:T(8,128)(2,1)}, u32[]{:S(2)}, u32[]{:S(2)}) collective-permute-start(bf16[256,640]{1,0:T(8,128)(2,1)} %shard_map.134), channel_id=1, source_target_pairs={{0,4},{4,0},{8,12},{12,8},{1,5},{5,1},{9,13},{13,9},{2,6},{6,2},{1... | collective-permute-start | bytes 983048 | tf_op jit(solution)/shard_map/ppermute | solution.py:42
  85.5 6.3 %copy-start.24 = (f32[1024]{0:T(1024)S(1)}, f32[1024]{0:T(1024)}, u32[]{:S(2)}) copy-start(f32[1024]{0:T(1024)} %param.15) | copy-start | bytes 12292
  85.5 6.2 %copy-start.25 = (s32[1,256]{1,0:T(1,128)S(1)}, s32[1,256]{1,0:T(1,128)}, u32[]{:S(2)}) copy-start(s32[1,256]{1,0:T(1,128)} %param.13) | copy-start | bytes 3076
  88.8 31.2 %collective-permute-start.16 = (bf16[1024,256]{1,0:T(8,128)(2,1)S(1)}, bf16[1024,256]{1,0:T(8,128)(2,1)S(1)}, u32[]{:S(2)}, u32[]{:S(2)}) collective-permute-start(bf16[1024,256]{1,0:T(8,128)(2,1)S(1)} %get-tuple-element.121), channel_id=1, source_target_pairs={{0,16},{16,0},{1,17},{17,1},{2,18},{18,2},{3,19},{19,3},{4,20},{20... | collective-permute-start | bytes 1572872 | tf_op jit(solution)/shard_map/ppermute | solution.py:42
  90.1 3.6 %collective-permute-start.10 = (f32[2,2,1,256]{3,2,1,0:T(1,128)S(1)}, f32[2,2,1,256]{3,2,1,0:T(1,128)S(1)}, u32[]{:S(2)}, u32[]{:S(2)}) collective-permute-start(f32[2,2,1,256]{3,2,1,0:T(1,128)S(1)} %bitcast.64), channel_id=1, source_target_pairs={{0,4},{4,0},{8,12},{12,8},{1,5},{5,1},{9,13},{13,9},{2,6},{6,2},{1... | collective-permute-start | bytes 12296 | tf_op jit(solution)/shard_map/ppermute | solution.py:42
  91.5 26.6 %collective-permute-start.15 = (bf16[1024,384]{1,0:T(8,128)(2,1)S(1)}, bf16[1024,384]{1,0:T(8,128)(2,1)S(1)}, u32[]{:S(2)}, u32[]{:S(2)}) collective-permute-start(bf16[1024,384]{1,0:T(8,128)(2,1)S(1)} %get-tuple-element.126), channel_id=1, source_target_pairs={{0,16},{16,0},{1,17},{17,1},{2,18},{18,2},{3,19},{19,3},{4,20},{20... | collective-permute-start | bytes 2359304 | tf_op jit(solution)/shard_map/ppermute | solution.py:42
  93.4 2.8 %collective-permute-start.13 = (f32[1,1,256]{2,1,0:T(1,128)S(1)}, f32[1,1,256]{2,1,0:T(1,128)S(1)}, u32[]{:S(2)}, u32[]{:S(2)}) collective-permute-start(f32[1,1,256]{2,1,0:T(1,128)S(1)} %compare_select_fusion), channel_id=1, source_target_pairs={{0,8},{4,12},{8,0},{12,4},{1,9},{5,13},{9,1},{13,5},{2,10},{6,14},... | collective-permute-start | bytes 3080 | tf_op jit(solution)/shard_map/ppermute | solution.py:42
  93.7 3.7 %collective-permute-start.11 = (f32[2,2,1,256]{3,2,1,0:T(1,128)S(1)}, f32[2,2,1,256]{3,2,1,0:T(1,128)S(1)}, u32[]{:S(2)}, u32[]{:S(2)}) collective-permute-start(f32[2,2,1,256]{3,2,1,0:T(1,128)S(1)} %reverse_add_fusion.2), channel_id=1, source_target_pairs={{0,8},{4,12},{8,0},{12,4},{1,9},{5,13},{9,1},{13,5},{2,10},{6,14},... | collective-permute-start | bytes 12296 | tf_op jit(solution)/shard_map/ppermute | solution.py:42
  96.2 2.5 %collective-permute-start.14 = (f32[2,1,256]{2,1,0:T(1,128)S(1)}, f32[2,1,256]{2,1,0:T(1,128)S(1)}, u32[]{:S(2)}, u32[]{:S(2)}) collective-permute-start(f32[2,1,256]{2,1,0:T(1,128)S(1)} %pad_maximum_fusion), channel_id=1, source_target_pairs={{0,4},{4,0},{8,12},{12,8},{1,5},{5,1},{9,13},{13,9},{2,6},{6,2},{1... | collective-permute-start | bytes 6152 | tf_op jit(solution)/shard_map/ppermute | solution.py:42
  97.4 20.7 %collective-permute-start.12 = (f32[4,1,256]{2,1,0:T(1,128)S(1)}, f32[4,1,256]{2,1,0:T(1,128)S(1)}, u32[]{:S(2)}, u32[]{:S(2)}) collective-permute-start(f32[4,1,256]{2,1,0:T(1,128)S(1)} %bitcast.52), channel_id=1, source_target_pairs={{0,16},{16,0},{1,17},{17,1},{2,18},{18,2},{3,19},{19,3},{4,20},{20... | collective-permute-start | bytes 12296 | tf_op jit(solution)/shard_map/ppermute | solution.py:42
  121.7 2.9 %collective-permute-start.17 = (f32[2,2,2,256]{3,2,1,0:T(2,128)S(1)}, f32[2,2,2,256]{3,2,1,0:T(2,128)S(1)}, u32[]{:S(2)}, u32[]{:S(2)}) collective-permute-start(f32[2,2,2,256]{3,2,1,0:T(2,128)S(1)} %bitcast.56), channel_id=1, source_target_pairs={{0,4},{4,0},{8,12},{12,8},{1,5},{5,1},{9,13},{13,9},{2,6},{6,2},{1... | collective-permute-start | bytes 24584 | tf_op jit(solution)/shard_map/ppermute | solution.py:42
  124.6 2.5 %collective-permute-start.18 = (f32[2,2,2,256]{3,2,1,0:T(2,128)S(1)}, f32[2,2,2,256]{3,2,1,0:T(2,128)S(1)}, u32[]{:S(2)}, u32[]{:S(2)}) collective-permute-start(f32[2,2,2,256]{3,2,1,0:T(2,128)S(1)} %reverse_add_fusion.1), channel_id=1, source_target_pairs={{0,8},{4,12},{8,0},{12,4},{1,9},{5,13},{9,1},{13,5},{2,10},{6,14},... | collective-permute-start | bytes 24584 | tf_op jit(solution)/shard_map/ppermute | solution.py:42
  133.0 4.4 %collective-permute-start.21 = (bf16[512,512]{1,0:T(8,128)(2,1)S(1)}, bf16[512,512]{1,0:T(8,128)(2,1)S(1)}, u32[]{:S(2)}, u32[]{:S(2)}) collective-permute-start(bf16[512,512]{1,0:T(8,128)(2,1)S(1)} %get-tuple-element.135), channel_id=1, source_target_pairs={{0,4},{4,0},{8,12},{12,8},{1,5},{5,1},{9,13},{13,9},{2,6},{6,2},{1... | collective-permute-start | bytes 1572872 | tf_op jit(solution)/shard_map/ppermute | solution.py:42
  134.5 2.9 %collective-permute-start.25 = (bf16[512,512]{1,0:T(8,128)(2,1)S(1)}, bf16[512,512]{1,0:T(8,128)(2,1)S(1)}, u32[]{:S(2)}, u32[]{:S(2)}) collective-permute-start(bf16[512,512]{1,0:T(8,128)(2,1)S(1)} %get-tuple-element.144), channel_id=1, source_target_pairs={{0,4},{4,0},{8,12},{12,8},{1,5},{5,1},{9,13},{13,9},{2,6},{6,2},{1... | collective-permute-start | bytes 1572872 | tf_op jit(solution)/shard_map/ppermute | solution.py:42
  134.6 18.6 %collective-permute-start.20 = (bf16[640,640]{1,0:T(8,128)(2,1)S(1)}, bf16[640,640]{1,0:T(8,128)(2,1)S(1)}, u32[]{:S(2)}, u32[]{:S(2)}) collective-permute-start(bf16[640,640]{1,0:T(8,128)(2,1)S(1)} %get-tuple-element.129), channel_id=1, source_target_pairs={{0,1},{3,2},{4,5},{7,6},{8,9},{11,10},{12,13},{15,14},{16,17},{19,... | collective-permute-start | bytes 2457608 | tf_op jit(solution)/shard_map/ppermute | solution.py:382
  136.0 17.3 %collective-permute-start.19 = (bf16[640,640]{1,0:T(8,128)(2,1)S(1)}, bf16[640,640]{1,0:T(8,128)(2,1)S(1)}, u32[]{:S(2)}, u32[]{:S(2)}) collective-permute-start(bf16[640,640]{1,0:T(8,128)(2,1)S(1)} %get-tuple-element.129), channel_id=1, source_target_pairs={{1,2},{2,1},{5,6},{6,5},{9,10},{10,9},{13,14},{14,13},{17,18},{18,... | collective-permute-start | bytes 2457608 | tf_op jit(solution)/shard_map/ppermute | solution.py:382
  136.7 9.3 %collective-permute-start.22 = (bf16[512,512]{1,0:T(8,128)(2,1)S(1)}, bf16[512,512]{1,0:T(8,128)(2,1)S(1)}, u32[]{:S(2)}, u32[]{:S(2)}) collective-permute-start(bf16[512,512]{1,0:T(8,128)(2,1)S(1)} %get-tuple-element.136), channel_id=1, source_target_pairs={{0,4},{4,0},{8,12},{12,8},{1,5},{5,1},{9,13},{13,9},{2,6},{6,2},{1... | collective-permute-start | bytes 1572872 | tf_op jit(solution)/shard_map/ppermute | solution.py:42
  137.3 10.4 %collective-permute-start.23 = (bf16[512,512]{1,0:T(8,128)(2,1)S(1)}, bf16[512,512]{1,0:T(8,128)(2,1)S(1)}, u32[]{:S(2)}, u32[]{:S(2)}) collective-permute-start(bf16[512,512]{1,0:T(8,128)(2,1)S(1)} %get-tuple-element.140), channel_id=1, source_target_pairs={{0,4},{4,0},{8,12},{12,8},{1,5},{5,1},{9,13},{13,9},{2,6},{6,2},{1... | collective-permute-start | bytes 1572872 | tf_op jit(solution)/shard_map/ppermute | solution.py:42
  137.4 10.3 %collective-permute-start.24 = (bf16[512,512]{1,0:T(8,128)(2,1)S(1)}, bf16[512,512]{1,0:T(8,128)(2,1)S(1)}, u32[]{:S(2)}, u32[]{:S(2)}) collective-permute-start(bf16[512,512]{1,0:T(8,128)(2,1)S(1)} %get-tuple-element.141), channel_id=1, source_target_pairs={{0,4},{4,0},{8,12},{12,8},{1,5},{5,1},{9,13},{13,9},{2,6},{6,2},{1... | collective-permute-start | bytes 1572872 | tf_op jit(solution)/shard_map/ppermute | solution.py:42
  145.1 10.4 %copy-start.7 = (bf16[1920,384]{1,0:T(8,128)(2,1)}, bf16[1920,384]{1,0:T(8,128)(2,1)S(1)}, u32[]{:S(2)}) copy-start(bf16[1920,384]{1,0:T(8,128)(2,1)S(1)} %get-tuple-element.182.refs_1_.in_ref.refs_3_) | copy-start | bytes 4423684
  148.7 7.7 %copy-start.17 = (bf16[256,1024]{1,0:T(8,128)(2,1)}, bf16[256,1024]{1,0:T(8,128)(2,1)S(1)}, u32[]{:S(2)}) copy-start(bf16[256,1024]{1,0:T(8,128)(2,1)S(1)} %get-tuple-element.165.one_ref) | copy-start | bytes 1572868
  153.2 12.6 %collective-permute-start.28 = (bf16[256,1024]{1,0:T(8,128)(2,1)}, bf16[256,1024]{1,0:T(8,128)(2,1)}, u32[]{:S(2)}, u32[]{:S(2)}) collective-permute-start(bf16[256,1024]{1,0:T(8,128)(2,1)} %get-tuple-element.152), channel_id=1, source_target_pairs={{0,8},{4,12},{8,0},{12,4},{1,9},{5,13},{9,1},{13,5},{2,10},{6,14},... | collective-permute-start | bytes 1572872 | tf_op jit(solution)/shard_map/ppermute | solution.py:42
  153.5 29.2 %collective-permute-start.29 = (bf16[256,1024]{1,0:T(8,128)(2,1)}, bf16[256,1024]{1,0:T(8,128)(2,1)}, u32[]{:S(2)}, u32[]{:S(2)}) collective-permute-start(bf16[256,1024]{1,0:T(8,128)(2,1)} %get-tuple-element.158), channel_id=1, source_target_pairs={{0,8},{4,12},{8,0},{12,4},{1,9},{5,13},{9,1},{13,5},{2,10},{6,14},... | collective-permute-start | bytes 1572872 | tf_op jit(solution)/shard_map/ppermute | solution.py:42
  156.4 26.2 %collective-permute-start.27 = (bf16[640,384]{1,0:T(8,128)(2,1)}, bf16[640,384]{1,0:T(8,128)(2,1)}, u32[]{:S(2)}, u32[]{:S(2)}) collective-permute-start(bf16[640,384]{1,0:T(8,128)(2,1)} %shard_map.149), channel_id=1, source_target_pairs={{0,1},{1,0},{2,3},{3,2},{4,5},{5,4},{6,7},{7,6},{8,9},{9,8},{10,11... | collective-permute-start | bytes 1474568 | tf_op jit(solution)/shard_map/ppermute | solution.py:42
  159.7 23.0 %collective-permute-start.26 = (bf16[640,384]{1,0:T(8,128)(2,1)}, bf16[640,384]{1,0:T(8,128)(2,1)}, u32[]{:S(2)}, u32[]{:S(2)}) collective-permute-start(bf16[640,384]{1,0:T(8,128)(2,1)} %shard_map.148), channel_id=1, source_target_pairs={{0,2},{1,3},{2,0},{3,1},{4,6},{5,7},{6,4},{7,5},{8,10},{9,11},{10,... | collective-permute-start | bytes 1474568 | tf_op jit(solution)/shard_map/ppermute | solution.py:42
  159.7 23.0 %collective-permute-start.30 = (bf16[256,512]{1,0:T(8,128)(2,1)}, bf16[256,512]{1,0:T(8,128)(2,1)}, u32[]{:S(2)}, u32[]{:S(2)}) collective-permute-start(bf16[256,512]{1,0:T(8,128)(2,1)} %get-tuple-element.159), channel_id=1, source_target_pairs={{0,8},{4,12},{8,0},{12,4},{1,9},{5,13},{9,1},{13,5},{2,10},{6,14},... | collective-permute-start | bytes 786440 | tf_op jit(solution)/shard_map/ppermute | solution.py:42
  168.2 14.5 %copy-start.10 = (bf16[1920,256]{1,0:T(8,128)(2,1)S(1)}, bf16[1920,256]{1,0:T(8,128)(2,1)}, u32[]{:S(2)}) copy-start(bf16[1920,256]{1,0:T(8,128)(2,1)} %copy-done.9) | copy-start | bytes 2949124
  182.8 18.1 %collective-permute-start.32 = (bf16[640,256]{1,0:T(8,128)(2,1)S(1)}, bf16[640,256]{1,0:T(8,128)(2,1)S(1)}, u32[]{:S(2)}, u32[]{:S(2)}) collective-permute-start(bf16[640,256]{1,0:T(8,128)(2,1)S(1)} %shard_map.152), channel_id=1, source_target_pairs={{0,1},{1,0},{2,3},{3,2},{4,5},{5,4},{6,7},{7,6},{8,9},{9,8},{10,11... | collective-permute-start | bytes 983048 | tf_op jit(solution)/shard_map/ppermute | solution.py:42
  186.0 14.9 %collective-permute-start.31 = (bf16[640,256]{1,0:T(8,128)(2,1)S(1)}, bf16[640,256]{1,0:T(8,128)(2,1)S(1)}, u32[]{:S(2)}, u32[]{:S(2)}) collective-permute-start(bf16[640,256]{1,0:T(8,128)(2,1)S(1)} %shard_map.151), channel_id=1, source_target_pairs={{0,2},{1,3},{2,0},{3,1},{4,6},{5,7},{6,4},{7,5},{8,10},{9,11},{10,... | collective-permute-start | bytes 983048 | tf_op jit(solution)/shard_map/ppermute | solution.py:42
  187.7 8.1 %copy-start.22 = (bf16[256,512]{1,0:T(8,128)(2,1)S(1)}, bf16[256,512]{1,0:T(8,128)(2,1)}, u32[]{:S(2)}) copy-start(bf16[256,512]{1,0:T(8,128)(2,1)} %copy-done.21) | copy-start | bytes 786436
  187.7 17.6 %collective-permute-start.33 = (bf16[640,384]{1,0:T(8,128)(2,1)S(1)}, bf16[640,384]{1,0:T(8,128)(2,1)S(1)}, u32[]{:S(2)}, u32[]{:S(2)}) collective-permute-start(bf16[640,384]{1,0:T(8,128)(2,1)S(1)} %shard_map.155.refs_0_), channel_id=1, source_target_pairs={{0,8},{4,12},{8,0},{12,4},{1,9},{5,13},{9,1},{13,5},{2,10},{6,14},... | collective-permute-start | bytes 1474568 | tf_op jit(solution)/shard_map/ppermute | solution.py:42
  201.1 6.0 %collective-permute-start.36 = (bf16[640,256]{1,0:T(8,128)(2,1)S(1)}, bf16[640,256]{1,0:T(8,128)(2,1)S(1)}, u32[]{:S(2)}, u32[]{:S(2)}) collective-permute-start(bf16[640,256]{1,0:T(8,128)(2,1)S(1)} %shard_map.156.refs_4_), channel_id=1, source_target_pairs={{0,8},{4,12},{8,0},{12,4},{1,9},{5,13},{9,1},{13,5},{2,10},{6,14},... | collective-permute-start | bytes 983048 | tf_op jit(solution)/shard_map/ppermute | solution.py:42
  202.4 9.1 %collective-permute-start.34 = (bf16[640,384]{1,0:T(8,128)(2,1)S(1)}, bf16[640,384]{1,0:T(8,128)(2,1)S(1)}, u32[]{:S(2)}, u32[]{:S(2)}) collective-permute-start(bf16[640,384]{1,0:T(8,128)(2,1)S(1)} %shard_map.155.refs_0_), channel_id=1, source_target_pairs={{0,4},{4,0},{8,12},{12,8},{1,5},{5,1},{9,13},{13,9},{2,6},{6,2},{1... | collective-permute-start | bytes 1474568 | tf_op jit(solution)/shard_map/ppermute | solution.py:42
  205.3 6.2 %collective-permute-start.35 = (bf16[640,384]{1,0:T(8,128)(2,1)S(1)}, bf16[640,384]{1,0:T(8,128)(2,1)S(1)}, u32[]{:S(2)}, u32[]{:S(2)}) collective-permute-start(bf16[640,384]{1,0:T(8,128)(2,1)S(1)} %collective-permute-done.33.refs_1_), channel_id=1, source_target_pairs={{0,4},{4,0},{8,12},{12,8},{1,5},{5,1},{9,13},{13,9},{2,6},{6,2},{1... | collective-permute-start | bytes 1474568 | tf_op jit(solution)/shard_map/ppermute | solution.py:42
  205.3 6.2 %collective-permute-start.37 = (bf16[640,256]{1,0:T(8,128)(2,1)S(1)}, bf16[640,256]{1,0:T(8,128)(2,1)S(1)}, u32[]{:S(2)}, u32[]{:S(2)}) collective-permute-start(bf16[640,256]{1,0:T(8,128)(2,1)S(1)} %shard_map.156.refs_4_), channel_id=1, source_target_pairs={{0,4},{4,0},{8,12},{12,8},{1,5},{5,1},{9,13},{13,9},{2,6},{6,2},{1... | collective-permute-start | bytes 983048 | tf_op jit(solution)/shard_map/ppermute | solution.py:42
  207.1 5.6 %collective-permute-start.38 = (bf16[640,256]{1,0:T(8,128)(2,1)S(1)}, bf16[640,256]{1,0:T(8,128)(2,1)S(1)}, u32[]{:S(2)}, u32[]{:S(2)}) collective-permute-start(bf16[640,256]{1,0:T(8,128)(2,1)S(1)} %collective-permute-done.36.refs_5_), channel_id=1, source_target_pairs={{0,4},{4,0},{8,12},{12,8},{1,5},{5,1},{9,13},{13,9},{2,6},{6,2},{1... | collective-permute-start | bytes 983048 | tf_op jit(solution)/shard_map/ppermute | solution.py:42
  (18 other events, 54.1 us)

commit v4 on v3

--- a/solution.py
+++ b/solution.py
@@ -92,7 +92,8 @@
 
 def hidden_kernel(team, low, gathered, *refs):
     if gathered:
-        pairs, refs, attn_ref = refs[: team // 2], refs[team // 2 : -1], refs[-1]
+        count = sum(gathered)
+        pieces, refs, attn_ref = refs[:count], refs[count:-1], refs[-1]
     else:
         attn_ref, refs = refs[0], refs[1:]
     weight_ref, gain_ref, *rest = refs[: 2 + team]
@@ -100,7 +101,12 @@
     n = rest[0].shape[0]
 
     def gather(i):
-        attn_ref[...] = pairs[i][...]
+        row, column = 0, 0
+        for piece in pieces[sum(gathered[:i]) : sum(gathered[: i + 1])]:
+            attn_ref[row : row + n, column : column + piece.shape[1]] = piece[...]
+            column += piece.shape[1]
+            if column == attn_ref.shape[1]:
+                row, column = row + n, 0
 
     def finish(i):
         for j in range(2):
@@ -404,8 +410,10 @@
     wide = width // team
     line = parts == LINE and shard_rows % LANES == 0
     two = line and wide % LANES == 0 and wide > LANES
-    cut = -(-wide * 3 // (5 * LANES)) * LANES
+    cut = -(-wide * 2 // (5 * LANES)) * LANES
     chunks = [(0, cut), (cut, wide)] if two else [(0, wide)]
+    back_cut = -(-wide * 3 // (5 * LANES)) * LANES
+    back_chunks = [(0, back_cut), (back_cut, wide)] if two else [(0, wide)]
     f32, bf16 = jnp.float32, jnp.bfloat16
     group = group_width(heads_width)
     steps = heads_width // group
@@ -439,22 +447,30 @@
             1.5 * (final - first), forward_kernel, length, (q, k, v), (), 1, first, final - first, group
         )
     far = [swap(a, "dp", bits[-1]) for a in attn]
+    if team == 4:
+        attn.append(stack_blocks([attn]))
     home, _ = tie(residual[0, 0], attn[-1])
     mine = cut_columns(home, [(member ^ s) * wide for s in order], [wide])
     if team == 4:
         mine = [mine[0], mine[2], stack_blocks([[mine[1]], [mine[3]]])]
-    tied = tie(*came, block, count, *attn, *far, *mine)
-    came, (block, count), attn, far, mine = split(tied, len(others), 2, len(attn), len(attn))
+    own_parts = attn
+    tied = tie(*came, block, count, *own_parts, *far, *mine)
+    came, (block, count), own_parts, far, mine = split(tied, len(others), 2, len(own_parts), len(far))
 
     last = [send(block, "fsdp", MIDDLE), send(came[1], "fsdp", ENDS_OUT)] if line else []
-    pairs = [stack_blocks([attn, far])]
-    for bit in reversed(bits[:-1]):
-        pairs = pairs + [swap(x, "dp", bit) for x in pairs]
+    pairs = [[*own_parts[: len(far)], *far]]
+    if team == 4:
+        pairs.append([swap(x, "dp", 1) for x in (own_parts[-1], *far)])
+    else:
+        for bit in reversed(bits[:-1]):
+            pairs = pairs + [[swap(x, "dp", bit) for x in pair] for pair in pairs]
+    each = [len(pair) for pair in pairs]
+    pairs = [x for pair in pairs for x in pair]
     if team == 4:
         here, beside, across = mine
         across = swap(across, "dp", 2)
-        rest = [across, swap(beside, "dp", 1), swap(take_rows(across, 1, seq), "dp", 1)]
-        rest = [here, *rest]
+        passed_on = swap(stack_blocks([[beside], [take_rows(across, 1, seq)]]), "dp", 1)
+        rest = [here, across, passed_on]
     else:
         rest = [swap(piece, "dp", s) if s else piece for s, piece in zip(order, mine)]
     tied = tie(*last, *pairs, *rest)
@@ -462,8 +478,8 @@
     spots = [part, *[part ^ s for s in others], *([part ^ 3] if line else [])]
     shapes = [(heads_width, n) for n in sizes]
 
-    def whole_weight(i):
-        ins = [(b, b.shape, fixed) for b in [block, *came, *last]]
+    def whole_weight(i, first):
+        ins = [(b, b.shape, fixed) for b in [first, *came, *last]]
         kernel = functools.partial(whole_kernel, lows[i], len(spots))
         return small_call(kernel, spots, ins, [(shapes[i], bf16, shapes[i], fixed)], micros=2.0)[0]
 
@@ -478,10 +494,17 @@
     gains = [my_gain[:, low:high] for low, high in chunks]
     tall = rows // 2
 
+    lower = lambda i, *_: (1, 0)
+    rest_blocks = [(a, fixed) for a in rest]
+    if team == 4:
+        rest_blocks = [(rest[0], fixed), (rest[1], fixed), (rest[2], fixed), (rest[2], lower)]
     hidden, sent, square, partner, weights = [], [], [], [], []
     for i, n in enumerate(sizes):
-        weights.append(whole_weight(i))
-        ins = [(a, a.shape, fixed) for a in (weights[i], gains[i])] + [(a, (seq, wide), fixed) for a in rest]
+        first = block
+        if i:
+            first, square[0] = tie(block, square[0])
+        weights.append(whole_weight(i, first))
+        ins = [(a, a.shape, fixed) for a in (weights[i], gains[i])] + [(a, (seq, wide), m) for a, m in rest_blocks]
         outs = [
             ((rows, n), f32, (2 * seq, n), row_at),
             ((rows, n), bf16, (2 * seq, n), row_at),
@@ -493,7 +516,7 @@
         else:
             ins = [(a, a.shape, fixed) for a in pairs] + ins
             outs.append(whole)
-        kernel = functools.partial(hidden_kernel, team, lows[i], i == 0)
+        kernel = functools.partial(hidden_kernel, team, lows[i], [] if i else each)
         h, x, sq, *new = call(2.0, kernel, (team // 2,), ins, outs)
         attn = new[0] if new else attn
         if i + 1 < len(chunks):
@@ -534,6 +557,8 @@
     loss = jnp.sum(tok_w[0] * both[0, :1]) / (width * count)
     mean = both[:, 1:] / width
 
+    back_lows = [low for low, _ in back_chunks]
+    back_sizes = [high - low for low, high in back_chunks]
     columns = shard_rows if line else heads_width
     d_hidden, terms = small_call(
         functools.partial(d_hidden_kernel, lows),
@@ -550,10 +575,10 @@
     if line:
         early = [send(terms, "fsdp", MIDDLE), send(terms, "fsdp", ENDS_IN)]
         terms = small_call(
-            functools.partial(terms_kernel, lows),
+            functools.partial(terms_kernel, back_lows),
             [part ^ 1, part ^ 2, part],
             [(attn, (rows, shard_rows), lambda i, at: (0, at[i])), (d_hidden, (rows, wide), fixed)],
-            [((3 * shard_rows, n), bf16, (shard_rows, n), lambda i, at: (i, 0)) for n in sizes],
+            [((3 * shard_rows, n), bf16, (shard_rows, n), lambda i, at: (i, 0)) for n in back_sizes],
             micros=4.0,
             grid=3,
         )
@@ -563,34 +588,42 @@
 
     across, each = group, 1
 
-    def d_attn_rows(half, d_hidden):
+    def d_attn_rows(half, d_hidden, first, count):
+        n = across * count
         return call(
-            3.0,
+            0.6 * count,
             functools.partial(d_attn_kernel, lows),
             (1,),
-            [(d_hidden, (tall, wide), lambda i: (half, 0))] + [(w, w.shape, fixed) for w in weights],
-            [((tall, across), bf16, (tall, across), fixed)] * (heads_width // across),
+            [(d_hidden, (tall, wide), lambda i: (half, 0))]
+            + [(w, (n, w.shape[1]), lambda i: (first // count, 0)) for w in weights],
+            [((tall, across), bf16, (tall, across), fixed)] * count,
         )
 
-    far = [swap(x, "dp", bits[0]) for x in d_attn_rows(1, d_hidden)]
-    near = d_attn_rows(0, d_hidden)
+    def d_attn_parts(half, d_hidden):
+        total = heads_width // across
+        parts = [(0, 2), (2, 2), (4, 1)] if total == 5 else [(0, total)]
+        return [x for first, count in parts for x in d_attn_rows(half, d_hidden, first, count)]
+
+    far = [swap(x, "dp", bits[0]) for x in d_attn_parts(1, d_hidden)]
+    near = d_attn_parts(0, d_hidden)
     for bit in bits[1:-1]:
         near, far = zip(*[fold([x], [y]) for x, y in zip(near, far)])
         far = [swap(x, "dp", bit) for x in far]
     folded = [fold(near[each * first : each * final], far[each * first : each * final]) for first, final in cuts]
     kept, passed = zip(*folded)
+    passed = [swap(passed[0], "dp", bits[-1]), *passed[1:]]
     tied = tie(*early, *terms, *kept, *passed)
-    early, terms, kept, passed, _ = split(tied, len(early), len(chunks), len(cuts), len(cuts))
+    early, terms, kept, passed, _ = split(tied, len(early), len(back_chunks), len(cuts), len(cuts))
 
     def late_sends(i):
         if not line:
             return []
-        beyond = sum_terms([early[1]], lows[i], terms[i], 1)
+        beyond = sum_terms([early[1]], back_lows[i], terms[i], 1)
         return [swap(beyond, "fsdp", 2), swap(take_rows(terms[i], 0, shard_rows), "fsdp", 1)]
 
     def team_pieces(i, got):
         got = early[:1] + got if line else early
-        total = sum_terms(got, lows[i], terms[i], 2 if line else part)
+        total = sum_terms(got, back_lows[i], terms[i], 2 if line else part)
         pieces = {0: total}
         for bit in reversed(bits):
             pieces.update({s ^ bit: swap(p, "dp", bit) for s, p in pieces.items()})
@@ -603,15 +636,15 @@
         return attention_call(micros, backward_kernel, length, *arrays, 3, first, last - first, group, grads)
 
     got = late_sends(0)
-    passed = [swap(x, "dp", bits[-1]) for x in passed]
+    passed = [passed[0], *[swap(x, "dp", bits[-1]) for x in passed[1:]]]
     grads = back(0, ())
     early_parts = passed
     tied = tie(*got, *grads, *terms, *early, loss, *early_parts)
-    got, grads, terms, early, (loss,), early_parts = split(tied, len(got), 3, len(chunks), len(early), 1)
+    got, grads, terms, early, (loss,), early_parts = split(tied, len(got), 3, len(back_chunks), len(early), 1)
     passed = [*early_parts, *passed[len(early_parts) :]]
 
     placed = []
-    for i in range(1, len(chunks)):
+    for i in range(1, len(back_chunks)):
         late = late_sends(i)
         placed += team_pieces(i - 1, got)
         if i == 1:
@@ -619,12 +652,12 @@
                 grads = back(j, grads)
         tied = tie(*late, *grads)
         got, grads, _ = split(tied, len(late), 3)
-    placed += team_pieces(len(chunks) - 1, got)
-    if len(chunks) == 1:
+    placed += team_pieces(len(back_chunks) - 1, got)
+    if len(back_chunks) == 1:
         for j in range(1, len(cuts)):
             grads = back(j, grads)
     d_queries, d_keys, d_values = grads
-    places = [(s, low) for low in lows for s in order]
+    places = [(s, low) for low in back_lows for s in order]
 
     if wide % LANES == 0:
         tall = next(t for t in (128, 64, 32, 16, shard_rows) if shard_rows % t == 0)

time: 218 us -> 208 us (0.954)
  waiting for transfers between devices: 78.5 us -> 66.3 us
  starting transfers between devices: 45.4 us -> 51.4 us
  Pallas kernels: 77.7 us -> 72.1 us
    ppermute x35 -> x36, waiting for transfers between devices: 68.8 us -> 55.6 us  [swap(): lax.ppermute(value, axis, [(i, i ^ bit) for i in range(lax.axis_size(axis...]
    ppermute x35 -> x36, starting transfers between devices: 40.3 us -> 46.3 us  [swap(): lax.ppermute(value, axis, [(i, i ^ bit) for i in range(lax.axis_size(axis...]
    unnamed x54 -> x68, local copies, waits for them, and re-layouts: 7.81 us -> 9.92 us
    pallas_call x9 -> x13, Pallas kernels: 20.8 us -> 19 us  [call(): pl.pallas_call(kernel, grid=grid, in_specs=[spec(b, m, a.shape) for a, b,...]
    pallas_call x15 -> x16, Pallas kernels: 23.9 us -> 22.2 us  [small_call(): pl.pallas_call(kernel, grid_spec=pltpu.PrefetchScalarGridSpec(num_scalar_...]
  transfers between devices with their start and end apart: 39 -> 40, of which waited for: 12 -> 12; matrix products, arithmetic and copies ran while one was open for 2% -> 2% of each run, Pallas kernels for 22% -> 25%
where the time goes in v4:
time: 208 us; the launch traced here: 207 us
  Pallas kernels  72.1 us (35%)
  waiting for transfers between devices  66.3 us (32%)
  starting transfers between devices  51.4 us (25%)
  local copies, waits for them, and re-layouts  10.5 us (5%)
  between operations  3.58 us (2%)
  other arithmetic  3.45 us (2%)
    ppermute x36, waiting for transfers between devices, swap(): lax.ppermute(value, axis, [(i, i ^ bit) for i in range(lax.axis_size(axis...  55.6 us
    ppermute x36, starting transfers between devices, swap(): lax.ppermute(value, axis, [(i, i ^ bit) for i in range(lax.axis_size(axis...  46.3 us
    pallas_call x5, Pallas kernels, attention_call(): pl.pallas_call(kernel, grid_spec=pltpu.PrefetchScalarGridSpec(num_scalar_...  27.4 us
    pallas_call x16, Pallas kernels, small_call(): pl.pallas_call(kernel, grid_spec=pltpu.PrefetchScalarGridSpec(num_scalar_...  22.2 us
    pallas_call x13, Pallas kernels, call(): pl.pallas_call(kernel, grid=grid, in_specs=[spec(b, m, a.shape) for a, b,...  19 us
    ppermute x4, waiting for transfers between devices, send(): return lax.ppermute(value, axis, pairs)  10.7 us
    unnamed x68, local copies, waits for them, and re-layouts  9.92 us
    ppermute x4, starting transfers between devices, send(): return lax.ppermute(value, axis, pairs)  5.06 us
  transfers between devices with their start and end apart: 40, of which 12 were waited for; matrix products, arithmetic and copies ran while one was open for 2% of the time, Pallas kernels for 25%

profile of v4, /device:TPU:1, one launch (start us, length us, event | category | flops | bytes accessed | tf_op | source)
XLA Modules:
  0.0 207.3 jit_solution(2440570014355542203)
XLA Ops:
  0.7 1.9 copy-done.15
  3.6 3.1 %collective-permute-start.1 = (bf16[640,640]{1,0:T(8,128)(2,1)}, bf16[640,640]{1,0:T(8,128)(2,1)}, u32[]{:S(2)}, u32[]{:S(2)}) collective-permute-start(bf16[640,640]{1,0:T(8,128)(2,1)} %shard_map.128.refs_0_), channel_id=1, source_target_pairs={{0,2},{1,3},{2,0},{3,1},{4,6},{5,7},{6,4},{7,5},{8,10},{9,11},{10,... | collective-permute-start | bytes 2457608 | tf_op jit(solution)/shard_map/ppermute | solution.py:42
  6.7 1.3 collective-permute-start
  8.6 1.3 copy-done.4
  9.9 4.2 %shard_map.130.refs_1_ = bf16[256,1536]{1,0:T(8,128)(2,1)S(1)} custom-call(s32[1]{0:T(128)} %dynamic_slice.6.length_ref, bf16[256,2560]{1,0:T(8,128)(2,1)S(1)} %bitcast.35, bf16[256,2560]{1,0:T(8,128)(2,1)S(1)} %bitcast.40, bf16[256,2560]{1,0:T(8,128)(2,1)S(1)} %bitcast.45), custom_call_target="tpu_custom_call" | custom-call | bytes 4718592 | tf_op jit(solution)/shard_map/pallas_call | solution.py:355
  14.1 1.3 collective-permute-start.3
  15.4 3.7 %shard_map.129.refs_0_ = bf16[256,1024]{1,0:T(8,128)(2,1)} custom-call(s32[1]{0:T(128)} %dynamic_slice.6.length_ref, bf16[256,2560]{1,0:T(8,128)(2,1)S(1)} %bitcast.36, bf16[256,2560]{1,0:T(8,128)(2,1)S(1)} %bitcast.41, bf16[256,2560]{1,0:T(8,128)(2,1)S(1)} %bitcast.46), custom_call_target="tpu_custom_call" | custom-call | bytes 3145728 | tf_op jit(solution)/shard_map/pallas_call | solution.py:355
  20.7 2.3 %shard_map.131 = bf16[256,2560]{1,0:T(8,128)(2,1)} custom-call(s32[1]{0:T(128)} %constant.13.clone.1.at_ref, bf16[256,1024]{1,0:T(8,128)(2,1)} %shard_map.129.refs_0_, bf16[256,1536]{1,0:T(8,128)(2,1)S(1)} %shard_map.130.refs_1_), custom_call_target="tpu_custom_call" | custom-call | bytes 1048576 | tf_op jit(solution)/shard_map/pallas_call | solution.py:215
  23.7 19.6 %collective-permute-done.2.refs_2_ = bf16[256,1024]{1,0:T(8,128)(2,1)} collective-permute-done((bf16[256,1024]{1,0:T(8,128)(2,1)}, bf16[256,1024]{1,0:T(8,128)(2,1)}, u32[]{:S(2)}, u32[]{:S(2)}) %collective-permute-start.2) | collective-permute-done | bytes 524320 | tf_op jit(solution)/shard_map/ppermute | solution.py:42
  43.3 1.3 collective-permute-start.9
  44.6 2.4 %collective-permute-start.6 = (bf16[256,2560]{1,0:T(8,128)(2,1)}, bf16[256,2560]{1,0:T(8,128)(2,1)}, u32[]{:S(2)}, u32[]{:S(2)}) collective-permute-start(bf16[256,2560]{1,0:T(8,128)(2,1)} %shard_map.131), channel_id=1, source_target_pairs={{0,4},{4,0},{8,12},{12,8},{1,5},{5,1},{9,13},{13,9},{2,6},{6,2},{1... | collective-permute-start | bytes 3932168 | tf_op jit(solution)/shard_map/ppermute | solution.py:42
  47.1 1.6 collective-permute-start.4
  48.6 1.3 collective-permute-start.5
  49.9 7.7 %collective-permute-done.9.in_ref.refs_10_.refs_4_ = bf16[512,640]{1,0:T(8,128)(2,1)S(1)} collective-permute-done((bf16[512,640]{1,0:T(8,128)(2,1)S(1)}, bf16[512,640]{1,0:T(8,128)(2,1)S(1)}, u32[]{:S(2)}, u32[]{:S(2)}) %collective-permute-start.9) | collective-permute-done | bytes 655392 | tf_op jit(solution)/shard_map/ppermute | solution.py:42
  57.6 3.0 %collective-permute-start.8 = (bf16[256,1536]{1,0:T(8,128)(2,1)}, bf16[256,1536]{1,0:T(8,128)(2,1)}, u32[]{:S(2)}, u32[]{:S(2)}) collective-permute-start(bf16[256,1536]{1,0:T(8,128)(2,1)} %collective-permute-done.3.refs_3_), channel_id=1, source_target_pairs={{0,4},{4,0},{8,12},{12,8},{1,5},{5,1},{9,13},{13,9},{2,6},{6,2},{1... | collective-permute-start | bytes 2359304 | tf_op jit(solution)/shard_map/ppermute | solution.py:42
  63.3 6.8 %collective-permute-done.5.refs_4_ = bf16[640,640]{1,0:T(8,128)(2,1)} collective-permute-done((bf16[640,640]{1,0:T(8,128)(2,1)}, bf16[640,640]{1,0:T(8,128)(2,1)}, u32[]{:S(2)}, u32[]{:S(2)}) %collective-permute-start.5) | collective-permute-done | bytes 819232 | tf_op jit(solution)/shard_map/ppermute | solution.py:388
  70.1 2.8 %shard_map.136.refs_7_.refs_0_ = bf16[2560,256]{1,0:T(8,128)(2,1)S(1)} custom-call(s32[4]{0:T(128)S(1)} %pad_add_fusion.1.at_ref, bf16[640,640]{1,0:T(8,128)(2,1)} %shard_map.128.refs_0_, bf16[640,640]{1,0:T(8,128)(2,1)} %collective-permute-done.refs_1_, bf16[640,640]{1,0:T(8,128)(2,1)} %collective-permute-done.1.refs_2_, ...), custom_call_target="tpu_custom_call" | custom-call | bytes 2097152 | tf_op jit(solution)/shard_map/pallas_call | solution.py:215
  72.9 4.6 %shard_map.137 = (f32[1024,256]{1,0:T(8,128)S(1)}, bf16[1024,256]{1,0:T(8,128)(2,1)S(1)}, f32[4,1,256]{2,1,0:T(1,128)S(1)}, bf16[1024,2560]{1,0:T(8,128)(2,1)S(1)}) custom-call(bf16[256,1024]{1,0:T(8,128)(2,1)} %shard_map.129.refs_0_, bf16[256,1536]{1,0:T(8,128)(2,1)S(1)} %copy-done.12, bf16[256,1024]{1,0:T(8,128)(2,1)} %collective-permute-done.2.refs_2_, ...), custom_call_target="tpu_custom_call" | custom-call | bytes 2097152 | tf_op jit(solution)/shard_map/pallas_call | solution.py:336
  77.5 2.9 %shard_map.138.refs_1_ = bf16[2560,384]{1,0:T(8,128)(2,1)S(1)} custom-call(s32[4]{0:T(128)S(1)} %pad_add_fusion.1.at_ref, bf16[640,640]{1,0:T(8,128)(2,1)} %shard_map.128.refs_0_, bf16[640,640]{1,0:T(8,128)(2,1)} %collective-permute-done.refs_1_, bf16[640,640]{1,0:T(8,128)(2,1)} %collective-permute-done.1.refs_2_, ...), custom_call_target="tpu_custom_call" | custom-call | bytes 2097152 | tf_op jit(solution)/shard_map/pallas_call | solution.py:215
  80.4 1.3 collective-permute-start.16
  81.7 3.6 %shard_map.139 = (f32[1024,384]{1,0:T(8,128)S(1)}, bf16[1024,384]{1,0:T(8,128)(2,1)S(1)}, f32[4,1,256]{2,1,0:T(1,128)S(1)}) custom-call(bf16[1024,2560]{1,0:T(8,128)(2,1)S(1)} %get-tuple-element.128.refs_0_.attn_ref, bf16[2560,384]{1,0:T(8,128)(2,1)S(1)} %shard_map.138.refs_1_, f32[1,384]{1,0:T(1,128)S(1)} %constant_dynamic-slice_fusion.1.refs_2_.gain_ref.refs_5_, ...), custom_call_target="tpu_custom_call" | custom-call | bytes 2097152 | tf_op jit(solution)/shard_map/pallas_call | solution.py:336
  85.6 1.9 collective-permute-start.11
  89.2 1.3 collective-permute-start.12
  90.5 1.2 collective-permute-done.14
  92.6 1.3 collective-permute-start.13
  93.9 15.6 %collective-permute-done.13.other_ref = f32[4,1,256]{2,1,0:T(1,128)S(1)} collective-permute-done((f32[4,1,256]{2,1,0:T(1,128)S(1)}, f32[4,1,256]{2,1,0:T(1,128)S(1)}, u32[]{:S(2)}, u32[]{:S(2)}) %collective-permute-start.13) | collective-permute-done | bytes 4128 | tf_op jit(solution)/shard_map/ppermute | solution.py:42
  109.4 1.7 shard_map.140.refs_0_
  111.1 1.9 shard_map.141
  113.0 2.3 %collective-permute-start.18 = (f32[2,2,2,256]{3,2,1,0:T(2,128)S(1)}, f32[2,2,2,256]{3,2,1,0:T(2,128)S(1)}, u32[]{:S(2)}, u32[]{:S(2)}) collective-permute-start(f32[2,2,2,256]{3,2,1,0:T(2,128)S(1)} %bitcast.56), channel_id=1, source_target_pairs={{0,4},{4,0},{8,12},{12,8},{1,5},{5,1},{9,13},{13,9},{2,6},{6,2},{1... | collective-permute-start | bytes 24584 | tf_op jit(solution)/shard_map/ppermute | solution.py:42
  116.4 2.2 %collective-permute-done.19 = f32[2,2,2,256]{3,2,1,0:T(2,128)S(1)} collective-permute-done((f32[2,2,2,256]{3,2,1,0:T(2,128)S(1)}, f32[2,2,2,256]{3,2,1,0:T(2,128)S(1)}, u32[]{:S(2)}, u32[]{:S(2)}) %collective-permute-start.19) | collective-permute-done | bytes 8224 | tf_op jit(solution)/shard_map/ppermute | solution.py:42
  118.7 3.6 %shard_map.142 = (bf16[1024,640]{1,0:T(8,128)(2,1)S(1)}, bf16[640,640]{1,0:T(8,128)(2,1)S(1)}) custom-call(s32[1]{0:T(128)} %bitcast.at_ref, bf16[1024,2560]{1,0:T(8,128)(2,1)S(1)} %get-tuple-element.128.refs_0_.attn_ref, f32[4,1,256]{2,1,0:T(1,128)S(1)} %bitcast.55, f32[4,1,256]{2,1,0:T(1,128)S(1)} %collective-permute-done.13.other_ref, ...), custom_call_target="tpu_custom_call" | custom-call | bytes 4194304 | tf_op jit(solution)/shard_map/pallas_call | solution.py:215
  123.3 1.6 collective-permute-start.22
  126.0 1.3 collective-permute-start.21
  133.9 4.6 %shard_map.143 = (bf16[1920,384]{1,0:T(8,128)(2,1)S(1)}, bf16[1920,256]{1,0:T(8,128)(2,1)S(1)}) custom-call(s32[3]{0:T(128)S(1)} %pad_add_fusion.2.at_ref, bf16[1024,2560]{1,0:T(8,128)(2,1)S(1)} %get-tuple-element.128.refs_0_.attn_ref, bf16[1024,640]{1,0:T(8,128)(2,1)S(1)} %get-tuple-element.142.d_ref), custom_call_target="tpu_custom_call" | custom-call | bytes 4194304 | tf_op jit(solution)/shard_map/pallas_call | solution.py:215
  141.1 3.9 %collective-permute-done.21.refs_0_ = bf16[640,640]{1,0:T(8,128)(2,1)S(1)} collective-permute-done((bf16[640,640]{1,0:T(8,128)(2,1)S(1)}, bf16[640,640]{1,0:T(8,128)(2,1)S(1)}, u32[]{:S(2)}, u32[]{:S(2)}) %collective-permute-start.21) | collective-permute-done | bytes 819232 | tf_op jit(solution)/shard_map/ppermute | solution.py:388
  147.3 3.3 %collective-permute-start.29 = (bf16[640,384]{1,0:T(8,128)(2,1)}, bf16[640,384]{1,0:T(8,128)(2,1)}, u32[]{:S(2)}, u32[]{:S(2)}) collective-permute-start(bf16[640,384]{1,0:T(8,128)(2,1)} %shard_map.154), channel_id=1, source_target_pairs={{0,1},{1,0},{2,3},{3,2},{4,5},{5,4},{6,7},{7,6},{8,9},{9,8},{10,11... | collective-permute-start | bytes 1474568 | tf_op jit(solution)/shard_map/ppermute | solution.py:42
  152.0 1.2 fusion.2
  153.9 1.3 copy-done.5
  157.3 6.9 %shard_map.155 = (bf16[256,2560]{1,0:T(8,128)(2,1)}, bf16[256,2560]{1,0:T(8,128)(2,1)}, bf16[256,2560]{1,0:T(8,128)(2,1)}) custom-call(s32[1]{0:T(128)} %dynamic_slice.6.length_ref, bf16[256,2560]{1,0:T(8,128)(2,1)S(1)} %bitcast.37, bf16[256,2560]{1,0:T(8,128)(2,1)S(1)} %bitcast.42, bf16[256,2560]{1,0:T(8,128)(2,1)S(1)} %bitcast.47, ...), custom_call_target="tpu_custom_call" | custom-call | bytes 4194304 | tf_op jit(solution)/shard_map/pallas_call | solution.py:355
  164.2 6.8 %collective-permute-done.29.refs_2_ = bf16[640,384]{1,0:T(8,128)(2,1)} collective-permute-done((bf16[640,384]{1,0:T(8,128)(2,1)}, bf16[640,384]{1,0:T(8,128)(2,1)}, u32[]{:S(2)}, u32[]{:S(2)}) %collective-permute-start.29) | collective-permute-done | bytes 491552 | tf_op jit(solution)/shard_map/ppermute | solution.py:42
  171.2 2.4 %collective-permute-start.33 = (bf16[640,256]{1,0:T(8,128)(2,1)S(1)}, bf16[640,256]{1,0:T(8,128)(2,1)S(1)}, u32[]{:S(2)}, u32[]{:S(2)}) collective-permute-start(bf16[640,256]{1,0:T(8,128)(2,1)S(1)} %shard_map.157), channel_id=1, source_target_pairs={{0,1},{1,0},{2,3},{3,2},{4,5},{5,4},{6,7},{7,6},{8,9},{9,8},{10,11... | collective-permute-start | bytes 983048 | tf_op jit(solution)/shard_map/ppermute | solution.py:42
  174.2 1.5 shard_map.160.refs_0_
  176.9 7.7 %shard_map.158 = (bf16[256,2560]{1,0:T(8,128)(2,1)}, bf16[256,2560]{1,0:T(8,128)(2,1)}, bf16[256,2560]{1,0:T(8,128)(2,1)}) custom-call(s32[1]{0:T(128)} %dynamic_slice.6.length_ref, bf16[256,2560]{1,0:T(8,128)(2,1)S(1)} %bitcast.38, bf16[256,2560]{1,0:T(8,128)(2,1)S(1)} %bitcast.43, ...), custom_call_target="tpu_custom_call", output_to_operand_aliasing={{0}: (6, {}), {1}: (7, {}), {2}: (8, {})} | custom-call | bytes 4194304 | tf_op jit(solution)/shard_map/pallas_call | solution.py:355
  184.5 5.0 %shard_map.159 = (bf16[256,2560]{1,0:T(8,128)(2,1)}, bf16[256,2560]{1,0:T(8,128)(2,1)}, bf16[256,2560]{1,0:T(8,128)(2,1)}) custom-call(s32[1]{0:T(128)} %dynamic_slice.6.length_ref, bf16[256,2560]{1,0:T(8,128)(2,1)S(1)} %bitcast.39, bf16[256,2560]{1,0:T(8,128)(2,1)S(1)} %bitcast.44, ...), custom_call_target="tpu_custom_call", output_to_operand_aliasing={{0}: (6, {}), {1}: (7, {}), {2}: (8, {})} | custom-call | bytes 2621440 | tf_op jit(solution)/shard_map/pallas_call | solution.py:355
  190.1 4.9 %collective-permute-start.35 = (bf16[640,384]{1,0:T(8,128)(2,1)S(1)}, bf16[640,384]{1,0:T(8,128)(2,1)S(1)}, u32[]{:S(2)}, u32[]{:S(2)}) collective-permute-start(bf16[640,384]{1,0:T(8,128)(2,1)S(1)} %shard_map.160.refs_0_), channel_id=1, source_target_pairs={{0,4},{4,0},{8,12},{12,8},{1,5},{5,1},{9,13},{13,9},{2,6},{6,2},{1... | collective-permute-start | bytes 1474568 | tf_op jit(solution)/shard_map/ppermute | solution.py:42
  195.7 5.8 %collective-permute-start.39 = (bf16[640,256]{1,0:T(8,128)(2,1)S(1)}, bf16[640,256]{1,0:T(8,128)(2,1)S(1)}, u32[]{:S(2)}, u32[]{:S(2)}) collective-permute-start(bf16[640,256]{1,0:T(8,128)(2,1)S(1)} %collective-permute-done.37.refs_5_), channel_id=1, source_target_pairs={{0,4},{4,0},{8,12},{12,8},{1,5},{5,1},{9,13},{13,9},{2,6},{6,2},{1... | collective-permute-start | bytes 983048 | tf_op jit(solution)/shard_map/ppermute | solution.py:42
  201.5 1.2 collective-permute-done.39.refs_7_
  202.7 3.5 %shard_map.162 = f32[640,2560]{1,0:T(8,128)} custom-call(s32[1]{0:T(128)} %bitcast.1.at_ref.member_ref, bf16[640,384]{1,0:T(8,128)(2,1)S(1)} %shard_map.160.refs_0_, bf16[640,384]{1,0:T(8,128)(2,1)S(1)} %collective-permute-done.34.refs_1_, bf16[640,384]{1,0:T(8,128)(2,1)S(1)} %collective-permute-done.35.refs_2_, ...), custom_call_target="tpu_custom_call" | custom-call | bytes 1048576 | tf_op jit(solution)/shard_map/pallas_call | solution.py:664
  (154 shorter events, 30.3 us)
Async XLA Ops:
  0.6 62.6 %copy-start = (f32[1,2560]{1,0:T(1,128)S(1)}, f32[1,2560]{1,0:T(1,128)}, u32[]{:S(2)}) copy-start(f32[1,2560]{1,0:T(1,128)} %param.17) | copy-start | bytes 30724
  3.6 39.7 %collective-permute-start.1 = (bf16[640,640]{1,0:T(8,128)(2,1)}, bf16[640,640]{1,0:T(8,128)(2,1)}, u32[]{:S(2)}, u32[]{:S(2)}) collective-permute-start(bf16[640,640]{1,0:T(8,128)(2,1)} %shard_map.128.refs_0_), channel_id=1, source_target_pairs={{0,2},{1,3},{2,0},{3,1},{4,6},{5,7},{6,4},{7,5},{8,10},{9,11},{10,... | collective-permute-start | bytes 2457608 | tf_op jit(solution)/shard_map/ppermute | solution.py:42
  6.7 36.6 %collective-permute-start = (bf16[640,640]{1,0:T(8,128)(2,1)}, bf16[640,640]{1,0:T(8,128)(2,1)}, u32[]{:S(2)}, u32[]{:S(2)}) collective-permute-start(bf16[640,640]{1,0:T(8,128)(2,1)} %shard_map.128.refs_0_), channel_id=1, source_target_pairs={{0,1},{1,0},{2,3},{3,2},{4,5},{5,4},{6,7},{7,6},{8,9},{9,8},{10,11... | collective-permute-start | bytes 2457608 | tf_op jit(solution)/shard_map/ppermute | solution.py:42
  14.1 29.2 %collective-permute-start.3 = (bf16[256,1536]{1,0:T(8,128)(2,1)S(1)}, bf16[256,1536]{1,0:T(8,128)(2,1)}, u32[]{:S(2)}, u32[]{:S(2)}) collective-permute-start(bf16[256,1536]{1,0:T(8,128)(2,1)S(1)} %shard_map.130.refs_1_), channel_id=1, source_target_pairs={{0,8},{4,12},{8,0},{12,4},{1,9},{5,13},{9,1},{13,5},{2,10},{6,14},... | collective-permute-start | bytes 2359304 | tf_op jit(solution)/shard_map/ppermute | solution.py:42
  19.1 24.2 %collective-permute-start.2 = (bf16[256,1024]{1,0:T(8,128)(2,1)}, bf16[256,1024]{1,0:T(8,128)(2,1)}, u32[]{:S(2)}, u32[]{:S(2)}) collective-permute-start(bf16[256,1024]{1,0:T(8,128)(2,1)} %shard_map.129.refs_0_), channel_id=1, source_target_pairs={{0,8},{4,12},{8,0},{12,4},{1,9},{5,13},{9,1},{13,5},{2,10},{6,14},... | collective-permute-start | bytes 1572872 | tf_op jit(solution)/shard_map/ppermute | solution.py:42
  23.7 38.6 %copy-start.18 = (bf16[256,640]{1,0:T(8,128)(2,1)}, bf16[256,640]{1,0:T(8,128)(2,1)S(1)}, u32[]{:S(2)}) copy-start(bf16[256,640]{1,0:T(8,128)(2,1)S(1)} %get-tuple-element.125.refs_9_.refs_3_) | copy-start | bytes 983044
  43.3 14.2 %collective-permute-start.9 = (bf16[512,640]{1,0:T(8,128)(2,1)S(1)}, bf16[512,640]{1,0:T(8,128)(2,1)S(1)}, u32[]{:S(2)}, u32[]{:S(2)}) collective-permute-start(bf16[512,640]{1,0:T(8,128)(2,1)S(1)} %shard_map.133), channel_id=1, source_target_pairs={{0,8},{4,12},{8,0},{12,4},{1,9},{5,13},{9,1},{13,5},{2,10},{6,14},... | collective-permute-start | bytes 1966088 | tf_op jit(solution)/shard_map/ppermute | solution.py:42
  44.6 25.5 %collective-permute-start.6 = (bf16[256,2560]{1,0:T(8,128)(2,1)}, bf16[256,2560]{1,0:T(8,128)(2,1)}, u32[]{:S(2)}, u32[]{:S(2)}) collective-permute-start(bf16[256,2560]{1,0:T(8,128)(2,1)} %shard_map.131), channel_id=1, source_target_pairs={{0,4},{4,0},{8,12},{12,8},{1,5},{5,1},{9,13},{13,9},{2,6},{6,2},{1... | collective-permute-start | bytes 3932168 | tf_op jit(solution)/shard_map/ppermute | solution.py:42
  47.0 15.3 %collective-permute-start.7 = (bf16[256,1024]{1,0:T(8,128)(2,1)}, bf16[256,1024]{1,0:T(8,128)(2,1)S(1)}, u32[]{:S(2)}, u32[]{:S(2)}) collective-permute-start(bf16[256,1024]{1,0:T(8,128)(2,1)} %collective-permute-done.2.refs_2_), channel_id=1, source_target_pairs={{0,4},{4,0},{8,12},{12,8},{1,5},{5,1},{9,13},{13,9},{2,6},{6,2},{1... | collective-permute-start | bytes 1572872 | tf_op jit(solution)/shard_map/ppermute | solution.py:42
  47.1 16.2 %collective-permute-start.4 = (bf16[640,640]{1,0:T(8,128)(2,1)}, bf16[640,640]{1,0:T(8,128)(2,1)}, u32[]{:S(2)}, u32[]{:S(2)}) collective-permute-start(bf16[640,640]{1,0:T(8,128)(2,1)} %shard_map.128.refs_0_), channel_id=1, source_target_pairs={{1,2},{2,1},{5,6},{6,5},{9,10},{10,9},{13,14},{14,13},{17,18},{18,... | collective-permute-start | bytes 2457608 | tf_op jit(solution)/shard_map/ppermute | solution.py:388
  48.6 21.5 %collective-permute-start.5 = (bf16[640,640]{1,0:T(8,128)(2,1)}, bf16[640,640]{1,0:T(8,128)(2,1)}, u32[]{:S(2)}, u32[]{:S(2)}) collective-permute-start(bf16[640,640]{1,0:T(8,128)(2,1)} %collective-permute-done.1.refs_2_), channel_id=1, source_target_pairs={{2,3},{1,0},{6,7},{5,4},{10,11},{9,8},{14,15},{13,12},{18,19},{17,... | collective-permute-start | bytes 2457608 | tf_op jit(solution)/shard_map/ppermute | solution.py:388
  57.6 5.7 %collective-permute-start.8 = (bf16[256,1536]{1,0:T(8,128)(2,1)}, bf16[256,1536]{1,0:T(8,128)(2,1)}, u32[]{:S(2)}, u32[]{:S(2)}) collective-permute-start(bf16[256,1536]{1,0:T(8,128)(2,1)} %collective-permute-done.3.refs_3_), channel_id=1, source_target_pairs={{0,4},{4,0},{8,12},{12,8},{1,5},{5,1},{9,13},{13,9},{2,6},{6,2},{1... | collective-permute-start | bytes 2359304 | tf_op jit(solution)/shard_map/ppermute | solution.py:42
  63.1 7.0 %collective-permute-start.10 = (bf16[512,640]{1,0:T(8,128)(2,1)}, bf16[512,640]{1,0:T(8,128)(2,1)S(1)}, u32[]{:S(2)}, u32[]{:S(2)}) collective-permute-start(bf16[512,640]{1,0:T(8,128)(2,1)} %shard_map.135), channel_id=1, source_target_pairs={{0,4},{4,0},{8,12},{12,8},{1,5},{5,1},{9,13},{13,9},{2,6},{6,2},{1... | collective-permute-start | bytes 1966088 | tf_op jit(solution)/shard_map/ppermute | solution.py:42
  63.2 9.7 %copy-start.12 = (bf16[256,1536]{1,0:T(8,128)(2,1)S(1)}, bf16[256,1536]{1,0:T(8,128)(2,1)}, u32[]{:S(2)}) copy-start(bf16[256,1536]{1,0:T(8,128)(2,1)} %copy-done.11) | copy-start | bytes 2359300
  63.2 9.7 %copy-start.14 = (bf16[512,640]{1,0:T(8,128)(2,1)S(1)}, bf16[512,640]{1,0:T(8,128)(2,1)}, u32[]{:S(2)}) copy-start(bf16[512,640]{1,0:T(8,128)(2,1)} %copy-done.13) | copy-start | bytes 1966084
  63.3 9.7 %copy-start.19 = (bf16[256,640]{1,0:T(8,128)(2,1)S(1)}, bf16[256,640]{1,0:T(8,128)(2,1)}, u32[]{:S(2)}) copy-start(bf16[256,640]{1,0:T(8,128)(2,1)} %copy-done.18) | copy-start | bytes 983044
  63.3 9.7 %copy-start.28 = (bf16[256,1024]{1,0:T(8,128)(2,1)S(1)}, bf16[256,1024]{1,0:T(8,128)(2,1)}, u32[]{:S(2)}) copy-start(bf16[256,1024]{1,0:T(8,128)(2,1)} %copy-done.27) | copy-start | bytes 1572868
  80.4 29.1 %collective-permute-start.16 = (bf16[1024,256]{1,0:T(8,128)(2,1)S(1)}, bf16[1024,256]{1,0:T(8,128)(2,1)S(1)}, u32[]{:S(2)}, u32[]{:S(2)}) collective-permute-start(bf16[1024,256]{1,0:T(8,128)(2,1)S(1)} %get-tuple-element.138), channel_id=1, source_target_pairs={{0,16},{16,0},{1,17},{17,1},{2,18},{18,2},{3,19},{19,3},{4,20},{20... | collective-permute-start | bytes 1572872 | tf_op jit(solution)/shard_map/ppermute | solution.py:42
  85.3 25.9 %collective-permute-start.17 = (bf16[1024,384]{1,0:T(8,128)(2,1)S(1)}, bf16[1024,384]{1,0:T(8,128)(2,1)S(1)}, u32[]{:S(2)}, u32[]{:S(2)}) collective-permute-start(bf16[1024,384]{1,0:T(8,128)(2,1)S(1)} %get-tuple-element.133), channel_id=1, source_target_pairs={{0,16},{16,0},{1,17},{17,1},{2,18},{18,2},{3,19},{19,3},{4,20},{20... | collective-permute-start | bytes 2359304 | tf_op jit(solution)/shard_map/ppermute | solution.py:42
  85.6 3.6 %collective-permute-start.11 = (f32[2,2,1,256]{3,2,1,0:T(1,128)S(1)}, f32[2,2,1,256]{3,2,1,0:T(1,128)S(1)}, u32[]{:S(2)}, u32[]{:S(2)}) collective-permute-start(f32[2,2,1,256]{3,2,1,0:T(1,128)S(1)} %bitcast.64), channel_id=1, source_target_pairs={{0,4},{4,0},{8,12},{12,8},{1,5},{5,1},{9,13},{13,9},{2,6},{6,2},{1... | collective-permute-start | bytes 12296 | tf_op jit(solution)/shard_map/ppermute | solution.py:42
  88.9 2.8 %collective-permute-start.14 = (f32[1,1,256]{2,1,0:T(1,128)S(1)}, f32[1,1,256]{2,1,0:T(1,128)S(1)}, u32[]{:S(2)}, u32[]{:S(2)}) collective-permute-start(f32[1,1,256]{2,1,0:T(1,128)S(1)} %compare_select_fusion), channel_id=1, source_target_pairs={{0,8},{4,12},{8,0},{12,4},{1,9},{5,13},{9,1},{13,5},{2,10},{6,14},... | collective-permute-start | bytes 3080 | tf_op jit(solution)/shard_map/ppermute | solution.py:42
  89.2 3.3 %collective-permute-start.12 = (f32[2,2,1,256]{3,2,1,0:T(1,128)S(1)}, f32[2,2,1,256]{3,2,1,0:T(1,128)S(1)}, u32[]{:S(2)}, u32[]{:S(2)}) collective-permute-start(f32[2,2,1,256]{3,2,1,0:T(1,128)S(1)} %reverse_add_fusion.2), channel_id=1, source_target_pairs={{0,8},{4,12},{8,0},{12,4},{1,9},{5,13},{9,1},{13,5},{2,10},{6,14},... | collective-permute-start | bytes 12296 | tf_op jit(solution)/shard_map/ppermute | solution.py:42
  91.7 2.2 %collective-permute-start.15 = (f32[2,1,256]{2,1,0:T(1,128)S(1)}, f32[2,1,256]{2,1,0:T(1,128)S(1)}, u32[]{:S(2)}, u32[]{:S(2)}) collective-permute-start(f32[2,1,256]{2,1,0:T(1,128)S(1)} %pad_maximum_fusion), channel_id=1, source_target_pairs={{0,4},{4,0},{8,12},{12,8},{1,5},{5,1},{9,13},{13,9},{2,6},{6,2},{1... | collective-permute-start | bytes 6152 | tf_op jit(solution)/shard_map/ppermute | solution.py:42
  92.6 16.9 %collective-permute-start.13 = (f32[4,1,256]{2,1,0:T(1,128)S(1)}, f32[4,1,256]{2,1,0:T(1,128)S(1)}, u32[]{:S(2)}, u32[]{:S(2)}) collective-permute-start(f32[4,1,256]{2,1,0:T(1,128)S(1)} %bitcast.52), channel_id=1, source_target_pairs={{0,16},{16,0},{1,17},{17,1},{2,18},{18,2},{3,19},{19,3},{4,20},{20... | collective-permute-start | bytes 12296 | tf_op jit(solution)/shard_map/ppermute | solution.py:42
  113.0 3.2 %collective-permute-start.18 = (f32[2,2,2,256]{3,2,1,0:T(2,128)S(1)}, f32[2,2,2,256]{3,2,1,0:T(2,128)S(1)}, u32[]{:S(2)}, u32[]{:S(2)}) collective-permute-start(f32[2,2,2,256]{3,2,1,0:T(2,128)S(1)} %bitcast.56), channel_id=1, source_target_pairs={{0,4},{4,0},{8,12},{12,8},{1,5},{5,1},{9,13},{13,9},{2,6},{6,2},{1... | collective-permute-start | bytes 24584 | tf_op jit(solution)/shard_map/ppermute | solution.py:42
  116.2 2.5 %collective-permute-start.19 = (f32[2,2,2,256]{3,2,1,0:T(2,128)S(1)}, f32[2,2,2,256]{3,2,1,0:T(2,128)S(1)}, u32[]{:S(2)}, u32[]{:S(2)}) collective-permute-start(f32[2,2,2,256]{3,2,1,0:T(2,128)S(1)} %reverse_add_fusion.1), channel_id=1, source_target_pairs={{0,8},{4,12},{8,0},{12,4},{1,9},{5,13},{9,1},{13,5},{2,10},{6,14},... | collective-permute-start | bytes 24584 | tf_op jit(solution)/shard_map/ppermute | solution.py:42
  123.3 7.0 %collective-permute-start.22 = (bf16[512,512]{1,0:T(8,128)(2,1)S(1)}, bf16[512,512]{1,0:T(8,128)(2,1)S(1)}, u32[]{:S(2)}, u32[]{:S(2)}) collective-permute-start(bf16[512,512]{1,0:T(8,128)(2,1)S(1)} %get-tuple-element.147), channel_id=1, source_target_pairs={{0,4},{4,0},{8,12},{12,8},{1,5},{5,1},{9,13},{13,9},{2,6},{6,2},{1... | collective-permute-start | bytes 1572872 | tf_op jit(solution)/shard_map/ppermute | solution.py:42
  124.9 5.8 %collective-permute-start.23 = (bf16[512,512]{1,0:T(8,128)(2,1)S(1)}, bf16[512,512]{1,0:T(8,128)(2,1)S(1)}, u32[]{:S(2)}, u32[]{:S(2)}) collective-permute-start(bf16[512,512]{1,0:T(8,128)(2,1)S(1)} %get-tuple-element.148), channel_id=1, source_target_pairs={{0,4},{4,0},{8,12},{12,8},{1,5},{5,1},{9,13},{13,9},{2,6},{6,2},{1... | collective-permute-start | bytes 1572872 | tf_op jit(solution)/shard_map/ppermute | solution.py:42
  125.5 6.4 %collective-permute-start.26 = (bf16[512,512]{1,0:T(8,128)(2,1)S(1)}, bf16[512,512]{1,0:T(8,128)(2,1)S(1)}, u32[]{:S(2)}, u32[]{:S(2)}) collective-permute-start(bf16[512,512]{1,0:T(8,128)(2,1)S(1)} %shard_map.151), channel_id=1, source_target_pairs={{0,4},{4,0},{8,12},{12,8},{1,5},{5,1},{9,13},{13,9},{2,6},{6,2},{1... | collective-permute-start | bytes 1572872 | tf_op jit(solution)/shard_map/ppermute | solution.py:42
  126.0 19.0 %collective-permute-start.21 = (bf16[640,640]{1,0:T(8,128)(2,1)S(1)}, bf16[640,640]{1,0:T(8,128)(2,1)S(1)}, u32[]{:S(2)}, u32[]{:S(2)}) collective-permute-start(bf16[640,640]{1,0:T(8,128)(2,1)S(1)} %get-tuple-element.141), channel_id=1, source_target_pairs={{0,1},{3,2},{4,5},{7,6},{8,9},{11,10},{12,13},{15,14},{16,17},{19,... | collective-permute-start | bytes 2457608 | tf_op jit(solution)/shard_map/ppermute | solution.py:388
  127.4 17.7 %collective-permute-start.20 = (bf16[640,640]{1,0:T(8,128)(2,1)S(1)}, bf16[640,640]{1,0:T(8,128)(2,1)S(1)}, u32[]{:S(2)}, u32[]{:S(2)}) collective-permute-start(bf16[640,640]{1,0:T(8,128)(2,1)S(1)} %get-tuple-element.141), channel_id=1, source_target_pairs={{1,2},{2,1},{5,6},{6,5},{9,10},{10,9},{13,14},{14,13},{17,18},{18,... | collective-permute-start | bytes 2457608 | tf_op jit(solution)/shard_map/ppermute | solution.py:388
  130.3 9.8 %collective-permute-start.24 = (bf16[512,512]{1,0:T(8,128)(2,1)S(1)}, bf16[512,512]{1,0:T(8,128)(2,1)S(1)}, u32[]{:S(2)}, u32[]{:S(2)}) collective-permute-start(bf16[512,512]{1,0:T(8,128)(2,1)S(1)} %get-tuple-element.152), channel_id=1, source_target_pairs={{0,4},{4,0},{8,12},{12,8},{1,5},{5,1},{9,13},{13,9},{2,6},{6,2},{1... | collective-permute-start | bytes 1572872 | tf_op jit(solution)/shard_map/ppermute | solution.py:42
  130.6 9.5 %collective-permute-start.25 = (bf16[512,512]{1,0:T(8,128)(2,1)S(1)}, bf16[512,512]{1,0:T(8,128)(2,1)S(1)}, u32[]{:S(2)}, u32[]{:S(2)}) collective-permute-start(bf16[512,512]{1,0:T(8,128)(2,1)S(1)} %get-tuple-element.153), channel_id=1, source_target_pairs={{0,4},{4,0},{8,12},{12,8},{1,5},{5,1},{9,13},{13,9},{2,6},{6,2},{1... | collective-permute-start | bytes 1572872 | tf_op jit(solution)/shard_map/ppermute | solution.py:42
  131.9 13.3 %collective-permute-start.27 = (bf16[256,1024]{1,0:T(8,128)(2,1)S(1)}, bf16[256,1024]{1,0:T(8,128)(2,1)S(1)}, u32[]{:S(2)}, u32[]{:S(2)}) collective-permute-start(bf16[256,1024]{1,0:T(8,128)(2,1)S(1)} %get-tuple-element.156), channel_id=1, source_target_pairs={{0,8},{4,12},{8,0},{12,4},{1,9},{5,13},{9,1},{13,5},{2,10},{6,14},... | collective-permute-start | bytes 1572872 | tf_op jit(solution)/shard_map/ppermute | solution.py:42
  145.2 25.8 %collective-permute-start.30 = (bf16[256,1024]{1,0:T(8,128)(2,1)}, bf16[256,1024]{1,0:T(8,128)(2,1)}, u32[]{:S(2)}, u32[]{:S(2)}) collective-permute-start(bf16[256,1024]{1,0:T(8,128)(2,1)} %get-tuple-element.168), channel_id=1, source_target_pairs={{0,8},{4,12},{8,0},{12,4},{1,9},{5,13},{9,1},{13,5},{2,10},{6,14},... | collective-permute-start | bytes 1572872 | tf_op jit(solution)/shard_map/ppermute | solution.py:42
  147.3 23.8 %collective-permute-start.29 = (bf16[640,384]{1,0:T(8,128)(2,1)}, bf16[640,384]{1,0:T(8,128)(2,1)}, u32[]{:S(2)}, u32[]{:S(2)}) collective-permute-start(bf16[640,384]{1,0:T(8,128)(2,1)} %shard_map.154), channel_id=1, source_target_pairs={{0,1},{1,0},{2,3},{3,2},{4,5},{5,4},{6,7},{7,6},{8,9},{9,8},{10,11... | collective-permute-start | bytes 1474568 | tf_op jit(solution)/shard_map/ppermute | solution.py:42
  150.5 20.5 %collective-permute-start.28 = (bf16[640,384]{1,0:T(8,128)(2,1)}, bf16[640,384]{1,0:T(8,128)(2,1)}, u32[]{:S(2)}, u32[]{:S(2)}) collective-permute-start(bf16[640,384]{1,0:T(8,128)(2,1)} %shard_map.153), channel_id=1, source_target_pairs={{0,2},{1,3},{2,0},{3,1},{4,6},{5,7},{6,4},{7,5},{8,10},{9,11},{10,... | collective-permute-start | bytes 1474568 | tf_op jit(solution)/shard_map/ppermute | solution.py:42
  150.9 13.3 %collective-permute-start.31 = (bf16[256,512]{1,0:T(8,128)(2,1)}, bf16[256,512]{1,0:T(8,128)(2,1)}, u32[]{:S(2)}, u32[]{:S(2)}) collective-permute-start(bf16[256,512]{1,0:T(8,128)(2,1)} %get-tuple-element.169), channel_id=1, source_target_pairs={{0,8},{4,12},{8,0},{12,4},{1,9},{5,13},{9,1},{13,5},{2,10},{6,14},... | collective-permute-start | bytes 786440 | tf_op jit(solution)/shard_map/ppermute | solution.py:42
  157.3 13.8 %copy-start.10 = (bf16[1920,256]{1,0:T(8,128)(2,1)S(1)}, bf16[1920,256]{1,0:T(8,128)(2,1)}, u32[]{:S(2)}) copy-start(bf16[1920,256]{1,0:T(8,128)(2,1)} %copy-done.9) | copy-start | bytes 2949124
  171.2 18.3 %collective-permute-start.33 = (bf16[640,256]{1,0:T(8,128)(2,1)S(1)}, bf16[640,256]{1,0:T(8,128)(2,1)S(1)}, u32[]{:S(2)}, u32[]{:S(2)}) collective-permute-start(bf16[640,256]{1,0:T(8,128)(2,1)S(1)} %shard_map.157), channel_id=1, source_target_pairs={{0,1},{1,0},{2,3},{3,2},{4,5},{5,4},{6,7},{7,6},{8,9},{9,8},{10,11... | collective-permute-start | bytes 983048 | tf_op jit(solution)/shard_map/ppermute | solution.py:42
  173.6 15.9 %collective-permute-start.32 = (bf16[640,256]{1,0:T(8,128)(2,1)S(1)}, bf16[640,256]{1,0:T(8,128)(2,1)S(1)}, u32[]{:S(2)}, u32[]{:S(2)}) collective-permute-start(bf16[640,256]{1,0:T(8,128)(2,1)S(1)} %shard_map.156), channel_id=1, source_target_pairs={{0,2},{1,3},{2,0},{3,1},{4,6},{5,7},{6,4},{7,5},{8,10},{9,11},{10,... | collective-permute-start | bytes 983048 | tf_op jit(solution)/shard_map/ppermute | solution.py:42
  175.7 8.8 %copy-start.30 = (bf16[256,512]{1,0:T(8,128)(2,1)S(1)}, bf16[256,512]{1,0:T(8,128)(2,1)}, u32[]{:S(2)}) copy-start(bf16[256,512]{1,0:T(8,128)(2,1)} %copy-done.29) | copy-start | bytes 786436
  175.7 19.3 %collective-permute-start.34 = (bf16[640,384]{1,0:T(8,128)(2,1)S(1)}, bf16[640,384]{1,0:T(8,128)(2,1)S(1)}, u32[]{:S(2)}, u32[]{:S(2)}) collective-permute-start(bf16[640,384]{1,0:T(8,128)(2,1)S(1)} %shard_map.160.refs_0_), channel_id=1, source_target_pairs={{0,8},{4,12},{8,0},{12,4},{1,9},{5,13},{9,1},{13,5},{2,10},{6,14},... | collective-permute-start | bytes 1474568 | tf_op jit(solution)/shard_map/ppermute | solution.py:42
  189.7 6.0 %collective-permute-start.37 = (bf16[640,256]{1,0:T(8,128)(2,1)S(1)}, bf16[640,256]{1,0:T(8,128)(2,1)S(1)}, u32[]{:S(2)}, u32[]{:S(2)}) collective-permute-start(bf16[640,256]{1,0:T(8,128)(2,1)S(1)} %shard_map.161.refs_4_), channel_id=1, source_target_pairs={{0,8},{4,12},{8,0},{12,4},{1,9},{5,13},{9,1},{13,5},{2,10},{6,14},... | collective-permute-start | bytes 983048 | tf_op jit(solution)/shard_map/ppermute | solution.py:42
  190.1 11.3 %collective-permute-start.35 = (bf16[640,384]{1,0:T(8,128)(2,1)S(1)}, bf16[640,384]{1,0:T(8,128)(2,1)S(1)}, u32[]{:S(2)}, u32[]{:S(2)}) collective-permute-start(bf16[640,384]{1,0:T(8,128)(2,1)S(1)} %shard_map.160.refs_0_), channel_id=1, source_target_pairs={{0,4},{4,0},{8,12},{12,8},{1,5},{5,1},{9,13},{13,9},{2,6},{6,2},{1... | collective-permute-start | bytes 1474568 | tf_op jit(solution)/shard_map/ppermute | solution.py:42
  195.0 6.5 %collective-permute-start.36 = (bf16[640,384]{1,0:T(8,128)(2,1)S(1)}, bf16[640,384]{1,0:T(8,128)(2,1)S(1)}, u32[]{:S(2)}, u32[]{:S(2)}) collective-permute-start(bf16[640,384]{1,0:T(8,128)(2,1)S(1)} %collective-permute-done.34.refs_1_), channel_id=1, source_target_pairs={{0,4},{4,0},{8,12},{12,8},{1,5},{5,1},{9,13},{13,9},{2,6},{6,2},{1... | collective-permute-start | bytes 1474568 | tf_op jit(solution)/shard_map/ppermute | solution.py:42
  195.0 6.5 %collective-permute-start.38 = (bf16[640,256]{1,0:T(8,128)(2,1)S(1)}, bf16[640,256]{1,0:T(8,128)(2,1)S(1)}, u32[]{:S(2)}, u32[]{:S(2)}) collective-permute-start(bf16[640,256]{1,0:T(8,128)(2,1)S(1)} %shard_map.161.refs_4_), channel_id=1, source_target_pairs={{0,4},{4,0},{8,12},{12,8},{1,5},{5,1},{9,13},{13,9},{2,6},{6,2},{1... | collective-permute-start | bytes 983048 | tf_op jit(solution)/shard_map/ppermute | solution.py:42
  195.7 7.0 %collective-permute-start.39 = (bf16[640,256]{1,0:T(8,128)(2,1)S(1)}, bf16[640,256]{1,0:T(8,128)(2,1)S(1)}, u32[]{:S(2)}, u32[]{:S(2)}) collective-permute-start(bf16[640,256]{1,0:T(8,128)(2,1)S(1)} %collective-permute-done.37.refs_5_), channel_id=1, source_target_pairs={{0,4},{4,0},{8,12},{12,8},{1,5},{5,1},{9,13},{13,9},{2,6},{6,2},{1... | collective-permute-start | bytes 983048 | tf_op jit(solution)/shard_map/ppermute | solution.py:42
  (26 other events, 89.8 us)

commit v5 on v4

--- a/solution.py
+++ b/solution.py
@@ -90,14 +90,23 @@
         ).astype(dk_ref.dtype)
 
 
-def hidden_kernel(team, low, gathered, *refs):
+def whole_kernel(low, count, at_ref, *refs):
+    out = refs[-1]
+    n, wide = refs[0].shape[0], out.shape[1]
+    for i in range(count):
+        block = refs[i][:, low : low + wide]
+        if i == count - 1 and len(refs) - 1 > count:
+            block = block + refs[count][:, low : low + wide]
+        out[pl.ds(pl.multiple_of(at_ref[i] * n, 16), n)] = block
+
+
+def hidden_kernel(team, low, gathered, blocks, at_ref, *refs):
     if gathered:
-        count = sum(gathered)
-        pieces, refs, attn_ref = refs[:count], refs[count:-1], refs[-1]
+        pieces, refs, attn_ref = refs[: sum(gathered)], refs[sum(gathered) : -1], refs[-1]
     else:
         attn_ref, refs = refs[0], refs[1:]
-    weight_ref, gain_ref, *rest = refs[: 2 + team]
-    hidden_ref, sent_ref, square_ref = refs[2 + team :]
+    weights, (gain_ref, *rest) = refs[:blocks], refs[blocks : blocks + 1 + team]
+    hidden_ref, sent_ref, square_ref, weight_ref = refs[blocks + 1 + team :]
     n = rest[0].shape[0]
 
     def gather(i):
@@ -118,6 +127,7 @@
 
     for i in range(team // 2 if gathered else 0):
         pl.when(pl.program_id(0) == i)(functools.partial(gather, i))
+    pl.when(pl.program_id(0) == 0)(functools.partial(whole_kernel, low, at_ref.shape[0], at_ref, *weights, weight_ref))
     pair = jnp.dot(attn_ref[...], weight_ref[...], preferred_element_type=jnp.float32)
     for i in range(team // 2):
         pl.when(pl.program_id(0) == i)(functools.partial(finish, i))
@@ -202,6 +212,39 @@
         out[...] = total[:, i * n : (i + 1) * n]
 
 
+def part_kernel(wide, places, member_ref, *refs):
+    pieces, out, (wide_ref, sems) = refs[: len(places)], refs[-3], refs[-2:]
+    copies = []
+    for i, (ref, (other, low)) in enumerate(zip(pieces, places)):
+        n = ref.shape[1]
+        wide_ref[i, :, :n] = ref[...].astype(wide_ref.dtype)
+        at = pl.multiple_of((member_ref[0] ^ other) * wide + low, LANES)
+        copies.append(pltpu.make_async_copy(wide_ref.at[i, :, pl.ds(0, n)], out.at[:, pl.ds(at, n)], sems.at[i]))
+        copies[-1].start()
+    for copy in copies:
+        copy.wait()
+
+
+def put_parts(pieces, places, wide, width, member, into):
+    rows, n = pieces[0].shape
+    shape = jax.ShapeDtypeStruct((rows, width), jnp.float32)
+    given = 1 + len(pieces)
+    return pl.pallas_call(
+        functools.partial(part_kernel, wide, places),
+        grid_spec=pltpu.PrefetchScalarGridSpec(
+            num_scalar_prefetch=1,
+            grid=(1,),
+            in_specs=[spec(p.shape, lambda i, *_: (0, 0), p.shape) for p in pieces] + [ANY] * len(into),
+            out_specs=ANY,
+            scratch_shapes=[pltpu.VMEM((len(pieces), rows, n), jnp.float32), pltpu.SemaphoreType.DMA((len(pieces),))],
+        ),
+        out_shape=shape,
+        input_output_aliases={given: 0} if into else {},
+        cost_estimate=cost(2.0),
+        compiler_params=pltpu.CompilerParams(vmem_limit_bytes=32 * MIB),
+    )(member.reshape(1), *pieces, *into)
+
+
 def assemble_kernel(wide, places, member_ref, *refs):
     for ref, (other, low) in zip(refs[:-1], places):
         at = pl.multiple_of((member_ref[0] ^ other) * wide + low, LANES)
@@ -211,7 +254,7 @@
 ANY = pl.BlockSpec(memory_space=pl.ANY)
 
 
-def small_call(kernel, indices, ins, outs, into=None, micros=1.0, grid=1, scratch=()):
+def small_call(kernel, indices, ins, outs, into=None, micros=1.0, grid=1, scratch=(), most=False):
     out = pl.pallas_call(
         kernel,
         grid_spec=pltpu.PrefetchScalarGridSpec(
@@ -224,7 +267,7 @@
         out_shape=[jax.ShapeDtypeStruct(shape, d) for shape, d, _, _ in outs],
         input_output_aliases={} if into is None else {1 + len(ins): 0},
         cost_estimate=cost(micros),
-        compiler_params=room(ins, outs),
+        compiler_params=pltpu.CompilerParams(vmem_limit_bytes=60 * MIB) if most else room(ins, outs),
     )(jnp.stack([jnp.int32(i) for i in indices]), *[a for a, _, _ in ins], *(() if into is None else (into,)))
     return out
 
@@ -276,6 +319,23 @@
         column = (column + ref.shape[1]) % refs[-1].shape[1]
 
 
+def pairs_kernel(at_ref, *refs):
+    n, row, column = refs[0].shape[0], 0, 0
+    for ref in refs[:-1]:
+        refs[-1][row : row + n, column : column + ref.shape[1]] = ref[...]
+        column += ref.shape[1]
+        if column == refs[-1].shape[1]:
+            row, column = row + n, 0
+
+
+def stack_pairs(pairs):
+    pieces = [x for pair in pairs for x in pair]
+    n, width = pieces[0].shape[0], sum(x.shape[1] for x in pairs[0]) // 2
+    shape = (2 * n * len(pairs), width)
+    ins = [(x, x.shape, ORIGIN) for x in pieces]
+    return small_call(pairs_kernel, [0], ins, [(shape, pieces[0].dtype, shape, ORIGIN)])[0]
+
+
 def stack_blocks(rows):
     n = rows[0][0].shape[0]
     shape = (n * len(rows), sum(x.shape[1] for x in rows[0]))
@@ -283,16 +343,6 @@
     ins = [(x, x.shape, ORIGIN) for x in pieces]
     kernel = functools.partial(stack_kernel, len(rows[0]))
     return small_call(kernel, [0], ins, [(shape, pieces[0].dtype, shape, ORIGIN)])[0]
-
-
-def whole_kernel(low, count, at_ref, *refs):
-    out = refs[-1]
-    n, wide = refs[0].shape[0], out.shape[1]
-    for i in range(count):
-        block = refs[i][:, low : low + wide]
-        if i == count - 1 and len(refs) - 1 > count:
-            block = block + refs[count][:, low : low + wide]
-        out[pl.ds(pl.multiple_of(at_ref[i] * n, 16), n)] = block
 
 
 def add_kernel(low, at_ref, *refs):
@@ -421,7 +471,7 @@
     cuts = list(zip(ends[:-1], ends[1:]))
     q, k, v = queries[0, 0], keys[0, 0], values[0, 0]
 
-    row_at = lambda i: (i, 0)
+    row_at = lambda i, *_: (i, 0)
     fixed = lambda i, *_: (0, 0)
     fixed3 = lambda i, *_: (0, 0, 0)
     stat_at = lambda i, *_: (i, 0, 0)
@@ -434,7 +484,7 @@
 
     column = (w_out[0], (shard_rows, wide), lambda i, at: (0, at[0]))
     if wide % LANES == 0:
-        (block,) = small_call(copy_kernel, [member], [column], [((shard_rows, wide), bf16, (shard_rows, wide), ORIGIN)])
+        (block,) = small_call(copy_kernel, [member], [column], [((shard_rows, wide), bf16, (shard_rows, wide), ORIGIN)], most=True)
     else:
         (block,) = cut_columns(w_out[0], [member * wide], [wide])
     others = [1, 2] if line else list(range(1, parts))
@@ -464,8 +514,8 @@
     else:
         for bit in reversed(bits[:-1]):
             pairs = pairs + [[swap(x, "dp", bit) for x in pair] for pair in pairs]
-    each = [len(pair) for pair in pairs]
-    pairs = [x for pair in pairs for x in pair]
+    pairs = [stack_pairs(pairs)]
+    each = []
     if team == 4:
         here, beside, across = mine
         across = swap(across, "dp", 2)
@@ -474,14 +524,11 @@
     else:
         rest = [swap(piece, "dp", s) if s else piece for s, piece in zip(order, mine)]
     tied = tie(*last, *pairs, *rest)
-    last, pairs, rest = split(tied, len(last), len(pairs))
+    last, (attn,), rest = split(tied, len(last), 1)
     spots = [part, *[part ^ s for s in others], *([part ^ 3] if line else [])]
     shapes = [(heads_width, n) for n in sizes]
 
-    def whole_weight(i, first):
-        ins = [(b, b.shape, fixed) for b in [first, *came, *last]]
-        kernel = functools.partial(whole_kernel, lows[i], len(spots))
-        return small_call(kernel, spots, ins, [(shapes[i], bf16, shapes[i], fixed)], micros=2.0)[0]
+    used = [block, *came, *last]
 
     def team_sum(value):
         shape = value.shape
@@ -500,25 +547,21 @@
         rest_blocks = [(rest[0], fixed), (rest[1], fixed), (rest[2], fixed), (rest[2], lower)]
     hidden, sent, square, partner, weights = [], [], [], [], []
     for i, n in enumerate(sizes):
-        first = block
+        first = used
         if i:
-            first, square[0] = tie(block, square[0])
-        weights.append(whole_weight(i, first))
-        ins = [(a, a.shape, fixed) for a in (weights[i], gains[i])] + [(a, (seq, wide), m) for a, m in rest_blocks]
+            square[0], *first = tie(square[0], *used)
+        ins = [(a, a.shape, fixed) for a in (*first, gains[i])] + [(a, (seq, wide), m) for a, m in rest_blocks]
         outs = [
             ((rows, n), f32, (2 * seq, n), row_at),
             ((rows, n), bf16, (2 * seq, n), row_at),
             ((team, 1, seq), f32, (2, 1, seq), stat_at),
+            (shapes[i], bf16, shapes[i], fixed),
         ]
         whole = ((rows, heads_width), bf16, (2 * seq, heads_width), row_at)
-        if i:
-            ins = [(attn, whole[2], row_at), *ins]
-        else:
-            ins = [(a, a.shape, fixed) for a in pairs] + ins
-            outs.append(whole)
-        kernel = functools.partial(hidden_kernel, team, lows[i], [] if i else each)
-        h, x, sq, *new = call(2.0, kernel, (team // 2,), ins, outs)
-        attn = new[0] if new else attn
+        ins = [(attn, whole[2], row_at), *ins]
+        kernel = functools.partial(hidden_kernel, team, lows[i], [] if i else each, len(used))
+        h, x, sq, weight, *new = small_call(kernel, spots, ins, outs, micros=2.0, grid=team // 2)
+        weights.append(weight)
         if i + 1 < len(chunks):
             partner.append(swap(x, "copy", 1))
         hidden.append(h)
@@ -612,14 +655,15 @@
     folded = [fold(near[each * first : each * final], far[each * first : each * final]) for first, final in cuts]
     kept, passed = zip(*folded)
     passed = [swap(passed[0], "dp", bits[-1]), *passed[1:]]
-    tied = tie(*early, *terms, *kept, *passed)
-    early, terms, kept, passed, _ = split(tied, len(early), len(back_chunks), len(cuts), len(cuts))
+    near_terms = [take_rows(x, 0, shard_rows) for x in terms] if line else []
+    tied = tie(*early, *terms, *kept, *passed, *near_terms)
+    early, terms, kept, passed, near_terms = split(tied, len(early), len(back_chunks), len(cuts), len(cuts))
 
     def late_sends(i):
         if not line:
             return []
         beyond = sum_terms([early[1]], back_lows[i], terms[i], 1)
-        return [swap(beyond, "fsdp", 2), swap(take_rows(terms[i], 0, shard_rows), "fsdp", 1)]
+        return [swap(beyond, "fsdp", 2), swap(near_terms[i], "fsdp", 1)]
 
     def team_pieces(i, got):
         got = early[:1] + got if line else early
@@ -639,8 +683,10 @@
     passed = [passed[0], *[swap(x, "dp", bits[-1]) for x in passed[1:]]]
     grads = back(0, ())
     early_parts = passed
-    tied = tie(*got, *grads, *terms, *early, loss, *early_parts)
-    got, grads, terms, early, (loss,), early_parts = split(tied, len(got), 3, len(back_chunks), len(early), 1)
+    tied = tie(*got, *grads, *terms, *early, *near_terms, loss, *early_parts)
+    got, grads, terms, early, near_terms, (loss,), early_parts = split(
+        tied, len(got), 3, len(back_chunks), len(early), len(near_terms), 1
+    )
     passed = [*early_parts, *passed[len(early_parts) :]]
 
     placed = []
@@ -659,7 +705,12 @@
     d_queries, d_keys, d_values = grads
     places = [(s, low) for low in back_lows for s in order]
 
-    if wide % LANES == 0:
+    if two:
+        out = ()
+        for i in range(0, len(placed), team):
+            out = (put_parts(placed[i : i + team], places[i : i + team], wide, width, member, out),)
+        (out,) = out
+    elif wide % LANES == 0:
         tall = next(t for t in (128, 64, 32, 16, shard_rows) if shard_rows % t == 0)
         out = pl.pallas_call(
             functools.partial(assemble_kernel, wide, places),

time: 208 us -> 199 us (0.957)
  waiting for transfers between devices: 66.3 us -> 61 us
  starting transfers between devices: 51.4 us -> 46.4 us
    pallas_call x16 -> x17, Pallas kernels: 22.2 us -> 31.8 us  [small_call(): pl.pallas_call(kernel, grid_spec=pltpu.PrefetchScalarGridSpec(num_scalar_...]
    pallas_call x13 -> x11, Pallas kernels: 19 us -> 10.8 us  [call(): pl.pallas_call(kernel, grid=grid, in_specs=[spec(b, m, a.shape) for a, b,...]
    ppermute x36, starting transfers between devices: 46.3 us -> 41.4 us  [swap(): lax.ppermute(value, axis, [(i, i ^ bit) for i in range(lax.axis_size(axis...]
    ppermute x4, waiting for transfers between devices: 10.7 us -> 6.39 us  [send(): return lax.ppermute(value, axis, pairs)]
    unnamed x68 -> x70, local copies, waits for them, and re-layouts: 9.92 us -> 8.89 us
  transfers between devices with their start and end apart: 40 -> 40, of which waited for: 12 -> 11; matrix products, arithmetic and copies ran while one was open for 2% -> 2% of each run, Pallas kernels for 25% -> 30%
where the time goes in v5:
time: 199 us; the launch traced here: 198 us
  Pallas kernels  74 us (37%)
  waiting for transfers between devices  61 us (31%)
  starting transfers between devices  46.4 us (23%)
  local copies, waits for them, and re-layouts  9.5 us (5%)
  other arithmetic  3.68 us (2%)
  between operations  3.63 us (2%)
    ppermute x36, waiting for transfers between devices, swap(): lax.ppermute(value, axis, [(i, i ^ bit) for i in range(lax.axis_size(axis...  54.7 us
    ppermute x36, starting transfers between devices, swap(): lax.ppermute(value, axis, [(i, i ^ bit) for i in range(lax.axis_size(axis...  41.4 us
    pallas_call x17, Pallas kernels, small_call(): pl.pallas_call(kernel, grid_spec=pltpu.PrefetchScalarGridSpec(num_scalar_...  31.8 us
    pallas_call x5, Pallas kernels, attention_call(): pl.pallas_call(kernel, grid_spec=pltpu.PrefetchScalarGridSpec(num_scalar_...  27.9 us
    pallas_call x11, Pallas kernels, call(): pl.pallas_call(kernel, grid=grid, in_specs=[spec(b, m, a.shape) for a, b,...  10.8 us
    unnamed x70, local copies, waits for them, and re-layouts  8.89 us
    ppermute x4, waiting for transfers between devices, send(): return lax.ppermute(value, axis, pairs)  6.39 us
    ppermute x4, starting transfers between devices, send(): return lax.ppermute(value, axis, pairs)  5.07 us
  transfers between devices with their start and end apart: 40, of which 11 were waited for; matrix products, arithmetic and copies ran while one was open for 2% of the time, Pallas kernels for 30%

profile of v5, /device:TPU:1, one launch (start us, length us, event | category | flops | bytes accessed | tf_op | source)
XLA Modules:
  0.0 198.3 jit_solution(17699741047302614777)
XLA Ops:
  0.7 2.3 %shard_map.128.refs_1_ = bf16[640,640]{1,0:T(8,128)(2,1)} custom-call(s32[1]{0:T(128)} %bitcast.1.at_ref.member_ref, bf16[640,2560]{1,0:T(8,128)(2,1)} %bitcast.61), custom_call_target="tpu_custom_call" | custom-call | bytes 1048576 | tf_op jit(solution)/shard_map/pallas_call | solution.py:258
  2.9 3.1 %collective-permute-start.1 = (bf16[640,640]{1,0:T(8,128)(2,1)}, bf16[640,640]{1,0:T(8,128)(2,1)}, u32[]{:S(2)}, u32[]{:S(2)}) collective-permute-start(bf16[640,640]{1,0:T(8,128)(2,1)} %shard_map.128.refs_1_), channel_id=1, source_target_pairs={{0,2},{1,3},{2,0},{3,1},{4,6},{5,7},{6,4},{7,5},{8,10},{9,11},{10,... | collective-permute-start | bytes 2457608 | tf_op jit(solution)/shard_map/ppermute | solution.py:42
  6.1 1.3 collective-permute-start
  8.0 1.3 copy-done.4
  9.3 4.2 %shard_map.130.refs_1_ = bf16[256,1536]{1,0:T(8,128)(2,1)S(1)} custom-call(s32[1]{0:T(128)} %dynamic_slice.6.length_ref, bf16[256,2560]{1,0:T(8,128)(2,1)S(1)} %bitcast.35, bf16[256,2560]{1,0:T(8,128)(2,1)S(1)} %bitcast.40, bf16[256,2560]{1,0:T(8,128)(2,1)S(1)} %bitcast.45), custom_call_target="tpu_custom_call" | custom-call | bytes 4718592 | tf_op jit(solution)/shard_map/pallas_call | solution.py:405
  13.6 1.3 collective-permute-start.3
  14.9 3.8 %shard_map.129.refs_0_ = bf16[256,1024]{1,0:T(8,128)(2,1)} custom-call(s32[1]{0:T(128)} %dynamic_slice.6.length_ref, bf16[256,2560]{1,0:T(8,128)(2,1)S(1)} %bitcast.36, bf16[256,2560]{1,0:T(8,128)(2,1)S(1)} %bitcast.41, bf16[256,2560]{1,0:T(8,128)(2,1)S(1)} %bitcast.46), custom_call_target="tpu_custom_call" | custom-call | bytes 3145728 | tf_op jit(solution)/shard_map/pallas_call | solution.py:405
  20.2 2.3 %shard_map.131 = bf16[256,2560]{1,0:T(8,128)(2,1)} custom-call(s32[1]{0:T(128)} %constant.13.clone.1.at_ref, bf16[256,1024]{1,0:T(8,128)(2,1)} %shard_map.129.refs_0_, bf16[256,1536]{1,0:T(8,128)(2,1)S(1)} %shard_map.130.refs_1_), custom_call_target="tpu_custom_call" | custom-call | bytes 1048576 | tf_op jit(solution)/shard_map/pallas_call | solution.py:258
  23.3 19.5 %collective-permute-done.2.refs_2_ = bf16[256,1024]{1,0:T(8,128)(2,1)} collective-permute-done((bf16[256,1024]{1,0:T(8,128)(2,1)}, bf16[256,1024]{1,0:T(8,128)(2,1)}, u32[]{:S(2)}, u32[]{:S(2)}) %collective-permute-start.2) | collective-permute-done | bytes 524320 | tf_op jit(solution)/shard_map/ppermute | solution.py:42
  42.8 1.3 collective-permute-start.9
  44.1 2.4 %collective-permute-start.6 = (bf16[256,2560]{1,0:T(8,128)(2,1)}, bf16[256,2560]{1,0:T(8,128)(2,1)}, u32[]{:S(2)}, u32[]{:S(2)}) collective-permute-start(bf16[256,2560]{1,0:T(8,128)(2,1)} %shard_map.131), channel_id=1, source_target_pairs={{0,4},{4,0},{8,12},{12,8},{1,5},{5,1},{9,13},{13,9},{2,6},{6,2},{1... | collective-permute-start | bytes 3932168 | tf_op jit(solution)/shard_map/ppermute | solution.py:42
  46.5 1.6 collective-permute-start.4
  48.1 1.3 collective-permute-start.5
  49.4 7.7 %collective-permute-done.9.in_ref.refs_8_ = bf16[512,640]{1,0:T(8,128)(2,1)S(1)} collective-permute-done((bf16[512,640]{1,0:T(8,128)(2,1)S(1)}, bf16[512,640]{1,0:T(8,128)(2,1)S(1)}, u32[]{:S(2)}, u32[]{:S(2)}) %collective-permute-start.9) | collective-permute-done | bytes 655392 | tf_op jit(solution)/shard_map/ppermute | solution.py:42
  57.0 3.0 %collective-permute-start.8 = (bf16[256,1536]{1,0:T(8,128)(2,1)}, bf16[256,1536]{1,0:T(8,128)(2,1)}, u32[]{:S(2)}, u32[]{:S(2)}) collective-permute-start(bf16[256,1536]{1,0:T(8,128)(2,1)} %collective-permute-done.3.refs_3_), channel_id=1, source_target_pairs={{0,4},{4,0},{8,12},{12,8},{1,5},{5,1},{9,13},{13,9},{2,6},{6,2},{1... | collective-permute-start | bytes 2359304 | tf_op jit(solution)/shard_map/ppermute | solution.py:42
  64.9 2.5 %shard_map.134.refs_0_.attn_ref = bf16[1024,2560]{1,0:T(8,128)(2,1)S(1)} custom-call(s32[1]{0:T(128)} %constant.13.clone.1.at_ref, bf16[256,1024]{1,0:T(8,128)(2,1)} %shard_map.129.refs_0_, bf16[256,1536]{1,0:T(8,128)(2,1)S(1)} %copy-done.12, bf16[256,1024]{1,0:T(8,128)(2,1)} %collective-permute-done.2.refs_2_, ...), custom_call_target="tpu_custom_call" | custom-call | bytes 1048576 | tf_op jit(solution)/shard_map/pallas_call | solution.py:258
  67.4 2.2 %collective-permute-done.5.refs_5_ = bf16[640,640]{1,0:T(8,128)(2,1)} collective-permute-done((bf16[640,640]{1,0:T(8,128)(2,1)}, bf16[640,640]{1,0:T(8,128)(2,1)}, u32[]{:S(2)}, u32[]{:S(2)}) %collective-permute-start.5) | collective-permute-done | bytes 819232 | tf_op jit(solution)/shard_map/ppermute | solution.py:438
  69.6 4.9 %shard_map.137 = (f32[1024,256]{1,0:T(8,128)S(1)}, bf16[1024,256]{1,0:T(8,128)(2,1)S(1)}, f32[4,1,256]{2,1,0:T(1,128)S(1)}, bf16[2560,256]{1,0:T(8,128)(2,1)S(1)}) custom-call(s32[4]{0:T(128)S(1)} %pad_add_fusion.1.at_ref, bf16[1024,2560]{1,0:T(8,128)(2,1)S(1)} %shard_map.134.refs_0_.attn_ref, bf16[640,640]{1,0:T(8,128)(2,1)} %shard_map.128.refs_1_, ...), custom_call_target="tpu_custom_call" | custom-call | bytes 2097152 | tf_op jit(solution)/shard_map/pallas_call | solution.py:258
  74.5 1.3 collective-permute-start.16
  75.8 6.5 %shard_map.138 = (f32[1024,384]{1,0:T(8,128)S(1)}, bf16[1024,384]{1,0:T(8,128)(2,1)S(1)}, f32[4,1,256]{2,1,0:T(1,128)S(1)}, bf16[2560,384]{1,0:T(8,128)(2,1)S(1)}) custom-call(s32[4]{0:T(128)S(1)} %pad_add_fusion.1.at_ref, bf16[1024,2560]{1,0:T(8,128)(2,1)S(1)} %shard_map.134.refs_0_.attn_ref, bf16[640,640]{1,0:T(8,128)(2,1)} %shard_map.128.refs_1_, ...), custom_call_target="tpu_custom_call" | custom-call | bytes 2097152 | tf_op jit(solution)/shard_map/pallas_call | solution.py:258
  82.6 1.9 collective-permute-start.11
  86.4 1.3 collective-permute-start.12
  89.8 1.3 collective-permute-start.13
  91.1 12.5 %collective-permute-done.13.other_ref = f32[4,1,256]{2,1,0:T(1,128)S(1)} collective-permute-done((f32[4,1,256]{2,1,0:T(1,128)S(1)}, f32[4,1,256]{2,1,0:T(1,128)S(1)}, u32[]{:S(2)}, u32[]{:S(2)}) %collective-permute-start.13) | collective-permute-done | bytes 4128 | tf_op jit(solution)/shard_map/ppermute | solution.py:42
  103.6 1.7 shard_map.139.refs_0_
  105.3 1.9 shard_map.140
  107.2 2.3 %collective-permute-start.18 = (f32[2,2,2,256]{3,2,1,0:T(2,128)S(1)}, f32[2,2,2,256]{3,2,1,0:T(2,128)S(1)}, u32[]{:S(2)}, u32[]{:S(2)}) collective-permute-start(f32[2,2,2,256]{3,2,1,0:T(2,128)S(1)} %bitcast.55), channel_id=1, source_target_pairs={{0,4},{4,0},{8,12},{12,8},{1,5},{5,1},{9,13},{13,9},{2,6},{6,2},{1... | collective-permute-start | bytes 24584 | tf_op jit(solution)/shard_map/ppermute | solution.py:42
  110.6 2.2 %collective-permute-done.19 = f32[2,2,2,256]{3,2,1,0:T(2,128)S(1)} collective-permute-done((f32[2,2,2,256]{3,2,1,0:T(2,128)S(1)}, f32[2,2,2,256]{3,2,1,0:T(2,128)S(1)}, u32[]{:S(2)}, u32[]{:S(2)}) %collective-permute-start.19) | collective-permute-done | bytes 8224 | tf_op jit(solution)/shard_map/ppermute | solution.py:42
  112.9 3.6 %shard_map.141 = (bf16[1024,640]{1,0:T(8,128)(2,1)S(1)}, bf16[640,640]{1,0:T(8,128)(2,1)S(1)}) custom-call(s32[1]{0:T(128)} %bitcast.at_ref, bf16[1024,2560]{1,0:T(8,128)(2,1)S(1)} %shard_map.134.refs_0_.attn_ref, f32[4,1,256]{2,1,0:T(1,128)S(1)} %bitcast.54, f32[4,1,256]{2,1,0:T(1,128)S(1)} %collective-permute-done.13.other_ref, ...), custom_call_target="tpu_custom_call" | custom-call | bytes 4194304 | tf_op jit(solution)/shard_map/pallas_call | solution.py:258
  117.4 1.6 collective-permute-start.22
  120.2 1.3 collective-permute-start.21
  127.3 4.6 %shard_map.142 = (bf16[1920,384]{1,0:T(8,128)(2,1)S(1)}, bf16[1920,256]{1,0:T(8,128)(2,1)S(1)}) custom-call(s32[3]{0:T(128)S(1)} %pad_add_fusion.2.at_ref, bf16[1024,2560]{1,0:T(8,128)(2,1)S(1)} %shard_map.134.refs_0_.attn_ref, bf16[1024,640]{1,0:T(8,128)(2,1)S(1)} %get-tuple-element.141.d_ref), custom_call_target="tpu_custom_call" | custom-call | bytes 4194304 | tf_op jit(solution)/shard_map/pallas_call | solution.py:258
  135.0 4.2 %collective-permute-done.21.refs_0_ = bf16[640,640]{1,0:T(8,128)(2,1)S(1)} collective-permute-done((bf16[640,640]{1,0:T(8,128)(2,1)S(1)}, bf16[640,640]{1,0:T(8,128)(2,1)S(1)}, u32[]{:S(2)}, u32[]{:S(2)}) %collective-permute-start.21) | collective-permute-done | bytes 819232 | tf_op jit(solution)/shard_map/ppermute | solution.py:438
  140.5 3.5 %collective-permute-start.28 = (bf16[640,384]{1,0:T(8,128)(2,1)}, bf16[640,384]{1,0:T(8,128)(2,1)}, u32[]{:S(2)}, u32[]{:S(2)}) collective-permute-start(bf16[640,384]{1,0:T(8,128)(2,1)} %shard_map.154), channel_id=1, source_target_pairs={{0,2},{1,3},{2,0},{3,1},{4,6},{5,7},{6,4},{7,5},{8,10},{9,11},{10,... | collective-permute-start | bytes 1474568 | tf_op jit(solution)/shard_map/ppermute | solution.py:42
  145.2 1.2 fusion.2
  147.1 1.3 copy-done.5
  150.5 7.0 %shard_map.155 = (bf16[256,2560]{1,0:T(8,128)(2,1)}, bf16[256,2560]{1,0:T(8,128)(2,1)}, bf16[256,2560]{1,0:T(8,128)(2,1)}) custom-call(s32[1]{0:T(128)} %dynamic_slice.6.length_ref, bf16[256,2560]{1,0:T(8,128)(2,1)S(1)} %bitcast.37, bf16[256,2560]{1,0:T(8,128)(2,1)S(1)} %bitcast.42, bf16[256,2560]{1,0:T(8,128)(2,1)S(1)} %bitcast.47, ...), custom_call_target="tpu_custom_call" | custom-call | bytes 4194304 | tf_op jit(solution)/shard_map/pallas_call | solution.py:405
  158.0 7.3 %collective-permute-done.28.refs_1_ = bf16[640,384]{1,0:T(8,128)(2,1)} collective-permute-done((bf16[640,384]{1,0:T(8,128)(2,1)}, bf16[640,384]{1,0:T(8,128)(2,1)}, u32[]{:S(2)}, u32[]{:S(2)}) %collective-permute-start.28) | collective-permute-done | bytes 491552 | tf_op jit(solution)/shard_map/ppermute | solution.py:42
  165.4 2.0 %collective-permute-start.32 = (bf16[640,256]{1,0:T(8,128)(2,1)S(1)}, bf16[640,256]{1,0:T(8,128)(2,1)S(1)}, u32[]{:S(2)}, u32[]{:S(2)}) collective-permute-start(bf16[640,256]{1,0:T(8,128)(2,1)S(1)} %shard_map.156), channel_id=1, source_target_pairs={{0,2},{1,3},{2,0},{3,1},{4,6},{5,7},{6,4},{7,5},{8,10},{9,11},{10,... | collective-permute-start | bytes 983048 | tf_op jit(solution)/shard_map/ppermute | solution.py:42
  167.6 1.5 shard_map.160.refs_0_
  169.1 1.3 collective-permute-start.37
  170.4 7.7 %shard_map.157 = (bf16[256,2560]{1,0:T(8,128)(2,1)}, bf16[256,2560]{1,0:T(8,128)(2,1)}, bf16[256,2560]{1,0:T(8,128)(2,1)}) custom-call(s32[1]{0:T(128)} %dynamic_slice.6.length_ref, bf16[256,2560]{1,0:T(8,128)(2,1)S(1)} %bitcast.38, bf16[256,2560]{1,0:T(8,128)(2,1)S(1)} %bitcast.43, ...), custom_call_target="tpu_custom_call", output_to_operand_aliasing={{0}: (6, {}), {1}: (7, {}), {2}: (8, {})} | custom-call | bytes 4194304 | tf_op jit(solution)/shard_map/pallas_call | solution.py:405
  178.1 5.1 %shard_map.158 = (bf16[256,2560]{1,0:T(8,128)(2,1)}, bf16[256,2560]{1,0:T(8,128)(2,1)}, bf16[256,2560]{1,0:T(8,128)(2,1)}) custom-call(s32[1]{0:T(128)} %dynamic_slice.6.length_ref, bf16[256,2560]{1,0:T(8,128)(2,1)S(1)} %bitcast.39, bf16[256,2560]{1,0:T(8,128)(2,1)S(1)} %bitcast.44, ...), custom_call_target="tpu_custom_call", output_to_operand_aliasing={{0}: (6, {}), {1}: (7, {}), {2}: (8, {})} | custom-call | bytes 2621440 | tf_op jit(solution)/shard_map/pallas_call | solution.py:405
  183.7 2.9 %collective-permute-start.38 = (bf16[640,384]{1,0:T(8,128)(2,1)S(1)}, bf16[640,384]{1,0:T(8,128)(2,1)S(1)}, u32[]{:S(2)}, u32[]{:S(2)}) collective-permute-start(bf16[640,384]{1,0:T(8,128)(2,1)S(1)} %shard_map.160.refs_0_), channel_id=1, source_target_pairs={{0,4},{4,0},{8,12},{12,8},{1,5},{5,1},{9,13},{13,9},{2,6},{6,2},{1... | collective-permute-start | bytes 1474568 | tf_op jit(solution)/shard_map/ppermute | solution.py:42
  187.1 2.9 %collective-permute-done.34.refs_1_ = bf16[640,256]{1,0:T(8,128)(2,1)S(1)} collective-permute-done((bf16[640,256]{1,0:T(8,128)(2,1)S(1)}, bf16[640,256]{1,0:T(8,128)(2,1)S(1)}, u32[]{:S(2)}, u32[]{:S(2)}) %collective-permute-start.34) | collective-permute-done | bytes 327712 | tf_op jit(solution)/shard_map/ppermute | solution.py:42
  190.0 3.5 %collective-permute-start.36 = (bf16[640,256]{1,0:T(8,128)(2,1)S(1)}, bf16[640,256]{1,0:T(8,128)(2,1)S(1)}, u32[]{:S(2)}, u32[]{:S(2)}) collective-permute-start(bf16[640,256]{1,0:T(8,128)(2,1)S(1)} %collective-permute-done.34.refs_1_), channel_id=1, source_target_pairs={{0,4},{4,0},{8,12},{12,8},{1,5},{5,1},{9,13},{13,9},{2,6},{6,2},{1... | collective-permute-start | bytes 983048 | tf_op jit(solution)/shard_map/ppermute | solution.py:42
  193.6 2.0 %shard_map.161.refs_4_ = f32[640,2560]{1,0:T(8,128)} custom-call(s32[1]{0:T(128)} %bitcast.1.at_ref.member_ref, bf16[640,384]{1,0:T(8,128)(2,1)S(1)} %shard_map.160.refs_0_, bf16[640,384]{1,0:T(8,128)(2,1)S(1)} %collective-permute-done.37.refs_1_, bf16[640,384]{1,0:T(8,128)(2,1)S(1)} %collective-permute-done.38.refs_2_, ...), custom_call_target="tpu_custom_call" | custom-call | bytes 2097152 | tf_op jit(solution)/shard_map/pallas_call | solution.py:232
  195.6 1.6 shard_map.162
  (156 shorter events, 29.7 us)
Async XLA Ops:
  0.6 62.0 %copy-start = (f32[1,2560]{1,0:T(1,128)S(1)}, f32[1,2560]{1,0:T(1,128)}, u32[]{:S(2)}) copy-start(f32[1,2560]{1,0:T(1,128)} %param.17) | copy-start | bytes 30724
  2.9 39.8 %collective-permute-start.1 = (bf16[640,640]{1,0:T(8,128)(2,1)}, bf16[640,640]{1,0:T(8,128)(2,1)}, u32[]{:S(2)}, u32[]{:S(2)}) collective-permute-start(bf16[640,640]{1,0:T(8,128)(2,1)} %shard_map.128.refs_1_), channel_id=1, source_target_pairs={{0,2},{1,3},{2,0},{3,1},{4,6},{5,7},{6,4},{7,5},{8,10},{9,11},{10,... | collective-permute-start | bytes 2457608 | tf_op jit(solution)/shard_map/ppermute | solution.py:42
  6.1 36.7 %collective-permute-start = (bf16[640,640]{1,0:T(8,128)(2,1)}, bf16[640,640]{1,0:T(8,128)(2,1)}, u32[]{:S(2)}, u32[]{:S(2)}) collective-permute-start(bf16[640,640]{1,0:T(8,128)(2,1)} %shard_map.128.refs_1_), channel_id=1, source_target_pairs={{0,1},{1,0},{2,3},{3,2},{4,5},{5,4},{6,7},{7,6},{8,9},{9,8},{10,11... | collective-permute-start | bytes 2457608 | tf_op jit(solution)/shard_map/ppermute | solution.py:42
  13.6 29.2 %collective-permute-start.3 = (bf16[256,1536]{1,0:T(8,128)(2,1)S(1)}, bf16[256,1536]{1,0:T(8,128)(2,1)}, u32[]{:S(2)}, u32[]{:S(2)}) collective-permute-start(bf16[256,1536]{1,0:T(8,128)(2,1)S(1)} %shard_map.130.refs_1_), channel_id=1, source_target_pairs={{0,8},{4,12},{8,0},{12,4},{1,9},{5,13},{9,1},{13,5},{2,10},{6,14},... | collective-permute-start | bytes 2359304 | tf_op jit(solution)/shard_map/ppermute | solution.py:42
  18.6 24.1 %collective-permute-start.2 = (bf16[256,1024]{1,0:T(8,128)(2,1)}, bf16[256,1024]{1,0:T(8,128)(2,1)}, u32[]{:S(2)}, u32[]{:S(2)}) collective-permute-start(bf16[256,1024]{1,0:T(8,128)(2,1)} %shard_map.129.refs_0_), channel_id=1, source_target_pairs={{0,8},{4,12},{8,0},{12,4},{1,9},{5,13},{9,1},{13,5},{2,10},{6,14},... | collective-permute-start | bytes 1572872 | tf_op jit(solution)/shard_map/ppermute | solution.py:42
  23.2 38.6 %copy-start.17 = (bf16[256,640]{1,0:T(8,128)(2,1)}, bf16[256,640]{1,0:T(8,128)(2,1)S(1)}, u32[]{:S(2)}) copy-start(bf16[256,640]{1,0:T(8,128)(2,1)S(1)} %get-tuple-element.121.refs_7_) | copy-start | bytes 983044
  42.8 14.2 %collective-permute-start.9 = (bf16[512,640]{1,0:T(8,128)(2,1)S(1)}, bf16[512,640]{1,0:T(8,128)(2,1)S(1)}, u32[]{:S(2)}, u32[]{:S(2)}) collective-permute-start(bf16[512,640]{1,0:T(8,128)(2,1)S(1)} %shard_map.133), channel_id=1, source_target_pairs={{0,8},{4,12},{8,0},{12,4},{1,9},{5,13},{9,1},{13,5},{2,10},{6,14},... | collective-permute-start | bytes 1966088 | tf_op jit(solution)/shard_map/ppermute | solution.py:42
  44.1 18.6 %collective-permute-start.6 = (bf16[256,2560]{1,0:T(8,128)(2,1)}, bf16[256,2560]{1,0:T(8,128)(2,1)}, u32[]{:S(2)}, u32[]{:S(2)}) collective-permute-start(bf16[256,2560]{1,0:T(8,128)(2,1)} %shard_map.131), channel_id=1, source_target_pairs={{0,4},{4,0},{8,12},{12,8},{1,5},{5,1},{9,13},{13,9},{2,6},{6,2},{1... | collective-permute-start | bytes 3932168 | tf_op jit(solution)/shard_map/ppermute | solution.py:42
  46.5 15.3 %collective-permute-start.7 = (bf16[256,1024]{1,0:T(8,128)(2,1)}, bf16[256,1024]{1,0:T(8,128)(2,1)S(1)}, u32[]{:S(2)}, u32[]{:S(2)}) collective-permute-start(bf16[256,1024]{1,0:T(8,128)(2,1)} %collective-permute-done.2.refs_2_), channel_id=1, source_target_pairs={{0,4},{4,0},{8,12},{12,8},{1,5},{5,1},{9,13},{13,9},{2,6},{6,2},{1... | collective-permute-start | bytes 1572872 | tf_op jit(solution)/shard_map/ppermute | solution.py:42
  46.5 20.9 %collective-permute-start.4 = (bf16[640,640]{1,0:T(8,128)(2,1)}, bf16[640,640]{1,0:T(8,128)(2,1)}, u32[]{:S(2)}, u32[]{:S(2)}) collective-permute-start(bf16[640,640]{1,0:T(8,128)(2,1)} %shard_map.128.refs_1_), channel_id=1, source_target_pairs={{1,2},{2,1},{5,6},{6,5},{9,10},{10,9},{13,14},{14,13},{17,18},{18,... | collective-permute-start | bytes 2457608 | tf_op jit(solution)/shard_map/ppermute | solution.py:438
  48.1 21.5 %collective-permute-start.5 = (bf16[640,640]{1,0:T(8,128)(2,1)}, bf16[640,640]{1,0:T(8,128)(2,1)}, u32[]{:S(2)}, u32[]{:S(2)}) collective-permute-start(bf16[640,640]{1,0:T(8,128)(2,1)} %collective-permute-done.1.refs_3_), channel_id=1, source_target_pairs={{2,3},{1,0},{6,7},{5,4},{10,11},{9,8},{14,15},{13,12},{18,19},{17,... | collective-permute-start | bytes 2457608 | tf_op jit(solution)/shard_map/ppermute | solution.py:438
  57.0 5.7 %collective-permute-start.8 = (bf16[256,1536]{1,0:T(8,128)(2,1)}, bf16[256,1536]{1,0:T(8,128)(2,1)}, u32[]{:S(2)}, u32[]{:S(2)}) collective-permute-start(bf16[256,1536]{1,0:T(8,128)(2,1)} %collective-permute-done.3.refs_3_), channel_id=1, source_target_pairs={{0,4},{4,0},{8,12},{12,8},{1,5},{5,1},{9,13},{13,9},{2,6},{6,2},{1... | collective-permute-start | bytes 2359304 | tf_op jit(solution)/shard_map/ppermute | solution.py:42
  62.6 7.0 %collective-permute-start.10 = (bf16[512,640]{1,0:T(8,128)(2,1)}, bf16[512,640]{1,0:T(8,128)(2,1)S(1)}, u32[]{:S(2)}, u32[]{:S(2)}) collective-permute-start(bf16[512,640]{1,0:T(8,128)(2,1)} %shard_map.136), channel_id=1, source_target_pairs={{0,4},{4,0},{8,12},{12,8},{1,5},{5,1},{9,13},{13,9},{2,6},{6,2},{1... | collective-permute-start | bytes 1966088 | tf_op jit(solution)/shard_map/ppermute | solution.py:42
  74.5 10.0 %copy-start.32 = (f32[1024]{0:T(1024)S(1)}, f32[1024]{0:T(1024)}, u32[]{:S(2)}) copy-start(f32[1024]{0:T(1024)} %param.15) | copy-start | bytes 12292
  74.5 10.0 %copy-start.33 = (s32[1,256]{1,0:T(1,128)S(1)}, s32[1,256]{1,0:T(1,128)}, u32[]{:S(2)}) copy-start(s32[1,256]{1,0:T(1,128)} %param.13) | copy-start | bytes 3076
  74.5 29.1 %collective-permute-start.16 = (bf16[1024,256]{1,0:T(8,128)(2,1)S(1)}, bf16[1024,256]{1,0:T(8,128)(2,1)S(1)}, u32[]{:S(2)}, u32[]{:S(2)}) collective-permute-start(bf16[1024,256]{1,0:T(8,128)(2,1)S(1)} %get-tuple-element.137), channel_id=1, source_target_pairs={{0,16},{16,0},{1,17},{17,1},{2,18},{18,2},{3,19},{19,3},{4,20},{20... | collective-permute-start | bytes 1572872 | tf_op jit(solution)/shard_map/ppermute | solution.py:42
  82.3 23.0 %collective-permute-start.17 = (bf16[1024,384]{1,0:T(8,128)(2,1)S(1)}, bf16[1024,384]{1,0:T(8,128)(2,1)S(1)}, u32[]{:S(2)}, u32[]{:S(2)}) collective-permute-start(bf16[1024,384]{1,0:T(8,128)(2,1)S(1)} %get-tuple-element.132), channel_id=1, source_target_pairs={{0,16},{16,0},{1,17},{17,1},{2,18},{18,2},{3,19},{19,3},{4,20},{20... | collective-permute-start | bytes 2359304 | tf_op jit(solution)/shard_map/ppermute | solution.py:42
  82.6 3.8 %collective-permute-start.11 = (f32[2,2,1,256]{3,2,1,0:T(1,128)S(1)}, f32[2,2,1,256]{3,2,1,0:T(1,128)S(1)}, u32[]{:S(2)}, u32[]{:S(2)}) collective-permute-start(f32[2,2,1,256]{3,2,1,0:T(1,128)S(1)} %bitcast.64), channel_id=1, source_target_pairs={{0,4},{4,0},{8,12},{12,8},{1,5},{5,1},{9,13},{13,9},{2,6},{6,2},{1... | collective-permute-start | bytes 12296 | tf_op jit(solution)/shard_map/ppermute | solution.py:42
  86.1 2.8 %collective-permute-start.14 = (f32[1,1,256]{2,1,0:T(1,128)S(1)}, f32[1,1,256]{2,1,0:T(1,128)S(1)}, u32[]{:S(2)}, u32[]{:S(2)}) collective-permute-start(f32[1,1,256]{2,1,0:T(1,128)S(1)} %compare_select_fusion), channel_id=1, source_target_pairs={{0,8},{4,12},{8,0},{12,4},{1,9},{5,13},{9,1},{13,5},{2,10},{6,14},... | collective-permute-start | bytes 3080 | tf_op jit(solution)/shard_map/ppermute | solution.py:42
  86.4 3.3 %collective-permute-start.12 = (f32[2,2,1,256]{3,2,1,0:T(1,128)S(1)}, f32[2,2,1,256]{3,2,1,0:T(1,128)S(1)}, u32[]{:S(2)}, u32[]{:S(2)}) collective-permute-start(f32[2,2,1,256]{3,2,1,0:T(1,128)S(1)} %reverse_add_fusion.2), channel_id=1, source_target_pairs={{0,8},{4,12},{8,0},{12,4},{1,9},{5,13},{9,1},{13,5},{2,10},{6,14},... | collective-permute-start | bytes 12296 | tf_op jit(solution)/shard_map/ppermute | solution.py:42
  88.9 2.2 %collective-permute-start.15 = (f32[2,1,256]{2,1,0:T(1,128)S(1)}, f32[2,1,256]{2,1,0:T(1,128)S(1)}, u32[]{:S(2)}, u32[]{:S(2)}) collective-permute-start(f32[2,1,256]{2,1,0:T(1,128)S(1)} %pad_maximum_fusion), channel_id=1, source_target_pairs={{0,4},{4,0},{8,12},{12,8},{1,5},{5,1},{9,13},{13,9},{2,6},{6,2},{1... | collective-permute-start | bytes 6152 | tf_op jit(solution)/shard_map/ppermute | solution.py:42
  89.8 13.8 %collective-permute-start.13 = (f32[4,1,256]{2,1,0:T(1,128)S(1)}, f32[4,1,256]{2,1,0:T(1,128)S(1)}, u32[]{:S(2)}, u32[]{:S(2)}) collective-permute-start(f32[4,1,256]{2,1,0:T(1,128)S(1)} %bitcast.51), channel_id=1, source_target_pairs={{0,16},{16,0},{1,17},{17,1},{2,18},{18,2},{3,19},{19,3},{4,20},{20... | collective-permute-start | bytes 12296 | tf_op jit(solution)/shard_map/ppermute | solution.py:42
  107.2 3.2 %collective-permute-start.18 = (f32[2,2,2,256]{3,2,1,0:T(2,128)S(1)}, f32[2,2,2,256]{3,2,1,0:T(2,128)S(1)}, u32[]{:S(2)}, u32[]{:S(2)}) collective-permute-start(f32[2,2,2,256]{3,2,1,0:T(2,128)S(1)} %bitcast.55), channel_id=1, source_target_pairs={{0,4},{4,0},{8,12},{12,8},{1,5},{5,1},{9,13},{13,9},{2,6},{6,2},{1... | collective-permute-start | bytes 24584 | tf_op jit(solution)/shard_map/ppermute | solution.py:42
  110.3 2.5 %collective-permute-start.19 = (f32[2,2,2,256]{3,2,1,0:T(2,128)S(1)}, f32[2,2,2,256]{3,2,1,0:T(2,128)S(1)}, u32[]{:S(2)}, u32[]{:S(2)}) collective-permute-start(f32[2,2,2,256]{3,2,1,0:T(2,128)S(1)} %reverse_add_fusion.1), channel_id=1, source_target_pairs={{0,8},{4,12},{8,0},{12,4},{1,9},{5,13},{9,1},{13,5},{2,10},{6,14},... | collective-permute-start | bytes 24584 | tf_op jit(solution)/shard_map/ppermute | solution.py:42
  117.4 7.0 %collective-permute-start.22 = (bf16[512,512]{1,0:T(8,128)(2,1)S(1)}, bf16[512,512]{1,0:T(8,128)(2,1)S(1)}, u32[]{:S(2)}, u32[]{:S(2)}) collective-permute-start(bf16[512,512]{1,0:T(8,128)(2,1)S(1)} %get-tuple-element.148), channel_id=1, source_target_pairs={{0,4},{4,0},{8,12},{12,8},{1,5},{5,1},{9,13},{13,9},{2,6},{6,2},{1... | collective-permute-start | bytes 1572872 | tf_op jit(solution)/shard_map/ppermute | solution.py:42
  119.0 5.8 %collective-permute-start.23 = (bf16[512,512]{1,0:T(8,128)(2,1)S(1)}, bf16[512,512]{1,0:T(8,128)(2,1)S(1)}, u32[]{:S(2)}, u32[]{:S(2)}) collective-permute-start(bf16[512,512]{1,0:T(8,128)(2,1)S(1)} %get-tuple-element.149), channel_id=1, source_target_pairs={{0,4},{4,0},{8,12},{12,8},{1,5},{5,1},{9,13},{13,9},{2,6},{6,2},{1... | collective-permute-start | bytes 1572872 | tf_op jit(solution)/shard_map/ppermute | solution.py:42
  119.7 5.6 %collective-permute-start.26 = (bf16[512,512]{1,0:T(8,128)(2,1)S(1)}, bf16[512,512]{1,0:T(8,128)(2,1)S(1)}, u32[]{:S(2)}, u32[]{:S(2)}) collective-permute-start(bf16[512,512]{1,0:T(8,128)(2,1)S(1)} %shard_map.150), channel_id=1, source_target_pairs={{0,4},{4,0},{8,12},{12,8},{1,5},{5,1},{9,13},{13,9},{2,6},{6,2},{1... | collective-permute-start | bytes 1572872 | tf_op jit(solution)/shard_map/ppermute | solution.py:42
  120.2 19.0 %collective-permute-start.21 = (bf16[640,640]{1,0:T(8,128)(2,1)S(1)}, bf16[640,640]{1,0:T(8,128)(2,1)S(1)}, u32[]{:S(2)}, u32[]{:S(2)}) collective-permute-start(bf16[640,640]{1,0:T(8,128)(2,1)S(1)} %get-tuple-element.140), channel_id=1, source_target_pairs={{0,1},{3,2},{4,5},{7,6},{8,9},{11,10},{12,13},{15,14},{16,17},{19,... | collective-permute-start | bytes 2457608 | tf_op jit(solution)/shard_map/ppermute | solution.py:438
  121.5 17.7 %collective-permute-start.20 = (bf16[640,640]{1,0:T(8,128)(2,1)S(1)}, bf16[640,640]{1,0:T(8,128)(2,1)S(1)}, u32[]{:S(2)}, u32[]{:S(2)}) collective-permute-start(bf16[640,640]{1,0:T(8,128)(2,1)S(1)} %get-tuple-element.140), channel_id=1, source_target_pairs={{1,2},{2,1},{5,6},{6,5},{9,10},{10,9},{13,14},{14,13},{17,18},{18,... | collective-permute-start | bytes 2457608 | tf_op jit(solution)/shard_map/ppermute | solution.py:438
  124.5 9.5 %collective-permute-start.24 = (bf16[512,512]{1,0:T(8,128)(2,1)S(1)}, bf16[512,512]{1,0:T(8,128)(2,1)S(1)}, u32[]{:S(2)}, u32[]{:S(2)}) collective-permute-start(bf16[512,512]{1,0:T(8,128)(2,1)S(1)} %get-tuple-element.153), channel_id=1, source_target_pairs={{0,4},{4,0},{8,12},{12,8},{1,5},{5,1},{9,13},{13,9},{2,6},{6,2},{1... | collective-permute-start | bytes 1572872 | tf_op jit(solution)/shard_map/ppermute | solution.py:42
  124.8 9.2 %collective-permute-start.25 = (bf16[512,512]{1,0:T(8,128)(2,1)S(1)}, bf16[512,512]{1,0:T(8,128)(2,1)S(1)}, u32[]{:S(2)}, u32[]{:S(2)}) collective-permute-start(bf16[512,512]{1,0:T(8,128)(2,1)S(1)} %get-tuple-element.154), channel_id=1, source_target_pairs={{0,4},{4,0},{8,12},{12,8},{1,5},{5,1},{9,13},{13,9},{2,6},{6,2},{1... | collective-permute-start | bytes 1572872 | tf_op jit(solution)/shard_map/ppermute | solution.py:42
  125.3 13.9 %collective-permute-start.27 = (bf16[256,1024]{1,0:T(8,128)(2,1)S(1)}, bf16[256,1024]{1,0:T(8,128)(2,1)S(1)}, u32[]{:S(2)}, u32[]{:S(2)}) collective-permute-start(bf16[256,1024]{1,0:T(8,128)(2,1)S(1)} %get-tuple-element.157), channel_id=1, source_target_pairs={{0,8},{4,12},{8,0},{12,4},{1,9},{5,13},{9,1},{13,5},{2,10},{6,14},... | collective-permute-start | bytes 1572872 | tf_op jit(solution)/shard_map/ppermute | solution.py:42
  139.2 26.1 %collective-permute-start.30 = (bf16[256,1024]{1,0:T(8,128)(2,1)}, bf16[256,1024]{1,0:T(8,128)(2,1)}, u32[]{:S(2)}, u32[]{:S(2)}) collective-permute-start(bf16[256,1024]{1,0:T(8,128)(2,1)} %get-tuple-element.171), channel_id=1, source_target_pairs={{0,8},{4,12},{8,0},{12,4},{1,9},{5,13},{9,1},{13,5},{2,10},{6,14},... | collective-permute-start | bytes 1572872 | tf_op jit(solution)/shard_map/ppermute | solution.py:42
  140.5 24.8 %collective-permute-start.28 = (bf16[640,384]{1,0:T(8,128)(2,1)}, bf16[640,384]{1,0:T(8,128)(2,1)}, u32[]{:S(2)}, u32[]{:S(2)}) collective-permute-start(bf16[640,384]{1,0:T(8,128)(2,1)} %shard_map.154), channel_id=1, source_target_pairs={{0,2},{1,3},{2,0},{3,1},{4,6},{5,7},{6,4},{7,5},{8,10},{9,11},{10,... | collective-permute-start | bytes 1474568 | tf_op jit(solution)/shard_map/ppermute | solution.py:42
  144.0 21.3 %collective-permute-start.29 = (bf16[640,384]{1,0:T(8,128)(2,1)}, bf16[640,384]{1,0:T(8,128)(2,1)}, u32[]{:S(2)}, u32[]{:S(2)}) collective-permute-start(bf16[640,384]{1,0:T(8,128)(2,1)} %shard_map.152), channel_id=1, source_target_pairs={{0,1},{1,0},{2,3},{3,2},{4,5},{5,4},{6,7},{7,6},{8,9},{9,8},{10,11... | collective-permute-start | bytes 1474568 | tf_op jit(solution)/shard_map/ppermute | solution.py:42
  144.0 13.9 %collective-permute-start.31 = (bf16[256,512]{1,0:T(8,128)(2,1)}, bf16[256,512]{1,0:T(8,128)(2,1)}, u32[]{:S(2)}, u32[]{:S(2)}) collective-permute-start(bf16[256,512]{1,0:T(8,128)(2,1)} %get-tuple-element.172), channel_id=1, source_target_pairs={{0,8},{4,12},{8,0},{12,4},{1,9},{5,13},{9,1},{13,5},{2,10},{6,14},... | collective-permute-start | bytes 786440 | tf_op jit(solution)/shard_map/ppermute | solution.py:42
  150.5 14.8 %copy-start.10 = (bf16[1920,256]{1,0:T(8,128)(2,1)S(1)}, bf16[1920,256]{1,0:T(8,128)(2,1)}, u32[]{:S(2)}) copy-start(bf16[1920,256]{1,0:T(8,128)(2,1)} %copy-done.9) | copy-start | bytes 2949124
  150.5 17.1 %copy-start.16 = (bf16[640,640]{1,0:T(8,128)(2,1)S(1)}, bf16[640,640]{1,0:T(8,128)(2,1)}, u32[]{:S(2)}) copy-start(bf16[640,640]{1,0:T(8,128)(2,1)} %copy-done.15) | copy-start | bytes 2457604
  157.6 9.8 %copy-start.29 = (bf16[640,256]{1,0:T(8,128)(2,1)S(1)}, bf16[640,256]{1,0:T(8,128)(2,1)}, u32[]{:S(2)}) copy-start(bf16[640,256]{1,0:T(8,128)(2,1)} %copy-done.28) | copy-start | bytes 983044
  157.6 10.1 %copy-start.8 = (bf16[1920,384]{1,0:T(8,128)(2,1)S(1)}, bf16[1920,384]{1,0:T(8,128)(2,1)}, u32[]{:S(2)}) copy-start(bf16[1920,384]{1,0:T(8,128)(2,1)} %copy-done.7) | copy-start | bytes 4423684
  165.4 17.8 %collective-permute-start.32 = (bf16[640,256]{1,0:T(8,128)(2,1)S(1)}, bf16[640,256]{1,0:T(8,128)(2,1)S(1)}, u32[]{:S(2)}, u32[]{:S(2)}) collective-permute-start(bf16[640,256]{1,0:T(8,128)(2,1)S(1)} %shard_map.156), channel_id=1, source_target_pairs={{0,2},{1,3},{2,0},{3,1},{4,6},{5,7},{6,4},{7,5},{8,10},{9,11},{10,... | collective-permute-start | bytes 983048 | tf_op jit(solution)/shard_map/ppermute | solution.py:42
  167.4 15.8 %collective-permute-start.33 = (bf16[640,256]{1,0:T(8,128)(2,1)S(1)}, bf16[640,256]{1,0:T(8,128)(2,1)S(1)}, u32[]{:S(2)}, u32[]{:S(2)}) collective-permute-start(bf16[640,256]{1,0:T(8,128)(2,1)S(1)} %copy-done.29), channel_id=1, source_target_pairs={{0,1},{1,0},{2,3},{3,2},{4,5},{5,4},{6,7},{7,6},{8,9},{9,8},{10,11... | collective-permute-start | bytes 983048 | tf_op jit(solution)/shard_map/ppermute | solution.py:42
  169.1 17.5 %collective-permute-start.37 = (bf16[640,384]{1,0:T(8,128)(2,1)S(1)}, bf16[640,384]{1,0:T(8,128)(2,1)S(1)}, u32[]{:S(2)}, u32[]{:S(2)}) collective-permute-start(bf16[640,384]{1,0:T(8,128)(2,1)S(1)} %shard_map.160.refs_0_), channel_id=1, source_target_pairs={{0,8},{4,12},{8,0},{12,4},{1,9},{5,13},{9,1},{13,5},{2,10},{6,14},... | collective-permute-start | bytes 1474568 | tf_op jit(solution)/shard_map/ppermute | solution.py:42
  183.4 6.7 %collective-permute-start.34 = (bf16[640,256]{1,0:T(8,128)(2,1)S(1)}, bf16[640,256]{1,0:T(8,128)(2,1)S(1)}, u32[]{:S(2)}, u32[]{:S(2)}) collective-permute-start(bf16[640,256]{1,0:T(8,128)(2,1)S(1)} %shard_map.159.refs_0_), channel_id=1, source_target_pairs={{0,8},{4,12},{8,0},{12,4},{1,9},{5,13},{9,1},{13,5},{2,10},{6,14},... | collective-permute-start | bytes 983048 | tf_op jit(solution)/shard_map/ppermute | solution.py:42
  183.7 9.9 %collective-permute-start.38 = (bf16[640,384]{1,0:T(8,128)(2,1)S(1)}, bf16[640,384]{1,0:T(8,128)(2,1)S(1)}, u32[]{:S(2)}, u32[]{:S(2)}) collective-permute-start(bf16[640,384]{1,0:T(8,128)(2,1)S(1)} %shard_map.160.refs_0_), channel_id=1, source_target_pairs={{0,4},{4,0},{8,12},{12,8},{1,5},{5,1},{9,13},{13,9},{2,6},{6,2},{1... | collective-permute-start | bytes 1474568 | tf_op jit(solution)/shard_map/ppermute | solution.py:42
  186.6 7.0 %collective-permute-start.39 = (bf16[640,384]{1,0:T(8,128)(2,1)S(1)}, bf16[640,384]{1,0:T(8,128)(2,1)S(1)}, u32[]{:S(2)}, u32[]{:S(2)}) collective-permute-start(bf16[640,384]{1,0:T(8,128)(2,1)S(1)} %collective-permute-done.37.refs_1_), channel_id=1, source_target_pairs={{0,4},{4,0},{8,12},{12,8},{1,5},{5,1},{9,13},{13,9},{2,6},{6,2},{1... | collective-permute-start | bytes 1474568 | tf_op jit(solution)/shard_map/ppermute | solution.py:42
  186.6 9.0 %collective-permute-start.35 = (bf16[640,256]{1,0:T(8,128)(2,1)S(1)}, bf16[640,256]{1,0:T(8,128)(2,1)S(1)}, u32[]{:S(2)}, u32[]{:S(2)}) collective-permute-start(bf16[640,256]{1,0:T(8,128)(2,1)S(1)} %shard_map.159.refs_0_), channel_id=1, source_target_pairs={{0,4},{4,0},{8,12},{12,8},{1,5},{5,1},{9,13},{13,9},{2,6},{6,2},{1... | collective-permute-start | bytes 983048 | tf_op jit(solution)/shard_map/ppermute | solution.py:42
  190.0 5.6 %collective-permute-start.36 = (bf16[640,256]{1,0:T(8,128)(2,1)S(1)}, bf16[640,256]{1,0:T(8,128)(2,1)S(1)}, u32[]{:S(2)}, u32[]{:S(2)}) collective-permute-start(bf16[640,256]{1,0:T(8,128)(2,1)S(1)} %collective-permute-done.34.refs_1_), channel_id=1, source_target_pairs={{0,4},{4,0},{8,12},{12,8},{1,5},{5,1},{9,13},{13,9},{2,6},{6,2},{1... | collective-permute-start | bytes 983048 | tf_op jit(solution)/shard_map/ppermute | solution.py:42
  (27 other events, 95.2 us)

commit v6 on v5

--- a/solution.py
+++ b/solution.py
@@ -94,9 +94,9 @@
     out = refs[-1]
     n, wide = refs[0].shape[0], out.shape[1]
     for i in range(count):
-        block = refs[i][:, low : low + wide]
+        block = refs[i][...] if refs[i].shape[1] == wide else refs[i][:, low : low + wide]
         if i == count - 1 and len(refs) - 1 > count:
-            block = block + refs[count][:, low : low + wide]
+            block = block + (refs[count][...] if refs[count].shape[1] == wide else refs[count][:, low : low + wide])
         out[pl.ds(pl.multiple_of(at_ref[i] * n, 16), n)] = block
 
 
@@ -120,7 +120,9 @@
     def finish(i):
         for j in range(2):
             at = slice(j * n, (j + 1) * n)
-            hidden = rest[2 * i + j][:, low : low + pair.shape[1]].astype(jnp.float32) + pair[at]
+            there = rest[2 * i + j]
+            there = there[...] if there.shape[1] == pair.shape[1] else there[:, low : low + pair.shape[1]]
+            hidden = there.astype(jnp.float32) + pair[at]
             hidden_ref[at] = hidden
             sent_ref[at] = (hidden * gain_ref[...]).astype(sent_ref.dtype)
             square_ref[j] = to_lanes(jnp.sum(hidden * hidden, axis=-1, keepdims=True))
@@ -467,7 +469,7 @@
     f32, bf16 = jnp.float32, jnp.bfloat16
     group = group_width(heads_width)
     steps = heads_width // group
-    ends = sorted({0, 2 * steps // 5, 4 * steps // 5, steps})
+    ends = sorted({0, steps // 5, 3 * steps // 5, steps})
     cuts = list(zip(ends[:-1], ends[1:]))
     q, k, v = queries[0, 0], keys[0, 0], values[0, 0]
 
@@ -550,7 +552,10 @@
         first = used
         if i:
             square[0], *first = tie(square[0], *used)
-        ins = [(a, a.shape, fixed) for a in (*first, gains[i])] + [(a, (seq, wide), m) for a, m in rest_blocks]
+        narrow = i == 0 and two
+        across = n if narrow else wide
+        ins = [(a, (shard_rows, across) if line else a.shape, fixed) for a in first] + [(gains[i], (1, n), fixed)]
+        ins += [(a, (seq, across), m) for a, m in rest_blocks]
         outs = [
             ((rows, n), f32, (2 * seq, n), row_at),
             ((rows, n), bf16, (2 * seq, n), row_at),
@@ -682,6 +687,9 @@
     got = late_sends(0)
     passed = [passed[0], *[swap(x, "dp", bits[-1]) for x in passed[1:]]]
     grads = back(0, ())
+    backed = max(1, len(cuts) - 1)
+    for j in range(1, backed):
+        grads = back(j, grads)
     early_parts = passed
     tied = tie(*got, *grads, *terms, *early, *near_terms, loss, *early_parts)
     got, grads, terms, early, near_terms, (loss,), early_parts = split(
@@ -694,13 +702,13 @@
         late = late_sends(i)
         placed += team_pieces(i - 1, got)
         if i == 1:
-            for j in range(1, len(cuts)):
+            for j in range(backed, len(cuts)):
                 grads = back(j, grads)
         tied = tie(*late, *grads)
         got, grads, _ = split(tied, len(late), 3)
     placed += team_pieces(len(back_chunks) - 1, got)
     if len(back_chunks) == 1:
-        for j in range(1, len(cuts)):
+        for j in range(backed, len(cuts)):
             grads = back(j, grads)
     d_queries, d_keys, d_values = grads
     places = [(s, low) for low in back_lows for s in order]

time: 199 us -> 197 us (0.990)
  starting transfers between devices: 46.4 us -> 43.7 us
    ppermute x36, starting transfers between devices: 41.4 us -> 38.7 us  [swap(): lax.ppermute(value, axis, [(i, i ^ bit) for i in range(lax.axis_size(axis...]
    ppermute x36, waiting for transfers between devices: 54.7 us -> 57.1 us  [swap(): lax.ppermute(value, axis, [(i, i ^ bit) for i in range(lax.axis_size(axis...]
where the time goes in v6:
time: 197 us; the launch traced here: 196 us
  Pallas kernels  73.2 us (37%)
  waiting for transfers between devices  61.6 us (31%)
  starting transfers between devices  43.7 us (22%)
  local copies, waits for them, and re-layouts  10.1 us (5%)
  other arithmetic  3.68 us (2%)
  between operations  3.61 us (2%)
    ppermute x36, waiting for transfers between devices, swap(): lax.ppermute(value, axis, [(i, i ^ bit) for i in range(lax.axis_size(axis...  57.1 us
    ppermute x36, starting transfers between devices, swap(): lax.ppermute(value, axis, [(i, i ^ bit) for i in range(lax.axis_size(axis...  38.7 us
    pallas_call x17, Pallas kernels, small_call(): pl.pallas_call(kernel, grid_spec=pltpu.PrefetchScalarGridSpec(num_scalar_...  31 us
    pallas_call x5, Pallas kernels, attention_call(): pl.pallas_call(kernel, grid_spec=pltpu.PrefetchScalarGridSpec(num_scalar_...  27.8 us
    pallas_call x11, Pallas kernels, call(): pl.pallas_call(kernel, grid=grid, in_specs=[spec(b, m, a.shape) for a, b,...  10.8 us
    unnamed x70, local copies, waits for them, and re-layouts  9.51 us
    ppermute x4, starting transfers between devices, send(): return lax.ppermute(value, axis, pairs)  5.07 us
    ppermute x4, waiting for transfers between devices, send(): return lax.ppermute(value, axis, pairs)  4.41 us
  transfers between devices with their start and end apart: 40, of which 11 were waited for; matrix products, arithmetic and copies ran while one was open for 2% of the time, Pallas kernels for 30%

profile of v6, /device:TPU:1, one launch (start us, length us, event | category | flops | bytes accessed | tf_op | source)
XLA Modules:
  0.0 195.9 jit_solution(13461415057816435511)
XLA Ops:
  0.7 2.3 %shard_map.128.refs_1_ = bf16[640,640]{1,0:T(8,128)(2,1)} custom-call(s32[1]{0:T(128)} %bitcast.1.at_ref.member_ref, bf16[640,2560]{1,0:T(8,128)(2,1)} %bitcast.61), custom_call_target="tpu_custom_call" | custom-call | bytes 1048576 | tf_op jit(solution)/shard_map/pallas_call | solution.py:260
  2.9 3.1 %collective-permute-start.1 = (bf16[640,640]{1,0:T(8,128)(2,1)}, bf16[640,640]{1,0:T(8,128)(2,1)}, u32[]{:S(2)}, u32[]{:S(2)}) collective-permute-start(bf16[640,640]{1,0:T(8,128)(2,1)} %shard_map.128.refs_1_), channel_id=1, source_target_pairs={{0,2},{1,3},{2,0},{3,1},{4,6},{5,7},{6,4},{7,5},{8,10},{9,11},{10,... | collective-permute-start | bytes 2457608 | tf_op jit(solution)/shard_map/ppermute | solution.py:42
  6.1 1.3 collective-permute-start
  8.0 1.3 copy-done.4
  9.3 4.2 %shard_map.130.refs_1_ = bf16[256,1536]{1,0:T(8,128)(2,1)S(1)} custom-call(s32[1]{0:T(128)} %dynamic_slice.6.length_ref, bf16[256,2560]{1,0:T(8,128)(2,1)S(1)} %bitcast.35, bf16[256,2560]{1,0:T(8,128)(2,1)S(1)} %bitcast.40, bf16[256,2560]{1,0:T(8,128)(2,1)S(1)} %bitcast.45), custom_call_target="tpu_custom_call" | custom-call | bytes 4718592 | tf_op jit(solution)/shard_map/pallas_call | solution.py:407
  13.6 1.3 collective-permute-start.3
  14.9 3.8 %shard_map.129.refs_0_ = bf16[256,1024]{1,0:T(8,128)(2,1)} custom-call(s32[1]{0:T(128)} %dynamic_slice.6.length_ref, bf16[256,2560]{1,0:T(8,128)(2,1)S(1)} %bitcast.36, bf16[256,2560]{1,0:T(8,128)(2,1)S(1)} %bitcast.41, bf16[256,2560]{1,0:T(8,128)(2,1)S(1)} %bitcast.46), custom_call_target="tpu_custom_call" | custom-call | bytes 3145728 | tf_op jit(solution)/shard_map/pallas_call | solution.py:407
  20.2 2.3 %shard_map.131 = bf16[256,2560]{1,0:T(8,128)(2,1)} custom-call(s32[1]{0:T(128)} %constant.13.clone.1.at_ref, bf16[256,1024]{1,0:T(8,128)(2,1)} %shard_map.129.refs_0_, bf16[256,1536]{1,0:T(8,128)(2,1)S(1)} %shard_map.130.refs_1_), custom_call_target="tpu_custom_call" | custom-call | bytes 1048576 | tf_op jit(solution)/shard_map/pallas_call | solution.py:260
  23.3 19.5 %collective-permute-done.2.refs_2_ = bf16[256,1024]{1,0:T(8,128)(2,1)} collective-permute-done((bf16[256,1024]{1,0:T(8,128)(2,1)}, bf16[256,1024]{1,0:T(8,128)(2,1)}, u32[]{:S(2)}, u32[]{:S(2)}) %collective-permute-start.2) | collective-permute-done | bytes 524320 | tf_op jit(solution)/shard_map/ppermute | solution.py:42
  42.8 1.3 collective-permute-start.9
  44.1 2.4 %collective-permute-start.6 = (bf16[256,2560]{1,0:T(8,128)(2,1)}, bf16[256,2560]{1,0:T(8,128)(2,1)}, u32[]{:S(2)}, u32[]{:S(2)}) collective-permute-start(bf16[256,2560]{1,0:T(8,128)(2,1)} %shard_map.131), channel_id=1, source_target_pairs={{0,4},{4,0},{8,12},{12,8},{1,5},{5,1},{9,13},{13,9},{2,6},{6,2},{1... | collective-permute-start | bytes 3932168 | tf_op jit(solution)/shard_map/ppermute | solution.py:42
  46.5 1.6 collective-permute-start.4
  48.1 1.3 collective-permute-start.5
  49.4 7.7 %collective-permute-done.9.in_ref.refs_8_ = bf16[512,640]{1,0:T(8,128)(2,1)S(1)} collective-permute-done((bf16[512,640]{1,0:T(8,128)(2,1)S(1)}, bf16[512,640]{1,0:T(8,128)(2,1)S(1)}, u32[]{:S(2)}, u32[]{:S(2)}) %collective-permute-start.9) | collective-permute-done | bytes 655392 | tf_op jit(solution)/shard_map/ppermute | solution.py:42
  57.0 3.0 %collective-permute-start.8 = (bf16[256,1536]{1,0:T(8,128)(2,1)}, bf16[256,1536]{1,0:T(8,128)(2,1)}, u32[]{:S(2)}, u32[]{:S(2)}) collective-permute-start(bf16[256,1536]{1,0:T(8,128)(2,1)} %collective-permute-done.3.refs_3_), channel_id=1, source_target_pairs={{0,4},{4,0},{8,12},{12,8},{1,5},{5,1},{9,13},{13,9},{2,6},{6,2},{1... | collective-permute-start | bytes 2359304 | tf_op jit(solution)/shard_map/ppermute | solution.py:42
  64.9 2.5 %shard_map.134.refs_0_.attn_ref = bf16[1024,2560]{1,0:T(8,128)(2,1)S(1)} custom-call(s32[1]{0:T(128)} %constant.13.clone.1.at_ref, bf16[256,1024]{1,0:T(8,128)(2,1)} %shard_map.129.refs_0_, bf16[256,1536]{1,0:T(8,128)(2,1)S(1)} %copy-done.12, bf16[256,1024]{1,0:T(8,128)(2,1)} %collective-permute-done.2.refs_2_, ...), custom_call_target="tpu_custom_call" | custom-call | bytes 1048576 | tf_op jit(solution)/shard_map/pallas_call | solution.py:260
  67.4 2.2 %collective-permute-done.5.refs_5_ = bf16[640,640]{1,0:T(8,128)(2,1)} collective-permute-done((bf16[640,640]{1,0:T(8,128)(2,1)}, bf16[640,640]{1,0:T(8,128)(2,1)}, u32[]{:S(2)}, u32[]{:S(2)}) %collective-permute-start.5) | collective-permute-done | bytes 819232 | tf_op jit(solution)/shard_map/ppermute | solution.py:440
  69.6 4.2 %shard_map.137 = (f32[1024,256]{1,0:T(8,128)S(1)}, bf16[1024,256]{1,0:T(8,128)(2,1)S(1)}, f32[4,1,256]{2,1,0:T(1,128)S(1)}, bf16[2560,256]{1,0:T(8,128)(2,1)S(1)}) custom-call(s32[4]{0:T(128)S(1)} %pad_add_fusion.1.at_ref, bf16[1024,2560]{1,0:T(8,128)(2,1)S(1)} %shard_map.134.refs_0_.attn_ref, bf16[640,640]{1,0:T(8,128)(2,1)} %shard_map.128.refs_1_, ...), custom_call_target="tpu_custom_call" | custom-call | bytes 2097152 | tf_op jit(solution)/shard_map/pallas_call | solution.py:260
  73.8 1.3 collective-permute-start.16
  75.1 6.5 %shard_map.138 = (f32[1024,384]{1,0:T(8,128)S(1)}, bf16[1024,384]{1,0:T(8,128)(2,1)S(1)}, f32[4,1,256]{2,1,0:T(1,128)S(1)}, bf16[2560,384]{1,0:T(8,128)(2,1)S(1)}) custom-call(s32[4]{0:T(128)S(1)} %pad_add_fusion.1.at_ref, bf16[1024,2560]{1,0:T(8,128)(2,1)S(1)} %shard_map.134.refs_0_.attn_ref, bf16[640,640]{1,0:T(8,128)(2,1)} %shard_map.128.refs_1_, ...), custom_call_target="tpu_custom_call" | custom-call | bytes 2097152 | tf_op jit(solution)/shard_map/pallas_call | solution.py:260
  81.9 1.9 collective-permute-start.11
  85.7 1.3 collective-permute-start.12
  89.0 1.3 collective-permute-start.13
  90.3 12.5 %collective-permute-done.13.other_ref = f32[4,1,256]{2,1,0:T(1,128)S(1)} collective-permute-done((f32[4,1,256]{2,1,0:T(1,128)S(1)}, f32[4,1,256]{2,1,0:T(1,128)S(1)}, u32[]{:S(2)}, u32[]{:S(2)}) %collective-permute-start.13) | collective-permute-done | bytes 4128 | tf_op jit(solution)/shard_map/ppermute | solution.py:42
  102.9 1.7 shard_map.139.refs_0_
  104.6 1.9 shard_map.140
  106.4 2.3 %collective-permute-start.18 = (f32[2,2,2,256]{3,2,1,0:T(2,128)S(1)}, f32[2,2,2,256]{3,2,1,0:T(2,128)S(1)}, u32[]{:S(2)}, u32[]{:S(2)}) collective-permute-start(f32[2,2,2,256]{3,2,1,0:T(2,128)S(1)} %bitcast.55), channel_id=1, source_target_pairs={{0,4},{4,0},{8,12},{12,8},{1,5},{5,1},{9,13},{13,9},{2,6},{6,2},{1... | collective-permute-start | bytes 24584 | tf_op jit(solution)/shard_map/ppermute | solution.py:42
  109.9 2.2 %collective-permute-done.19 = f32[2,2,2,256]{3,2,1,0:T(2,128)S(1)} collective-permute-done((f32[2,2,2,256]{3,2,1,0:T(2,128)S(1)}, f32[2,2,2,256]{3,2,1,0:T(2,128)S(1)}, u32[]{:S(2)}, u32[]{:S(2)}) %collective-permute-start.19) | collective-permute-done | bytes 8224 | tf_op jit(solution)/shard_map/ppermute | solution.py:42
  112.1 3.6 %shard_map.141 = (bf16[1024,640]{1,0:T(8,128)(2,1)S(1)}, bf16[640,640]{1,0:T(8,128)(2,1)S(1)}) custom-call(s32[1]{0:T(128)} %bitcast.at_ref, bf16[1024,2560]{1,0:T(8,128)(2,1)S(1)} %shard_map.134.refs_0_.attn_ref, f32[4,1,256]{2,1,0:T(1,128)S(1)} %bitcast.54, f32[4,1,256]{2,1,0:T(1,128)S(1)} %collective-permute-done.13.other_ref, ...), custom_call_target="tpu_custom_call" | custom-call | bytes 4194304 | tf_op jit(solution)/shard_map/pallas_call | solution.py:260
  116.3 1.6 collective-permute-start.26
  119.0 1.3 collective-permute-start.21
  126.6 4.6 %shard_map.142 = (bf16[1920,384]{1,0:T(8,128)(2,1)S(1)}, bf16[1920,256]{1,0:T(8,128)(2,1)S(1)}) custom-call(s32[3]{0:T(128)S(1)} %pad_add_fusion.2.at_ref, bf16[1024,2560]{1,0:T(8,128)(2,1)S(1)} %shard_map.134.refs_0_.attn_ref, bf16[1024,640]{1,0:T(8,128)(2,1)S(1)} %get-tuple-element.140.d_ref), custom_call_target="tpu_custom_call" | custom-call | bytes 4194304 | tf_op jit(solution)/shard_map/pallas_call | solution.py:260
  135.3 2.2 %collective-permute-done.21.refs_0_ = bf16[640,640]{1,0:T(8,128)(2,1)S(1)} collective-permute-done((bf16[640,640]{1,0:T(8,128)(2,1)S(1)}, bf16[640,640]{1,0:T(8,128)(2,1)S(1)}, u32[]{:S(2)}, u32[]{:S(2)}) %collective-permute-start.21) | collective-permute-done | bytes 819232 | tf_op jit(solution)/shard_map/ppermute | solution.py:440
  139.9 3.5 %collective-permute-start.28 = (bf16[640,384]{1,0:T(8,128)(2,1)}, bf16[640,384]{1,0:T(8,128)(2,1)}, u32[]{:S(2)}, u32[]{:S(2)}) collective-permute-start(bf16[640,384]{1,0:T(8,128)(2,1)} %shard_map.154), channel_id=1, source_target_pairs={{0,2},{1,3},{2,0},{3,1},{4,6},{5,7},{6,4},{7,5},{8,10},{9,11},{10,... | collective-permute-start | bytes 1474568 | tf_op jit(solution)/shard_map/ppermute | solution.py:42
  143.4 1.2 fusion.2
  145.3 1.3 copy-done.5
  148.5 4.1 %shard_map.155 = (bf16[256,2560]{1,0:T(8,128)(2,1)}, bf16[256,2560]{1,0:T(8,128)(2,1)}, bf16[256,2560]{1,0:T(8,128)(2,1)}) custom-call(s32[1]{0:T(128)} %dynamic_slice.6.length_ref, bf16[256,2560]{1,0:T(8,128)(2,1)S(1)} %bitcast.37, bf16[256,2560]{1,0:T(8,128)(2,1)S(1)} %bitcast.42, bf16[256,2560]{1,0:T(8,128)(2,1)S(1)} %bitcast.47, ...), custom_call_target="tpu_custom_call" | custom-call | bytes 2621440 | tf_op jit(solution)/shard_map/pallas_call | solution.py:407
  152.7 7.9 %shard_map.156 = (bf16[256,2560]{1,0:T(8,128)(2,1)}, bf16[256,2560]{1,0:T(8,128)(2,1)}, bf16[256,2560]{1,0:T(8,128)(2,1)}) custom-call(s32[1]{0:T(128)} %dynamic_slice.6.length_ref, bf16[256,2560]{1,0:T(8,128)(2,1)S(1)} %bitcast.38, bf16[256,2560]{1,0:T(8,128)(2,1)S(1)} %bitcast.43, ...), custom_call_target="tpu_custom_call", output_to_operand_aliasing={{0}: (6, {}), {1}: (7, {}), {2}: (8, {})} | custom-call | bytes 4194304 | tf_op jit(solution)/shard_map/pallas_call | solution.py:407
  160.5 3.4 %collective-permute-done.28.refs_1_ = bf16[640,384]{1,0:T(8,128)(2,1)} collective-permute-done((bf16[640,384]{1,0:T(8,128)(2,1)}, bf16[640,384]{1,0:T(8,128)(2,1)}, u32[]{:S(2)}, u32[]{:S(2)}) %collective-permute-start.28) | collective-permute-done | bytes 491552 | tf_op jit(solution)/shard_map/ppermute | solution.py:42
  164.1 1.9 collective-permute-start.32
  166.8 1.5 shard_map.160.refs_0_
  168.6 7.7 %shard_map.158 = (bf16[256,2560]{1,0:T(8,128)(2,1)}, bf16[256,2560]{1,0:T(8,128)(2,1)}, bf16[256,2560]{1,0:T(8,128)(2,1)}) custom-call(s32[1]{0:T(128)} %dynamic_slice.6.length_ref, bf16[256,2560]{1,0:T(8,128)(2,1)S(1)} %bitcast.39, bf16[256,2560]{1,0:T(8,128)(2,1)S(1)} %bitcast.44, ...), custom_call_target="tpu_custom_call", output_to_operand_aliasing={{0}: (6, {}), {1}: (7, {}), {2}: (8, {})} | custom-call | bytes 4194304 | tf_op jit(solution)/shard_map/pallas_call | solution.py:407
  176.3 4.4 %collective-permute-done.32.refs_1_ = bf16[640,256]{1,0:T(8,128)(2,1)S(1)} collective-permute-done((bf16[640,256]{1,0:T(8,128)(2,1)S(1)}, bf16[640,256]{1,0:T(8,128)(2,1)S(1)}, u32[]{:S(2)}, u32[]{:S(2)}) %collective-permute-start.32) | collective-permute-done | bytes 327712 | tf_op jit(solution)/shard_map/ppermute | solution.py:42
  181.3 1.7 collective-permute-start.38
  183.5 5.2 %collective-permute-done.34.refs_1_ = bf16[640,256]{1,0:T(8,128)(2,1)S(1)} collective-permute-done((bf16[640,256]{1,0:T(8,128)(2,1)S(1)}, bf16[640,256]{1,0:T(8,128)(2,1)S(1)}, u32[]{:S(2)}, u32[]{:S(2)}) %collective-permute-start.34) | collective-permute-done | bytes 327712 | tf_op jit(solution)/shard_map/ppermute | solution.py:42
  188.8 2.4 %collective-permute-start.36 = (bf16[640,256]{1,0:T(8,128)(2,1)S(1)}, bf16[640,256]{1,0:T(8,128)(2,1)S(1)}, u32[]{:S(2)}, u32[]{:S(2)}) collective-permute-start(bf16[640,256]{1,0:T(8,128)(2,1)S(1)} %collective-permute-done.34.refs_1_), channel_id=1, source_target_pairs={{0,4},{4,0},{8,12},{12,8},{1,5},{5,1},{9,13},{13,9},{2,6},{6,2},{1... | collective-permute-start | bytes 983048 | tf_op jit(solution)/shard_map/ppermute | solution.py:42
  191.1 2.0 %shard_map.161.refs_4_ = f32[640,2560]{1,0:T(8,128)} custom-call(s32[1]{0:T(128)} %bitcast.1.at_ref.member_ref, bf16[640,384]{1,0:T(8,128)(2,1)S(1)} %shard_map.160.refs_0_, bf16[640,384]{1,0:T(8,128)(2,1)S(1)} %collective-permute-done.37.refs_1_, bf16[640,384]{1,0:T(8,128)(2,1)S(1)} %collective-permute-done.38.refs_2_, ...), custom_call_target="tpu_custom_call" | custom-call | bytes 2097152 | tf_op jit(solution)/shard_map/pallas_call | solution.py:234
  193.2 1.6 shard_map.162
  (156 shorter events, 31.0 us)
Async XLA Ops:
  0.6 62.0 %copy-start = (f32[1,2560]{1,0:T(1,128)S(1)}, f32[1,2560]{1,0:T(1,128)}, u32[]{:S(2)}) copy-start(f32[1,2560]{1,0:T(1,128)} %param.17) | copy-start | bytes 30724
  0.7 7.3 %copy-start.2 = (bf16[1,1,256,2560]{3,2,1,0:T(8,128)(2,1)S(1)}, bf16[1,1,256,2560]{3,2,1,0:T(8,128)(2,1)}, u32[]{:S(2)}) copy-start(bf16[1,1,256,2560]{3,2,1,0:T(8,128)(2,1)} %param.9) | copy-start | bytes 3932164
  2.9 39.8 %collective-permute-start.1 = (bf16[640,640]{1,0:T(8,128)(2,1)}, bf16[640,640]{1,0:T(8,128)(2,1)}, u32[]{:S(2)}, u32[]{:S(2)}) collective-permute-start(bf16[640,640]{1,0:T(8,128)(2,1)} %shard_map.128.refs_1_), channel_id=1, source_target_pairs={{0,2},{1,3},{2,0},{3,1},{4,6},{5,7},{6,4},{7,5},{8,10},{9,11},{10,... | collective-permute-start | bytes 2457608 | tf_op jit(solution)/shard_map/ppermute | solution.py:42
  6.1 36.7 %collective-permute-start = (bf16[640,640]{1,0:T(8,128)(2,1)}, bf16[640,640]{1,0:T(8,128)(2,1)}, u32[]{:S(2)}, u32[]{:S(2)}) collective-permute-start(bf16[640,640]{1,0:T(8,128)(2,1)} %shard_map.128.refs_1_), channel_id=1, source_target_pairs={{0,1},{1,0},{2,3},{3,2},{4,5},{5,4},{6,7},{7,6},{8,9},{9,8},{10,11... | collective-permute-start | bytes 2457608 | tf_op jit(solution)/shard_map/ppermute | solution.py:42
  13.6 29.2 %collective-permute-start.3 = (bf16[256,1536]{1,0:T(8,128)(2,1)S(1)}, bf16[256,1536]{1,0:T(8,128)(2,1)}, u32[]{:S(2)}, u32[]{:S(2)}) collective-permute-start(bf16[256,1536]{1,0:T(8,128)(2,1)S(1)} %shard_map.130.refs_1_), channel_id=1, source_target_pairs={{0,8},{4,12},{8,0},{12,4},{1,9},{5,13},{9,1},{13,5},{2,10},{6,14},... | collective-permute-start | bytes 2359304 | tf_op jit(solution)/shard_map/ppermute | solution.py:42
  18.6 24.1 %collective-permute-start.2 = (bf16[256,1024]{1,0:T(8,128)(2,1)}, bf16[256,1024]{1,0:T(8,128)(2,1)}, u32[]{:S(2)}, u32[]{:S(2)}) collective-permute-start(bf16[256,1024]{1,0:T(8,128)(2,1)} %shard_map.129.refs_0_), channel_id=1, source_target_pairs={{0,8},{4,12},{8,0},{12,4},{1,9},{5,13},{9,1},{13,5},{2,10},{6,14},... | collective-permute-start | bytes 1572872 | tf_op jit(solution)/shard_map/ppermute | solution.py:42
  23.2 38.6 %copy-start.17 = (bf16[256,640]{1,0:T(8,128)(2,1)}, bf16[256,640]{1,0:T(8,128)(2,1)S(1)}, u32[]{:S(2)}) copy-start(bf16[256,640]{1,0:T(8,128)(2,1)S(1)} %get-tuple-element.120.refs_7_) | copy-start | bytes 983044
  42.8 14.2 %collective-permute-start.9 = (bf16[512,640]{1,0:T(8,128)(2,1)S(1)}, bf16[512,640]{1,0:T(8,128)(2,1)S(1)}, u32[]{:S(2)}, u32[]{:S(2)}) collective-permute-start(bf16[512,640]{1,0:T(8,128)(2,1)S(1)} %shard_map.133), channel_id=1, source_target_pairs={{0,8},{4,12},{8,0},{12,4},{1,9},{5,13},{9,1},{13,5},{2,10},{6,14},... | collective-permute-start | bytes 1966088 | tf_op jit(solution)/shard_map/ppermute | solution.py:42
  44.1 18.6 %collective-permute-start.6 = (bf16[256,2560]{1,0:T(8,128)(2,1)}, bf16[256,2560]{1,0:T(8,128)(2,1)}, u32[]{:S(2)}, u32[]{:S(2)}) collective-permute-start(bf16[256,2560]{1,0:T(8,128)(2,1)} %shard_map.131), channel_id=1, source_target_pairs={{0,4},{4,0},{8,12},{12,8},{1,5},{5,1},{9,13},{13,9},{2,6},{6,2},{1... | collective-permute-start | bytes 3932168 | tf_op jit(solution)/shard_map/ppermute | solution.py:42
  46.5 15.3 %collective-permute-start.7 = (bf16[256,1024]{1,0:T(8,128)(2,1)}, bf16[256,1024]{1,0:T(8,128)(2,1)S(1)}, u32[]{:S(2)}, u32[]{:S(2)}) collective-permute-start(bf16[256,1024]{1,0:T(8,128)(2,1)} %collective-permute-done.2.refs_2_), channel_id=1, source_target_pairs={{0,4},{4,0},{8,12},{12,8},{1,5},{5,1},{9,13},{13,9},{2,6},{6,2},{1... | collective-permute-start | bytes 1572872 | tf_op jit(solution)/shard_map/ppermute | solution.py:42
  46.5 20.9 %collective-permute-start.4 = (bf16[640,640]{1,0:T(8,128)(2,1)}, bf16[640,640]{1,0:T(8,128)(2,1)}, u32[]{:S(2)}, u32[]{:S(2)}) collective-permute-start(bf16[640,640]{1,0:T(8,128)(2,1)} %shard_map.128.refs_1_), channel_id=1, source_target_pairs={{1,2},{2,1},{5,6},{6,5},{9,10},{10,9},{13,14},{14,13},{17,18},{18,... | collective-permute-start | bytes 2457608 | tf_op jit(solution)/shard_map/ppermute | solution.py:440
  48.1 21.5 %collective-permute-start.5 = (bf16[640,640]{1,0:T(8,128)(2,1)}, bf16[640,640]{1,0:T(8,128)(2,1)}, u32[]{:S(2)}, u32[]{:S(2)}) collective-permute-start(bf16[640,640]{1,0:T(8,128)(2,1)} %collective-permute-done.1.refs_3_), channel_id=1, source_target_pairs={{2,3},{1,0},{6,7},{5,4},{10,11},{9,8},{14,15},{13,12},{18,19},{17,... | collective-permute-start | bytes 2457608 | tf_op jit(solution)/shard_map/ppermute | solution.py:440
  57.0 5.7 %collective-permute-start.8 = (bf16[256,1536]{1,0:T(8,128)(2,1)}, bf16[256,1536]{1,0:T(8,128)(2,1)}, u32[]{:S(2)}, u32[]{:S(2)}) collective-permute-start(bf16[256,1536]{1,0:T(8,128)(2,1)} %collective-permute-done.3.refs_3_), channel_id=1, source_target_pairs={{0,4},{4,0},{8,12},{12,8},{1,5},{5,1},{9,13},{13,9},{2,6},{6,2},{1... | collective-permute-start | bytes 2359304 | tf_op jit(solution)/shard_map/ppermute | solution.py:42
  62.6 7.0 %collective-permute-start.10 = (bf16[512,640]{1,0:T(8,128)(2,1)}, bf16[512,640]{1,0:T(8,128)(2,1)S(1)}, u32[]{:S(2)}, u32[]{:S(2)}) collective-permute-start(bf16[512,640]{1,0:T(8,128)(2,1)} %shard_map.136), channel_id=1, source_target_pairs={{0,4},{4,0},{8,12},{12,8},{1,5},{5,1},{9,13},{13,9},{2,6},{6,2},{1... | collective-permute-start | bytes 1966088 | tf_op jit(solution)/shard_map/ppermute | solution.py:42
  73.8 10.0 %copy-start.32 = (f32[1024]{0:T(1024)S(1)}, f32[1024]{0:T(1024)}, u32[]{:S(2)}) copy-start(f32[1024]{0:T(1024)} %param.15) | copy-start | bytes 12292
  73.8 10.0 %copy-start.33 = (s32[1,256]{1,0:T(1,128)S(1)}, s32[1,256]{1,0:T(1,128)}, u32[]{:S(2)}) copy-start(s32[1,256]{1,0:T(1,128)} %param.13) | copy-start | bytes 3076
  73.8 29.1 %collective-permute-start.16 = (bf16[1024,256]{1,0:T(8,128)(2,1)S(1)}, bf16[1024,256]{1,0:T(8,128)(2,1)S(1)}, u32[]{:S(2)}, u32[]{:S(2)}) collective-permute-start(bf16[1024,256]{1,0:T(8,128)(2,1)S(1)} %get-tuple-element.136), channel_id=1, source_target_pairs={{0,16},{16,0},{1,17},{17,1},{2,18},{18,2},{3,19},{19,3},{4,20},{20... | collective-permute-start | bytes 1572872 | tf_op jit(solution)/shard_map/ppermute | solution.py:42
  81.6 23.0 %collective-permute-start.17 = (bf16[1024,384]{1,0:T(8,128)(2,1)S(1)}, bf16[1024,384]{1,0:T(8,128)(2,1)S(1)}, u32[]{:S(2)}, u32[]{:S(2)}) collective-permute-start(bf16[1024,384]{1,0:T(8,128)(2,1)S(1)} %get-tuple-element.131), channel_id=1, source_target_pairs={{0,16},{16,0},{1,17},{17,1},{2,18},{18,2},{3,19},{19,3},{4,20},{20... | collective-permute-start | bytes 2359304 | tf_op jit(solution)/shard_map/ppermute | solution.py:42
  81.9 3.8 %collective-permute-start.11 = (f32[2,2,1,256]{3,2,1,0:T(1,128)S(1)}, f32[2,2,1,256]{3,2,1,0:T(1,128)S(1)}, u32[]{:S(2)}, u32[]{:S(2)}) collective-permute-start(f32[2,2,1,256]{3,2,1,0:T(1,128)S(1)} %bitcast.64), channel_id=1, source_target_pairs={{0,4},{4,0},{8,12},{12,8},{1,5},{5,1},{9,13},{13,9},{2,6},{6,2},{1... | collective-permute-start | bytes 12296 | tf_op jit(solution)/shard_map/ppermute | solution.py:42
  85.3 2.8 %collective-permute-start.14 = (f32[1,1,256]{2,1,0:T(1,128)S(1)}, f32[1,1,256]{2,1,0:T(1,128)S(1)}, u32[]{:S(2)}, u32[]{:S(2)}) collective-permute-start(f32[1,1,256]{2,1,0:T(1,128)S(1)} %compare_select_fusion), channel_id=1, source_target_pairs={{0,8},{4,12},{8,0},{12,4},{1,9},{5,13},{9,1},{13,5},{2,10},{6,14},... | collective-permute-start | bytes 3080 | tf_op jit(solution)/shard_map/ppermute | solution.py:42
  85.7 3.3 %collective-permute-start.12 = (f32[2,2,1,256]{3,2,1,0:T(1,128)S(1)}, f32[2,2,1,256]{3,2,1,0:T(1,128)S(1)}, u32[]{:S(2)}, u32[]{:S(2)}) collective-permute-start(f32[2,2,1,256]{3,2,1,0:T(1,128)S(1)} %reverse_add_fusion.2), channel_id=1, source_target_pairs={{0,8},{4,12},{8,0},{12,4},{1,9},{5,13},{9,1},{13,5},{2,10},{6,14},... | collective-permute-start | bytes 12296 | tf_op jit(solution)/shard_map/ppermute | solution.py:42
  88.1 2.2 %collective-permute-start.15 = (f32[2,1,256]{2,1,0:T(1,128)S(1)}, f32[2,1,256]{2,1,0:T(1,128)S(1)}, u32[]{:S(2)}, u32[]{:S(2)}) collective-permute-start(f32[2,1,256]{2,1,0:T(1,128)S(1)} %pad_maximum_fusion), channel_id=1, source_target_pairs={{0,4},{4,0},{8,12},{12,8},{1,5},{5,1},{9,13},{13,9},{2,6},{6,2},{1... | collective-permute-start | bytes 6152 | tf_op jit(solution)/shard_map/ppermute | solution.py:42
  89.0 13.8 %collective-permute-start.13 = (f32[4,1,256]{2,1,0:T(1,128)S(1)}, f32[4,1,256]{2,1,0:T(1,128)S(1)}, u32[]{:S(2)}, u32[]{:S(2)}) collective-permute-start(f32[4,1,256]{2,1,0:T(1,128)S(1)} %bitcast.51), channel_id=1, source_target_pairs={{0,16},{16,0},{1,17},{17,1},{2,18},{18,2},{3,19},{19,3},{4,20},{20... | collective-permute-start | bytes 12296 | tf_op jit(solution)/shard_map/ppermute | solution.py:42
  106.4 3.2 %collective-permute-start.18 = (f32[2,2,2,256]{3,2,1,0:T(2,128)S(1)}, f32[2,2,2,256]{3,2,1,0:T(2,128)S(1)}, u32[]{:S(2)}, u32[]{:S(2)}) collective-permute-start(f32[2,2,2,256]{3,2,1,0:T(2,128)S(1)} %bitcast.55), channel_id=1, source_target_pairs={{0,4},{4,0},{8,12},{12,8},{1,5},{5,1},{9,13},{13,9},{2,6},{6,2},{1... | collective-permute-start | bytes 24584 | tf_op jit(solution)/shard_map/ppermute | solution.py:42
  109.6 2.5 %collective-permute-start.19 = (f32[2,2,2,256]{3,2,1,0:T(2,128)S(1)}, f32[2,2,2,256]{3,2,1,0:T(2,128)S(1)}, u32[]{:S(2)}, u32[]{:S(2)}) collective-permute-start(f32[2,2,2,256]{3,2,1,0:T(2,128)S(1)} %reverse_add_fusion.1), channel_id=1, source_target_pairs={{0,8},{4,12},{8,0},{12,4},{1,9},{5,13},{9,1},{13,5},{2,10},{6,14},... | collective-permute-start | bytes 24584 | tf_op jit(solution)/shard_map/ppermute | solution.py:42
  116.3 6.6 %collective-permute-start.26 = (bf16[512,512]{1,0:T(8,128)(2,1)S(1)}, bf16[512,512]{1,0:T(8,128)(2,1)S(1)}, u32[]{:S(2)}, u32[]{:S(2)}) collective-permute-start(bf16[512,512]{1,0:T(8,128)(2,1)S(1)} %shard_map.150), channel_id=1, source_target_pairs={{0,4},{4,0},{8,12},{12,8},{1,5},{5,1},{9,13},{13,9},{2,6},{6,2},{1... | collective-permute-start | bytes 1572872 | tf_op jit(solution)/shard_map/ppermute | solution.py:42
  118.9 4.1 %collective-permute-start.22 = (bf16[512,512]{1,0:T(8,128)(2,1)S(1)}, bf16[512,512]{1,0:T(8,128)(2,1)S(1)}, u32[]{:S(2)}, u32[]{:S(2)}) collective-permute-start(bf16[512,512]{1,0:T(8,128)(2,1)S(1)} %get-tuple-element.146), channel_id=1, source_target_pairs={{0,4},{4,0},{8,12},{12,8},{1,5},{5,1},{9,13},{13,9},{2,6},{6,2},{1... | collective-permute-start | bytes 1572872 | tf_op jit(solution)/shard_map/ppermute | solution.py:42
  119.0 18.5 %collective-permute-start.21 = (bf16[640,640]{1,0:T(8,128)(2,1)S(1)}, bf16[640,640]{1,0:T(8,128)(2,1)S(1)}, u32[]{:S(2)}, u32[]{:S(2)}) collective-permute-start(bf16[640,640]{1,0:T(8,128)(2,1)S(1)} %get-tuple-element.139), channel_id=1, source_target_pairs={{0,1},{3,2},{4,5},{7,6},{8,9},{11,10},{12,13},{15,14},{16,17},{19,... | collective-permute-start | bytes 2457608 | tf_op jit(solution)/shard_map/ppermute | solution.py:440
  120.3 17.2 %collective-permute-start.20 = (bf16[640,640]{1,0:T(8,128)(2,1)S(1)}, bf16[640,640]{1,0:T(8,128)(2,1)S(1)}, u32[]{:S(2)}, u32[]{:S(2)}) collective-permute-start(bf16[640,640]{1,0:T(8,128)(2,1)S(1)} %get-tuple-element.139), channel_id=1, source_target_pairs={{1,2},{2,1},{5,6},{6,5},{9,10},{10,9},{13,14},{14,13},{17,18},{18,... | collective-permute-start | bytes 2457608 | tf_op jit(solution)/shard_map/ppermute | solution.py:440
  122.2 2.4 %collective-permute-start.25 = (bf16[512,512]{1,0:T(8,128)(2,1)S(1)}, bf16[512,512]{1,0:T(8,128)(2,1)S(1)}, u32[]{:S(2)}, u32[]{:S(2)}) collective-permute-start(bf16[512,512]{1,0:T(8,128)(2,1)S(1)} %get-tuple-element.154), channel_id=1, source_target_pairs={{0,4},{4,0},{8,12},{12,8},{1,5},{5,1},{9,13},{13,9},{2,6},{6,2},{1... | collective-permute-start | bytes 1572872 | tf_op jit(solution)/shard_map/ppermute | solution.py:42
  122.9 11.4 %collective-permute-start.24 = (bf16[512,512]{1,0:T(8,128)(2,1)S(1)}, bf16[512,512]{1,0:T(8,128)(2,1)S(1)}, u32[]{:S(2)}, u32[]{:S(2)}) collective-permute-start(bf16[512,512]{1,0:T(8,128)(2,1)S(1)} %get-tuple-element.151), channel_id=1, source_target_pairs={{0,4},{4,0},{8,12},{12,8},{1,5},{5,1},{9,13},{13,9},{2,6},{6,2},{1... | collective-permute-start | bytes 1572872 | tf_op jit(solution)/shard_map/ppermute | solution.py:42
  123.0 11.3 %collective-permute-start.23 = (bf16[512,512]{1,0:T(8,128)(2,1)S(1)}, bf16[512,512]{1,0:T(8,128)(2,1)S(1)}, u32[]{:S(2)}, u32[]{:S(2)}) collective-permute-start(bf16[512,512]{1,0:T(8,128)(2,1)S(1)} %get-tuple-element.150), channel_id=1, source_target_pairs={{0,4},{4,0},{8,12},{12,8},{1,5},{5,1},{9,13},{13,9},{2,6},{6,2},{1... | collective-permute-start | bytes 1572872 | tf_op jit(solution)/shard_map/ppermute | solution.py:42
  124.6 10.7 %collective-permute-start.27 = (bf16[256,512]{1,0:T(8,128)(2,1)S(1)}, bf16[256,512]{1,0:T(8,128)(2,1)S(1)}, u32[]{:S(2)}, u32[]{:S(2)}) collective-permute-start(bf16[256,512]{1,0:T(8,128)(2,1)S(1)} %get-tuple-element.156), channel_id=1, source_target_pairs={{0,8},{4,12},{8,0},{12,4},{1,9},{5,13},{9,1},{13,5},{2,10},{6,14},... | collective-permute-start | bytes 786440 | tf_op jit(solution)/shard_map/ppermute | solution.py:42
  131.3 7.7 %copy-start.7 = (bf16[1920,384]{1,0:T(8,128)(2,1)}, bf16[1920,384]{1,0:T(8,128)(2,1)S(1)}, u32[]{:S(2)}) copy-start(bf16[1920,384]{1,0:T(8,128)(2,1)S(1)} %get-tuple-element.196.in_ref.refs_1_.refs_3_) | copy-start | bytes 4423684
  137.5 15.1 %collective-permute-start.30 = (bf16[256,1024]{1,0:T(8,128)(2,1)}, bf16[256,1024]{1,0:T(8,128)(2,1)}, u32[]{:S(2)}, u32[]{:S(2)}) collective-permute-start(bf16[256,1024]{1,0:T(8,128)(2,1)} %get-tuple-element.163), channel_id=1, source_target_pairs={{0,8},{4,12},{8,0},{12,4},{1,9},{5,13},{9,1},{13,5},{2,10},{6,14},... | collective-permute-start | bytes 1572872 | tf_op jit(solution)/shard_map/ppermute | solution.py:42
  137.8 26.2 %collective-permute-start.31 = (bf16[256,1024]{1,0:T(8,128)(2,1)}, bf16[256,1024]{1,0:T(8,128)(2,1)}, u32[]{:S(2)}, u32[]{:S(2)}) collective-permute-start(bf16[256,1024]{1,0:T(8,128)(2,1)} %get-tuple-element.175), channel_id=1, source_target_pairs={{0,8},{4,12},{8,0},{12,4},{1,9},{5,13},{9,1},{13,5},{2,10},{6,14},... | collective-permute-start | bytes 1572872 | tf_op jit(solution)/shard_map/ppermute | solution.py:42
  139.9 24.1 %collective-permute-start.28 = (bf16[640,384]{1,0:T(8,128)(2,1)}, bf16[640,384]{1,0:T(8,128)(2,1)}, u32[]{:S(2)}, u32[]{:S(2)}) collective-permute-start(bf16[640,384]{1,0:T(8,128)(2,1)} %shard_map.154), channel_id=1, source_target_pairs={{0,2},{1,3},{2,0},{3,1},{4,6},{5,7},{6,4},{7,5},{8,10},{9,11},{10,... | collective-permute-start | bytes 1474568 | tf_op jit(solution)/shard_map/ppermute | solution.py:42
  143.4 20.6 %collective-permute-start.29 = (bf16[640,384]{1,0:T(8,128)(2,1)}, bf16[640,384]{1,0:T(8,128)(2,1)}, u32[]{:S(2)}, u32[]{:S(2)}) collective-permute-start(bf16[640,384]{1,0:T(8,128)(2,1)} %shard_map.152), channel_id=1, source_target_pairs={{0,1},{1,0},{2,3},{3,2},{4,5},{5,4},{6,7},{7,6},{8,9},{9,8},{10,11... | collective-permute-start | bytes 1474568 | tf_op jit(solution)/shard_map/ppermute | solution.py:42
  152.6 11.3 %copy-start.10 = (bf16[1920,256]{1,0:T(8,128)(2,1)S(1)}, bf16[1920,256]{1,0:T(8,128)(2,1)}, u32[]{:S(2)}) copy-start(bf16[1920,256]{1,0:T(8,128)(2,1)} %copy-done.9) | copy-start | bytes 2949124
  152.7 14.2 %copy-start.16 = (bf16[640,640]{1,0:T(8,128)(2,1)S(1)}, bf16[640,640]{1,0:T(8,128)(2,1)}, u32[]{:S(2)}) copy-start(bf16[640,640]{1,0:T(8,128)(2,1)} %copy-done.15) | copy-start | bytes 2457604
  164.1 16.7 %collective-permute-start.32 = (bf16[640,256]{1,0:T(8,128)(2,1)S(1)}, bf16[640,256]{1,0:T(8,128)(2,1)S(1)}, u32[]{:S(2)}, u32[]{:S(2)}) collective-permute-start(bf16[640,256]{1,0:T(8,128)(2,1)S(1)} %shard_map.157), channel_id=1, source_target_pairs={{0,2},{1,3},{2,0},{3,1},{4,6},{5,7},{6,4},{7,5},{8,10},{9,11},{10,... | collective-permute-start | bytes 983048 | tf_op jit(solution)/shard_map/ppermute | solution.py:42
  166.0 14.8 %collective-permute-start.33 = (bf16[640,256]{1,0:T(8,128)(2,1)S(1)}, bf16[640,256]{1,0:T(8,128)(2,1)S(1)}, u32[]{:S(2)}, u32[]{:S(2)}) collective-permute-start(bf16[640,256]{1,0:T(8,128)(2,1)S(1)} %copy-done.27), channel_id=1, source_target_pairs={{0,1},{1,0},{2,3},{3,2},{4,5},{5,4},{6,7},{7,6},{8,9},{9,8},{10,11... | collective-permute-start | bytes 983048 | tf_op jit(solution)/shard_map/ppermute | solution.py:42
  168.3 14.7 %collective-permute-start.37 = (bf16[640,384]{1,0:T(8,128)(2,1)S(1)}, bf16[640,384]{1,0:T(8,128)(2,1)S(1)}, u32[]{:S(2)}, u32[]{:S(2)}) collective-permute-start(bf16[640,384]{1,0:T(8,128)(2,1)S(1)} %shard_map.160.refs_0_), channel_id=1, source_target_pairs={{0,8},{4,12},{8,0},{12,4},{1,9},{5,13},{9,1},{13,5},{2,10},{6,14},... | collective-permute-start | bytes 1474568 | tf_op jit(solution)/shard_map/ppermute | solution.py:42
  180.9 7.8 %collective-permute-start.34 = (bf16[640,256]{1,0:T(8,128)(2,1)S(1)}, bf16[640,256]{1,0:T(8,128)(2,1)S(1)}, u32[]{:S(2)}, u32[]{:S(2)}) collective-permute-start(bf16[640,256]{1,0:T(8,128)(2,1)S(1)} %shard_map.159.refs_0_), channel_id=1, source_target_pairs={{0,8},{4,12},{8,0},{12,4},{1,9},{5,13},{9,1},{13,5},{2,10},{6,14},... | collective-permute-start | bytes 983048 | tf_op jit(solution)/shard_map/ppermute | solution.py:42
  181.3 9.8 %collective-permute-start.38 = (bf16[640,384]{1,0:T(8,128)(2,1)S(1)}, bf16[640,384]{1,0:T(8,128)(2,1)S(1)}, u32[]{:S(2)}, u32[]{:S(2)}) collective-permute-start(bf16[640,384]{1,0:T(8,128)(2,1)S(1)} %shard_map.160.refs_0_), channel_id=1, source_target_pairs={{0,4},{4,0},{8,12},{12,8},{1,5},{5,1},{9,13},{13,9},{2,6},{6,2},{1... | collective-permute-start | bytes 1474568 | tf_op jit(solution)/shard_map/ppermute | solution.py:42
  183.0 8.1 %collective-permute-start.39 = (bf16[640,384]{1,0:T(8,128)(2,1)S(1)}, bf16[640,384]{1,0:T(8,128)(2,1)S(1)}, u32[]{:S(2)}, u32[]{:S(2)}) collective-permute-start(bf16[640,384]{1,0:T(8,128)(2,1)S(1)} %collective-permute-done.37.refs_1_), channel_id=1, source_target_pairs={{0,4},{4,0},{8,12},{12,8},{1,5},{5,1},{9,13},{13,9},{2,6},{6,2},{1... | collective-permute-start | bytes 1474568 | tf_op jit(solution)/shard_map/ppermute | solution.py:42
  183.0 10.2 %collective-permute-start.35 = (bf16[640,256]{1,0:T(8,128)(2,1)S(1)}, bf16[640,256]{1,0:T(8,128)(2,1)S(1)}, u32[]{:S(2)}, u32[]{:S(2)}) collective-permute-start(bf16[640,256]{1,0:T(8,128)(2,1)S(1)} %shard_map.159.refs_0_), channel_id=1, source_target_pairs={{0,4},{4,0},{8,12},{12,8},{1,5},{5,1},{9,13},{13,9},{2,6},{6,2},{1... | collective-permute-start | bytes 983048 | tf_op jit(solution)/shard_map/ppermute | solution.py:42
  188.8 4.4 %collective-permute-start.36 = (bf16[640,256]{1,0:T(8,128)(2,1)S(1)}, bf16[640,256]{1,0:T(8,128)(2,1)S(1)}, u32[]{:S(2)}, u32[]{:S(2)}) collective-permute-start(bf16[640,256]{1,0:T(8,128)(2,1)S(1)} %collective-permute-done.34.refs_1_), channel_id=1, source_target_pairs={{0,4},{4,0},{8,12},{12,8},{1,5},{5,1},{9,13},{13,9},{2,6},{6,2},{1... | collective-permute-start | bytes 983048 | tf_op jit(solution)/shard_map/ppermute | solution.py:42
  (27 other events, 83.2 us)

commit v7 on v6

--- a/solution.py
+++ b/solution.py
@@ -649,7 +649,7 @@
 
     def d_attn_parts(half, d_hidden):
         total = heads_width // across
-        parts = [(0, 2), (2, 2), (4, 1)] if total == 5 else [(0, total)]
+        parts = [(i, 1) for i in range(total)]
         return [x for first, count in parts for x in d_attn_rows(half, d_hidden, first, count)]
 
     far = [swap(x, "dp", bits[0]) for x in d_attn_parts(1, d_hidden)]

time: 197 us -> 196 us (level)
    ppermute x4, waiting for transfers between devices: 4.41 us -> 2.15 us  [send(): return lax.ppermute(value, axis, pairs)]
    pallas_call x11 -> x15, Pallas kernels: 10.8 us -> 11.6 us  [call(): pl.pallas_call(kernel, grid=grid, in_specs=[spec(b, m, a.shape) for a, b,...]
  transfers between devices with their start and end apart: 40 -> 40, of which waited for: 11 -> 10; matrix products, arithmetic and copies ran while one was open for 2% -> 2% of each run, Pallas kernels for 30% -> 30%
where the time goes in v7:
time: 196 us
  Pallas kernels  73.6 us (38%)
  waiting for transfers between devices  60.1 us (31%)
  starting transfers between devices  43.3 us (22%)
  local copies, waits for them, and re-layouts  11.5 us (6%)
  between operations  3.64 us (2%)
  other arithmetic  3.46 us (2%)
    ppermute x36, waiting for transfers between devices, swap(): lax.ppermute(value, axis, [(i, i ^ bit) for i in range(lax.axis_size(axis...  57.9 us
    ppermute x36, starting transfers between devices, swap(): lax.ppermute(value, axis, [(i, i ^ bit) for i in range(lax.axis_size(axis...  38.3 us
    pallas_call x17, Pallas kernels, small_call(): pl.pallas_call(kernel, grid_spec=pltpu.PrefetchScalarGridSpec(num_scalar_...  31.1 us
    pallas_call x5, Pallas kernels, attention_call(): pl.pallas_call(kernel, grid_spec=pltpu.PrefetchScalarGridSpec(num_scalar_...  27.4 us
    pallas_call x15, Pallas kernels, call(): pl.pallas_call(kernel, grid=grid, in_specs=[spec(b, m, a.shape) for a, b,...  11.6 us
    unnamed x70, local copies, waits for them, and re-layouts  10.9 us
    ppermute x4, starting transfers between devices, send(): return lax.ppermute(value, axis, pairs)  5.06 us
  transfers between devices with their start and end apart: 40, of which 10 were waited for; matrix products, arithmetic and copies ran while one was open for 2% of the time, Pallas kernels for 30%

profile of v7, /device:TPU:1, one launch (start us, length us, event | category | flops | bytes accessed | tf_op | source)
XLA Modules:
  0.0 195.6 jit_solution(16409326310154190958)
XLA Ops:
  0.7 2.3 %shard_map.128.refs_1_ = bf16[640,640]{1,0:T(8,128)(2,1)} custom-call(s32[1]{0:T(128)} %bitcast.1.at_ref.member_ref, bf16[640,2560]{1,0:T(8,128)(2,1)} %bitcast.61), custom_call_target="tpu_custom_call" | custom-call | bytes 1048576 | tf_op jit(solution)/shard_map/pallas_call | solution.py:260
  2.9 3.1 %collective-permute-start.1 = (bf16[640,640]{1,0:T(8,128)(2,1)}, bf16[640,640]{1,0:T(8,128)(2,1)}, u32[]{:S(2)}, u32[]{:S(2)}) collective-permute-start(bf16[640,640]{1,0:T(8,128)(2,1)} %shard_map.128.refs_1_), channel_id=1, source_target_pairs={{0,2},{1,3},{2,0},{3,1},{4,6},{5,7},{6,4},{7,5},{8,10},{9,11},{10,... | collective-permute-start | bytes 2457608 | tf_op jit(solution)/shard_map/ppermute | solution.py:42
  6.1 1.3 collective-permute-start
  8.0 1.3 copy-done.4
  9.3 4.2 %shard_map.130.refs_1_ = bf16[256,1536]{1,0:T(8,128)(2,1)S(1)} custom-call(s32[1]{0:T(128)} %dynamic_slice.6.length_ref, bf16[256,2560]{1,0:T(8,128)(2,1)S(1)} %bitcast.35, bf16[256,2560]{1,0:T(8,128)(2,1)S(1)} %bitcast.40, bf16[256,2560]{1,0:T(8,128)(2,1)S(1)} %bitcast.45), custom_call_target="tpu_custom_call" | custom-call | bytes 4718592 | tf_op jit(solution)/shard_map/pallas_call | solution.py:407
  13.5 1.3 collective-permute-start.3
  14.8 3.7 %shard_map.129.refs_0_ = bf16[256,1024]{1,0:T(8,128)(2,1)} custom-call(s32[1]{0:T(128)} %dynamic_slice.6.length_ref, bf16[256,2560]{1,0:T(8,128)(2,1)S(1)} %bitcast.36, bf16[256,2560]{1,0:T(8,128)(2,1)S(1)} %bitcast.41, bf16[256,2560]{1,0:T(8,128)(2,1)S(1)} %bitcast.46), custom_call_target="tpu_custom_call" | custom-call | bytes 3145728 | tf_op jit(solution)/shard_map/pallas_call | solution.py:407
  20.0 2.3 %shard_map.131 = bf16[256,2560]{1,0:T(8,128)(2,1)} custom-call(s32[1]{0:T(128)} %constant.13.clone.1.at_ref, bf16[256,1024]{1,0:T(8,128)(2,1)} %shard_map.129.refs_0_, bf16[256,1536]{1,0:T(8,128)(2,1)S(1)} %shard_map.130.refs_1_), custom_call_target="tpu_custom_call" | custom-call | bytes 1048576 | tf_op jit(solution)/shard_map/pallas_call | solution.py:260
  23.1 19.6 %collective-permute-done.2.refs_2_ = bf16[256,1024]{1,0:T(8,128)(2,1)} collective-permute-done((bf16[256,1024]{1,0:T(8,128)(2,1)}, bf16[256,1024]{1,0:T(8,128)(2,1)}, u32[]{:S(2)}, u32[]{:S(2)}) %collective-permute-start.2) | collective-permute-done | bytes 524320 | tf_op jit(solution)/shard_map/ppermute | solution.py:42
  42.7 1.3 collective-permute-start.9
  44.0 2.4 %collective-permute-start.6 = (bf16[256,2560]{1,0:T(8,128)(2,1)}, bf16[256,2560]{1,0:T(8,128)(2,1)}, u32[]{:S(2)}, u32[]{:S(2)}) collective-permute-start(bf16[256,2560]{1,0:T(8,128)(2,1)} %shard_map.131), channel_id=1, source_target_pairs={{0,4},{4,0},{8,12},{12,8},{1,5},{5,1},{9,13},{13,9},{2,6},{6,2},{1... | collective-permute-start | bytes 3932168 | tf_op jit(solution)/shard_map/ppermute | solution.py:42
  46.4 1.5 collective-permute-start.4
  48.0 1.3 collective-permute-start.5
  49.3 7.7 %collective-permute-done.9.in_ref.refs_8_ = bf16[512,640]{1,0:T(8,128)(2,1)S(1)} collective-permute-done((bf16[512,640]{1,0:T(8,128)(2,1)S(1)}, bf16[512,640]{1,0:T(8,128)(2,1)S(1)}, u32[]{:S(2)}, u32[]{:S(2)}) %collective-permute-start.9) | collective-permute-done | bytes 655392 | tf_op jit(solution)/shard_map/ppermute | solution.py:42
  56.9 3.0 %collective-permute-start.8 = (bf16[256,1536]{1,0:T(8,128)(2,1)}, bf16[256,1536]{1,0:T(8,128)(2,1)}, u32[]{:S(2)}, u32[]{:S(2)}) collective-permute-start(bf16[256,1536]{1,0:T(8,128)(2,1)} %collective-permute-done.3.refs_3_), channel_id=1, source_target_pairs={{0,4},{4,0},{8,12},{12,8},{1,5},{5,1},{9,13},{13,9},{2,6},{6,2},{1... | collective-permute-start | bytes 2359304 | tf_op jit(solution)/shard_map/ppermute | solution.py:42
  64.8 2.5 %shard_map.134.refs_0_.attn_ref = bf16[1024,2560]{1,0:T(8,128)(2,1)S(1)} custom-call(s32[1]{0:T(128)} %constant.13.clone.1.at_ref, bf16[256,1024]{1,0:T(8,128)(2,1)} %shard_map.129.refs_0_, bf16[256,1536]{1,0:T(8,128)(2,1)S(1)} %copy-done.12, bf16[256,1024]{1,0:T(8,128)(2,1)} %collective-permute-done.2.refs_2_, ...), custom_call_target="tpu_custom_call" | custom-call | bytes 1048576 | tf_op jit(solution)/shard_map/pallas_call | solution.py:260
  67.3 2.1 %collective-permute-done.5.refs_5_ = bf16[640,640]{1,0:T(8,128)(2,1)} collective-permute-done((bf16[640,640]{1,0:T(8,128)(2,1)}, bf16[640,640]{1,0:T(8,128)(2,1)}, u32[]{:S(2)}, u32[]{:S(2)}) %collective-permute-start.5) | collective-permute-done | bytes 819232 | tf_op jit(solution)/shard_map/ppermute | solution.py:440
  69.5 4.2 %shard_map.137 = (f32[1024,256]{1,0:T(8,128)S(1)}, bf16[1024,256]{1,0:T(8,128)(2,1)S(1)}, f32[4,1,256]{2,1,0:T(1,128)S(1)}, bf16[2560,256]{1,0:T(8,128)(2,1)S(1)}) custom-call(s32[4]{0:T(128)S(1)} %pad_add_fusion.1.at_ref, bf16[1024,2560]{1,0:T(8,128)(2,1)S(1)} %shard_map.134.refs_0_.attn_ref, bf16[640,640]{1,0:T(8,128)(2,1)} %shard_map.128.refs_1_, ...), custom_call_target="tpu_custom_call" | custom-call | bytes 2097152 | tf_op jit(solution)/shard_map/pallas_call | solution.py:260
  73.7 1.3 collective-permute-start.16
  75.0 6.5 %shard_map.138 = (f32[1024,384]{1,0:T(8,128)S(1)}, bf16[1024,384]{1,0:T(8,128)(2,1)S(1)}, f32[4,1,256]{2,1,0:T(1,128)S(1)}, bf16[2560,384]{1,0:T(8,128)(2,1)S(1)}) custom-call(s32[4]{0:T(128)S(1)} %pad_add_fusion.1.at_ref, bf16[1024,2560]{1,0:T(8,128)(2,1)S(1)} %shard_map.134.refs_0_.attn_ref, bf16[640,640]{1,0:T(8,128)(2,1)} %shard_map.128.refs_1_, ...), custom_call_target="tpu_custom_call" | custom-call | bytes 2097152 | tf_op jit(solution)/shard_map/pallas_call | solution.py:260
  81.8 1.9 collective-permute-start.11
  85.4 1.3 collective-permute-start.12
  86.7 1.2 collective-permute-done.14
  88.8 1.3 collective-permute-start.13
  90.1 12.7 %collective-permute-done.13.other_ref = f32[4,1,256]{2,1,0:T(1,128)S(1)} collective-permute-done((f32[4,1,256]{2,1,0:T(1,128)S(1)}, f32[4,1,256]{2,1,0:T(1,128)S(1)}, u32[]{:S(2)}, u32[]{:S(2)}) %collective-permute-start.13) | collective-permute-done | bytes 4128 | tf_op jit(solution)/shard_map/ppermute | solution.py:42
  102.8 1.7 shard_map.139.refs_0_
  104.4 1.9 shard_map.140
  106.3 2.3 %collective-permute-start.18 = (f32[2,2,2,256]{3,2,1,0:T(2,128)S(1)}, f32[2,2,2,256]{3,2,1,0:T(2,128)S(1)}, u32[]{:S(2)}, u32[]{:S(2)}) collective-permute-start(f32[2,2,2,256]{3,2,1,0:T(2,128)S(1)} %bitcast.55), channel_id=1, source_target_pairs={{0,4},{4,0},{8,12},{12,8},{1,5},{5,1},{9,13},{13,9},{2,6},{6,2},{1... | collective-permute-start | bytes 24584 | tf_op jit(solution)/shard_map/ppermute | solution.py:42
  109.7 2.2 %collective-permute-done.19 = f32[2,2,2,256]{3,2,1,0:T(2,128)S(1)} collective-permute-done((f32[2,2,2,256]{3,2,1,0:T(2,128)S(1)}, f32[2,2,2,256]{3,2,1,0:T(2,128)S(1)}, u32[]{:S(2)}, u32[]{:S(2)}) %collective-permute-start.19) | collective-permute-done | bytes 8224 | tf_op jit(solution)/shard_map/ppermute | solution.py:42
  112.0 3.6 %shard_map.141 = (bf16[1024,640]{1,0:T(8,128)(2,1)S(1)}, bf16[640,640]{1,0:T(8,128)(2,1)S(1)}) custom-call(s32[1]{0:T(128)} %bitcast.at_ref, bf16[1024,2560]{1,0:T(8,128)(2,1)S(1)} %shard_map.134.refs_0_.attn_ref, f32[4,1,256]{2,1,0:T(1,128)S(1)} %bitcast.54, f32[4,1,256]{2,1,0:T(1,128)S(1)} %collective-permute-done.13.other_ref, ...), custom_call_target="tpu_custom_call" | custom-call | bytes 4194304 | tf_op jit(solution)/shard_map/pallas_call | solution.py:260
  116.2 1.6 collective-permute-start.22
  118.4 1.3 collective-permute-start.21
  128.0 4.6 %shard_map.142 = (bf16[1920,384]{1,0:T(8,128)(2,1)S(1)}, bf16[1920,256]{1,0:T(8,128)(2,1)S(1)}) custom-call(s32[3]{0:T(128)S(1)} %pad_add_fusion.2.at_ref, bf16[1024,2560]{1,0:T(8,128)(2,1)S(1)} %shard_map.134.refs_0_.attn_ref, bf16[1024,640]{1,0:T(8,128)(2,1)S(1)} %get-tuple-element.132.d_ref), custom_call_target="tpu_custom_call" | custom-call | bytes 4194304 | tf_op jit(solution)/shard_map/pallas_call | solution.py:260
  137.3 1.3 collective-permute-start.30
  139.8 3.1 %collective-permute-start.28 = (bf16[640,384]{1,0:T(8,128)(2,1)}, bf16[640,384]{1,0:T(8,128)(2,1)}, u32[]{:S(2)}, u32[]{:S(2)}) collective-permute-start(bf16[640,384]{1,0:T(8,128)(2,1)} %shard_map.158), channel_id=1, source_target_pairs={{0,2},{1,3},{2,0},{3,1},{4,6},{5,7},{6,4},{7,5},{8,10},{9,11},{10,... | collective-permute-start | bytes 1474568 | tf_op jit(solution)/shard_map/ppermute | solution.py:42
  144.7 1.3 copy-done.5
  148.0 4.1 %shard_map.159 = (bf16[256,2560]{1,0:T(8,128)(2,1)}, bf16[256,2560]{1,0:T(8,128)(2,1)}, bf16[256,2560]{1,0:T(8,128)(2,1)}) custom-call(s32[1]{0:T(128)} %dynamic_slice.6.length_ref, bf16[256,2560]{1,0:T(8,128)(2,1)S(1)} %bitcast.37, bf16[256,2560]{1,0:T(8,128)(2,1)S(1)} %bitcast.42, bf16[256,2560]{1,0:T(8,128)(2,1)S(1)} %bitcast.47, ...), custom_call_target="tpu_custom_call" | custom-call | bytes 2621440 | tf_op jit(solution)/shard_map/pallas_call | solution.py:407
  152.0 7.8 %shard_map.160 = (bf16[256,2560]{1,0:T(8,128)(2,1)}, bf16[256,2560]{1,0:T(8,128)(2,1)}, bf16[256,2560]{1,0:T(8,128)(2,1)}) custom-call(s32[1]{0:T(128)} %dynamic_slice.6.length_ref, bf16[256,2560]{1,0:T(8,128)(2,1)S(1)} %bitcast.38, bf16[256,2560]{1,0:T(8,128)(2,1)S(1)} %bitcast.43, ...), custom_call_target="tpu_custom_call", output_to_operand_aliasing={{0}: (6, {}), {1}: (7, {}), {2}: (8, {})} | custom-call | bytes 4194304 | tf_op jit(solution)/shard_map/pallas_call | solution.py:407
  159.8 3.7 %collective-permute-done.28.refs_1_ = bf16[640,384]{1,0:T(8,128)(2,1)} collective-permute-done((bf16[640,384]{1,0:T(8,128)(2,1)}, bf16[640,384]{1,0:T(8,128)(2,1)}, u32[]{:S(2)}, u32[]{:S(2)}) %collective-permute-start.28) | collective-permute-done | bytes 491552 | tf_op jit(solution)/shard_map/ppermute | solution.py:42
  163.7 1.7 collective-permute-start.32
  166.1 1.5 shard_map.164.refs_0_
  167.9 7.7 %shard_map.162 = (bf16[256,2560]{1,0:T(8,128)(2,1)}, bf16[256,2560]{1,0:T(8,128)(2,1)}, bf16[256,2560]{1,0:T(8,128)(2,1)}) custom-call(s32[1]{0:T(128)} %dynamic_slice.6.length_ref, bf16[256,2560]{1,0:T(8,128)(2,1)S(1)} %bitcast.39, bf16[256,2560]{1,0:T(8,128)(2,1)S(1)} %bitcast.44, ...), custom_call_target="tpu_custom_call", output_to_operand_aliasing={{0}: (6, {}), {1}: (7, {}), {2}: (8, {})} | custom-call | bytes 4194304 | tf_op jit(solution)/shard_map/pallas_call | solution.py:407
  175.6 4.9 %collective-permute-done.32.refs_1_ = bf16[640,256]{1,0:T(8,128)(2,1)S(1)} collective-permute-done((bf16[640,256]{1,0:T(8,128)(2,1)S(1)}, bf16[640,256]{1,0:T(8,128)(2,1)S(1)}, u32[]{:S(2)}, u32[]{:S(2)}) %collective-permute-start.32) | collective-permute-done | bytes 327712 | tf_op jit(solution)/shard_map/ppermute | solution.py:42
  180.7 1.2 collective-permute-start.34
  183.6 5.0 %collective-permute-done.34.refs_1_ = bf16[640,256]{1,0:T(8,128)(2,1)S(1)} collective-permute-done((bf16[640,256]{1,0:T(8,128)(2,1)S(1)}, bf16[640,256]{1,0:T(8,128)(2,1)S(1)}, u32[]{:S(2)}, u32[]{:S(2)}) %collective-permute-start.34) | collective-permute-done | bytes 327712 | tf_op jit(solution)/shard_map/ppermute | solution.py:42
  188.6 2.3 %collective-permute-start.36 = (bf16[640,256]{1,0:T(8,128)(2,1)S(1)}, bf16[640,256]{1,0:T(8,128)(2,1)S(1)}, u32[]{:S(2)}, u32[]{:S(2)}) collective-permute-start(bf16[640,256]{1,0:T(8,128)(2,1)S(1)} %collective-permute-done.34.refs_1_), channel_id=1, source_target_pairs={{0,4},{4,0},{8,12},{12,8},{1,5},{5,1},{9,13},{13,9},{2,6},{6,2},{1... | collective-permute-start | bytes 983048 | tf_op jit(solution)/shard_map/ppermute | solution.py:42
  190.9 2.0 %shard_map.165.refs_4_ = f32[640,2560]{1,0:T(8,128)} custom-call(s32[1]{0:T(128)} %bitcast.1.at_ref.member_ref, bf16[640,384]{1,0:T(8,128)(2,1)S(1)} %shard_map.164.refs_0_, bf16[640,384]{1,0:T(8,128)(2,1)S(1)} %collective-permute-done.37.refs_1_, bf16[640,384]{1,0:T(8,128)(2,1)S(1)} %collective-permute-done.38.refs_2_, ...), custom_call_target="tpu_custom_call" | custom-call | bytes 2097152 | tf_op jit(solution)/shard_map/pallas_call | solution.py:234
  192.9 1.6 shard_map.166
  (160 shorter events, 32.5 us)
Async XLA Ops:
  0.6 62.0 %copy-start = (f32[1,2560]{1,0:T(1,128)S(1)}, f32[1,2560]{1,0:T(1,128)}, u32[]{:S(2)}) copy-start(f32[1,2560]{1,0:T(1,128)} %param.17) | copy-start | bytes 30724
  0.7 7.3 %copy-start.2 = (bf16[1,1,256,2560]{3,2,1,0:T(8,128)(2,1)S(1)}, bf16[1,1,256,2560]{3,2,1,0:T(8,128)(2,1)}, u32[]{:S(2)}) copy-start(bf16[1,1,256,2560]{3,2,1,0:T(8,128)(2,1)} %param.9) | copy-start | bytes 3932164
  0.7 7.3 %copy-start.3 = (bf16[1,1,256,2560]{3,2,1,0:T(8,128)(2,1)S(1)}, bf16[1,1,256,2560]{3,2,1,0:T(8,128)(2,1)}, u32[]{:S(2)}) copy-start(bf16[1,1,256,2560]{3,2,1,0:T(8,128)(2,1)} %param.10) | copy-start | bytes 3932164
  2.9 39.8 %collective-permute-start.1 = (bf16[640,640]{1,0:T(8,128)(2,1)}, bf16[640,640]{1,0:T(8,128)(2,1)}, u32[]{:S(2)}, u32[]{:S(2)}) collective-permute-start(bf16[640,640]{1,0:T(8,128)(2,1)} %shard_map.128.refs_1_), channel_id=1, source_target_pairs={{0,2},{1,3},{2,0},{3,1},{4,6},{5,7},{6,4},{7,5},{8,10},{9,11},{10,... | collective-permute-start | bytes 2457608 | tf_op jit(solution)/shard_map/ppermute | solution.py:42
  6.1 36.6 %collective-permute-start = (bf16[640,640]{1,0:T(8,128)(2,1)}, bf16[640,640]{1,0:T(8,128)(2,1)}, u32[]{:S(2)}, u32[]{:S(2)}) collective-permute-start(bf16[640,640]{1,0:T(8,128)(2,1)} %shard_map.128.refs_1_), channel_id=1, source_target_pairs={{0,1},{1,0},{2,3},{3,2},{4,5},{5,4},{6,7},{7,6},{8,9},{9,8},{10,11... | collective-permute-start | bytes 2457608 | tf_op jit(solution)/shard_map/ppermute | solution.py:42
  13.5 29.2 %collective-permute-start.3 = (bf16[256,1536]{1,0:T(8,128)(2,1)S(1)}, bf16[256,1536]{1,0:T(8,128)(2,1)}, u32[]{:S(2)}, u32[]{:S(2)}) collective-permute-start(bf16[256,1536]{1,0:T(8,128)(2,1)S(1)} %shard_map.130.refs_1_), channel_id=1, source_target_pairs={{0,8},{4,12},{8,0},{12,4},{1,9},{5,13},{9,1},{13,5},{2,10},{6,14},... | collective-permute-start | bytes 2359304 | tf_op jit(solution)/shard_map/ppermute | solution.py:42
  18.4 24.2 %collective-permute-start.2 = (bf16[256,1024]{1,0:T(8,128)(2,1)}, bf16[256,1024]{1,0:T(8,128)(2,1)}, u32[]{:S(2)}, u32[]{:S(2)}) collective-permute-start(bf16[256,1024]{1,0:T(8,128)(2,1)} %shard_map.129.refs_0_), channel_id=1, source_target_pairs={{0,8},{4,12},{8,0},{12,4},{1,9},{5,13},{9,1},{13,5},{2,10},{6,14},... | collective-permute-start | bytes 1572872 | tf_op jit(solution)/shard_map/ppermute | solution.py:42
  23.0 38.6 %copy-start.17 = (bf16[256,640]{1,0:T(8,128)(2,1)}, bf16[256,640]{1,0:T(8,128)(2,1)S(1)}, u32[]{:S(2)}) copy-start(bf16[256,640]{1,0:T(8,128)(2,1)S(1)} %get-tuple-element.112.refs_7_) | copy-start | bytes 983044
  42.7 14.2 %collective-permute-start.9 = (bf16[512,640]{1,0:T(8,128)(2,1)S(1)}, bf16[512,640]{1,0:T(8,128)(2,1)S(1)}, u32[]{:S(2)}, u32[]{:S(2)}) collective-permute-start(bf16[512,640]{1,0:T(8,128)(2,1)S(1)} %shard_map.133), channel_id=1, source_target_pairs={{0,8},{4,12},{8,0},{12,4},{1,9},{5,13},{9,1},{13,5},{2,10},{6,14},... | collective-permute-start | bytes 1966088 | tf_op jit(solution)/shard_map/ppermute | solution.py:42
  44.0 18.6 %collective-permute-start.6 = (bf16[256,2560]{1,0:T(8,128)(2,1)}, bf16[256,2560]{1,0:T(8,128)(2,1)}, u32[]{:S(2)}, u32[]{:S(2)}) collective-permute-start(bf16[256,2560]{1,0:T(8,128)(2,1)} %shard_map.131), channel_id=1, source_target_pairs={{0,4},{4,0},{8,12},{12,8},{1,5},{5,1},{9,13},{13,9},{2,6},{6,2},{1... | collective-permute-start | bytes 3932168 | tf_op jit(solution)/shard_map/ppermute | solution.py:42
  46.4 15.3 %collective-permute-start.7 = (bf16[256,1024]{1,0:T(8,128)(2,1)}, bf16[256,1024]{1,0:T(8,128)(2,1)S(1)}, u32[]{:S(2)}, u32[]{:S(2)}) collective-permute-start(bf16[256,1024]{1,0:T(8,128)(2,1)} %collective-permute-done.2.refs_2_), channel_id=1, source_target_pairs={{0,4},{4,0},{8,12},{12,8},{1,5},{5,1},{9,13},{13,9},{2,6},{6,2},{1... | collective-permute-start | bytes 1572872 | tf_op jit(solution)/shard_map/ppermute | solution.py:42
  46.4 20.9 %collective-permute-start.4 = (bf16[640,640]{1,0:T(8,128)(2,1)}, bf16[640,640]{1,0:T(8,128)(2,1)}, u32[]{:S(2)}, u32[]{:S(2)}) collective-permute-start(bf16[640,640]{1,0:T(8,128)(2,1)} %shard_map.128.refs_1_), channel_id=1, source_target_pairs={{1,2},{2,1},{5,6},{6,5},{9,10},{10,9},{13,14},{14,13},{17,18},{18,... | collective-permute-start | bytes 2457608 | tf_op jit(solution)/shard_map/ppermute | solution.py:440
  48.0 21.5 %collective-permute-start.5 = (bf16[640,640]{1,0:T(8,128)(2,1)}, bf16[640,640]{1,0:T(8,128)(2,1)}, u32[]{:S(2)}, u32[]{:S(2)}) collective-permute-start(bf16[640,640]{1,0:T(8,128)(2,1)} %collective-permute-done.1.refs_3_), channel_id=1, source_target_pairs={{2,3},{1,0},{6,7},{5,4},{10,11},{9,8},{14,15},{13,12},{18,19},{17,... | collective-permute-start | bytes 2457608 | tf_op jit(solution)/shard_map/ppermute | solution.py:440
  56.9 5.7 %collective-permute-start.8 = (bf16[256,1536]{1,0:T(8,128)(2,1)}, bf16[256,1536]{1,0:T(8,128)(2,1)}, u32[]{:S(2)}, u32[]{:S(2)}) collective-permute-start(bf16[256,1536]{1,0:T(8,128)(2,1)} %collective-permute-done.3.refs_3_), channel_id=1, source_target_pairs={{0,4},{4,0},{8,12},{12,8},{1,5},{5,1},{9,13},{13,9},{2,6},{6,2},{1... | collective-permute-start | bytes 2359304 | tf_op jit(solution)/shard_map/ppermute | solution.py:42
  62.5 7.0 %collective-permute-start.10 = (bf16[512,640]{1,0:T(8,128)(2,1)}, bf16[512,640]{1,0:T(8,128)(2,1)S(1)}, u32[]{:S(2)}, u32[]{:S(2)}) collective-permute-start(bf16[512,640]{1,0:T(8,128)(2,1)} %shard_map.136), channel_id=1, source_target_pairs={{0,4},{4,0},{8,12},{12,8},{1,5},{5,1},{9,13},{13,9},{2,6},{6,2},{1... | collective-permute-start | bytes 1966088 | tf_op jit(solution)/shard_map/ppermute | solution.py:42
  73.7 10.0 %copy-start.32 = (f32[1024]{0:T(1024)S(1)}, f32[1024]{0:T(1024)}, u32[]{:S(2)}) copy-start(f32[1024]{0:T(1024)} %param.15) | copy-start | bytes 12292
  73.7 10.0 %copy-start.33 = (s32[1,256]{1,0:T(1,128)S(1)}, s32[1,256]{1,0:T(1,128)}, u32[]{:S(2)}) copy-start(s32[1,256]{1,0:T(1,128)} %param.13) | copy-start | bytes 3076
  73.7 29.1 %collective-permute-start.16 = (bf16[1024,256]{1,0:T(8,128)(2,1)S(1)}, bf16[1024,256]{1,0:T(8,128)(2,1)S(1)}, u32[]{:S(2)}, u32[]{:S(2)}) collective-permute-start(bf16[1024,256]{1,0:T(8,128)(2,1)S(1)} %get-tuple-element.128), channel_id=1, source_target_pairs={{0,16},{16,0},{1,17},{17,1},{2,18},{18,2},{3,19},{19,3},{4,20},{20... | collective-permute-start | bytes 1572872 | tf_op jit(solution)/shard_map/ppermute | solution.py:42
  81.5 23.0 %collective-permute-start.17 = (bf16[1024,384]{1,0:T(8,128)(2,1)S(1)}, bf16[1024,384]{1,0:T(8,128)(2,1)S(1)}, u32[]{:S(2)}, u32[]{:S(2)}) collective-permute-start(bf16[1024,384]{1,0:T(8,128)(2,1)S(1)} %get-tuple-element.123), channel_id=1, source_target_pairs={{0,16},{16,0},{1,17},{17,1},{2,18},{18,2},{3,19},{19,3},{4,20},{20... | collective-permute-start | bytes 2359304 | tf_op jit(solution)/shard_map/ppermute | solution.py:42
  81.8 3.6 %collective-permute-start.11 = (f32[2,2,1,256]{3,2,1,0:T(1,128)S(1)}, f32[2,2,1,256]{3,2,1,0:T(1,128)S(1)}, u32[]{:S(2)}, u32[]{:S(2)}) collective-permute-start(f32[2,2,1,256]{3,2,1,0:T(1,128)S(1)} %bitcast.64), channel_id=1, source_target_pairs={{0,4},{4,0},{8,12},{12,8},{1,5},{5,1},{9,13},{13,9},{2,6},{6,2},{1... | collective-permute-start | bytes 12296 | tf_op jit(solution)/shard_map/ppermute | solution.py:42
  85.1 2.8 %collective-permute-start.14 = (f32[1,1,256]{2,1,0:T(1,128)S(1)}, f32[1,1,256]{2,1,0:T(1,128)S(1)}, u32[]{:S(2)}, u32[]{:S(2)}) collective-permute-start(f32[1,1,256]{2,1,0:T(1,128)S(1)} %compare_select_fusion), channel_id=1, source_target_pairs={{0,8},{4,12},{8,0},{12,4},{1,9},{5,13},{9,1},{13,5},{2,10},{6,14},... | collective-permute-start | bytes 3080 | tf_op jit(solution)/shard_map/ppermute | solution.py:42
  85.4 3.3 %collective-permute-start.12 = (f32[2,2,1,256]{3,2,1,0:T(1,128)S(1)}, f32[2,2,1,256]{3,2,1,0:T(1,128)S(1)}, u32[]{:S(2)}, u32[]{:S(2)}) collective-permute-start(f32[2,2,1,256]{3,2,1,0:T(1,128)S(1)} %reverse_add_fusion.2), channel_id=1, source_target_pairs={{0,8},{4,12},{8,0},{12,4},{1,9},{5,13},{9,1},{13,5},{2,10},{6,14},... | collective-permute-start | bytes 12296 | tf_op jit(solution)/shard_map/ppermute | solution.py:42
  87.9 2.2 %collective-permute-start.15 = (f32[2,1,256]{2,1,0:T(1,128)S(1)}, f32[2,1,256]{2,1,0:T(1,128)S(1)}, u32[]{:S(2)}, u32[]{:S(2)}) collective-permute-start(f32[2,1,256]{2,1,0:T(1,128)S(1)} %pad_maximum_fusion), channel_id=1, source_target_pairs={{0,4},{4,0},{8,12},{12,8},{1,5},{5,1},{9,13},{13,9},{2,6},{6,2},{1... | collective-permute-start | bytes 6152 | tf_op jit(solution)/shard_map/ppermute | solution.py:42
  88.8 14.0 %collective-permute-start.13 = (f32[4,1,256]{2,1,0:T(1,128)S(1)}, f32[4,1,256]{2,1,0:T(1,128)S(1)}, u32[]{:S(2)}, u32[]{:S(2)}) collective-permute-start(f32[4,1,256]{2,1,0:T(1,128)S(1)} %bitcast.51), channel_id=1, source_target_pairs={{0,16},{16,0},{1,17},{17,1},{2,18},{18,2},{3,19},{19,3},{4,20},{20... | collective-permute-start | bytes 12296 | tf_op jit(solution)/shard_map/ppermute | solution.py:42
  106.3 3.2 %collective-permute-start.18 = (f32[2,2,2,256]{3,2,1,0:T(2,128)S(1)}, f32[2,2,2,256]{3,2,1,0:T(2,128)S(1)}, u32[]{:S(2)}, u32[]{:S(2)}) collective-permute-start(f32[2,2,2,256]{3,2,1,0:T(2,128)S(1)} %bitcast.55), channel_id=1, source_target_pairs={{0,4},{4,0},{8,12},{12,8},{1,5},{5,1},{9,13},{13,9},{2,6},{6,2},{1... | collective-permute-start | bytes 24584 | tf_op jit(solution)/shard_map/ppermute | solution.py:42
  109.5 2.5 %collective-permute-start.19 = (f32[2,2,2,256]{3,2,1,0:T(2,128)S(1)}, f32[2,2,2,256]{3,2,1,0:T(2,128)S(1)}, u32[]{:S(2)}, u32[]{:S(2)}) collective-permute-start(f32[2,2,2,256]{3,2,1,0:T(2,128)S(1)} %reverse_add_fusion.1), channel_id=1, source_target_pairs={{0,8},{4,12},{8,0},{12,4},{1,9},{5,13},{9,1},{13,5},{2,10},{6,14},... | collective-permute-start | bytes 24584 | tf_op jit(solution)/shard_map/ppermute | solution.py:42
  116.2 7.0 %collective-permute-start.22 = (bf16[512,512]{1,0:T(8,128)(2,1)S(1)}, bf16[512,512]{1,0:T(8,128)(2,1)S(1)}, u32[]{:S(2)}, u32[]{:S(2)}) collective-permute-start(bf16[512,512]{1,0:T(8,128)(2,1)S(1)} %shard_map.144), channel_id=1, source_target_pairs={{0,4},{4,0},{8,12},{12,8},{1,5},{5,1},{9,13},{13,9},{2,6},{6,2},{1... | collective-permute-start | bytes 1572872 | tf_op jit(solution)/shard_map/ppermute | solution.py:42
  118.3 5.0 %collective-permute-start.23 = (bf16[512,512]{1,0:T(8,128)(2,1)S(1)}, bf16[512,512]{1,0:T(8,128)(2,1)S(1)}, u32[]{:S(2)}, u32[]{:S(2)}) collective-permute-start(bf16[512,512]{1,0:T(8,128)(2,1)S(1)} %shard_map.148), channel_id=1, source_target_pairs={{0,4},{4,0},{8,12},{12,8},{1,5},{5,1},{9,13},{13,9},{2,6},{6,2},{1... | collective-permute-start | bytes 1572872 | tf_op jit(solution)/shard_map/ppermute | solution.py:42
  118.4 18.9 %collective-permute-start.21 = (bf16[640,640]{1,0:T(8,128)(2,1)S(1)}, bf16[640,640]{1,0:T(8,128)(2,1)S(1)}, u32[]{:S(2)}, u32[]{:S(2)}) collective-permute-start(bf16[640,640]{1,0:T(8,128)(2,1)S(1)} %get-tuple-element.131), channel_id=1, source_target_pairs={{0,1},{3,2},{4,5},{7,6},{8,9},{11,10},{12,13},{15,14},{16,17},{19,... | collective-permute-start | bytes 2457608 | tf_op jit(solution)/shard_map/ppermute | solution.py:440
  119.8 17.6 %collective-permute-start.20 = (bf16[640,640]{1,0:T(8,128)(2,1)S(1)}, bf16[640,640]{1,0:T(8,128)(2,1)S(1)}, u32[]{:S(2)}, u32[]{:S(2)}) collective-permute-start(bf16[640,640]{1,0:T(8,128)(2,1)S(1)} %get-tuple-element.131), channel_id=1, source_target_pairs={{1,2},{2,1},{5,6},{6,5},{9,10},{10,9},{13,14},{14,13},{17,18},{18,... | collective-permute-start | bytes 2457608 | tf_op jit(solution)/shard_map/ppermute | solution.py:440
  121.3 4.0 %collective-permute-start.24 = (bf16[512,512]{1,0:T(8,128)(2,1)S(1)}, bf16[512,512]{1,0:T(8,128)(2,1)S(1)}, u32[]{:S(2)}, u32[]{:S(2)}) collective-permute-start(bf16[512,512]{1,0:T(8,128)(2,1)S(1)} %shard_map.149), channel_id=1, source_target_pairs={{0,4},{4,0},{8,12},{12,8},{1,5},{5,1},{9,13},{13,9},{2,6},{6,2},{1... | collective-permute-start | bytes 1572872 | tf_op jit(solution)/shard_map/ppermute | solution.py:42
  123.2 12.4 %collective-permute-start.25 = (bf16[512,512]{1,0:T(8,128)(2,1)S(1)}, bf16[512,512]{1,0:T(8,128)(2,1)S(1)}, u32[]{:S(2)}, u32[]{:S(2)}) collective-permute-start(bf16[512,512]{1,0:T(8,128)(2,1)S(1)} %shard_map.153), channel_id=1, source_target_pairs={{0,4},{4,0},{8,12},{12,8},{1,5},{5,1},{9,13},{13,9},{2,6},{6,2},{1... | collective-permute-start | bytes 1572872 | tf_op jit(solution)/shard_map/ppermute | solution.py:42
  123.3 12.3 %collective-permute-start.26 = (bf16[512,512]{1,0:T(8,128)(2,1)S(1)}, bf16[512,512]{1,0:T(8,128)(2,1)S(1)}, u32[]{:S(2)}, u32[]{:S(2)}) collective-permute-start(bf16[512,512]{1,0:T(8,128)(2,1)S(1)} %shard_map.154), channel_id=1, source_target_pairs={{0,4},{4,0},{8,12},{12,8},{1,5},{5,1},{9,13},{13,9},{2,6},{6,2},{1... | collective-permute-start | bytes 1572872 | tf_op jit(solution)/shard_map/ppermute | solution.py:42
  125.2 11.4 %collective-permute-start.27 = (bf16[256,512]{1,0:T(8,128)(2,1)S(1)}, bf16[256,512]{1,0:T(8,128)(2,1)S(1)}, u32[]{:S(2)}, u32[]{:S(2)}) collective-permute-start(bf16[256,512]{1,0:T(8,128)(2,1)S(1)} %get-tuple-element.140), channel_id=1, source_target_pairs={{0,8},{4,12},{8,0},{12,4},{1,9},{5,13},{9,1},{13,5},{2,10},{6,14},... | collective-permute-start | bytes 786440 | tf_op jit(solution)/shard_map/ppermute | solution.py:42
  137.3 14.7 %collective-permute-start.30 = (bf16[256,1024]{1,0:T(8,128)(2,1)}, bf16[256,1024]{1,0:T(8,128)(2,1)}, u32[]{:S(2)}, u32[]{:S(2)}) collective-permute-start(bf16[256,1024]{1,0:T(8,128)(2,1)} %get-tuple-element.147), channel_id=1, source_target_pairs={{0,8},{4,12},{8,0},{12,4},{1,9},{5,13},{9,1},{13,5},{2,10},{6,14},... | collective-permute-start | bytes 1572872 | tf_op jit(solution)/shard_map/ppermute | solution.py:42
  138.6 25.0 %collective-permute-start.31 = (bf16[256,1024]{1,0:T(8,128)(2,1)}, bf16[256,1024]{1,0:T(8,128)(2,1)}, u32[]{:S(2)}, u32[]{:S(2)}) collective-permute-start(bf16[256,1024]{1,0:T(8,128)(2,1)} %get-tuple-element.159), channel_id=1, source_target_pairs={{0,8},{4,12},{8,0},{12,4},{1,9},{5,13},{9,1},{13,5},{2,10},{6,14},... | collective-permute-start | bytes 1572872 | tf_op jit(solution)/shard_map/ppermute | solution.py:42
  139.8 23.8 %collective-permute-start.28 = (bf16[640,384]{1,0:T(8,128)(2,1)}, bf16[640,384]{1,0:T(8,128)(2,1)}, u32[]{:S(2)}, u32[]{:S(2)}) collective-permute-start(bf16[640,384]{1,0:T(8,128)(2,1)} %shard_map.158), channel_id=1, source_target_pairs={{0,2},{1,3},{2,0},{3,1},{4,6},{5,7},{6,4},{7,5},{8,10},{9,11},{10,... | collective-permute-start | bytes 1474568 | tf_op jit(solution)/shard_map/ppermute | solution.py:42
  142.9 20.7 %collective-permute-start.29 = (bf16[640,384]{1,0:T(8,128)(2,1)}, bf16[640,384]{1,0:T(8,128)(2,1)}, u32[]{:S(2)}, u32[]{:S(2)}) collective-permute-start(bf16[640,384]{1,0:T(8,128)(2,1)} %shard_map.156), channel_id=1, source_target_pairs={{0,1},{1,0},{2,3},{3,2},{4,5},{5,4},{6,7},{7,6},{8,9},{9,8},{10,11... | collective-permute-start | bytes 1474568 | tf_op jit(solution)/shard_map/ppermute | solution.py:42
  152.0 11.6 %copy-start.10 = (bf16[1920,256]{1,0:T(8,128)(2,1)S(1)}, bf16[1920,256]{1,0:T(8,128)(2,1)}, u32[]{:S(2)}) copy-start(bf16[1920,256]{1,0:T(8,128)(2,1)} %copy-done.9) | copy-start | bytes 2949124
  152.0 14.1 %copy-start.16 = (bf16[640,640]{1,0:T(8,128)(2,1)S(1)}, bf16[640,640]{1,0:T(8,128)(2,1)}, u32[]{:S(2)}) copy-start(bf16[640,640]{1,0:T(8,128)(2,1)} %copy-done.15) | copy-start | bytes 2457604
  163.7 16.8 %collective-permute-start.32 = (bf16[640,256]{1,0:T(8,128)(2,1)S(1)}, bf16[640,256]{1,0:T(8,128)(2,1)S(1)}, u32[]{:S(2)}, u32[]{:S(2)}) collective-permute-start(bf16[640,256]{1,0:T(8,128)(2,1)S(1)} %shard_map.161), channel_id=1, source_target_pairs={{0,2},{1,3},{2,0},{3,1},{4,6},{5,7},{6,4},{7,5},{8,10},{9,11},{10,... | collective-permute-start | bytes 983048 | tf_op jit(solution)/shard_map/ppermute | solution.py:42
  165.4 15.1 %collective-permute-start.33 = (bf16[640,256]{1,0:T(8,128)(2,1)S(1)}, bf16[640,256]{1,0:T(8,128)(2,1)S(1)}, u32[]{:S(2)}, u32[]{:S(2)}) collective-permute-start(bf16[640,256]{1,0:T(8,128)(2,1)S(1)} %copy-done.27), channel_id=1, source_target_pairs={{0,1},{1,0},{2,3},{3,2},{4,5},{5,4},{6,7},{7,6},{8,9},{9,8},{10,11... | collective-permute-start | bytes 983048 | tf_op jit(solution)/shard_map/ppermute | solution.py:42
  167.6 15.5 %collective-permute-start.37 = (bf16[640,384]{1,0:T(8,128)(2,1)S(1)}, bf16[640,384]{1,0:T(8,128)(2,1)S(1)}, u32[]{:S(2)}, u32[]{:S(2)}) collective-permute-start(bf16[640,384]{1,0:T(8,128)(2,1)S(1)} %shard_map.164.refs_0_), channel_id=1, source_target_pairs={{0,8},{4,12},{8,0},{12,4},{1,9},{5,13},{9,1},{13,5},{2,10},{6,14},... | collective-permute-start | bytes 1474568 | tf_op jit(solution)/shard_map/ppermute | solution.py:42
  180.7 7.9 %collective-permute-start.34 = (bf16[640,256]{1,0:T(8,128)(2,1)S(1)}, bf16[640,256]{1,0:T(8,128)(2,1)S(1)}, u32[]{:S(2)}, u32[]{:S(2)}) collective-permute-start(bf16[640,256]{1,0:T(8,128)(2,1)S(1)} %shard_map.163.refs_0_), channel_id=1, source_target_pairs={{0,8},{4,12},{8,0},{12,4},{1,9},{5,13},{9,1},{13,5},{2,10},{6,14},... | collective-permute-start | bytes 983048 | tf_op jit(solution)/shard_map/ppermute | solution.py:42
  181.9 9.0 %collective-permute-start.38 = (bf16[640,384]{1,0:T(8,128)(2,1)S(1)}, bf16[640,384]{1,0:T(8,128)(2,1)S(1)}, u32[]{:S(2)}, u32[]{:S(2)}) collective-permute-start(bf16[640,384]{1,0:T(8,128)(2,1)S(1)} %shard_map.164.refs_0_), channel_id=1, source_target_pairs={{0,4},{4,0},{8,12},{12,8},{1,5},{5,1},{9,13},{13,9},{2,6},{6,2},{1... | collective-permute-start | bytes 1474568 | tf_op jit(solution)/shard_map/ppermute | solution.py:42
  183.1 7.8 %collective-permute-start.39 = (bf16[640,384]{1,0:T(8,128)(2,1)S(1)}, bf16[640,384]{1,0:T(8,128)(2,1)S(1)}, u32[]{:S(2)}, u32[]{:S(2)}) collective-permute-start(bf16[640,384]{1,0:T(8,128)(2,1)S(1)} %collective-permute-done.37.refs_1_), channel_id=1, source_target_pairs={{0,4},{4,0},{8,12},{12,8},{1,5},{5,1},{9,13},{13,9},{2,6},{6,2},{1... | collective-permute-start | bytes 1474568 | tf_op jit(solution)/shard_map/ppermute | solution.py:42
  183.1 9.8 %collective-permute-start.35 = (bf16[640,256]{1,0:T(8,128)(2,1)S(1)}, bf16[640,256]{1,0:T(8,128)(2,1)S(1)}, u32[]{:S(2)}, u32[]{:S(2)}) collective-permute-start(bf16[640,256]{1,0:T(8,128)(2,1)S(1)} %shard_map.163.refs_0_), channel_id=1, source_target_pairs={{0,4},{4,0},{8,12},{12,8},{1,5},{5,1},{9,13},{13,9},{2,6},{6,2},{1... | collective-permute-start | bytes 983048 | tf_op jit(solution)/shard_map/ppermute | solution.py:42
  188.6 4.3 %collective-permute-start.36 = (bf16[640,256]{1,0:T(8,128)(2,1)S(1)}, bf16[640,256]{1,0:T(8,128)(2,1)S(1)}, u32[]{:S(2)}, u32[]{:S(2)}) collective-permute-start(bf16[640,256]{1,0:T(8,128)(2,1)S(1)} %collective-permute-done.34.refs_1_), channel_id=1, source_target_pairs={{0,4},{4,0},{8,12},{12,8},{1,5},{5,1},{9,13},{13,9},{2,6},{6,2},{1... | collective-permute-start | bytes 983048 | tf_op jit(solution)/shard_map/ppermute | solution.py:42
  (27 other events, 76.9 us)

commit v8 on v7

--- a/solution.py
+++ b/solution.py
@@ -525,8 +525,7 @@
         rest = [here, across, passed_on]
     else:
         rest = [swap(piece, "dp", s) if s else piece for s, piece in zip(order, mine)]
-    tied = tie(*last, *pairs, *rest)
-    last, (attn,), rest = split(tied, len(last), 1)
+    (attn,) = pairs
     spots = [part, *[part ^ s for s in others], *([part ^ 3] if line else [])]
     shapes = [(heads_width, n) for n in sizes]
 

time: 196 us -> 196 us (level)
  no operation moved by 1% of the time
where the time goes in v8:
time: 196 us
  Pallas kernels  73.6 us (38%)
  waiting for transfers between devices  60.1 us (31%)
  starting transfers between devices  43.3 us (22%)
  local copies, waits for them, and re-layouts  11.5 us (6%)
  between operations  3.64 us (2%)
  other arithmetic  3.46 us (2%)
    ppermute x36, waiting for transfers between devices, swap(): lax.ppermute(value, axis, [(i, i ^ bit) for i in range(lax.axis_size(axis...  57.9 us
    ppermute x36, starting transfers between devices, swap(): lax.ppermute(value, axis, [(i, i ^ bit) for i in range(lax.axis_size(axis...  38.3 us
    pallas_call x17, Pallas kernels, small_call(): pl.pallas_call(kernel, grid_spec=pltpu.PrefetchScalarGridSpec(num_scalar_...  31.1 us
    pallas_call x5, Pallas kernels, attention_call(): pl.pallas_call(kernel, grid_spec=pltpu.PrefetchScalarGridSpec(num_scalar_...  27.4 us
    pallas_call x15, Pallas kernels, call(): pl.pallas_call(kernel, grid=grid, in_specs=[spec(b, m, a.shape) for a, b,...  11.6 us
    unnamed x70, local copies, waits for them, and re-layouts  10.9 us
    ppermute x4, starting transfers between devices, send(): return lax.ppermute(value, axis, pairs)  5.06 us
  transfers between devices with their start and end apart: 40, of which 10 were waited for; matrix products, arithmetic and copies ran while one was open for 2% of the time, Pallas kernels for 30%

profile of v8, /device:TPU:1, one launch (start us, length us, event | category | flops | bytes accessed | tf_op | source)
XLA Modules:
  0.0 195.6 jit_solution(16409326310154190958)
XLA Ops:
  0.7 2.3 %shard_map.128.refs_1_ = bf16[640,640]{1,0:T(8,128)(2,1)} custom-call(s32[1]{0:T(128)} %bitcast.1.at_ref.member_ref, bf16[640,2560]{1,0:T(8,128)(2,1)} %bitcast.61), custom_call_target="tpu_custom_call" | custom-call | bytes 1048576 | tf_op jit(solution)/shard_map/pallas_call | solution.py:260
  2.9 3.1 %collective-permute-start.1 = (bf16[640,640]{1,0:T(8,128)(2,1)}, bf16[640,640]{1,0:T(8,128)(2,1)}, u32[]{:S(2)}, u32[]{:S(2)}) collective-permute-start(bf16[640,640]{1,0:T(8,128)(2,1)} %shard_map.128.refs_1_), channel_id=1, source_target_pairs={{0,2},{1,3},{2,0},{3,1},{4,6},{5,7},{6,4},{7,5},{8,10},{9,11},{10,... | collective-permute-start | bytes 2457608 | tf_op jit(solution)/shard_map/ppermute | solution.py:42
  6.1 1.3 collective-permute-start
  8.0 1.3 copy-done.4
  9.3 4.2 %shard_map.130.refs_1_ = bf16[256,1536]{1,0:T(8,128)(2,1)S(1)} custom-call(s32[1]{0:T(128)} %dynamic_slice.6.length_ref, bf16[256,2560]{1,0:T(8,128)(2,1)S(1)} %bitcast.35, bf16[256,2560]{1,0:T(8,128)(2,1)S(1)} %bitcast.40, bf16[256,2560]{1,0:T(8,128)(2,1)S(1)} %bitcast.45), custom_call_target="tpu_custom_call" | custom-call | bytes 4718592 | tf_op jit(solution)/shard_map/pallas_call | solution.py:407
  13.5 1.3 collective-permute-start.3
  14.8 3.7 %shard_map.129.refs_0_ = bf16[256,1024]{1,0:T(8,128)(2,1)} custom-call(s32[1]{0:T(128)} %dynamic_slice.6.length_ref, bf16[256,2560]{1,0:T(8,128)(2,1)S(1)} %bitcast.36, bf16[256,2560]{1,0:T(8,128)(2,1)S(1)} %bitcast.41, bf16[256,2560]{1,0:T(8,128)(2,1)S(1)} %bitcast.46), custom_call_target="tpu_custom_call" | custom-call | bytes 3145728 | tf_op jit(solution)/shard_map/pallas_call | solution.py:407
  20.0 2.3 %shard_map.131 = bf16[256,2560]{1,0:T(8,128)(2,1)} custom-call(s32[1]{0:T(128)} %constant.9.clone.1.at_ref, bf16[256,1024]{1,0:T(8,128)(2,1)} %shard_map.129.refs_0_, bf16[256,1536]{1,0:T(8,128)(2,1)S(1)} %shard_map.130.refs_1_), custom_call_target="tpu_custom_call" | custom-call | bytes 1048576 | tf_op jit(solution)/shard_map/pallas_call | solution.py:260
  23.1 19.6 %collective-permute-done.2.refs_2_ = bf16[256,1024]{1,0:T(8,128)(2,1)} collective-permute-done((bf16[256,1024]{1,0:T(8,128)(2,1)}, bf16[256,1024]{1,0:T(8,128)(2,1)}, u32[]{:S(2)}, u32[]{:S(2)}) %collective-permute-start.2) | collective-permute-done | bytes 524320 | tf_op jit(solution)/shard_map/ppermute | solution.py:42
  42.7 1.3 collective-permute-start.9
  44.0 2.4 %collective-permute-start.4 = (bf16[256,2560]{1,0:T(8,128)(2,1)}, bf16[256,2560]{1,0:T(8,128)(2,1)}, u32[]{:S(2)}, u32[]{:S(2)}) collective-permute-start(bf16[256,2560]{1,0:T(8,128)(2,1)} %shard_map.131), channel_id=1, source_target_pairs={{0,4},{4,0},{8,12},{12,8},{1,5},{5,1},{9,13},{13,9},{2,6},{6,2},{1... | collective-permute-start | bytes 3932168 | tf_op jit(solution)/shard_map/ppermute | solution.py:42
  46.4 1.5 collective-permute-start.7
  48.0 1.3 collective-permute-start.8
  49.3 7.7 %collective-permute-done.9.in_ref.refs_8_ = bf16[512,640]{1,0:T(8,128)(2,1)S(1)} collective-permute-done((bf16[512,640]{1,0:T(8,128)(2,1)S(1)}, bf16[512,640]{1,0:T(8,128)(2,1)S(1)}, u32[]{:S(2)}, u32[]{:S(2)}) %collective-permute-start.9) | collective-permute-done | bytes 655392 | tf_op jit(solution)/shard_map/ppermute | solution.py:42
  56.9 3.0 %collective-permute-start.6 = (bf16[256,1536]{1,0:T(8,128)(2,1)}, bf16[256,1536]{1,0:T(8,128)(2,1)}, u32[]{:S(2)}, u32[]{:S(2)}) collective-permute-start(bf16[256,1536]{1,0:T(8,128)(2,1)} %collective-permute-done.3.refs_3_), channel_id=1, source_target_pairs={{0,4},{4,0},{8,12},{12,8},{1,5},{5,1},{9,13},{13,9},{2,6},{6,2},{1... | collective-permute-start | bytes 2359304 | tf_op jit(solution)/shard_map/ppermute | solution.py:42
  64.8 2.5 %shard_map.134.refs_0_.attn_ref = bf16[1024,2560]{1,0:T(8,128)(2,1)S(1)} custom-call(s32[1]{0:T(128)} %constant.9.clone.1.at_ref, bf16[256,1024]{1,0:T(8,128)(2,1)} %shard_map.129.refs_0_, bf16[256,1536]{1,0:T(8,128)(2,1)S(1)} %copy-done.12, bf16[256,1024]{1,0:T(8,128)(2,1)} %collective-permute-done.2.refs_2_, ...), custom_call_target="tpu_custom_call" | custom-call | bytes 1048576 | tf_op jit(solution)/shard_map/pallas_call | solution.py:260
  67.3 2.1 %collective-permute-done.8.refs_5_ = bf16[640,640]{1,0:T(8,128)(2,1)} collective-permute-done((bf16[640,640]{1,0:T(8,128)(2,1)}, bf16[640,640]{1,0:T(8,128)(2,1)}, u32[]{:S(2)}, u32[]{:S(2)}) %collective-permute-start.8) | collective-permute-done | bytes 819232 | tf_op jit(solution)/shard_map/ppermute | solution.py:440
  69.5 4.2 %shard_map.137 = (f32[1024,256]{1,0:T(8,128)S(1)}, bf16[1024,256]{1,0:T(8,128)(2,1)S(1)}, f32[4,1,256]{2,1,0:T(1,128)S(1)}, bf16[2560,256]{1,0:T(8,128)(2,1)S(1)}) custom-call(s32[4]{0:T(128)S(1)} %pad_add_fusion.1.at_ref, bf16[1024,2560]{1,0:T(8,128)(2,1)S(1)} %shard_map.134.refs_0_.attn_ref, bf16[640,640]{1,0:T(8,128)(2,1)} %shard_map.128.refs_1_, ...), custom_call_target="tpu_custom_call" | custom-call | bytes 2097152 | tf_op jit(solution)/shard_map/pallas_call | solution.py:260
  73.7 1.3 collective-permute-start.16
  75.0 6.5 %shard_map.138 = (f32[1024,384]{1,0:T(8,128)S(1)}, bf16[1024,384]{1,0:T(8,128)(2,1)S(1)}, f32[4,1,256]{2,1,0:T(1,128)S(1)}, bf16[2560,384]{1,0:T(8,128)(2,1)S(1)}) custom-call(s32[4]{0:T(128)S(1)} %pad_add_fusion.1.at_ref, bf16[1024,2560]{1,0:T(8,128)(2,1)S(1)} %shard_map.134.refs_0_.attn_ref, bf16[640,640]{1,0:T(8,128)(2,1)} %shard_map.128.refs_1_, ...), custom_call_target="tpu_custom_call" | custom-call | bytes 2097152 | tf_op jit(solution)/shard_map/pallas_call | solution.py:260
  81.8 1.9 collective-permute-start.11
  85.4 1.3 collective-permute-start.12
  86.7 1.2 collective-permute-done.14
  88.8 1.3 collective-permute-start.13
  90.1 12.7 %collective-permute-done.13.other_ref = f32[4,1,256]{2,1,0:T(1,128)S(1)} collective-permute-done((f32[4,1,256]{2,1,0:T(1,128)S(1)}, f32[4,1,256]{2,1,0:T(1,128)S(1)}, u32[]{:S(2)}, u32[]{:S(2)}) %collective-permute-start.13) | collective-permute-done | bytes 4128 | tf_op jit(solution)/shard_map/ppermute | solution.py:42
  102.8 1.7 shard_map.139.refs_0_
  104.4 1.9 shard_map.140
  106.3 2.3 %collective-permute-start.18 = (f32[2,2,2,256]{3,2,1,0:T(2,128)S(1)}, f32[2,2,2,256]{3,2,1,0:T(2,128)S(1)}, u32[]{:S(2)}, u32[]{:S(2)}) collective-permute-start(f32[2,2,2,256]{3,2,1,0:T(2,128)S(1)} %bitcast.55), channel_id=1, source_target_pairs={{0,4},{4,0},{8,12},{12,8},{1,5},{5,1},{9,13},{13,9},{2,6},{6,2},{1... | collective-permute-start | bytes 24584 | tf_op jit(solution)/shard_map/ppermute | solution.py:42
  109.7 2.2 %collective-permute-done.19 = f32[2,2,2,256]{3,2,1,0:T(2,128)S(1)} collective-permute-done((f32[2,2,2,256]{3,2,1,0:T(2,128)S(1)}, f32[2,2,2,256]{3,2,1,0:T(2,128)S(1)}, u32[]{:S(2)}, u32[]{:S(2)}) %collective-permute-start.19) | collective-permute-done | bytes 8224 | tf_op jit(solution)/shard_map/ppermute | solution.py:42
  112.0 3.6 %shard_map.141 = (bf16[1024,640]{1,0:T(8,128)(2,1)S(1)}, bf16[640,640]{1,0:T(8,128)(2,1)S(1)}) custom-call(s32[1]{0:T(128)} %bitcast.at_ref, bf16[1024,2560]{1,0:T(8,128)(2,1)S(1)} %shard_map.134.refs_0_.attn_ref, f32[4,1,256]{2,1,0:T(1,128)S(1)} %bitcast.54, f32[4,1,256]{2,1,0:T(1,128)S(1)} %collective-permute-done.13.other_ref, ...), custom_call_target="tpu_custom_call" | custom-call | bytes 4194304 | tf_op jit(solution)/shard_map/pallas_call | solution.py:260
  116.2 1.6 collective-permute-start.22
  118.4 1.3 collective-permute-start.21
  128.0 4.6 %shard_map.142 = (bf16[1920,384]{1,0:T(8,128)(2,1)S(1)}, bf16[1920,256]{1,0:T(8,128)(2,1)S(1)}) custom-call(s32[3]{0:T(128)S(1)} %pad_add_fusion.2.at_ref, bf16[1024,2560]{1,0:T(8,128)(2,1)S(1)} %shard_map.134.refs_0_.attn_ref, bf16[1024,640]{1,0:T(8,128)(2,1)S(1)} %get-tuple-element.120.d_ref), custom_call_target="tpu_custom_call" | custom-call | bytes 4194304 | tf_op jit(solution)/shard_map/pallas_call | solution.py:260
  137.3 1.3 collective-permute-start.30
  139.8 3.1 %collective-permute-start.28 = (bf16[640,384]{1,0:T(8,128)(2,1)}, bf16[640,384]{1,0:T(8,128)(2,1)}, u32[]{:S(2)}, u32[]{:S(2)}) collective-permute-start(bf16[640,384]{1,0:T(8,128)(2,1)} %shard_map.158), channel_id=1, source_target_pairs={{0,2},{1,3},{2,0},{3,1},{4,6},{5,7},{6,4},{7,5},{8,10},{9,11},{10,... | collective-permute-start | bytes 1474568 | tf_op jit(solution)/shard_map/ppermute | solution.py:42
  144.7 1.3 copy-done.5
  148.0 4.1 %shard_map.159 = (bf16[256,2560]{1,0:T(8,128)(2,1)}, bf16[256,2560]{1,0:T(8,128)(2,1)}, bf16[256,2560]{1,0:T(8,128)(2,1)}) custom-call(s32[1]{0:T(128)} %dynamic_slice.6.length_ref, bf16[256,2560]{1,0:T(8,128)(2,1)S(1)} %bitcast.37, bf16[256,2560]{1,0:T(8,128)(2,1)S(1)} %bitcast.42, bf16[256,2560]{1,0:T(8,128)(2,1)S(1)} %bitcast.47, ...), custom_call_target="tpu_custom_call" | custom-call | bytes 2621440 | tf_op jit(solution)/shard_map/pallas_call | solution.py:407
  152.0 7.8 %shard_map.160 = (bf16[256,2560]{1,0:T(8,128)(2,1)}, bf16[256,2560]{1,0:T(8,128)(2,1)}, bf16[256,2560]{1,0:T(8,128)(2,1)}) custom-call(s32[1]{0:T(128)} %dynamic_slice.6.length_ref, bf16[256,2560]{1,0:T(8,128)(2,1)S(1)} %bitcast.38, bf16[256,2560]{1,0:T(8,128)(2,1)S(1)} %bitcast.43, ...), custom_call_target="tpu_custom_call", output_to_operand_aliasing={{0}: (6, {}), {1}: (7, {}), {2}: (8, {})} | custom-call | bytes 4194304 | tf_op jit(solution)/shard_map/pallas_call | solution.py:407
  159.8 3.7 %collective-permute-done.28.refs_1_ = bf16[640,384]{1,0:T(8,128)(2,1)} collective-permute-done((bf16[640,384]{1,0:T(8,128)(2,1)}, bf16[640,384]{1,0:T(8,128)(2,1)}, u32[]{:S(2)}, u32[]{:S(2)}) %collective-permute-start.28) | collective-permute-done | bytes 491552 | tf_op jit(solution)/shard_map/ppermute | solution.py:42
  163.7 1.7 collective-permute-start.32
  166.1 1.5 shard_map.164.refs_0_
  167.9 7.7 %shard_map.162 = (bf16[256,2560]{1,0:T(8,128)(2,1)}, bf16[256,2560]{1,0:T(8,128)(2,1)}, bf16[256,2560]{1,0:T(8,128)(2,1)}) custom-call(s32[1]{0:T(128)} %dynamic_slice.6.length_ref, bf16[256,2560]{1,0:T(8,128)(2,1)S(1)} %bitcast.39, bf16[256,2560]{1,0:T(8,128)(2,1)S(1)} %bitcast.44, ...), custom_call_target="tpu_custom_call", output_to_operand_aliasing={{0}: (6, {}), {1}: (7, {}), {2}: (8, {})} | custom-call | bytes 4194304 | tf_op jit(solution)/shard_map/pallas_call | solution.py:407
  175.6 4.9 %collective-permute-done.32.refs_1_ = bf16[640,256]{1,0:T(8,128)(2,1)S(1)} collective-permute-done((bf16[640,256]{1,0:T(8,128)(2,1)S(1)}, bf16[640,256]{1,0:T(8,128)(2,1)S(1)}, u32[]{:S(2)}, u32[]{:S(2)}) %collective-permute-start.32) | collective-permute-done | bytes 327712 | tf_op jit(solution)/shard_map/ppermute | solution.py:42
  180.7 1.2 collective-permute-start.34
  183.6 5.0 %collective-permute-done.34.refs_1_ = bf16[640,256]{1,0:T(8,128)(2,1)S(1)} collective-permute-done((bf16[640,256]{1,0:T(8,128)(2,1)S(1)}, bf16[640,256]{1,0:T(8,128)(2,1)S(1)}, u32[]{:S(2)}, u32[]{:S(2)}) %collective-permute-start.34) | collective-permute-done | bytes 327712 | tf_op jit(solution)/shard_map/ppermute | solution.py:42
  188.6 2.3 %collective-permute-start.36 = (bf16[640,256]{1,0:T(8,128)(2,1)S(1)}, bf16[640,256]{1,0:T(8,128)(2,1)S(1)}, u32[]{:S(2)}, u32[]{:S(2)}) collective-permute-start(bf16[640,256]{1,0:T(8,128)(2,1)S(1)} %collective-permute-done.34.refs_1_), channel_id=1, source_target_pairs={{0,4},{4,0},{8,12},{12,8},{1,5},{5,1},{9,13},{13,9},{2,6},{6,2},{1... | collective-permute-start | bytes 983048 | tf_op jit(solution)/shard_map/ppermute | solution.py:42
  190.9 2.0 %shard_map.165.refs_4_ = f32[640,2560]{1,0:T(8,128)} custom-call(s32[1]{0:T(128)} %bitcast.1.at_ref.member_ref, bf16[640,384]{1,0:T(8,128)(2,1)S(1)} %shard_map.164.refs_0_, bf16[640,384]{1,0:T(8,128)(2,1)S(1)} %collective-permute-done.37.refs_1_, bf16[640,384]{1,0:T(8,128)(2,1)S(1)} %collective-permute-done.38.refs_2_, ...), custom_call_target="tpu_custom_call" | custom-call | bytes 2097152 | tf_op jit(solution)/shard_map/pallas_call | solution.py:234
  192.9 1.6 shard_map.166
  (160 shorter events, 32.5 us)
Async XLA Ops:
  0.6 62.0 %copy-start = (f32[1,2560]{1,0:T(1,128)S(1)}, f32[1,2560]{1,0:T(1,128)}, u32[]{:S(2)}) copy-start(f32[1,2560]{1,0:T(1,128)} %param.17) | copy-start | bytes 30724
  0.7 7.3 %copy-start.2 = (bf16[1,1,256,2560]{3,2,1,0:T(8,128)(2,1)S(1)}, bf16[1,1,256,2560]{3,2,1,0:T(8,128)(2,1)}, u32[]{:S(2)}) copy-start(bf16[1,1,256,2560]{3,2,1,0:T(8,128)(2,1)} %param.9) | copy-start | bytes 3932164
  0.7 7.3 %copy-start.3 = (bf16[1,1,256,2560]{3,2,1,0:T(8,128)(2,1)S(1)}, bf16[1,1,256,2560]{3,2,1,0:T(8,128)(2,1)}, u32[]{:S(2)}) copy-start(bf16[1,1,256,2560]{3,2,1,0:T(8,128)(2,1)} %param.10) | copy-start | bytes 3932164
  2.9 39.8 %collective-permute-start.1 = (bf16[640,640]{1,0:T(8,128)(2,1)}, bf16[640,640]{1,0:T(8,128)(2,1)}, u32[]{:S(2)}, u32[]{:S(2)}) collective-permute-start(bf16[640,640]{1,0:T(8,128)(2,1)} %shard_map.128.refs_1_), channel_id=1, source_target_pairs={{0,2},{1,3},{2,0},{3,1},{4,6},{5,7},{6,4},{7,5},{8,10},{9,11},{10,... | collective-permute-start | bytes 2457608 | tf_op jit(solution)/shard_map/ppermute | solution.py:42
  6.1 36.6 %collective-permute-start = (bf16[640,640]{1,0:T(8,128)(2,1)}, bf16[640,640]{1,0:T(8,128)(2,1)}, u32[]{:S(2)}, u32[]{:S(2)}) collective-permute-start(bf16[640,640]{1,0:T(8,128)(2,1)} %shard_map.128.refs_1_), channel_id=1, source_target_pairs={{0,1},{1,0},{2,3},{3,2},{4,5},{5,4},{6,7},{7,6},{8,9},{9,8},{10,11... | collective-permute-start | bytes 2457608 | tf_op jit(solution)/shard_map/ppermute | solution.py:42
  13.5 29.2 %collective-permute-start.3 = (bf16[256,1536]{1,0:T(8,128)(2,1)S(1)}, bf16[256,1536]{1,0:T(8,128)(2,1)}, u32[]{:S(2)}, u32[]{:S(2)}) collective-permute-start(bf16[256,1536]{1,0:T(8,128)(2,1)S(1)} %shard_map.130.refs_1_), channel_id=1, source_target_pairs={{0,8},{4,12},{8,0},{12,4},{1,9},{5,13},{9,1},{13,5},{2,10},{6,14},... | collective-permute-start | bytes 2359304 | tf_op jit(solution)/shard_map/ppermute | solution.py:42
  18.4 24.2 %collective-permute-start.2 = (bf16[256,1024]{1,0:T(8,128)(2,1)}, bf16[256,1024]{1,0:T(8,128)(2,1)}, u32[]{:S(2)}, u32[]{:S(2)}) collective-permute-start(bf16[256,1024]{1,0:T(8,128)(2,1)} %shard_map.129.refs_0_), channel_id=1, source_target_pairs={{0,8},{4,12},{8,0},{12,4},{1,9},{5,13},{9,1},{13,5},{2,10},{6,14},... | collective-permute-start | bytes 1572872 | tf_op jit(solution)/shard_map/ppermute | solution.py:42
  23.0 38.6 %copy-start.17 = (bf16[256,640]{1,0:T(8,128)(2,1)}, bf16[256,640]{1,0:T(8,128)(2,1)S(1)}, u32[]{:S(2)}) copy-start(bf16[256,640]{1,0:T(8,128)(2,1)S(1)} %get-tuple-element.100.refs_7_) | copy-start | bytes 983044
  42.7 14.2 %collective-permute-start.9 = (bf16[512,640]{1,0:T(8,128)(2,1)S(1)}, bf16[512,640]{1,0:T(8,128)(2,1)S(1)}, u32[]{:S(2)}, u32[]{:S(2)}) collective-permute-start(bf16[512,640]{1,0:T(8,128)(2,1)S(1)} %shard_map.133), channel_id=1, source_target_pairs={{0,8},{4,12},{8,0},{12,4},{1,9},{5,13},{9,1},{13,5},{2,10},{6,14},... | collective-permute-start | bytes 1966088 | tf_op jit(solution)/shard_map/ppermute | solution.py:42
  44.0 18.6 %collective-permute-start.4 = (bf16[256,2560]{1,0:T(8,128)(2,1)}, bf16[256,2560]{1,0:T(8,128)(2,1)}, u32[]{:S(2)}, u32[]{:S(2)}) collective-permute-start(bf16[256,2560]{1,0:T(8,128)(2,1)} %shard_map.131), channel_id=1, source_target_pairs={{0,4},{4,0},{8,12},{12,8},{1,5},{5,1},{9,13},{13,9},{2,6},{6,2},{1... | collective-permute-start | bytes 3932168 | tf_op jit(solution)/shard_map/ppermute | solution.py:42
  46.4 15.3 %collective-permute-start.5 = (bf16[256,1024]{1,0:T(8,128)(2,1)}, bf16[256,1024]{1,0:T(8,128)(2,1)S(1)}, u32[]{:S(2)}, u32[]{:S(2)}) collective-permute-start(bf16[256,1024]{1,0:T(8,128)(2,1)} %collective-permute-done.2.refs_2_), channel_id=1, source_target_pairs={{0,4},{4,0},{8,12},{12,8},{1,5},{5,1},{9,13},{13,9},{2,6},{6,2},{1... | collective-permute-start | bytes 1572872 | tf_op jit(solution)/shard_map/ppermute | solution.py:42
  46.4 20.9 %collective-permute-start.7 = (bf16[640,640]{1,0:T(8,128)(2,1)}, bf16[640,640]{1,0:T(8,128)(2,1)}, u32[]{:S(2)}, u32[]{:S(2)}) collective-permute-start(bf16[640,640]{1,0:T(8,128)(2,1)} %shard_map.128.refs_1_), channel_id=1, source_target_pairs={{1,2},{2,1},{5,6},{6,5},{9,10},{10,9},{13,14},{14,13},{17,18},{18,... | collective-permute-start | bytes 2457608 | tf_op jit(solution)/shard_map/ppermute | solution.py:440
  48.0 21.5 %collective-permute-start.8 = (bf16[640,640]{1,0:T(8,128)(2,1)}, bf16[640,640]{1,0:T(8,128)(2,1)}, u32[]{:S(2)}, u32[]{:S(2)}) collective-permute-start(bf16[640,640]{1,0:T(8,128)(2,1)} %collective-permute-done.1.refs_3_), channel_id=1, source_target_pairs={{2,3},{1,0},{6,7},{5,4},{10,11},{9,8},{14,15},{13,12},{18,19},{17,... | collective-permute-start | bytes 2457608 | tf_op jit(solution)/shard_map/ppermute | solution.py:440
  56.9 5.7 %collective-permute-start.6 = (bf16[256,1536]{1,0:T(8,128)(2,1)}, bf16[256,1536]{1,0:T(8,128)(2,1)}, u32[]{:S(2)}, u32[]{:S(2)}) collective-permute-start(bf16[256,1536]{1,0:T(8,128)(2,1)} %collective-permute-done.3.refs_3_), channel_id=1, source_target_pairs={{0,4},{4,0},{8,12},{12,8},{1,5},{5,1},{9,13},{13,9},{2,6},{6,2},{1... | collective-permute-start | bytes 2359304 | tf_op jit(solution)/shard_map/ppermute | solution.py:42
  62.5 7.0 %collective-permute-start.10 = (bf16[512,640]{1,0:T(8,128)(2,1)}, bf16[512,640]{1,0:T(8,128)(2,1)S(1)}, u32[]{:S(2)}, u32[]{:S(2)}) collective-permute-start(bf16[512,640]{1,0:T(8,128)(2,1)} %shard_map.136), channel_id=1, source_target_pairs={{0,4},{4,0},{8,12},{12,8},{1,5},{5,1},{9,13},{13,9},{2,6},{6,2},{1... | collective-permute-start | bytes 1966088 | tf_op jit(solution)/shard_map/ppermute | solution.py:42
  73.7 10.0 %copy-start.32 = (f32[1024]{0:T(1024)S(1)}, f32[1024]{0:T(1024)}, u32[]{:S(2)}) copy-start(f32[1024]{0:T(1024)} %param.15) | copy-start | bytes 12292
  73.7 10.0 %copy-start.33 = (s32[1,256]{1,0:T(1,128)S(1)}, s32[1,256]{1,0:T(1,128)}, u32[]{:S(2)}) copy-start(s32[1,256]{1,0:T(1,128)} %param.13) | copy-start | bytes 3076
  73.7 29.1 %collective-permute-start.16 = (bf16[1024,256]{1,0:T(8,128)(2,1)S(1)}, bf16[1024,256]{1,0:T(8,128)(2,1)S(1)}, u32[]{:S(2)}, u32[]{:S(2)}) collective-permute-start(bf16[1024,256]{1,0:T(8,128)(2,1)S(1)} %get-tuple-element.116), channel_id=1, source_target_pairs={{0,16},{16,0},{1,17},{17,1},{2,18},{18,2},{3,19},{19,3},{4,20},{20... | collective-permute-start | bytes 1572872 | tf_op jit(solution)/shard_map/ppermute | solution.py:42
  81.5 23.0 %collective-permute-start.17 = (bf16[1024,384]{1,0:T(8,128)(2,1)S(1)}, bf16[1024,384]{1,0:T(8,128)(2,1)S(1)}, u32[]{:S(2)}, u32[]{:S(2)}) collective-permute-start(bf16[1024,384]{1,0:T(8,128)(2,1)S(1)} %get-tuple-element.111), channel_id=1, source_target_pairs={{0,16},{16,0},{1,17},{17,1},{2,18},{18,2},{3,19},{19,3},{4,20},{20... | collective-permute-start | bytes 2359304 | tf_op jit(solution)/shard_map/ppermute | solution.py:42
  81.8 3.6 %collective-permute-start.11 = (f32[2,2,1,256]{3,2,1,0:T(1,128)S(1)}, f32[2,2,1,256]{3,2,1,0:T(1,128)S(1)}, u32[]{:S(2)}, u32[]{:S(2)}) collective-permute-start(f32[2,2,1,256]{3,2,1,0:T(1,128)S(1)} %bitcast.64), channel_id=1, source_target_pairs={{0,4},{4,0},{8,12},{12,8},{1,5},{5,1},{9,13},{13,9},{2,6},{6,2},{1... | collective-permute-start | bytes 12296 | tf_op jit(solution)/shard_map/ppermute | solution.py:42
  85.1 2.8 %collective-permute-start.14 = (f32[1,1,256]{2,1,0:T(1,128)S(1)}, f32[1,1,256]{2,1,0:T(1,128)S(1)}, u32[]{:S(2)}, u32[]{:S(2)}) collective-permute-start(f32[1,1,256]{2,1,0:T(1,128)S(1)} %compare_select_fusion), channel_id=1, source_target_pairs={{0,8},{4,12},{8,0},{12,4},{1,9},{5,13},{9,1},{13,5},{2,10},{6,14},... | collective-permute-start | bytes 3080 | tf_op jit(solution)/shard_map/ppermute | solution.py:42
  85.4 3.3 %collective-permute-start.12 = (f32[2,2,1,256]{3,2,1,0:T(1,128)S(1)}, f32[2,2,1,256]{3,2,1,0:T(1,128)S(1)}, u32[]{:S(2)}, u32[]{:S(2)}) collective-permute-start(f32[2,2,1,256]{3,2,1,0:T(1,128)S(1)} %reverse_add_fusion.2), channel_id=1, source_target_pairs={{0,8},{4,12},{8,0},{12,4},{1,9},{5,13},{9,1},{13,5},{2,10},{6,14},... | collective-permute-start | bytes 12296 | tf_op jit(solution)/shard_map/ppermute | solution.py:42
  87.9 2.2 %collective-permute-start.15 = (f32[2,1,256]{2,1,0:T(1,128)S(1)}, f32[2,1,256]{2,1,0:T(1,128)S(1)}, u32[]{:S(2)}, u32[]{:S(2)}) collective-permute-start(f32[2,1,256]{2,1,0:T(1,128)S(1)} %pad_maximum_fusion), channel_id=1, source_target_pairs={{0,4},{4,0},{8,12},{12,8},{1,5},{5,1},{9,13},{13,9},{2,6},{6,2},{1... | collective-permute-start | bytes 6152 | tf_op jit(solution)/shard_map/ppermute | solution.py:42
  88.8 14.0 %collective-permute-start.13 = (f32[4,1,256]{2,1,0:T(1,128)S(1)}, f32[4,1,256]{2,1,0:T(1,128)S(1)}, u32[]{:S(2)}, u32[]{:S(2)}) collective-permute-start(f32[4,1,256]{2,1,0:T(1,128)S(1)} %bitcast.51), channel_id=1, source_target_pairs={{0,16},{16,0},{1,17},{17,1},{2,18},{18,2},{3,19},{19,3},{4,20},{20... | collective-permute-start | bytes 12296 | tf_op jit(solution)/shard_map/ppermute | solution.py:42
  106.3 3.2 %collective-permute-start.18 = (f32[2,2,2,256]{3,2,1,0:T(2,128)S(1)}, f32[2,2,2,256]{3,2,1,0:T(2,128)S(1)}, u32[]{:S(2)}, u32[]{:S(2)}) collective-permute-start(f32[2,2,2,256]{3,2,1,0:T(2,128)S(1)} %bitcast.55), channel_id=1, source_target_pairs={{0,4},{4,0},{8,12},{12,8},{1,5},{5,1},{9,13},{13,9},{2,6},{6,2},{1... | collective-permute-start | bytes 24584 | tf_op jit(solution)/shard_map/ppermute | solution.py:42
  109.5 2.5 %collective-permute-start.19 = (f32[2,2,2,256]{3,2,1,0:T(2,128)S(1)}, f32[2,2,2,256]{3,2,1,0:T(2,128)S(1)}, u32[]{:S(2)}, u32[]{:S(2)}) collective-permute-start(f32[2,2,2,256]{3,2,1,0:T(2,128)S(1)} %reverse_add_fusion.1), channel_id=1, source_target_pairs={{0,8},{4,12},{8,0},{12,4},{1,9},{5,13},{9,1},{13,5},{2,10},{6,14},... | collective-permute-start | bytes 24584 | tf_op jit(solution)/shard_map/ppermute | solution.py:42
  116.2 7.0 %collective-permute-start.22 = (bf16[512,512]{1,0:T(8,128)(2,1)S(1)}, bf16[512,512]{1,0:T(8,128)(2,1)S(1)}, u32[]{:S(2)}, u32[]{:S(2)}) collective-permute-start(bf16[512,512]{1,0:T(8,128)(2,1)S(1)} %shard_map.144), channel_id=1, source_target_pairs={{0,4},{4,0},{8,12},{12,8},{1,5},{5,1},{9,13},{13,9},{2,6},{6,2},{1... | collective-permute-start | bytes 1572872 | tf_op jit(solution)/shard_map/ppermute | solution.py:42
  118.3 5.0 %collective-permute-start.23 = (bf16[512,512]{1,0:T(8,128)(2,1)S(1)}, bf16[512,512]{1,0:T(8,128)(2,1)S(1)}, u32[]{:S(2)}, u32[]{:S(2)}) collective-permute-start(bf16[512,512]{1,0:T(8,128)(2,1)S(1)} %shard_map.148), channel_id=1, source_target_pairs={{0,4},{4,0},{8,12},{12,8},{1,5},{5,1},{9,13},{13,9},{2,6},{6,2},{1... | collective-permute-start | bytes 1572872 | tf_op jit(solution)/shard_map/ppermute | solution.py:42
  118.4 18.9 %collective-permute-start.21 = (bf16[640,640]{1,0:T(8,128)(2,1)S(1)}, bf16[640,640]{1,0:T(8,128)(2,1)S(1)}, u32[]{:S(2)}, u32[]{:S(2)}) collective-permute-start(bf16[640,640]{1,0:T(8,128)(2,1)S(1)} %get-tuple-element.119), channel_id=1, source_target_pairs={{0,1},{3,2},{4,5},{7,6},{8,9},{11,10},{12,13},{15,14},{16,17},{19,... | collective-permute-start | bytes 2457608 | tf_op jit(solution)/shard_map/ppermute | solution.py:440
  119.8 17.6 %collective-permute-start.20 = (bf16[640,640]{1,0:T(8,128)(2,1)S(1)}, bf16[640,640]{1,0:T(8,128)(2,1)S(1)}, u32[]{:S(2)}, u32[]{:S(2)}) collective-permute-start(bf16[640,640]{1,0:T(8,128)(2,1)S(1)} %get-tuple-element.119), channel_id=1, source_target_pairs={{1,2},{2,1},{5,6},{6,5},{9,10},{10,9},{13,14},{14,13},{17,18},{18,... | collective-permute-start | bytes 2457608 | tf_op jit(solution)/shard_map/ppermute | solution.py:440
  121.3 4.0 %collective-permute-start.24 = (bf16[512,512]{1,0:T(8,128)(2,1)S(1)}, bf16[512,512]{1,0:T(8,128)(2,1)S(1)}, u32[]{:S(2)}, u32[]{:S(2)}) collective-permute-start(bf16[512,512]{1,0:T(8,128)(2,1)S(1)} %shard_map.149), channel_id=1, source_target_pairs={{0,4},{4,0},{8,12},{12,8},{1,5},{5,1},{9,13},{13,9},{2,6},{6,2},{1... | collective-permute-start | bytes 1572872 | tf_op jit(solution)/shard_map/ppermute | solution.py:42
  123.2 12.4 %collective-permute-start.25 = (bf16[512,512]{1,0:T(8,128)(2,1)S(1)}, bf16[512,512]{1,0:T(8,128)(2,1)S(1)}, u32[]{:S(2)}, u32[]{:S(2)}) collective-permute-start(bf16[512,512]{1,0:T(8,128)(2,1)S(1)} %shard_map.153), channel_id=1, source_target_pairs={{0,4},{4,0},{8,12},{12,8},{1,5},{5,1},{9,13},{13,9},{2,6},{6,2},{1... | collective-permute-start | bytes 1572872 | tf_op jit(solution)/shard_map/ppermute | solution.py:42
  123.3 12.3 %collective-permute-start.26 = (bf16[512,512]{1,0:T(8,128)(2,1)S(1)}, bf16[512,512]{1,0:T(8,128)(2,1)S(1)}, u32[]{:S(2)}, u32[]{:S(2)}) collective-permute-start(bf16[512,512]{1,0:T(8,128)(2,1)S(1)} %shard_map.154), channel_id=1, source_target_pairs={{0,4},{4,0},{8,12},{12,8},{1,5},{5,1},{9,13},{13,9},{2,6},{6,2},{1... | collective-permute-start | bytes 1572872 | tf_op jit(solution)/shard_map/ppermute | solution.py:42
  125.2 11.4 %collective-permute-start.27 = (bf16[256,512]{1,0:T(8,128)(2,1)S(1)}, bf16[256,512]{1,0:T(8,128)(2,1)S(1)}, u32[]{:S(2)}, u32[]{:S(2)}) collective-permute-start(bf16[256,512]{1,0:T(8,128)(2,1)S(1)} %get-tuple-element.128), channel_id=1, source_target_pairs={{0,8},{4,12},{8,0},{12,4},{1,9},{5,13},{9,1},{13,5},{2,10},{6,14},... | collective-permute-start | bytes 786440 | tf_op jit(solution)/shard_map/ppermute | solution.py:42
  137.3 14.7 %collective-permute-start.30 = (bf16[256,1024]{1,0:T(8,128)(2,1)}, bf16[256,1024]{1,0:T(8,128)(2,1)}, u32[]{:S(2)}, u32[]{:S(2)}) collective-permute-start(bf16[256,1024]{1,0:T(8,128)(2,1)} %get-tuple-element.135), channel_id=1, source_target_pairs={{0,8},{4,12},{8,0},{12,4},{1,9},{5,13},{9,1},{13,5},{2,10},{6,14},... | collective-permute-start | bytes 1572872 | tf_op jit(solution)/shard_map/ppermute | solution.py:42
  138.6 25.0 %collective-permute-start.31 = (bf16[256,1024]{1,0:T(8,128)(2,1)}, bf16[256,1024]{1,0:T(8,128)(2,1)}, u32[]{:S(2)}, u32[]{:S(2)}) collective-permute-start(bf16[256,1024]{1,0:T(8,128)(2,1)} %get-tuple-element.147), channel_id=1, source_target_pairs={{0,8},{4,12},{8,0},{12,4},{1,9},{5,13},{9,1},{13,5},{2,10},{6,14},... | collective-permute-start | bytes 1572872 | tf_op jit(solution)/shard_map/ppermute | solution.py:42
  139.8 23.8 %collective-permute-start.28 = (bf16[640,384]{1,0:T(8,128)(2,1)}, bf16[640,384]{1,0:T(8,128)(2,1)}, u32[]{:S(2)}, u32[]{:S(2)}) collective-permute-start(bf16[640,384]{1,0:T(8,128)(2,1)} %shard_map.158), channel_id=1, source_target_pairs={{0,2},{1,3},{2,0},{3,1},{4,6},{5,7},{6,4},{7,5},{8,10},{9,11},{10,... | collective-permute-start | bytes 1474568 | tf_op jit(solution)/shard_map/ppermute | solution.py:42
  142.9 20.7 %collective-permute-start.29 = (bf16[640,384]{1,0:T(8,128)(2,1)}, bf16[640,384]{1,0:T(8,128)(2,1)}, u32[]{:S(2)}, u32[]{:S(2)}) collective-permute-start(bf16[640,384]{1,0:T(8,128)(2,1)} %shard_map.156), channel_id=1, source_target_pairs={{0,1},{1,0},{2,3},{3,2},{4,5},{5,4},{6,7},{7,6},{8,9},{9,8},{10,11... | collective-permute-start | bytes 1474568 | tf_op jit(solution)/shard_map/ppermute | solution.py:42
  152.0 11.6 %copy-start.10 = (bf16[1920,256]{1,0:T(8,128)(2,1)S(1)}, bf16[1920,256]{1,0:T(8,128)(2,1)}, u32[]{:S(2)}) copy-start(bf16[1920,256]{1,0:T(8,128)(2,1)} %copy-done.9) | copy-start | bytes 2949124
  152.0 14.1 %copy-start.16 = (bf16[640,640]{1,0:T(8,128)(2,1)S(1)}, bf16[640,640]{1,0:T(8,128)(2,1)}, u32[]{:S(2)}) copy-start(bf16[640,640]{1,0:T(8,128)(2,1)} %copy-done.15) | copy-start | bytes 2457604
  163.7 16.8 %collective-permute-start.32 = (bf16[640,256]{1,0:T(8,128)(2,1)S(1)}, bf16[640,256]{1,0:T(8,128)(2,1)S(1)}, u32[]{:S(2)}, u32[]{:S(2)}) collective-permute-start(bf16[640,256]{1,0:T(8,128)(2,1)S(1)} %shard_map.161), channel_id=1, source_target_pairs={{0,2},{1,3},{2,0},{3,1},{4,6},{5,7},{6,4},{7,5},{8,10},{9,11},{10,... | collective-permute-start | bytes 983048 | tf_op jit(solution)/shard_map/ppermute | solution.py:42
  165.4 15.1 %collective-permute-start.33 = (bf16[640,256]{1,0:T(8,128)(2,1)S(1)}, bf16[640,256]{1,0:T(8,128)(2,1)S(1)}, u32[]{:S(2)}, u32[]{:S(2)}) collective-permute-start(bf16[640,256]{1,0:T(8,128)(2,1)S(1)} %copy-done.27), channel_id=1, source_target_pairs={{0,1},{1,0},{2,3},{3,2},{4,5},{5,4},{6,7},{7,6},{8,9},{9,8},{10,11... | collective-permute-start | bytes 983048 | tf_op jit(solution)/shard_map/ppermute | solution.py:42
  167.6 15.5 %collective-permute-start.37 = (bf16[640,384]{1,0:T(8,128)(2,1)S(1)}, bf16[640,384]{1,0:T(8,128)(2,1)S(1)}, u32[]{:S(2)}, u32[]{:S(2)}) collective-permute-start(bf16[640,384]{1,0:T(8,128)(2,1)S(1)} %shard_map.164.refs_0_), channel_id=1, source_target_pairs={{0,8},{4,12},{8,0},{12,4},{1,9},{5,13},{9,1},{13,5},{2,10},{6,14},... | collective-permute-start | bytes 1474568 | tf_op jit(solution)/shard_map/ppermute | solution.py:42
  180.7 7.9 %collective-permute-start.34 = (bf16[640,256]{1,0:T(8,128)(2,1)S(1)}, bf16[640,256]{1,0:T(8,128)(2,1)S(1)}, u32[]{:S(2)}, u32[]{:S(2)}) collective-permute-start(bf16[640,256]{1,0:T(8,128)(2,1)S(1)} %shard_map.163.refs_0_), channel_id=1, source_target_pairs={{0,8},{4,12},{8,0},{12,4},{1,9},{5,13},{9,1},{13,5},{2,10},{6,14},... | collective-permute-start | bytes 983048 | tf_op jit(solution)/shard_map/ppermute | solution.py:42
  181.9 9.0 %collective-permute-start.38 = (bf16[640,384]{1,0:T(8,128)(2,1)S(1)}, bf16[640,384]{1,0:T(8,128)(2,1)S(1)}, u32[]{:S(2)}, u32[]{:S(2)}) collective-permute-start(bf16[640,384]{1,0:T(8,128)(2,1)S(1)} %shard_map.164.refs_0_), channel_id=1, source_target_pairs={{0,4},{4,0},{8,12},{12,8},{1,5},{5,1},{9,13},{13,9},{2,6},{6,2},{1... | collective-permute-start | bytes 1474568 | tf_op jit(solution)/shard_map/ppermute | solution.py:42
  183.1 7.8 %collective-permute-start.39 = (bf16[640,384]{1,0:T(8,128)(2,1)S(1)}, bf16[640,384]{1,0:T(8,128)(2,1)S(1)}, u32[]{:S(2)}, u32[]{:S(2)}) collective-permute-start(bf16[640,384]{1,0:T(8,128)(2,1)S(1)} %collective-permute-done.37.refs_1_), channel_id=1, source_target_pairs={{0,4},{4,0},{8,12},{12,8},{1,5},{5,1},{9,13},{13,9},{2,6},{6,2},{1... | collective-permute-start | bytes 1474568 | tf_op jit(solution)/shard_map/ppermute | solution.py:42
  183.1 9.8 %collective-permute-start.35 = (bf16[640,256]{1,0:T(8,128)(2,1)S(1)}, bf16[640,256]{1,0:T(8,128)(2,1)S(1)}, u32[]{:S(2)}, u32[]{:S(2)}) collective-permute-start(bf16[640,256]{1,0:T(8,128)(2,1)S(1)} %shard_map.163.refs_0_), channel_id=1, source_target_pairs={{0,4},{4,0},{8,12},{12,8},{1,5},{5,1},{9,13},{13,9},{2,6},{6,2},{1... | collective-permute-start | bytes 983048 | tf_op jit(solution)/shard_map/ppermute | solution.py:42
  188.6 4.3 %collective-permute-start.36 = (bf16[640,256]{1,0:T(8,128)(2,1)S(1)}, bf16[640,256]{1,0:T(8,128)(2,1)S(1)}, u32[]{:S(2)}, u32[]{:S(2)}) collective-permute-start(bf16[640,256]{1,0:T(8,128)(2,1)S(1)} %collective-permute-done.34.refs_1_), channel_id=1, source_target_pairs={{0,4},{4,0},{8,12},{12,8},{1,5},{5,1},{9,13},{13,9},{2,6},{6,2},{1... | collective-permute-start | bytes 983048 | tf_op jit(solution)/shard_map/ppermute | solution.py:42
  (27 other events, 76.9 us)
